TPU v7x, 32 devices: a whole 2x2x4 slice. The times are simulated.
32 devices in a mesh: dp: 4 (over y, x), seq: 8 (over z, core).
Axes of the slice: x: 2, y: 2, z: 4, core: 2. Of those that a mesh axis runs over, the one named last changes fastest.
Arguments:
- inputs: bfloat16 [8, 1024, 768], P('dp', 'seq'), may hold values from -6 to 6
- segments: int32 [8, 1024], P('dp', 'seq'), may hold values from 0 to 10, as said below
- cotangent: bfloat16 [8, 1024, 768], P('dp', 'seq'), may hold values from -6 to 6
- ln1_gain: bfloat16 [768], P(('dp', 'seq')), may hold values from 0.5 to 1.5
- ln1_bias: bfloat16 [768], P(('dp', 'seq')), may hold values from -3 to 3
- w_qkv: bfloat16 [1769472], P(('dp', 'seq')), may hold values from -0.3125 to 0.3125
- b_qv: bfloat16 [1536], P(('dp', 'seq')), may hold values from -3 to 3
- w_out: bfloat16 [589824], P(('dp', 'seq')), may hold values from -1.75 to 1.75
- b_out: bfloat16 [768], P(('dp', 'seq')), may hold values from -3 to 3
- ln2_gain: bfloat16 [768], P(('dp', 'seq')), may hold values from 0.5 to 1.5
- ln2_bias: bfloat16 [768], P(('dp', 'seq')), may hold values from -3 to 3
- w_fc: bfloat16 [2359296], P(('dp', 'seq')), may hold values from -0.21875 to 0.21875
- b_fc: bfloat16 [3072], P(('dp', 'seq')), may hold values from -3 to 3
- w_proj: bfloat16 [2359296], P(('dp', 'seq')), may hold values from -0.15625 to 0.15625
- b_proj: bfloat16 [768], P(('dp', 'seq')), may hold values from -3 to 3
Outputs:
- outputs: bfloat16 [8, 1024, 768], P('dp', 'seq')
- grad_inputs: bfloat16 [8, 1024, 768], P('dp', 'seq')
- grad_ln1_gain: float32 [768], P(('dp', 'seq'))
- grad_ln1_bias: float32 [768], P(('dp', 'seq'))
- grad_w_qkv: float32 [1769472], P(('dp', 'seq'))
- grad_b_qv: float32 [1536], P(('dp', 'seq'))
- grad_w_out: float32 [589824], P(('dp', 'seq'))
- grad_b_out: float32 [768], P(('dp', 'seq'))
- grad_ln2_gain: float32 [768], P(('dp', 'seq'))
- grad_ln2_bias: float32 [768], P(('dp', 'seq'))
- grad_w_fc: float32 [2359296], P(('dp', 'seq'))
- grad_b_fc: float32 [3072], P(('dp', 'seq'))
- grad_w_proj: float32 [2359296], P(('dp', 'seq'))
- grad_b_proj: float32 [768], P(('dp', 'seq'))
Inputs may be any that keep to these rules, and one draw needn't show every extreme that they name: `segments`: along each sequence the document numbers start at 0 and rise by one from each document to the next; documents are consecutive runs of tokens. Every document has 102 tokens or more, except possibly the first or the last of a sequence.
All inputs are finite; a program needn't handle non-finite values.
Results may differ from a plain program's by a relative error of at most 0.014.
Values may be sent and summed in bfloat16 or wider, within the bound.
No kernel may reach another device: no remote copies, remote signals or barrier semaphores. Data moves between devices by JAX's collectives and lax.ppermute only.
A program may use at most 192 MiB of HBM per device.

v0:
```python
import functools

import jax
import jax.numpy as jnp
from jax import lax
from jax.experimental import pallas as pl
from jax.experimental.pallas import tpu as pltpu
from jax.sharding import PartitionSpec as P

HEADS = 12
CORES = 2


EPSILON = 1e-05
MASKED = -1e30
F32 = jnp.float32
BF16 = jnp.bfloat16


def norm_affine(values, gain, bias):
    center = jnp.mean(values, -1, keepdims=True)
    centered = values - center
    variance = jnp.mean(centered * centered, -1, keepdims=True)
    return centered * lax.rsqrt(variance + EPSILON) * gain + bias


def shift_z(value, step):
    size = lax.axis_size("seq")
    return lax.ppermute(value, "seq", [(i, (i + CORES * step) % size) for i in range(size)])


def swap_core(value):
    size = lax.axis_size("seq")
    return lax.ppermute(value, "seq", [(i, i ^ 1) for i in range(size)])


def swap_dp(value, bit):
    size = lax.axis_size("dp")
    return lax.ppermute(value, "dp", [(i, i ^ bit) for i in range(size)])


def ordered(flag, mine, other, axis):
    first = jnp.where(flag == 0, mine, other)
    second = jnp.where(flag == 0, other, mine)
    return jnp.stack([first, second], axis)


def roll_blocks(pieces, place):
    count = len(pieces)
    stacked = jnp.stack(pieces)
    twice = jnp.concatenate([stacked, stacked])
    return lax.dynamic_slice_in_dim(twice, lax.rem(count - place, count), count, 0)


def gather_z(shard):
    heights = lax.axis_size("seq") // CORES
    level = lax.axis_index("seq") // CORES
    pieces = [shard] + [shift_z(shard, -step) for step in range(1, heights)]
    return roll_blocks(pieces, level)


def gather_plane(tower):
    heights = tower.shape[0]
    shard = tower.shape[1:]
    core = lax.axis_index("seq") % CORES
    if lax.axis_size("dp") == 4:
        plane = lax.axis_index("dp")
        y, x = plane // 2, plane % 2
        low, high = tower[: heights // 2], tower[heights // 2 :]
        low_x = ordered(x, low, swap_dp(low, 1), 0)
        high_y = ordered(y, high, swap_dp(high, 2), 0)
        low_all = ordered(y, low_x, swap_dp(low_x, 2), 0)
        high_all = ordered(x, high_y, swap_dp(high_y, 1), 1)
        half = jnp.concatenate([low_all, high_all], 2)
    else:
        half = lax.all_gather(tower, "dp", axis=0, tiled=False)
    half = half.reshape(-1, *shard)
    return ordered(core, half, swap_core(half), 1).reshape(-1, *shard)


def pick(value, index, axis):
    return lax.dynamic_index_in_dim(value, index, axis, keepdims=False)


def split_cores(parts):
    core = lax.axis_index("seq") % CORES
    parts = [part.reshape(-1, CORES, *part.shape[1:]) for part in parts]
    send = jnp.concatenate([pick(part, 1 - core, 1) for part in parts], 1)
    keep = jnp.concatenate([pick(part, core, 1) for part in parts], 1)
    return send, keep


def scatter_sum(send, keep):
    kind = send.dtype
    rows, columns = send.shape[1:]
    planes = lax.axis_size("dp")
    heights = lax.axis_size("seq") // CORES
    level = lax.axis_index("seq") // CORES

    def add(mine, other):
        return (mine.astype(F32) + other.astype(F32)).astype(kind)

    split = add(keep, swap_core(send))
    if planes == 4:
        plane = lax.axis_index("dp")
        y, x = plane // 2, plane % 2
        split = split.reshape(2, 2, heights, rows, columns)
        low, high = split[:, :, : heights // 2], split[:, :, heights // 2 :]
        low = add(pick(low, y, 0), swap_dp(pick(low, 1 - y, 0), 2))
        high = add(pick(high, x, 1), swap_dp(pick(high, 1 - x, 1), 1))
        low = add(pick(low, x, 0), swap_dp(pick(low, 1 - x, 0), 1))
        high = add(pick(high, y, 0), swap_dp(pick(high, 1 - y, 0), 2))
        tower = jnp.concatenate([low, high], 0)
    else:
        split = split.reshape(planes, heights, rows, columns)
        tower = lax.psum_scatter(split, "dp", scatter_dimension=0, tiled=False)
    mine = pick(tower, level, 0).astype(F32)
    for step in range(1, heights):
        mine += shift_z(pick(tower, lax.rem(level + step, heights), 0), step).astype(F32)
    return mine


def exchange(blocks):
    return lax.all_to_all(blocks, "seq", split_axis=0, concat_axis=0, tiled=True)


ROWS = 8
LANES = 128


def vmem_specs(count):
    return [pl.BlockSpec(memory_space=pltpu.VMEM) for _ in range(count)]


def place_lanes(size, total):
    source = lax.broadcasted_iota(jnp.int32, (LANES, total), 0)
    target = lax.rem(lax.broadcasted_iota(jnp.int32, (LANES, total), 1), size)
    return jnp.where(source == target, 1.0, 0.0).astype(BF16)


def owned_lanes(devices, size):
    device = lax.broadcasted_iota(jnp.int32, (devices, devices * size), 0)
    lane = lax.broadcasted_iota(jnp.int32, (devices, devices * size), 1)
    offset = lane - device * size
    return (offset >= 0) & (offset < size)


def unpack_kernel(sizes, small_ref, *outs):
    devices = small_ref.shape[0]
    small = small_ref[...].astype(F32)
    for i, (size, out) in enumerate(zip(sizes, outs)):
        spread = jnp.dot(
            small[:, i, :].astype(BF16),
            place_lanes(size, devices * size),
            preferred_element_type=F32,
        )
        out[...] = jnp.sum(jnp.where(owned_lanes(devices, size), spread, 0.0), 0, keepdims=True)


def unpack_small(small, sizes):
    devices = small.shape[0]
    return pl.pallas_call(
        functools.partial(unpack_kernel, sizes),
        out_shape=[jax.ShapeDtypeStruct((1, devices * size), F32) for size in sizes],
        in_specs=vmem_specs(1),
        out_specs=vmem_specs(len(sizes)),
        compiler_params=pltpu.CompilerParams(vmem_limit_bytes=32 * 2**20),
    )(small)


def pack_kernel(sizes, *refs):
    grads, packed, rows = refs[: len(sizes)], refs[len(sizes)], refs[len(sizes) + 1]
    devices = packed.shape[0]
    for i, (size, grad) in enumerate(zip(sizes, grads)):
        owned = jnp.where(owned_lanes(devices, size), grad[...], 0.0).astype(BF16)
        rows[:, i, :] = lax.dot_general(
            owned,
            place_lanes(size, devices * size),
            (((1,), (1,)), ((), ())),
            preferred_element_type=F32,
        )
    packed[...] = rows[...].astype(BF16)


def pack_small(grads, sizes, devices):
    return pl.pallas_call(
        functools.partial(pack_kernel, sizes),
        out_shape=jax.ShapeDtypeStruct((devices, ROWS, LANES), BF16),
        in_specs=vmem_specs(len(sizes)),
        out_specs=vmem_specs(1)[0],
        scratch_shapes=[pltpu.VMEM((devices, ROWS, LANES), F32)],
        compiler_params=pltpu.CompilerParams(vmem_limit_bytes=32 * 2**20),
    )(*grads)


def stack_kernel(out_ref, fc_ref, proj_ref, after_ref, stacked):
    width = out_ref.shape[1]
    stacked[0] = out_ref[...]
    parts = fc_ref.shape[1] // width
    for i in range(parts):
        stacked[1 + i] = fc_ref[:, i * width : (i + 1) * width]
    for i in range(parts):
        stacked[1 + parts + i] = proj_ref[i]


def stack_weights(w_out, w_fc, w_proj, after):
    rows, width = w_out.shape
    parts = w_fc.shape[1] // width
    return pl.pallas_call(
        stack_kernel,
        out_shape=jax.ShapeDtypeStruct((1 + 2 * parts, rows, width), BF16),
        in_specs=vmem_specs(3) + [pl.BlockSpec(memory_space=pl.ANY)],
        out_specs=vmem_specs(1)[0],
    )(w_out, w_fc, w_proj, after)


def masked_scores(keys, queries, id_column, id_row, first, last):
    scores = lax.dot_general(keys, queries, (((1,), (1,)), ((), ())), preferred_element_type=F32)
    key_pos = lax.broadcasted_iota(jnp.int32, scores.shape, 0)
    query_pos = lax.broadcasted_iota(jnp.int32, scores.shape, 1) + first
    allowed = (key_pos <= query_pos) & (id_column == id_row)
    return jnp.where(allowed, scores, MASKED)


def read_ids(whole):
    width = whole.shape[1]
    tail = whole[:, width - 128 :].astype(F32)
    return tail[:, 127:128], tail.T[127:128, :]


def forward_kernel(heads, head_size, step_rows, block, whole, out, stats, result):
    length = whole.shape[0]
    group = heads * head_size
    id_column, id_row = read_ids(whole)
    values_t = whole[:, 2 * group : 3 * group].astype(F32).T.astype(BF16)
    for first in range(0, length, step_rows):
        last = first + step_rows
        tops = []
        for head in range(heads):
            lo = head * head_size
            queries = whole[first:last, lo : lo + head_size] * BF16(head_size**-0.5)
            keys = whole[:last, group + lo : group + lo + head_size]
            scores = masked_scores(
                keys, queries, id_column[:last], id_row[:, first:last], first, last
            )
            highest = jnp.max(scores, 0, keepdims=True)
            weights = jnp.exp(scores - highest)
            total = jnp.sum(weights, 0, keepdims=True)
            probs = (weights * (1.0 / total)).astype(BF16)
            tops.append(
                jnp.dot(
                    values_t[lo : lo + head_size, :last], probs, preferred_element_type=F32
                )
            )
            stats[head : head + 1, first:last] = highest + jnp.log(total)
        result[first:last, :] = jnp.concatenate(tops, 0).T.astype(BF16)
    half = block // 2
    for start in range(0, length, block):
        out[start // 2 : start // 2 + half, :group] = result[start : start + half, :]
        out[start // 2 : start // 2 + half, group:] = result[start + half : start + block, :]


def backward_kernel(
    heads,
    head_size,
    step_rows,
    block,
    whole,
    grads,
    stats,
    out,
    grad_out,
    grad_query,
    grad_key,
    grad_value,
):
    length = whole.shape[0]
    group = heads * head_size
    half = block // 2
    for start in range(0, length, block):
        packed = grads[start // 2 : start // 2 + half, :]
        grad_out[start : start + half, :] = packed[:, :group]
        grad_out[start + half : start + block, :] = packed[:, group:]
    id_column, id_row = read_ids(whole)
    keys_t = whole[:, group : 2 * group].astype(F32).T.astype(BF16)
    factor = head_size**-0.5
    grad_key[...] = jnp.zeros_like(grad_key)
    grad_value[...] = jnp.zeros_like(grad_value)
    for first in range(0, length, step_rows):
        last = first + step_rows
        tops = []
        for head in range(heads):
            lo = head * head_size
            queries = whole[first:last, lo : lo + head_size] * BF16(factor)
            keys = whole[:last, group + lo : group + lo + head_size]
            values = whole[:last, 2 * group + lo : 2 * group + lo + head_size]
            grad = grad_out[first:last, lo : lo + head_size]
            scores = masked_scores(
                keys, queries, id_column[:last], id_row[:, first:last], first, last
            )
            probs = jnp.exp(scores - stats[head : head + 1, first:last])
            grad_probs = lax.dot_general(
                values, grad, (((1,), (1,)), ((), ())), preferred_element_type=F32
            )
            delta = jnp.sum(probs * grad_probs, 0, keepdims=True)
            grad_scores = (probs * (grad_probs - delta)).astype(BF16)
            tops.append(
                jnp.dot(
                    keys_t[lo : lo + head_size, :last], grad_scores, preferred_element_type=F32
                )
                * factor
            )
            grad_key[head, :last, :] += jnp.dot(
                grad_scores, queries, preferred_element_type=F32
            )
            grad_value[head, :last, :] += jnp.dot(
                probs.astype(BF16), grad, preferred_element_type=F32
            )
        grad_query[first:last, :] = jnp.concatenate(tops, 0).T.astype(BF16)
    out[:, :group] = grad_query[...]
    for head in range(heads):
        lo = head * head_size
        out[:, group + lo : group + lo + head_size] = grad_key[head].astype(BF16)
        out[:, 2 * group + lo : 2 * group + lo + head_size] = grad_value[head].astype(BF16)


def attend_forward(whole, heads, head_size, block):
    length, width = whole.shape
    group = heads * head_size
    pairs = length * length // 2 * heads
    return pl.pallas_call(
        functools.partial(forward_kernel, heads, head_size, min(256, length), block),
        out_shape=[
            jax.ShapeDtypeStruct((length // 2, 2 * group), BF16),
            jax.ShapeDtypeStruct((heads, length), F32),
        ],
        in_specs=vmem_specs(1),
        out_specs=vmem_specs(2),
        scratch_shapes=[pltpu.VMEM((length, group), BF16)],
        compiler_params=pltpu.CompilerParams(vmem_limit_bytes=48 * 2**20),
        cost_estimate=pl.CostEstimate(
            flops=pairs * head_size * 4, bytes_accessed=length * width * 3, transcendentals=pairs
        ),
    )(whole)


def attend_backward(whole, grads, stats, heads, head_size, block):
    length, width = whole.shape
    group = heads * head_size
    pairs = length * length // 2 * heads
    return pl.pallas_call(
        functools.partial(backward_kernel, heads, head_size, min(256, length), block),
        out_shape=jax.ShapeDtypeStruct((length, 3 * group), BF16),
        in_specs=vmem_specs(3),
        out_specs=vmem_specs(1)[0],
        scratch_shapes=[
            pltpu.VMEM((length, group), BF16),
            pltpu.VMEM((length, group), BF16),
            pltpu.VMEM((heads, length, head_size), F32),
            pltpu.VMEM((heads, length, head_size), F32),
        ],
        compiler_params=pltpu.CompilerParams(vmem_limit_bytes=48 * 2**20),
        cost_estimate=pl.CostEstimate(
            flops=pairs * head_size * 10, bytes_accessed=length * width * 6, transcendentals=pairs
        ),
    )(whole, grads, stats)


def on_device(
    inputs,
    segments,
    cotangent,
    ln1_gain,
    ln1_bias,
    w_qkv,
    b_qv,
    w_out,
    b_out,
    ln2_gain,
    ln2_bias,
    w_fc,
    b_fc,
    w_proj,
    b_proj,
):
    seq_count, block, width = inputs.shape
    head_size = width // HEADS
    tokens = seq_count * block
    count = lax.axis_size("seq")
    devices = count * lax.axis_size("dp")
    groups = count // seq_count
    heads = -(-HEADS // groups)
    spare = groups * heads - HEADS
    group = heads * head_size

    vectors = (ln1_gain, ln1_bias, b_qv, b_out, ln2_gain, ln2_bias, b_fc, b_proj)
    sizes = tuple(vector.shape[0] for vector in vectors)
    shard_rows = w_out.shape[0] // width
    parts = w_fc.shape[0] // w_out.shape[0]
    small = [jnp.pad(vector[None], ((0, 0), (0, width - vector.shape[0]))) for vector in vectors]
    thirds = w_qkv.reshape(shard_rows, 3, width).transpose(1, 0, 2).reshape(-1, width)
    tower_a = gather_z(jnp.concatenate([thirds] + small, 0))
    stacked = stack_weights(
        w_out.reshape(-1, width),
        w_fc.reshape(-1, parts * width),
        w_proj.reshape(parts, -1, width),
        tower_a,
    )
    tower_b = gather_z(stacked)
    whole_a = gather_plane(tower_a)
    whole_b = gather_plane(tower_b)
    gain1, bias1, bqv, bout, gain2, bias2, bfc, bproj = unpack_small(
        whole_a[:, 3 * shard_rows :, :LANES], sizes
    )
    wqkv = jnp.concatenate(
        [whole_a[:, i * shard_rows : (i + 1) * shard_rows] for i in range(3)], -1
    ).reshape(width, 3 * width)
    wout = whole_b[:, 0].reshape(width, width)
    wfc = whole_b[:, 1 : 1 + parts].transpose(0, 2, 1, 3).reshape(width, parts * width)
    wproj = whole_b[:, 1 + parts :].reshape(parts * width, width)

    def by_group(value, parts):
        value = value.reshape(seq_count, block, parts, HEADS, head_size)
        if spare:
            value = jnp.pad(value, ((0, 0), (0, 0), (0, 0), (0, spare), (0, 0)))
        value = value.reshape(seq_count, block, parts, groups, group)
        return value.transpose(0, 3, 1, 2, 4).reshape(count, block, parts * group)

    def from_group(value, parts):
        value = value.reshape(seq_count, groups, block, parts, group).transpose(0, 2, 3, 1, 4)
        value = value.reshape(tokens, parts, groups * heads, head_size)
        return value[:, :, :HEADS].reshape(tokens, parts * width)

    def pack(value):
        value = value.reshape(value.shape[0], 2, block // 2, group).transpose(0, 2, 1, 3)
        return value.reshape(-1, block // 2, 2 * group)

    def unpack(value):
        value = value.reshape(value.shape[0], block // 2, 2, group).transpose(0, 2, 1, 3)
        return value.reshape(-1, block, group)

    rows = inputs.astype(F32).reshape(tokens, width)
    normed1 = norm_affine(rows, gain1, bias1).astype(BF16)
    qkv_bias = jnp.concatenate(
        [bqv[:, :width], jnp.zeros((1, width), F32), bqv[:, width:]], axis=1
    )
    qkv = (jnp.dot(normed1, wqkv, preferred_element_type=F32) + qkv_bias).astype(BF16)
    fill = -(3 * group) % 128 or 128
    ids = jnp.broadcast_to(
        segments.astype(BF16)[:, None, :, None], (seq_count, groups, block, fill)
    )
    blocks = jnp.concatenate([by_group(qkv, 3), ids.reshape(count, block, fill)], -1)
    whole = exchange(blocks).reshape(count * block, 3 * group + fill)
    attended, stats = attend_forward(whole, heads, head_size, block)
    attended = exchange(attended.reshape(count, block // 2, 2 * group))
    attended_rows = from_group(unpack(attended), 1)

    middle = rows + (jnp.dot(attended_rows, wout, preferred_element_type=F32) + bout)
    normed2 = norm_affine(middle, gain2, bias2).astype(BF16)
    hidden_pre = jnp.dot(normed2, wfc, preferred_element_type=F32) + bfc
    hidden = jax.nn.gelu(hidden_pre, approximate=True).astype(BF16)
    result_rows = middle + (jnp.dot(hidden, wproj, preferred_element_type=F32) + bproj)
    outputs = result_rows.astype(BF16).reshape(inputs.shape)

    grad_rows = cotangent.astype(F32).reshape(tokens, width)
    grad_branch = cotangent.reshape(tokens, width)
    grad_bproj = jnp.sum(grad_branch, 0, dtype=F32)
    grad_wproj = jnp.einsum("tf,td->fd", hidden, grad_branch, preferred_element_type=F32)
    grad_hidden = jnp.einsum("td,fd->tf", grad_branch, wproj, preferred_element_type=F32)
    _, gelu_back = jax.vjp(lambda value: jax.nn.gelu(value, approximate=True), hidden_pre)
    grad_pre = gelu_back(grad_hidden)[0].astype(BF16)
    grad_bfc = jnp.sum(grad_pre, 0, dtype=F32)
    grad_wfc = jnp.einsum("td,tf->df", normed2, grad_pre, preferred_element_type=F32)
    grad_normed2 = jnp.einsum("tf,df->td", grad_pre, wfc, preferred_element_type=F32)
    _, norm2_back = jax.vjp(norm_affine, middle, gain2, bias2)
    grad_mid_part, grad_gain2, grad_bias2 = norm2_back(grad_normed2)
    grad_middle = grad_rows + grad_mid_part
    grad_attn_out = grad_middle.astype(BF16)
    grad_bout = jnp.sum(grad_attn_out, 0, dtype=F32)
    grad_wout = jnp.einsum("td,te->de", attended_rows, grad_attn_out, preferred_element_type=F32)
    grad_attended = jnp.einsum("te,de->td", grad_attn_out, wout, preferred_element_type=F32)
    grad_blocks = exchange(pack(by_group(grad_attended.astype(BF16), 1)))
    by_part = grad_wfc.astype(BF16).reshape(devices, shard_rows, parts, width)
    send_b, keep_b = split_cores(
        [
            grad_wout.astype(BF16).reshape(devices, -1, width),
            by_part.transpose(0, 2, 1, 3).reshape(devices, -1, width),
            grad_wproj.astype(BF16).reshape(devices, -1, width),
        ]
    )
    own_b = scatter_sum(send_b, keep_b)

    grad_back = attend_backward(
        whole, grad_blocks.reshape(-1, 2 * group), stats, heads, head_size, block
    )
    grad_qkv = from_group(exchange(grad_back.reshape(count, block, 3 * group)), 3)
    grad_bqv = jnp.concatenate(
        [
            jnp.sum(grad_qkv[:, :width], 0, dtype=F32),
            jnp.sum(grad_qkv[:, 2 * width :], 0, dtype=F32),
        ]
    )
    grad_wqkv = jnp.einsum("td,te->de", normed1, grad_qkv, preferred_element_type=F32)
    grad_normed1 = jnp.einsum("te,de->td", grad_qkv, wqkv, preferred_element_type=F32)
    _, norm1_back = jax.vjp(norm_affine, rows, gain1, bias1)
    grad_in_part, grad_gain1, grad_bias1 = norm1_back(grad_normed1)
    grad_inputs = (grad_middle + grad_in_part).astype(BF16).reshape(inputs.shape)
    grads = (
        grad_gain1,
        grad_bias1,
        grad_bqv,
        grad_bout,
        grad_gain2,
        grad_bias2,
        grad_bfc,
        grad_bproj,
    )
    small_grads = pack_small([grad.reshape(1, -1) for grad in grads], sizes, devices)
    by_part = grad_wqkv.astype(BF16).reshape(devices, shard_rows, 3, width)
    send_a, keep_a = split_cores(
        [
            by_part.transpose(0, 2, 1, 3).reshape(devices, -1, width),
            jnp.pad(small_grads, ((0, 0), (0, 0), (0, width - LANES))),
        ]
    )
    own_a = scatter_sum(send_a, keep_a)
    own_small = own_a[3 * shard_rows :]
    own = [own_small[i, :size] for i, size in enumerate(sizes)]

    def by_row(value, parts):
        return value.reshape(parts, shard_rows, width).transpose(1, 0, 2).reshape(-1)

    own_fc = own_b[shard_rows : (1 + parts) * shard_rows]
    return (
        outputs,
        grad_inputs,
        own[0],
        own[1],
        by_row(own_a[: 3 * shard_rows], 3),
        own[2],
        own_b[:shard_rows].reshape(-1),
        own[3],
        own[4],
        own[5],
        by_row(own_fc, parts),
        own[6],
        own_b[(1 + parts) * shard_rows :].reshape(-1),
        own[7],
    )


def solution(mesh):
    token_spec = P("dp", "seq", None)
    flat_spec = P(("dp", "seq"))
    in_specs = (token_spec, P("dp", "seq"), token_spec) + (flat_spec,) * 12
    out_specs = (token_spec, token_spec) + (flat_spec,) * 12
    return jax.shard_map(
        on_device, mesh=mesh, in_specs=in_specs, out_specs=out_specs, check_vma=False
    )
```

profile of v0, /device:TPU:8, one launch (start us, length us, event | category | flops | bytes accessed | tf_op | source)
XLA Modules:
  0.0 437.6 jit_solution(13948182204292174591)
XLA Ops:
  16.4 4.4 %collective-permute-done = bf16[80,768]{1,0:T(8,128)(2,1)S(1)} collective-permute-done((bf16[80,768]{1,0:T(8,128)(2,1)S(1)}, bf16[80,768]{1,0:T(8,128)(2,1)S(1)}, u32[]{:S(2)}, u32[]{:S(2)}) %collective-permute-start) | collective-permute-done | bytes 122912 | tf_op jit(solution)/shard_map/ppermute | solution.py:29
  32.0 5.7 %collective-permute-done.5 = bf16[2,80,768]{2,1,0:T(8,128)(2,1)S(1)} collective-permute-done((bf16[2,80,768]{2,1,0:T(8,128)(2,1)S(1)}, bf16[2,80,768]{2,1,0:T(8,128)(2,1)S(1)}, u32[]{:S(2)}, u32[]{:S(2)}) %collective-permute-start.5) | collective-permute-done | bytes 245792 | tf_op jit(solution)/shard_map/ppermute | solution.py:39
  38.2 17.1 %collective-permute-done.8 = bf16[9,24,768]{2,1,0:T(8,128)(2,1)S(1)} collective-permute-done((bf16[9,24,768]{2,1,0:T(8,128)(2,1)}, bf16[9,24,768]{2,1,0:T(8,128)(2,1)S(1)}, u32[]{:S(2)}, u32[]{:S(2)}) %collective-permute-start.8) | collective-permute-done | bytes 331808 | tf_op jit(solution)/shard_map/ppermute | solution.py:29
  58.0 14.6 %collective-permute-done.11 = bf16[2,9,24,768]{3,2,1,0:T(8,128)(2,1)S(1)} collective-permute-done((bf16[2,9,24,768]{3,2,1,0:T(8,128)(2,1)S(1)}, bf16[2,9,24,768]{3,2,1,0:T(8,128)(2,1)S(1)}, u32[]{:S(2)}, u32[]{:S(2)}) %collective-permute-start.11) | collective-permute-done | bytes 663584 | tf_op jit(solution)/shard_map/ppermute | solution.py:39
  79.2 25.3 %collective-permute-done.12 = bf16[2,2,9,24,768]{4,3,2,1,0:T(8,128)(2,1)} collective-permute-done((bf16[2,2,9,24,768]{4,3,2,1,0:T(8,128)(2,1)}, bf16[2,2,9,24,768]{4,3,2,1,0:T(8,128)(2,1)}, u32[]{:S(2)}, u32[]{:S(2)}) %collective-permute-start.12) | collective-permute-done | bytes 1327136 | tf_op jit(solution)/shard_map/ppermute | solution.py:39
  123.8 33.3 %all_to_all.20 = bf16[8,128,640]{1,2,0:T(8,128)(2,1)} all-to-all(bf16[8,128,640]{1,2,0:T(8,128)(2,1)S(1)} %pad_maximum_fusion.7), channel_id=1, replica_groups=mesh['dp'=4,'seq'=8] {'seq'}, dimensions={0} | all-to-all | bytes 2621440 | tf_op jit(solution)/shard_map/all_to_all | solution.py:124
  158.9 7.9 %shard_map.255 = (bf16[512,384]{1,0:T(8,128)(2,1)}, f32[3,1024]{1,0:T(4,128)S(1)}) custom-call(bf16[1024,640]{1,0:T(8,128)(2,1)S(1)} %bitcast.308), custom_call_target="tpu_custom_call" | custom-call | flops 402653184 | bytes 1966080 | tf_op jit(solution)/shard_map/pallas_call | solution.py:331
  166.8 6.1 %all-to-all-start.1 = ((bf16[8,64,384]{2,1,0:T(8,128)(2,1)}), bf16[8,64,384]{2,1,0:T(8,128)(2,1)S(1)}, u32[]{:S(2)}, u32[]{:S(2)}) async-start(bf16[8,64,384]{2,1,0:T(8,128)(2,1)} %bitcast.34), calls=%async_computation.1 | async-start | bytes 786432 | tf_op jit(solution)/shard_map/all_to_all | solution.py:124
  172.9 9.9 %all-to-all-done.1 = bf16[8,64,384]{2,1,0:T(8,128)(2,1)S(1)} async-done(((bf16[8,64,384]{2,1,0:T(8,128)(2,1)}), bf16[8,64,384]{2,1,0:T(8,128)(2,1)S(1)}, u32[]{:S(2)}, u32[]{:S(2)}) %all-to-all-start.1) | async-done | bytes 393248 | tf_op jit(solution)/shard_map/all_to_all | solution.py:124
  183.7 8.8 %select_bitcast_fusion.1 = (bf16[16,1,9,24,768]{4,3,2,0,1:T(8,128)(2,1)}, bf16[16,1,9,24,768]{4,3,2,0,1:T(8,128)(2,1)}) fusion(bf16[16,9,24,768]{3,2,1,0:T(8,128)(2,1)} %collective-permute-done.15, pred[]{:T(512)S(6)} %eq.15, bf16[2,2,4,9,24,768]{5,4,3,2,1,0:T(8,128)(2,1)} %copy.84), kind=kLoop, calls=%fused_computation.5 | loop fusion | flops 5308416 | bytes 21233664 | tf_op jit(solution)/shard_map/stack | solution.py:45
  192.5 5.6 %pad_maximum_fusion = bf16[16,2,9,24,768]{4,3,2,0,1:T(8,128)(2,1)S(1)} fusion(bf16[16,1,9,24,768]{4,3,2,0,1:T(8,128)(2,1)} %get-tuple-element.50, bf16[16,1,9,24,768]{4,3,2,0,1:T(8,128)(2,1)} %get-tuple-element.49), kind=kLoop, calls=%fused_computation | loop fusion | flops 5308416 | bytes 21233664 | tf_op jit(solution)/shard_map/stack | solution.py:45
  203.6 6.6 %slice_bitcast_fusion = (bf16[32,24,4,768]{3,1,2,0:T(8,128)(2,1)S(1)}, bf16[32,4,24,768]{3,2,1,0:T(8,128)(2,1)}) fusion(bf16[32,9,24,768]{3,2,1,0:T(8,128)(2,1)} %bitcast.315), kind=kLoop, calls=%fused_computation.9 | loop fusion | bytes 18874368 | tf_op jit(solution)/shard_map/transpose | solution.py:419
  226.0 26.8 %all_to_all.21 = bf16[8,64,384]{2,1,0:T(8,128)(2,1)S(1)} all-to-all(bf16[8,64,384]{2,1,0:T(8,128)(2,1)S(1)} %reshape.312), channel_id=1, replica_groups=mesh['dp'=4,'seq'=8] {'seq'}, dimensions={0} | all-to-all | bytes 786432 | tf_op jit(solution)/shard_map/all_to_all | solution.py:124
  252.8 8.8 %shard_map.257 = bf16[1024,576]{1,0:T(8,128)(2,1)S(1)} custom-call(bf16[1024,640]{1,0:T(8,128)(2,1)S(1)} %bitcast.309, bf16[512,384]{1,0:T(8,128)(2,1)S(1)} %bitcast.311, f32[3,1024]{1,0:T(4,128)S(1)} %get-tuple-element.33.stats), custom_call_target="tpu_custom_call" | custom-call | flops 1006632960 | bytes 3932160 | tf_op jit(solution)/shard_map/pallas_call | solution.py:351
  263.1 6.1 %all-to-all-start.3 = ((bf16[8,128,576]{1,2,0:T(8,128)(2,1)}), bf16[8,128,576]{1,2,0:T(8,128)(2,1)}, u32[]{:S(2)}, u32[]{:S(2)}) async-start(bf16[8,128,576]{1,2,0:T(8,128)(2,1)} %copy.90), calls=%async_computation.3 | async-start | bytes 2359296 | tf_op jit(solution)/shard_map/all_to_all | solution.py:124
  273.0 9.7 %reshape.330 = bf16[32,24,4,768]{3,2,1,0:T(4,128)(2,1)} reshape(bf16[768,3072]{1,0:T(8,128)(2,1)} %convolution_convert_fusion.1) | data formatting | bytes 9437184 | tf_op jit(solution)/shard_map/reshape | solution.py:483
  288.2 4.4 %convolution_convert_fusion = bf16[3072,768]{1,0:T(8,128)(2,1)} fusion(bf16[256,768]{1,0:T(8,128)(2,1)S(1)} %bitcast.344, f32[256,3072]{1,0:T(8,128)S(1)} %copy-done.39), kind=kOutput, calls=%fused_computation.6 | convolution fusion | flops 1217396736 | bytes 8257536 | tf_op jit(solution)/shard_map/tf,td->fd/dot_general | solution.py:468
  292.6 5.4 %dynamic-slice_bitcast_fusion.2 = (bf16[16,96,768]{2,1,0:T(8,128)(2,1)}, bf16[16,96,768]{2,1,0:T(8,128)(2,1)S(1)}, bf16[16,96,768]{2,1,0:T(8,128)(2,1)S(1)}, bf16[16,96,768]{2,1,0:T(8,128)(2,1)}) fusion(bf16[16,2,96,768]{3,2,1,0:T(8,128)(2,1)} %bitcast.340, s32[]{:T(128)S(6)} %select_n.253, s32[]{:T(128)S(6)} %select_n.254, ...), kind=kLoop, calls=%fused_computation.34 | loop fusion | bytes 18874376 | tf_op jit(solution)/shard_map/jit(dynamic_index_in_dim)/squeeze | solution.py:82
  311.4 5.5 %reshape.317 = bf16[32,24,3,768]{3,2,1,0:T(4,128)(2,1)} reshape(bf16[768,2304]{1,0:T(8,128)(2,1)S(1)} %convolution_convert_fusion.2) | data formatting | bytes 7077888 | tf_op jit(solution)/shard_map/reshape | solution.py:519
  330.2 5.2 %fusion.14 = bf16[256,768]{1,0:T(8,128)(2,1)} fusion(f32[256,768]{1,0:T(8,128)S(1)} %copy-done.8, bf16[3072,768]{1,0:T(8,128)(2,1)} %bitcast.336, f32[768]{0:T(1024)S(1)} %reduce.9, f32[256,3072]{1,0:T(8,128)S(1)} %copy-done.40), kind=kOutput, calls=%fused_computation.68 | convolution fusion | flops 1215627264 | bytes 9047040 | tf_op jit(solution)/shard_map/dot_general | solution.py:462
  336.0 5.8 %collective-permute-done.17 = bf16[2,2,80,768]{3,2,1,0:T(8,128)(2,1)S(1)} collective-permute-done((bf16[2,2,80,768]{3,2,1,0:T(8,128)(2,1)S(1)}, bf16[2,2,80,768]{3,2,1,0:T(8,128)(2,1)S(1)}, u32[]{:S(2)}, u32[]{:S(2)}) %collective-permute-start.17) | collective-permute-done | bytes 491552 | tf_op jit(solution)/shard_map/ppermute | solution.py:39
  354.9 27.9 %collective-permute-done.20 = bf16[2,80,768]{2,1,0:T(8,128)(2,1)S(1)} collective-permute-done((bf16[2,80,768]{2,1,0:T(8,128)(2,1)S(1)}, bf16[2,80,768]{2,1,0:T(8,128)(2,1)S(1)}, u32[]{:S(2)}, u32[]{:S(2)}) %collective-permute-start.20) | collective-permute-done | bytes 245792 | tf_op jit(solution)/shard_map/ppermute | solution.py:39
  395.8 6.7 %collective-permute-done.26 = bf16[2,216,768]{2,1,0:T(8,128)(2,1)S(1)} collective-permute-done((bf16[2,216,768]{2,1,0:T(8,128)(2,1)S(1)}, bf16[2,216,768]{2,1,0:T(8,128)(2,1)S(1)}, u32[]{:S(2)}, u32[]{:S(2)}) %collective-permute-start.26) | collective-permute-done | bytes 663584 | tf_op jit(solution)/shard_map/ppermute | solution.py:39
  410.7 16.1 %collective-permute-done.29 = bf16[216,768]{1,0:T(8,128)(2,1)S(1)} collective-permute-done((bf16[216,768]{1,0:T(8,128)(2,1)S(1)}, bf16[216,768]{1,0:T(8,128)(2,1)S(1)}, u32[]{:S(2)}, u32[]{:S(2)}) %collective-permute-start.29) | collective-permute-done | bytes 331808 | tf_op jit(solution)/shard_map/ppermute | solution.py:29
  (314 shorter events, 161.4 us)
Async XLA Ops:
  7.0 13.9 %collective-permute-start.2 = (bf16[80,768]{1,0:T(8,128)(2,1)S(1)}, bf16[80,768]{1,0:T(8,128)(2,1)S(1)}, u32[]{:S(2)}, u32[]{:S(2)}) collective-permute-start(bf16[80,768]{1,0:T(8,128)(2,1)S(1)} %concatenate.47), channel_id=1, source_target_pairs={{0,2},{1,3},{2,4},{3,5},{4,6},{5,7},{6,0},{7,1},{8,10},{9,11},{10,... | collective-permute-start | bytes 368648 | tf_op jit(solution)/shard_map/ppermute | solution.py:29
  25.2 30.2 %collective-permute-start.10 = (bf16[9,24,768]{2,1,0:T(8,128)(2,1)}, bf16[9,24,768]{2,1,0:T(8,128)(2,1)S(1)}, u32[]{:S(2)}, u32[]{:S(2)}) collective-permute-start(bf16[9,24,768]{2,1,0:T(8,128)(2,1)} %shard_map.256), channel_id=1, source_target_pairs={{0,2},{1,3},{2,4},{3,5},{4,6},{5,7},{6,0},{7,1},{8,10},{9,11},{10,... | collective-permute-start | bytes 995336 | tf_op jit(solution)/shard_map/ppermute | solution.py:29
  25.2 30.2 %collective-permute-start.9 = (bf16[9,24,768]{2,1,0:T(8,128)(2,1)}, bf16[9,24,768]{2,1,0:T(8,128)(2,1)S(1)}, u32[]{:S(2)}, u32[]{:S(2)}) collective-permute-start(bf16[9,24,768]{2,1,0:T(8,128)(2,1)} %shard_map.256), channel_id=1, source_target_pairs={{0,4},{1,5},{2,6},{3,7},{4,0},{5,1},{6,2},{7,3},{8,12},{9,13},{10,... | collective-permute-start | bytes 995336 | tf_op jit(solution)/shard_map/ppermute | solution.py:29
  26.8 28.6 %collective-permute-start.8 = (bf16[9,24,768]{2,1,0:T(8,128)(2,1)}, bf16[9,24,768]{2,1,0:T(8,128)(2,1)S(1)}, u32[]{:S(2)}, u32[]{:S(2)}) collective-permute-start(bf16[9,24,768]{2,1,0:T(8,128)(2,1)} %shard_map.256), channel_id=1, source_target_pairs={{0,6},{1,7},{2,0},{3,1},{4,2},{5,3},{6,4},{7,5},{8,14},{9,15},{10,... | collective-permute-start | bytes 995336 | tf_op jit(solution)/shard_map/ppermute | solution.py:29
  31.4 26.4 %collective-permute-start.4 = (bf16[2,2,80,768]{3,2,1,0:T(8,128)(2,1)S(1)}, bf16[2,2,80,768]{3,2,1,0:T(8,128)(2,1)S(1)}, u32[]{:S(2)}, u32[]{:S(2)}) collective-permute-start(bf16[2,2,80,768]{3,2,1,0:T(8,128)(2,1)S(1)} %pad_maximum_fusion.8), channel_id=1, source_target_pairs={{0,16},{8,24},{16,0},{24,8},{1,17},{9,25},{17,1},{25,9},{2,18},{10... | collective-permute-start | bytes 1474568 | tf_op jit(solution)/shard_map/ppermute | solution.py:39
  37.8 20.1 %collective-permute-start.6 = (bf16[2,2,80,768]{3,2,1,0:T(8,128)(2,1)S(1)}, bf16[2,2,80,768]{3,2,1,0:T(8,128)(2,1)S(1)}, u32[]{:S(2)}, u32[]{:S(2)}) collective-permute-start(bf16[2,2,80,768]{3,2,1,0:T(8,128)(2,1)S(1)} %pad_maximum_fusion.9), channel_id=1, source_target_pairs={{0,8},{8,0},{16,24},{24,16},{1,9},{9,1},{17,25},{25,17},{2,10},{10... | collective-permute-start | bytes 1474568 | tf_op jit(solution)/shard_map/ppermute | solution.py:39
  55.7 16.9 %collective-permute-start.11 = (bf16[2,9,24,768]{3,2,1,0:T(8,128)(2,1)S(1)}, bf16[2,9,24,768]{3,2,1,0:T(8,128)(2,1)S(1)}, u32[]{:S(2)}, u32[]{:S(2)}) collective-permute-start(bf16[2,9,24,768]{3,2,1,0:T(8,128)(2,1)S(1)} %get-tuple-element.66), channel_id=1, source_target_pairs={{0,8},{8,0},{16,24},{24,16},{1,9},{9,1},{17,25},{25,17},{2,10},{10... | collective-permute-start | bytes 1990664 | tf_op jit(solution)/shard_map/ppermute | solution.py:39
  56.3 19.3 %collective-permute-start.13 = (bf16[2,9,24,768]{3,2,1,0:T(8,128)(2,1)S(1)}, bf16[2,9,24,768]{3,2,1,0:T(8,128)(2,1)S(1)}, u32[]{:S(2)}, u32[]{:S(2)}) collective-permute-start(bf16[2,9,24,768]{3,2,1,0:T(8,128)(2,1)S(1)} %get-tuple-element.67), channel_id=1, source_target_pairs={{0,16},{8,24},{16,0},{24,8},{1,17},{9,25},{17,1},{25,9},{2,18},{10... | collective-permute-start | bytes 1990664 | tf_op jit(solution)/shard_map/ppermute | solution.py:39
  74.0 30.5 %collective-permute-start.12 = (bf16[2,2,9,24,768]{4,3,2,1,0:T(8,128)(2,1)}, bf16[2,2,9,24,768]{4,3,2,1,0:T(8,128)(2,1)}, u32[]{:S(2)}, u32[]{:S(2)}) collective-permute-start(bf16[2,2,9,24,768]{4,3,2,1,0:T(8,128)(2,1)} %pad_maximum_fusion.5), channel_id=1, source_target_pairs={{0,16},{8,24},{16,0},{24,8},{1,17},{9,25},{17,1},{25,9},{2,18},{10... | collective-permute-start | bytes 3981320 | tf_op jit(solution)/shard_map/ppermute | solution.py:39
  77.1 30.2 %collective-permute-start.14 = (bf16[2,2,9,24,768]{4,3,2,1,0:T(8,128)(2,1)}, bf16[2,2,9,24,768]{4,3,2,1,0:T(8,128)(2,1)}, u32[]{:S(2)}, u32[]{:S(2)}) collective-permute-start(bf16[2,2,9,24,768]{4,3,2,1,0:T(8,128)(2,1)} %pad_maximum_fusion.6), channel_id=1, source_target_pairs={{0,8},{8,0},{16,24},{24,16},{1,9},{9,1},{17,25},{25,17},{2,10},{10... | collective-permute-start | bytes 3981320 | tf_op jit(solution)/shard_map/ppermute | solution.py:39
  77.9 34.1 %collective-permute-start.7 = (bf16[16,80,768]{2,1,0:T(8,128)(2,1)S(1)}, bf16[16,80,768]{2,1,0:T(8,128)(2,1)}, u32[]{:S(2)}, u32[]{:S(2)}) collective-permute-start(bf16[16,80,768]{2,1,0:T(8,128)(2,1)S(1)} %bitcast.328), channel_id=1, source_target_pairs={{0,1},{1,0},{2,3},{3,2},{4,5},{5,4},{6,7},{7,6},{8,9},{9,8},{10,11... | collective-permute-start | bytes 5898248 | tf_op jit(solution)/shard_map/ppermute | solution.py:34
  112.1 71.6 %collective-permute-start.15 = (bf16[16,9,24,768]{3,2,1,0:T(8,128)(2,1)}, bf16[16,9,24,768]{3,2,1,0:T(8,128)(2,1)}, u32[]{:S(2)}, u32[]{:S(2)}) collective-permute-start(bf16[16,9,24,768]{3,2,1,0:T(8,128)(2,1)} %bitcast.51), channel_id=1, source_target_pairs={{0,1},{1,0},{2,3},{3,2},{4,5},{5,4},{6,7},{7,6},{8,9},{9,8},{10,11... | collective-permute-start | bytes 15925256 | tf_op jit(solution)/shard_map/ppermute | solution.py:34
  166.8 16.1 %all-to-all-start.1 = ((bf16[8,64,384]{2,1,0:T(8,128)(2,1)}), bf16[8,64,384]{2,1,0:T(8,128)(2,1)S(1)}, u32[]{:S(2)}, u32[]{:S(2)}) async-start(bf16[8,64,384]{2,1,0:T(8,128)(2,1)} %bitcast.34), calls=%async_computation.1 | async-start | bytes 786432 | tf_op jit(solution)/shard_map/all_to_all | solution.py:124
  263.1 38.2 %all-to-all-start.3 = ((bf16[8,128,576]{1,2,0:T(8,128)(2,1)}), bf16[8,128,576]{1,2,0:T(8,128)(2,1)}, u32[]{:S(2)}, u32[]{:S(2)}) async-start(bf16[8,128,576]{1,2,0:T(8,128)(2,1)} %copy.90), calls=%async_computation.3 | async-start | bytes 2359296 | tf_op jit(solution)/shard_map/all_to_all | solution.py:124
  301.0 41.5 %collective-permute-start.24 = (bf16[16,216,768]{2,1,0:T(8,128)(2,1)}, bf16[16,216,768]{2,1,0:T(8,128)(2,1)}, u32[]{:S(2)}, u32[]{:S(2)}) collective-permute-start(bf16[16,216,768]{2,1,0:T(8,128)(2,1)} %pad_maximum_fusion.1), channel_id=1, source_target_pairs={{0,1},{1,0},{2,3},{3,2},{4,5},{5,4},{6,7},{7,6},{8,9},{9,8},{10,11... | collective-permute-start | bytes 15925256 | tf_op jit(solution)/shard_map/ppermute | solution.py:34
  335.4 14.1 %collective-permute-start.19 = (bf16[2,2,80,768]{3,2,1,0:T(8,128)(2,1)S(1)}, bf16[2,2,80,768]{3,2,1,0:T(8,128)(2,1)S(1)}, u32[]{:S(2)}, u32[]{:S(2)}) collective-permute-start(bf16[2,2,80,768]{3,2,1,0:T(8,128)(2,1)S(1)} %dynamic-slice_bitcast_fusion.12), channel_id=1, source_target_pairs={{0,8},{8,0},{16,24},{24,16},{1,9},{9,1},{17,25},{25,17},{2,10},{10... | collective-permute-start | bytes 1474568 | tf_op jit(solution)/shard_map/ppermute | solution.py:39
  347.1 40.6 %collective-permute-start.25 = (bf16[2,2,216,768]{3,2,1,0:T(8,128)(2,1)S(1)}, bf16[2,2,216,768]{3,2,1,0:T(8,128)(2,1)S(1)}, u32[]{:S(2)}, u32[]{:S(2)}) collective-permute-start(bf16[2,2,216,768]{3,2,1,0:T(8,128)(2,1)S(1)} %dynamic-slice_bitcast_fusion.7), channel_id=1, source_target_pairs={{0,16},{8,24},{16,0},{24,8},{1,17},{9,25},{17,1},{25,9},{2,18},{10... | collective-permute-start | bytes 3981320 | tf_op jit(solution)/shard_map/ppermute | solution.py:39
  349.8 39.9 %collective-permute-start.27 = (bf16[2,2,216,768]{3,2,1,0:T(8,128)(2,1)S(1)}, bf16[2,2,216,768]{3,2,1,0:T(8,128)(2,1)S(1)}, u32[]{:S(2)}, u32[]{:S(2)}) collective-permute-start(bf16[2,2,216,768]{3,2,1,0:T(8,128)(2,1)S(1)} %dynamic-slice_bitcast_fusion.6), channel_id=1, source_target_pairs={{0,8},{8,0},{16,24},{24,16},{1,9},{9,1},{17,25},{25,17},{2,10},{10... | collective-permute-start | bytes 3981320 | tf_op jit(solution)/shard_map/ppermute | solution.py:39
  350.4 32.4 %collective-permute-start.20 = (bf16[2,80,768]{2,1,0:T(8,128)(2,1)S(1)}, bf16[2,80,768]{2,1,0:T(8,128)(2,1)S(1)}, u32[]{:S(2)}, u32[]{:S(2)}) collective-permute-start(bf16[2,80,768]{2,1,0:T(8,128)(2,1)S(1)} %dynamic-slice_bitcast_fusion.14), channel_id=1, source_target_pairs={{0,16},{8,24},{16,0},{24,8},{1,17},{9,25},{17,1},{25,9},{2,18},{10... | collective-permute-start | bytes 737288 | tf_op jit(solution)/shard_map/ppermute | solution.py:39
  388.1 14.4 %collective-permute-start.26 = (bf16[2,216,768]{2,1,0:T(8,128)(2,1)S(1)}, bf16[2,216,768]{2,1,0:T(8,128)(2,1)S(1)}, u32[]{:S(2)}, u32[]{:S(2)}) collective-permute-start(bf16[2,216,768]{2,1,0:T(8,128)(2,1)S(1)} %dynamic-slice_bitcast_fusion.9), channel_id=1, source_target_pairs={{0,8},{8,0},{16,24},{24,16},{1,9},{9,1},{17,25},{25,17},{2,10},{10... | collective-permute-start | bytes 1990664 | tf_op jit(solution)/shard_map/ppermute | solution.py:39
  390.1 14.1 %collective-permute-start.28 = (bf16[2,216,768]{2,1,0:T(8,128)(2,1)S(1)}, bf16[2,216,768]{2,1,0:T(8,128)(2,1)S(1)}, u32[]{:S(2)}, u32[]{:S(2)}) collective-permute-start(bf16[2,216,768]{2,1,0:T(8,128)(2,1)S(1)} %dynamic-slice_bitcast_fusion.8), channel_id=1, source_target_pairs={{0,16},{8,24},{16,0},{24,8},{1,17},{9,25},{17,1},{25,9},{2,18},{10... | collective-permute-start | bytes 1990664 | tf_op jit(solution)/shard_map/ppermute | solution.py:39
  404.8 22.0 %collective-permute-start.29 = (bf16[216,768]{1,0:T(8,128)(2,1)S(1)}, bf16[216,768]{1,0:T(8,128)(2,1)S(1)}, u32[]{:S(2)}, u32[]{:S(2)}) collective-permute-start(bf16[216,768]{1,0:T(8,128)(2,1)S(1)} %get-tuple-element.72), channel_id=1, source_target_pairs={{0,2},{1,3},{2,4},{3,5},{4,6},{5,7},{6,0},{7,1},{8,10},{9,11},{10,... | collective-permute-start | bytes 995336 | tf_op jit(solution)/shard_map/ppermute | solution.py:29
  405.2 25.1 %collective-permute-start.30 = (bf16[216,768]{1,0:T(8,128)(2,1)S(1)}, bf16[216,768]{1,0:T(8,128)(2,1)S(1)}, u32[]{:S(2)}, u32[]{:S(2)}) collective-permute-start(bf16[216,768]{1,0:T(8,128)(2,1)S(1)} %get-tuple-element.73), channel_id=1, source_target_pairs={{0,4},{1,5},{2,6},{3,7},{4,0},{5,1},{6,2},{7,3},{8,12},{9,13},{10,... | collective-permute-start | bytes 995336 | tf_op jit(solution)/shard_map/ppermute | solution.py:29
  408.7 24.9 %collective-permute-start.31 = (bf16[216,768]{1,0:T(8,128)(2,1)S(1)}, bf16[216,768]{1,0:T(8,128)(2,1)}, u32[]{:S(2)}, u32[]{:S(2)}) collective-permute-start(bf16[216,768]{1,0:T(8,128)(2,1)S(1)} %get-tuple-element.74), channel_id=1, source_target_pairs={{0,6},{1,7},{2,0},{3,1},{4,2},{5,3},{6,4},{7,5},{8,14},{9,15},{10,... | collective-permute-start | bytes 995336 | tf_op jit(solution)/shard_map/ppermute | solution.py:29
  (53 other events, 348.0 us)
where the time goes:
time: 446 us; the launch traced here: 438 us
  waiting for transfers between devices  156 us (35%)
  local copies, waits for them, and re-layouts  86.7 us (19%)
  blocking collectives  60.1 us (13%)
  starting transfers between devices  43.8 us (10%)
  other arithmetic  42 us (9%)
  matrix products  26.6 us (6%)
  Pallas kernels  20.1 us (5%)
    ppermute x16, waiting for transfers between devices, swap_dp(): return lax.ppermute(value, 'dp', [(i, i ^ bit) for i in range(size)])  93.1 us
    all_to_all x2, blocking collectives, exchange(): lax.all_to_all(blocks, 'seq', split_axis=0, concat_axis=0, tiled=True)  60.1 us
    ppermute x12, waiting for transfers between devices, shift_z(): lax.ppermute(value, 'seq', [(i, (i + CORES * step) % size) for i in range...  48.9 us
    another operation x16, other arithmetic, ordered(): return jnp.stack([first, second], axis)  23 us
    ppermute x12, starting transfers between devices, shift_z(): lax.ppermute(value, 'seq', [(i, (i + CORES * step) % size) for i in range...  16.9 us
    unnamed x102, local copies, waits for them, and re-layouts  14.8 us
    ppermute x16, starting transfers between devices, swap_dp(): return lax.ppermute(value, 'dp', [(i, i ^ bit) for i in range(size)])  14.1 us
    reshape x2, local copies, waits for them, and re-layouts, on_device(): by_part = grad_wfc.astype(BF16).reshape(devices, shard_rows, parts, width)  13.1 us
  transfers between devices with their start and end apart: 34, of which 20 were waited for; matrix products, arithmetic and copies ran while one was open for 22% of the time, Pallas kernels for 3%

commit v1 on v0

--- a/solution.py
+++ b/solution.py
@@ -59,10 +59,14 @@
     return roll_blocks(pieces, level)
 
 
+def swap_z(value, bit):
+    size = lax.axis_size("seq")
+    return lax.ppermute(value, "seq", [(i, i ^ (CORES * bit)) for i in range(size)])
+
+
 def gather_plane(tower):
     heights = tower.shape[0]
     shard = tower.shape[1:]
-    core = lax.axis_index("seq") % CORES
     if lax.axis_size("dp") == 4:
         plane = lax.axis_index("dp")
         y, x = plane // 2, plane % 2
@@ -74,8 +78,7 @@
         half = jnp.concatenate([low_all, high_all], 2)
     else:
         half = lax.all_gather(tower, "dp", axis=0, tiled=False)
-    half = half.reshape(-1, *shard)
-    return ordered(core, half, swap_core(half), 1).reshape(-1, *shard)
+    return half.reshape(-1, *shard)
 
 
 def pick(value, index, axis):
@@ -90,17 +93,14 @@
     return send, keep
 
 
-def scatter_sum(send, keep):
-    kind = send.dtype
-    rows, columns = send.shape[1:]
+def add(mine, other):
+    return (mine.astype(F32) + other.astype(F32)).astype(mine.dtype)
+
+
+def scatter_plane(split):
+    rows, columns = split.shape[1:]
     planes = lax.axis_size("dp")
     heights = lax.axis_size("seq") // CORES
-    level = lax.axis_index("seq") // CORES
-
-    def add(mine, other):
-        return (mine.astype(F32) + other.astype(F32)).astype(kind)
-
-    split = add(keep, swap_core(send))
     if planes == 4:
         plane = lax.axis_index("dp")
         y, x = plane // 2, plane % 2
@@ -110,14 +110,80 @@
         high = add(pick(high, x, 1), swap_dp(pick(high, 1 - x, 1), 1))
         low = add(pick(low, x, 0), swap_dp(pick(low, 1 - x, 0), 1))
         high = add(pick(high, y, 0), swap_dp(pick(high, 1 - y, 0), 2))
-        tower = jnp.concatenate([low, high], 0)
-    else:
-        split = split.reshape(planes, heights, rows, columns)
-        tower = lax.psum_scatter(split, "dp", scatter_dimension=0, tiled=False)
+        return jnp.concatenate([low, high], 0)
+    split = split.reshape(planes, heights, rows, columns)
+    return lax.psum_scatter(split, "dp", scatter_dimension=0, tiled=False)
+
+
+def scatter_z(tower):
+    heights = tower.shape[0]
+    level = lax.axis_index("seq") // CORES
     mine = pick(tower, level, 0).astype(F32)
     for step in range(1, heights):
         mine += shift_z(pick(tower, lax.rem(level + step, heights), 0), step).astype(F32)
     return mine
+
+
+def z_bits():
+    heights = lax.axis_size("seq") // CORES
+    level = lax.axis_index("seq") // CORES
+    top = heights // 2
+    return level, top, level // top
+
+
+def gather_sequence(blocks):
+    level, top, half = z_bits()
+    core = lax.axis_index("seq") % CORES
+    held = ordered(half, pick(blocks, half, 0), swap_z(pick(blocks, 1 - half, 0), top), 0)
+    axis, bit = 1, top // 2
+    while bit:
+        held = ordered(level // bit % 2, held, swap_z(held, bit), axis)
+        axis, bit = axis + 1, bit // 2
+    return ordered(core, held, swap_core(held), axis).reshape(-1, *blocks.shape[1:])
+
+
+def scatter_sequence(partial):
+    level, top, half = z_bits()
+    core = lax.axis_index("seq") % CORES
+    shape = partial.shape[1:]
+    count = top.bit_length()
+    held = partial.reshape(*[2] * (count + 1), *shape)
+    held = add(pick(held, core, count), swap_core(pick(held, 1 - core, count)))
+    axis, bit = count - 1, 1
+    while bit < top:
+        flag = level // bit % 2
+        held = add(pick(held, flag, axis), swap_z(pick(held, 1 - flag, axis), bit))
+        axis, bit = axis - 1, bit * 2
+    return ordered(half, pick(held, half, 0), swap_z(pick(held, 1 - half, 0), top), 0)
+
+
+def gather_columns(blocks):
+    level, top, half = z_bits()
+    shape = blocks.shape[1:]
+    count = top.bit_length() - 1
+    held = blocks.reshape(*[2] * count, *shape)
+    bit = top // 2
+    while bit:
+        flag = level // bit % 2
+        got = swap_z(pick(held, 1 - flag, 0), bit)
+        held = ordered(flag, pick(held, flag, 0), got, count - 1)
+        bit //= 2
+    return ordered(half, held, swap_z(held, top), 0).reshape(-1, *shape)
+
+
+def scatter_columns(tower):
+    level, top, half = z_bits()
+    shape = tower.shape[1:]
+    count = top.bit_length() - 1
+    held = tower.reshape(*[2] * (count + 1), *shape)
+    held = add(pick(held, half, 0), swap_z(pick(held, 1 - half, 0), top))
+    bit = 1
+    while bit < top:
+        flag = level // bit % 2
+        got = swap_z(pick(held, 1 - flag, count - 1), bit)
+        held = ordered(flag, pick(held, flag, count - 1), got, 0)
+        bit *= 2
+    return held.reshape(-1, *shape).astype(F32)
 
 
 def exchange(blocks):
@@ -214,7 +280,44 @@
     )(w_out, w_fc, w_proj, after)
 
 
-def masked_scores(keys, queries, id_column, id_row, first, last):
+def spread_kernel(parts, half, other, out_ref, fc_ref, proj_ref, sems):
+    core = lax.rem(lax.axis_index("seq"), CORES)
+    copies = []
+    for source, place in ((half, core), (other, 1 - core)):
+        pairs = [(source.at[:, 0], out_ref.at[:, place])]
+        pairs += [(source.at[:, 1 + i], fc_ref.at[i, :, place]) for i in range(parts)]
+        pairs += [(source.at[:, pl.ds(1 + parts, parts)], proj_ref.at[:, place])]
+        for pair in pairs:
+            copies.append(pltpu.make_async_copy(*pair, sems.at[len(copies)]))
+    for copy in copies:
+        copy.start()
+    for copy in copies:
+        copy.wait()
+
+
+def spread_weights(half, other):
+    chips, kinds, rows, width = half.shape
+    parts = (kinds - 1) // 2
+    anywhere = pl.BlockSpec(memory_space=pl.ANY)
+    wout, wfc, wproj = pl.pallas_call(
+        functools.partial(spread_kernel, parts),
+        out_shape=[
+            jax.ShapeDtypeStruct((chips, CORES, rows, width), BF16),
+            jax.ShapeDtypeStruct((parts, chips, CORES, rows, width), BF16),
+            jax.ShapeDtypeStruct((chips, CORES, parts, rows, width), BF16),
+        ],
+        in_specs=[anywhere] * 2,
+        out_specs=[anywhere] * 3,
+        scratch_shapes=[pltpu.SemaphoreType.DMA((2 * (parts + 2),))],
+    )(half, other)
+    return (
+        wout.reshape(width, width),
+        wfc.reshape(parts, width, width),
+        wproj.reshape(parts, width, width),
+    )
+
+
+def masked_scores(keys, queries, id_column, id_row, first):
     scores = lax.dot_general(keys, queries, (((1,), (1,)), ((), ())), preferred_element_type=F32)
     key_pos = lax.broadcasted_iota(jnp.int32, scores.shape, 0)
     query_pos = lax.broadcasted_iota(jnp.int32, scores.shape, 1) + first
@@ -222,16 +325,41 @@
     return jnp.where(allowed, scores, MASKED)
 
 
-def read_ids(whole):
-    width = whole.shape[1]
-    tail = whole[:, width - 128 :].astype(F32)
-    return tail[:, 127:128], tail.T[127:128, :]
-
-
-def forward_kernel(heads, head_size, step_rows, block, whole, out, stats, result):
+def column_of(id_row):
+    length = id_row.shape[1]
+    return jnp.broadcast_to(id_row, (LANES, length)).T[:, :1]
+
+
+def forward_kernel(
+    heads,
+    head_size,
+    step_rows,
+    block,
+    rows_ref,
+    weight,
+    gain,
+    bias,
+    qkv_bias,
+    out,
+    stats,
+    whole,
+    normed,
+    ids,
+    result,
+):
     length = whole.shape[0]
     group = heads * head_size
-    id_column, id_row = read_ids(whole)
+    for i in range(length // block):
+        rows = norm_affine(rows_ref[i, :block, :].astype(F32), gain[...], bias[...])
+        normed[i * block : (i + 1) * block, :] = rows.astype(BF16)
+    id_rows = [rows_ref[i, block:, :block].astype(F32)[:1] for i in range(length // block)]
+    id_row = jnp.concatenate(id_rows, 1)
+    ids[...] = id_row
+    id_column = column_of(id_row)
+    for first in range(0, length, step_rows):
+        last = first + step_rows
+        product = jnp.dot(normed[first:last, :], weight[...], preferred_element_type=F32)
+        whole[first:last, :] = (product + qkv_bias[...]).astype(BF16)
     values_t = whole[:, 2 * group : 3 * group].astype(F32).T.astype(BF16)
     for first in range(0, length, step_rows):
         last = first + step_rows
@@ -240,9 +368,7 @@
             lo = head * head_size
             queries = whole[first:last, lo : lo + head_size] * BF16(head_size**-0.5)
             keys = whole[:last, group + lo : group + lo + head_size]
-            scores = masked_scores(
-                keys, queries, id_column[:last], id_row[:, first:last], first, last
-            )
+            scores = masked_scores(keys, queries, id_column[:last], id_row[:, first:last], first)
             highest = jnp.max(scores, 0, keepdims=True)
             weights = jnp.exp(scores - highest)
             total = jnp.sum(weights, 0, keepdims=True)
@@ -268,6 +394,7 @@
     whole,
     grads,
     stats,
+    ids,
     out,
     grad_out,
     grad_query,
@@ -281,7 +408,8 @@
         packed = grads[start // 2 : start // 2 + half, :]
         grad_out[start : start + half, :] = packed[:, :group]
         grad_out[start + half : start + block, :] = packed[:, group:]
-    id_column, id_row = read_ids(whole)
+    id_row = ids[...]
+    id_column = column_of(id_row)
     keys_t = whole[:, group : 2 * group].astype(F32).T.astype(BF16)
     factor = head_size**-0.5
     grad_key[...] = jnp.zeros_like(grad_key)
@@ -295,9 +423,7 @@
             keys = whole[:last, group + lo : group + lo + head_size]
             values = whole[:last, 2 * group + lo : 2 * group + lo + head_size]
             grad = grad_out[first:last, lo : lo + head_size]
-            scores = masked_scores(
-                keys, queries, id_column[:last], id_row[:, first:last], first, last
-            )
+            scores = masked_scores(keys, queries, id_column[:last], id_row[:, first:last], first)
             probs = jnp.exp(scores - stats[head : head + 1, first:last])
             grad_probs = lax.dot_general(
                 values, grad, (((1,), (1,)), ((), ())), preferred_element_type=F32
@@ -324,8 +450,9 @@
         out[:, 2 * group + lo : 2 * group + lo + head_size] = grad_value[head].astype(BF16)
 
 
-def attend_forward(whole, heads, head_size, block):
-    length, width = whole.shape
+def attend_forward(rows, weight, gain, bias, qkv_bias, heads, head_size, block):
+    length = rows.shape[0] * block
+    width = rows.shape[2]
     group = heads * head_size
     pairs = length * length // 2 * heads
     return pl.pallas_call(
@@ -333,25 +460,30 @@
         out_shape=[
             jax.ShapeDtypeStruct((length // 2, 2 * group), BF16),
             jax.ShapeDtypeStruct((heads, length), F32),
+            jax.ShapeDtypeStruct((length, 3 * group), BF16),
+            jax.ShapeDtypeStruct((length, width), BF16),
+            jax.ShapeDtypeStruct((1, length), F32),
         ],
-        in_specs=vmem_specs(1),
-        out_specs=vmem_specs(2),
+        in_specs=vmem_specs(5),
+        out_specs=vmem_specs(5),
         scratch_shapes=[pltpu.VMEM((length, group), BF16)],
         compiler_params=pltpu.CompilerParams(vmem_limit_bytes=48 * 2**20),
         cost_estimate=pl.CostEstimate(
-            flops=pairs * head_size * 4, bytes_accessed=length * width * 3, transcendentals=pairs
+            flops=pairs * head_size * 4 + length * width * group * 6,
+            bytes_accessed=length * width * 8,
+            transcendentals=pairs,
         ),
-    )(whole)
-
-
-def attend_backward(whole, grads, stats, heads, head_size, block):
+    )(rows, weight, gain, bias, qkv_bias)
+
+
+def attend_backward(whole, grads, stats, ids, heads, head_size, block):
     length, width = whole.shape
     group = heads * head_size
     pairs = length * length // 2 * heads
     return pl.pallas_call(
         functools.partial(backward_kernel, heads, head_size, min(256, length), block),
         out_shape=jax.ShapeDtypeStruct((length, 3 * group), BF16),
-        in_specs=vmem_specs(3),
+        in_specs=vmem_specs(4),
         out_specs=vmem_specs(1)[0],
         scratch_shapes=[
             pltpu.VMEM((length, group), BF16),
@@ -363,7 +495,7 @@
         cost_estimate=pl.CostEstimate(
             flops=pairs * head_size * 10, bytes_accessed=length * width * 6, transcendentals=pairs
         ),
-    )(whole, grads, stats)
+    )(whole, grads, stats, ids)
 
 
 def on_device(
@@ -397,9 +529,29 @@
     sizes = tuple(vector.shape[0] for vector in vectors)
     shard_rows = w_out.shape[0] // width
     parts = w_fc.shape[0] // w_out.shape[0]
-    small = [jnp.pad(vector[None], ((0, 0), (0, width - vector.shape[0]))) for vector in vectors]
-    thirds = w_qkv.reshape(shard_rows, 3, width).transpose(1, 0, 2).reshape(-1, width)
-    tower_a = gather_z(jnp.concatenate([thirds] + small, 0))
+    small = jnp.concatenate(
+        [jnp.pad(vector[None], ((0, 0), (0, 3 * group - vector.shape[0]))) for vector in vectors]
+    )
+    classes = groups // CORES
+    place = lax.axis_index("seq")
+    core = place % CORES
+    group_index = place % groups
+
+    def by_head(value, axis):
+        if not spare:
+            return value
+        pads = [(0, 0)] * value.ndim
+        pads[axis] = (0, spare)
+        return jnp.pad(value, pads)
+
+    marks = jnp.pad(segments.astype(BF16)[:, None], ((0, 0), (0, 15), (0, width - block)))
+    sequence = gather_sequence(jnp.concatenate([inputs, marks], 1))
+
+    columns = by_head(w_qkv.reshape(shard_rows, 3, HEADS, head_size), 2)
+    columns = columns.reshape(shard_rows, 3, classes, CORES, group).transpose(2, 0, 3, 1, 4)
+    columns = columns.reshape(classes, shard_rows, CORES * 3 * group)
+    extra = jnp.broadcast_to(jnp.concatenate([small] * CORES, 1), (classes, ROWS, 6 * group))
+    tower_a = gather_columns(jnp.concatenate([columns, extra], 1))
     stacked = stack_weights(
         w_out.reshape(-1, width),
         w_fc.reshape(-1, parts * width),
@@ -407,71 +559,48 @@
         tower_a,
     )
     tower_b = gather_z(stacked)
-    whole_a = gather_plane(tower_a)
-    whole_b = gather_plane(tower_b)
+    half_a = gather_plane(tower_a)
+    left, right = half_a[..., : 3 * group], half_a[..., 3 * group :]
+    mine_a = jnp.where(core == 0, left, right)
+    whole_a = ordered(core, mine_a, swap_core(jnp.where(core == 0, right, left)), 1)
+    whole_a = whole_a.reshape(devices, shard_rows + ROWS, 3 * group)
+    wqkv = whole_a[:, :shard_rows].reshape(width, 3 * group)
     gain1, bias1, bqv, bout, gain2, bias2, bfc, bproj = unpack_small(
-        whole_a[:, 3 * shard_rows :, :LANES], sizes
-    )
-    wqkv = jnp.concatenate(
-        [whole_a[:, i * shard_rows : (i + 1) * shard_rows] for i in range(3)], -1
-    ).reshape(width, 3 * width)
-    wout = whole_b[:, 0].reshape(width, width)
-    wfc = whole_b[:, 1 : 1 + parts].transpose(0, 2, 1, 3).reshape(width, parts * width)
-    wproj = whole_b[:, 1 + parts :].reshape(parts * width, width)
-
-    def by_group(value, parts):
-        value = value.reshape(seq_count, block, parts, HEADS, head_size)
-        if spare:
-            value = jnp.pad(value, ((0, 0), (0, 0), (0, 0), (0, spare), (0, 0)))
-        value = value.reshape(seq_count, block, parts, groups, group)
-        return value.transpose(0, 3, 1, 2, 4).reshape(count, block, parts * group)
-
-    def from_group(value, parts):
-        value = value.reshape(seq_count, groups, block, parts, group).transpose(0, 2, 3, 1, 4)
-        value = value.reshape(tokens, parts, groups * heads, head_size)
-        return value[:, :, :HEADS].reshape(tokens, parts * width)
-
-    def pack(value):
-        value = value.reshape(value.shape[0], 2, block // 2, group).transpose(0, 2, 1, 3)
-        return value.reshape(-1, block // 2, 2 * group)
-
-    def unpack(value):
-        value = value.reshape(value.shape[0], block // 2, 2, group).transpose(0, 2, 1, 3)
-        return value.reshape(-1, block, group)
+        whole_a[:, shard_rows:, :LANES], sizes
+    )
+    half_b = gather_plane(tower_b)
+    wout, wfc, wproj = spread_weights(half_b, swap_core(half_b))
+
+    both = by_head(bqv.reshape(2, HEADS, head_size), 1).reshape(2, groups, group)
+    both = pick(both, group_index, 1)
+    qkv_bias = jnp.concatenate([both[0], jnp.zeros((group,), F32), both[1]]).reshape(1, -1)
+    attended, stats, qkv, normed1, ids = attend_forward(
+        sequence, wqkv, gain1, bias1, qkv_bias, heads, head_size, block
+    )
+    attended = exchange(attended.reshape(count, block // 2, 2 * group))
+    attended = attended.reshape(seq_count, groups, block // 2, 2, heads, head_size)
+    attended = attended.transpose(0, 3, 2, 1, 4, 5).reshape(tokens, groups * heads, head_size)
+    attended_rows = attended[:, :HEADS].reshape(tokens, width)
 
     rows = inputs.astype(F32).reshape(tokens, width)
-    normed1 = norm_affine(rows, gain1, bias1).astype(BF16)
-    qkv_bias = jnp.concatenate(
-        [bqv[:, :width], jnp.zeros((1, width), F32), bqv[:, width:]], axis=1
-    )
-    qkv = (jnp.dot(normed1, wqkv, preferred_element_type=F32) + qkv_bias).astype(BF16)
-    fill = -(3 * group) % 128 or 128
-    ids = jnp.broadcast_to(
-        segments.astype(BF16)[:, None, :, None], (seq_count, groups, block, fill)
-    )
-    blocks = jnp.concatenate([by_group(qkv, 3), ids.reshape(count, block, fill)], -1)
-    whole = exchange(blocks).reshape(count * block, 3 * group + fill)
-    attended, stats = attend_forward(whole, heads, head_size, block)
-    attended = exchange(attended.reshape(count, block // 2, 2 * group))
-    attended_rows = from_group(unpack(attended), 1)
-
     middle = rows + (jnp.dot(attended_rows, wout, preferred_element_type=F32) + bout)
     normed2 = norm_affine(middle, gain2, bias2).astype(BF16)
-    hidden_pre = jnp.dot(normed2, wfc, preferred_element_type=F32) + bfc
+    bfc_parts = bfc.reshape(parts, 1, width)
+    hidden_pre = jnp.einsum("td,qde->qte", normed2, wfc, preferred_element_type=F32) + bfc_parts
     hidden = jax.nn.gelu(hidden_pre, approximate=True).astype(BF16)
-    result_rows = middle + (jnp.dot(hidden, wproj, preferred_element_type=F32) + bproj)
-    outputs = result_rows.astype(BF16).reshape(inputs.shape)
+    projected = jnp.einsum("qte,qed->td", hidden, wproj, preferred_element_type=F32)
+    outputs = (middle + (projected + bproj)).astype(BF16).reshape(inputs.shape)
 
     grad_rows = cotangent.astype(F32).reshape(tokens, width)
     grad_branch = cotangent.reshape(tokens, width)
     grad_bproj = jnp.sum(grad_branch, 0, dtype=F32)
-    grad_wproj = jnp.einsum("tf,td->fd", hidden, grad_branch, preferred_element_type=F32)
-    grad_hidden = jnp.einsum("td,fd->tf", grad_branch, wproj, preferred_element_type=F32)
+    grad_wproj = jnp.einsum("qte,td->qed", hidden, grad_branch, preferred_element_type=F32)
+    grad_hidden = jnp.einsum("td,qed->qte", grad_branch, wproj, preferred_element_type=F32)
     _, gelu_back = jax.vjp(lambda value: jax.nn.gelu(value, approximate=True), hidden_pre)
     grad_pre = gelu_back(grad_hidden)[0].astype(BF16)
-    grad_bfc = jnp.sum(grad_pre, 0, dtype=F32)
-    grad_wfc = jnp.einsum("td,tf->df", normed2, grad_pre, preferred_element_type=F32)
-    grad_normed2 = jnp.einsum("tf,df->td", grad_pre, wfc, preferred_element_type=F32)
+    grad_bfc = jnp.sum(grad_pre, 1, dtype=F32)
+    grad_wfc = jnp.einsum("td,qte->qde", normed2, grad_pre, preferred_element_type=F32)
+    grad_normed2 = jnp.einsum("qte,qde->td", grad_pre, wfc, preferred_element_type=F32)
     _, norm2_back = jax.vjp(norm_affine, middle, gain2, bias2)
     grad_mid_part, grad_gain2, grad_bias2 = norm2_back(grad_normed2)
     grad_middle = grad_rows + grad_mid_part
@@ -479,32 +608,43 @@
     grad_bout = jnp.sum(grad_attn_out, 0, dtype=F32)
     grad_wout = jnp.einsum("td,te->de", attended_rows, grad_attn_out, preferred_element_type=F32)
     grad_attended = jnp.einsum("te,de->td", grad_attn_out, wout, preferred_element_type=F32)
-    grad_blocks = exchange(pack(by_group(grad_attended.astype(BF16), 1)))
-    by_part = grad_wfc.astype(BF16).reshape(devices, shard_rows, parts, width)
+    grad_attended = by_head(
+        grad_attended.astype(BF16).reshape(seq_count, 2, block // 2, HEADS, head_size), 3
+    )
+    grad_blocks = grad_attended.reshape(seq_count, 2, block // 2, groups, group)
+    grad_blocks = grad_blocks.transpose(0, 3, 2, 1, 4).reshape(count, block // 2, 2 * group)
+    grad_blocks = exchange(grad_blocks).reshape(-1, 2 * group)
+
+    def blocks_of(value, rows):
+        return value.astype(BF16).reshape(devices, rows, -1)
+
     send_b, keep_b = split_cores(
-        [
-            grad_wout.astype(BF16).reshape(devices, -1, width),
-            by_part.transpose(0, 2, 1, 3).reshape(devices, -1, width),
-            grad_wproj.astype(BF16).reshape(devices, -1, width),
-        ]
-    )
-    own_b = scatter_sum(send_b, keep_b)
-
-    grad_back = attend_backward(
-        whole, grad_blocks.reshape(-1, 2 * group), stats, heads, head_size, block
-    )
-    grad_qkv = from_group(exchange(grad_back.reshape(count, block, 3 * group)), 3)
-    grad_bqv = jnp.concatenate(
-        [
-            jnp.sum(grad_qkv[:, :width], 0, dtype=F32),
-            jnp.sum(grad_qkv[:, 2 * width :], 0, dtype=F32),
-        ]
-    )
-    grad_wqkv = jnp.einsum("td,te->de", normed1, grad_qkv, preferred_element_type=F32)
-    grad_normed1 = jnp.einsum("te,de->td", grad_qkv, wqkv, preferred_element_type=F32)
-    _, norm1_back = jax.vjp(norm_affine, rows, gain1, bias1)
-    grad_in_part, grad_gain1, grad_bias1 = norm1_back(grad_normed1)
+        [blocks_of(grad_wout, shard_rows)]
+        + [blocks_of(grad_wfc[i], shard_rows) for i in range(parts)]
+        + [blocks_of(grad_wproj, parts * shard_rows)]
+    )
+    tower_b = scatter_plane(add(keep_b, swap_core(send_b)))
+    own_b = scatter_z(tower_b)
+
+    grad_qkv = attend_backward(qkv, grad_blocks, stats, ids, heads, head_size, block)
+    grad_normed1 = lax.dot_general(
+        grad_qkv, wqkv, (((1,), (1,)), ((), ())), preferred_element_type=F32
+    )
+    own_normed1 = scatter_sequence(grad_normed1.astype(BF16).reshape(count, block, width))
+    _, norm1_back = jax.vjp(lambda value: norm_affine(value, gain1, bias1), rows)
+    (grad_in_part,) = norm1_back(own_normed1.astype(F32).reshape(tokens, width))
     grad_inputs = (grad_middle + grad_in_part).astype(BF16).reshape(inputs.shape)
+
+    long_rows = sequence[:, :block].astype(F32).reshape(count * block, width)
+    _, norm1_long_back = jax.vjp(lambda g, b: norm_affine(long_rows, g, b), gain1, bias1)
+    grad_gain1, grad_bias1 = norm1_long_back(grad_normed1)
+    grad_wqkv = lax.dot_general(
+        normed1, grad_qkv, (((0,), (0,)), ((), ())), preferred_element_type=F32
+    )
+    sums = jnp.sum(grad_qkv, 0, dtype=F32).reshape(3, group)
+    here = (jnp.arange(groups) == group_index)[None, :, None]
+    grad_bqv = jnp.where(here, jnp.stack([sums[0], sums[2]])[:, None], 0.0)
+    grad_bqv = grad_bqv.reshape(2, groups * heads, head_size)[:, :HEADS]
     grads = (
         grad_gain1,
         grad_bias1,
@@ -516,33 +656,33 @@
         grad_bproj,
     )
     small_grads = pack_small([grad.reshape(1, -1) for grad in grads], sizes, devices)
-    by_part = grad_wqkv.astype(BF16).reshape(devices, shard_rows, 3, width)
-    send_a, keep_a = split_cores(
-        [
-            by_part.transpose(0, 2, 1, 3).reshape(devices, -1, width),
-            jnp.pad(small_grads, ((0, 0), (0, 0), (0, width - LANES))),
-        ]
-    )
-    own_a = scatter_sum(send_a, keep_a)
-    own_small = own_a[3 * shard_rows :]
+    small_grads = jnp.pad(small_grads, ((0, 0), (0, 0), (0, 3 * group - LANES)))
+    send_a, keep_a = split_cores([blocks_of(grad_wqkv, shard_rows), small_grads])
+    got_a = swap_core(send_a)
+    pair_a = jnp.concatenate(
+        [jnp.where(core == 0, keep_a, got_a), jnp.where(core == 0, got_a, keep_a)], -1
+    )
+    own_a = scatter_columns(scatter_plane(pair_a))
+    own_small = jnp.sum(
+        own_a[:, shard_rows:].reshape(classes, ROWS, CORES, 3 * group)[..., :LANES], (0, 2)
+    )
     own = [own_small[i, :size] for i, size in enumerate(sizes)]
-
-    def by_row(value, parts):
-        return value.reshape(parts, shard_rows, width).transpose(1, 0, 2).reshape(-1)
-
-    own_fc = own_b[shard_rows : (1 + parts) * shard_rows]
+    own_qkv = own_a[:, :shard_rows].reshape(classes, shard_rows, CORES, 3, group)
+    own_qkv = own_qkv.transpose(1, 3, 0, 2, 4).reshape(shard_rows, 3, groups * heads, head_size)
+    own_qkv = own_qkv[:, :, :HEADS].reshape(-1)
+    own_fc = own_b[shard_rows : (1 + parts) * shard_rows].reshape(parts, shard_rows, width)
     return (
         outputs,
         grad_inputs,
         own[0],
         own[1],
-        by_row(own_a[: 3 * shard_rows], 3),
+        own_qkv,
         own[2],
         own_b[:shard_rows].reshape(-1),
         own[3],
         own[4],
         own[5],
-        by_row(own_fc, parts),
+        own_fc.transpose(1, 0, 2).reshape(-1),
         own[6],
         own_b[(1 + parts) * shard_rows :].reshape(-1),
         own[7],

time: 446 us -> 683 us (1.53)
  the two profiles are of different devices: /device:TPU:8 before, /device:TPU:0 now
where the time goes in v1:
time: 683 us; the launch traced here: 678 us
  Pallas kernels  345 us (51%)
  waiting for transfers between devices  159 us (23%)
  local copies, waits for them, and re-layouts  61.7 us (9%)
  starting transfers between devices  50.6 us (7%)
  matrix products  30.6 us (4%)
  other arithmetic  29.6 us (4%)
    pallas_call x1, Pallas kernels, spread_weights(): pl.pallas_call(functools.partial(spread_kernel, parts), out_shape=[jax.Sh...  323 us
    ppermute x16, waiting for transfers between devices, swap_dp(): return lax.ppermute(value, 'dp', [(i, i ^ bit) for i in range(size)])  88.8 us
    ppermute x6, waiting for transfers between devices, shift_z(): lax.ppermute(value, 'seq', [(i, (i + CORES * step) % size) for i in range...  46.9 us
    ppermute x16, starting transfers between devices, swap_dp(): return lax.ppermute(value, 'dp', [(i, i ^ bit) for i in range(size)])  16.6 us
    unnamed x76, local copies, waits for them, and re-layouts  15.5 us
    ppermute x8, starting transfers between devices, swap_z(): lax.ppermute(value, 'seq', [(i, i ^ CORES * bit) for i in range(size)])  15.2 us
  transfers between devices with their start and end apart: 38, of which 21 were waited for; matrix products, arithmetic and copies ran while one was open for 12% of the time, Pallas kernels for 3%

profile of v1, /device:TPU:0, one launch (start us, length us, event | category | flops | bytes accessed | tf_op | source)
XLA Modules:
  0.0 678.2 jit_solution(5472310504980086806)
XLA Ops:
  24.4 3.5 collective-permute-start.10
  29.6 7.0 %collective-permute-done.10 = bf16[9,24,768]{2,1,0:T(8,128)(2,1)S(1)} collective-permute-done((bf16[9,24,768]{2,1,0:T(8,128)(2,1)}, bf16[9,24,768]{2,1,0:T(8,128)(2,1)S(1)}, u32[]{:S(2)}, u32[]{:S(2)}) %collective-permute-start.10) | collective-permute-done | bytes 331808 | tf_op jit(solution)/shard_map/ppermute | solution.py:29
  36.6 18.5 %collective-permute-done.11 = bf16[9,24,768]{2,1,0:T(8,128)(2,1)S(1)} collective-permute-done((bf16[9,24,768]{2,1,0:T(8,128)(2,1)}, bf16[9,24,768]{2,1,0:T(8,128)(2,1)S(1)}, u32[]{:S(2)}, u32[]{:S(2)}) %collective-permute-start.11) | collective-permute-done | bytes 331808 | tf_op jit(solution)/shard_map/ppermute | solution.py:29
  64.8 7.4 %collective-permute-done.15 = bf16[2,9,24,768]{3,2,1,0:T(8,128)(2,1)S(1)} collective-permute-done((bf16[2,9,24,768]{3,2,1,0:T(8,128)(2,1)S(1)}, bf16[2,9,24,768]{3,2,1,0:T(8,128)(2,1)S(1)}, u32[]{:S(2)}, u32[]{:S(2)}) %collective-permute-start.15) | collective-permute-done | bytes 663584 | tf_op jit(solution)/shard_map/ppermute | solution.py:39
  74.0 5.3 collective-permute-done.13
  82.9 27.9 %collective-permute-done.16 = bf16[2,2,9,24,768]{4,3,2,1,0:T(8,128)(2,1)S(1)} collective-permute-done((bf16[2,2,9,24,768]{4,3,2,1,0:T(8,128)(2,1)S(1)}, bf16[2,2,9,24,768]{4,3,2,1,0:T(8,128)(2,1)S(1)}, u32[]{:S(2)}, u32[]{:S(2)}) %collective-permute-start.16) | collective-permute-done | bytes 1327136 | tf_op jit(solution)/shard_map/ppermute | solution.py:39
  115.7 8.7 %collective-permute-done.6 = bf16[2,2,32,1152]{3,2,1,0:T(8,128)(2,1)S(1)} collective-permute-done((bf16[2,2,32,1152]{3,2,1,0:T(8,128)(2,1)S(1)}, bf16[2,2,32,1152]{3,2,1,0:T(8,128)(2,1)S(1)}, u32[]{:S(2)}, u32[]{:S(2)}) %collective-permute-start.6) | collective-permute-done | bytes 294944 | tf_op jit(solution)/shard_map/ppermute | solution.py:39
  132.2 9.8 %shard_map.255 = (bf16[512,384]{1,0:T(8,128)(2,1)}, f32[3,1024]{1,0:T(4,128)S(1)}, bf16[1024,576]{1,0:T(8,128)(2,1)S(1)}, bf16[1024,768]{1,0:T(8,128)(2,1)S(1)}, f32[1,1024]{1,0:T(1,128)S(1)}) custom-call(bf16[8,144,768]{2,1,0:T(8,128)(2,1)S(1)} %bitcast.395, bf16[768,576]{1,0:T(8,128)(2,1)S(1)} %bitcast.399, f32[1,768]{1,0:T(1,128)S(1)} %get-tuple-element.30.gain, ...), custom_call_target="tpu_custom_call" | custom-call | flops 1308622848 | bytes 6291456 | tf_op jit(solution)/shard_map/pallas_call | solution.py:458
  144.4 4.3 all-to-all-start
  152.7 8.5 %all-to-all-done = bf16[8,64,384]{2,1,0:T(8,128)(2,1)} async-done(((bf16[8,64,384]{2,1,0:T(8,128)(2,1)}), bf16[8,64,384]{2,1,0:T(8,128)(2,1)}, u32[]{:S(2)}, u32[]{:S(2)}) %all-to-all-start) | async-done | bytes 393248 | tf_op jit(solution)/shard_map/all_to_all | solution.py:190
  165.0 322.8 %shard_map.257 = (bf16[16,2,24,768]{3,2,1,0:T(8,128)(2,1)}, bf16[4,16,2,24,768]{4,3,2,1,0:T(8,128)(2,1)}, bf16[16,2,4,24,768]{4,3,2,1,0:T(8,128)(2,1)}) custom-call(bf16[16,9,24,768]{3,2,1,0:T(8,128)(2,1)} %bitcast.60.half, bf16[16,9,24,768]{3,2,1,0:T(8,128)(2,1)} %collective-permute-done.17.other), custom_call_target="tpu_custom_call" | custom-call | tf_op jit(solution)/shard_map/pallas_call | solution.py:302
  490.0 4.2 fusion.67
  502.2 3.7 convert_bitcast_fusion
  511.6 3.9 all-to-all-start.1
  531.5 8.8 %shard_map.258 = bf16[1024,576]{1,0:T(8,128)(2,1)S(1)} custom-call(bf16[1024,576]{1,0:T(8,128)(2,1)S(1)} %copy-done.1, bf16[512,384]{1,0:T(8,128)(2,1)S(1)} %bitcast.401, f32[3,1024]{1,0:T(4,128)S(1)} %get-tuple-element.43.stats, f32[1,1024]{1,0:T(1,128)S(1)} %get-tuple-element.44.ids), custom_call_target="tpu_custom_call" | custom-call | flops 1006632960 | bytes 3538944 | tf_op jit(solution)/shard_map/pallas_call | solution.py:483
  553.0 5.2 fusion.22
  561.5 6.7 collective-permute-done.24
  580.3 4.4 collective-permute-done.26
  585.4 5.9 collective-permute-done.19
  594.6 5.4 add_convert_fusion
  613.3 16.7 %collective-permute-done.29 = bf16[2,2,216,768]{3,2,1,0:T(8,128)(2,1)} collective-permute-done((bf16[2,2,216,768]{3,2,1,0:T(8,128)(2,1)}, bf16[2,2,216,768]{3,2,1,0:T(8,128)(2,1)}, u32[]{:S(2)}, u32[]{:S(2)}) %collective-permute-start.29) | collective-permute-done | bytes 1327136 | tf_op jit(solution)/shard_map/ppermute | solution.py:39
  636.5 9.2 %collective-permute-done.30 = bf16[2,216,768]{2,1,0:T(8,128)(2,1)S(1)} collective-permute-done((bf16[2,216,768]{2,1,0:T(8,128)(2,1)S(1)}, bf16[2,216,768]{2,1,0:T(8,128)(2,1)S(1)}, u32[]{:S(2)}, u32[]{:S(2)}) %collective-permute-start.30) | collective-permute-done | bytes 663584 | tf_op jit(solution)/shard_map/ppermute | solution.py:39
  653.9 3.6 collective-permute-done.35
  657.5 17.9 %collective-permute-done.34 = bf16[216,768]{1,0:T(8,128)(2,1)S(1)} collective-permute-done((bf16[216,768]{1,0:T(8,128)(2,1)S(1)}, bf16[216,768]{1,0:T(8,128)(2,1)S(1)}, u32[]{:S(2)}, u32[]{:S(2)}) %collective-permute-start.34) | collective-permute-done | bytes 331808 | tf_op jit(solution)/shard_map/ppermute | solution.py:29
  (310 shorter events, 156.9 us)
Async XLA Ops:
  27.9 27.1 %collective-permute-start.11 = (bf16[9,24,768]{2,1,0:T(8,128)(2,1)}, bf16[9,24,768]{2,1,0:T(8,128)(2,1)S(1)}, u32[]{:S(2)}, u32[]{:S(2)}) collective-permute-start(bf16[9,24,768]{2,1,0:T(8,128)(2,1)} %shard_map.256), channel_id=1, source_target_pairs={{0,4},{1,5},{2,6},{3,7},{4,0},{5,1},{6,2},{7,3},{8,12},{9,13},{10,... | collective-permute-start | bytes 995336 | tf_op jit(solution)/shard_map/ppermute | solution.py:29
  29.0 26.1 %collective-permute-start.12 = (bf16[9,24,768]{2,1,0:T(8,128)(2,1)}, bf16[9,24,768]{2,1,0:T(8,128)(2,1)S(1)}, u32[]{:S(2)}, u32[]{:S(2)}) collective-permute-start(bf16[9,24,768]{2,1,0:T(8,128)(2,1)} %shard_map.256), channel_id=1, source_target_pairs={{0,2},{1,3},{2,4},{3,5},{4,6},{5,7},{6,0},{7,1},{8,10},{9,11},{10,... | collective-permute-start | bytes 995336 | tf_op jit(solution)/shard_map/ppermute | solution.py:29
  55.4 16.8 %collective-permute-start.15 = (bf16[2,9,24,768]{3,2,1,0:T(8,128)(2,1)S(1)}, bf16[2,9,24,768]{3,2,1,0:T(8,128)(2,1)S(1)}, u32[]{:S(2)}, u32[]{:S(2)}) collective-permute-start(bf16[2,9,24,768]{3,2,1,0:T(8,128)(2,1)S(1)} %get-tuple-element.69), channel_id=1, source_target_pairs={{0,16},{8,24},{16,0},{24,8},{1,17},{9,25},{17,1},{25,9},{2,18},{10... | collective-permute-start | bytes 1990664 | tf_op jit(solution)/shard_map/ppermute | solution.py:39
  57.8 22.4 %collective-permute-start = (bf16[144,768]{1,0:T(8,128)(2,1)}, bf16[144,768]{1,0:T(8,128)(2,1)}, u32[]{:S(2)}, u32[]{:S(2)}) collective-permute-start(bf16[144,768]{1,0:T(8,128)(2,1)} %dynamic-slice_bitcast_fusion.10), channel_id=1, source_target_pairs={{0,4},{1,5},{2,6},{3,7},{4,0},{5,1},{6,2},{7,3},{8,12},{9,13},{10,... | collective-permute-start | bytes 663560 | tf_op jit(solution)/shard_map/ppermute | solution.py:64
  61.3 17.9 %collective-permute-start.13 = (bf16[2,9,24,768]{3,2,1,0:T(8,128)(2,1)S(1)}, bf16[2,9,24,768]{3,2,1,0:T(8,128)(2,1)S(1)}, u32[]{:S(2)}, u32[]{:S(2)}) collective-permute-start(bf16[2,9,24,768]{3,2,1,0:T(8,128)(2,1)S(1)} %get-tuple-element.68), channel_id=1, source_target_pairs={{0,8},{8,0},{16,24},{24,16},{1,9},{9,1},{17,25},{25,17},{2,10},{10... | collective-permute-start | bytes 1990664 | tf_op jit(solution)/shard_map/ppermute | solution.py:39
  63.5 17.8 %collective-permute-start.7 = (bf16[2,32,1152]{2,1,0:T(8,128)(2,1)S(1)}, bf16[2,32,1152]{2,1,0:T(8,128)(2,1)S(1)}, u32[]{:S(2)}, u32[]{:S(2)}) collective-permute-start(bf16[2,32,1152]{2,1,0:T(8,128)(2,1)S(1)} %get-tuple-element.116), channel_id=1, source_target_pairs={{0,16},{8,24},{16,0},{24,8},{1,17},{9,25},{17,1},{25,9},{2,18},{10... | collective-permute-start | bytes 442376 | tf_op jit(solution)/shard_map/ppermute | solution.py:39
  64.2 50.6 %collective-permute-start.5 = (bf16[2,32,1152]{2,1,0:T(8,128)(2,1)S(1)}, bf16[2,32,1152]{2,1,0:T(8,128)(2,1)S(1)}, u32[]{:S(2)}, u32[]{:S(2)}) collective-permute-start(bf16[2,32,1152]{2,1,0:T(8,128)(2,1)S(1)} %get-tuple-element.115), channel_id=1, source_target_pairs={{0,8},{8,0},{16,24},{24,16},{1,9},{9,1},{17,25},{25,17},{2,10},{10... | collective-permute-start | bytes 442376 | tf_op jit(solution)/shard_map/ppermute | solution.py:39
  72.4 38.4 %collective-permute-start.16 = (bf16[2,2,9,24,768]{4,3,2,1,0:T(8,128)(2,1)S(1)}, bf16[2,2,9,24,768]{4,3,2,1,0:T(8,128)(2,1)S(1)}, u32[]{:S(2)}, u32[]{:S(2)}) collective-permute-start(bf16[2,2,9,24,768]{4,3,2,1,0:T(8,128)(2,1)S(1)} %pad_maximum_fusion.2), channel_id=1, source_target_pairs={{0,8},{8,0},{16,24},{24,16},{1,9},{9,1},{17,25},{25,17},{2,10},{10... | collective-permute-start | bytes 3981320 | tf_op jit(solution)/shard_map/ppermute | solution.py:39
  79.5 31.6 %collective-permute-start.14 = (bf16[2,2,9,24,768]{4,3,2,1,0:T(8,128)(2,1)S(1)}, bf16[2,2,9,24,768]{4,3,2,1,0:T(8,128)(2,1)S(1)}, u32[]{:S(2)}, u32[]{:S(2)}) collective-permute-start(bf16[2,2,9,24,768]{4,3,2,1,0:T(8,128)(2,1)S(1)} %pad_maximum_fusion.1), channel_id=1, source_target_pairs={{0,16},{8,24},{16,0},{24,8},{1,17},{9,25},{17,1},{25,9},{2,18},{10... | collective-permute-start | bytes 3981320 | tf_op jit(solution)/shard_map/ppermute | solution.py:39
  81.2 43.8 %collective-permute-start.1 = (bf16[2,144,768]{2,1,0:T(8,128)(2,1)S(1)}, bf16[2,144,768]{2,1,0:T(8,128)(2,1)S(1)}, u32[]{:S(2)}, u32[]{:S(2)}) collective-permute-start(bf16[2,144,768]{2,1,0:T(8,128)(2,1)S(1)} %pad_maximum_fusion.8), channel_id=1, source_target_pairs={{0,2},{1,3},{2,0},{3,1},{4,6},{5,7},{6,4},{7,5},{8,10},{9,11},{10,... | collective-permute-start | bytes 1327112 | tf_op jit(solution)/shard_map/ppermute | solution.py:64
  81.4 34.3 %collective-permute-start.8 = (bf16[2,2,32,1152]{3,2,1,0:T(8,128)(2,1)S(1)}, bf16[2,2,32,1152]{3,2,1,0:T(8,128)(2,1)S(1)}, u32[]{:S(2)}, u32[]{:S(2)}) collective-permute-start(bf16[2,2,32,1152]{3,2,1,0:T(8,128)(2,1)S(1)} %pad_maximum_fusion.11), channel_id=1, source_target_pairs={{0,8},{8,0},{16,24},{24,16},{1,9},{9,1},{17,25},{25,17},{2,10},{10... | collective-permute-start | bytes 884744 | tf_op jit(solution)/shard_map/ppermute | solution.py:39
  114.8 50.1 %collective-permute-start.17 = (bf16[16,9,24,768]{3,2,1,0:T(8,128)(2,1)}, bf16[16,9,24,768]{3,2,1,0:T(8,128)(2,1)}, u32[]{:S(2)}, u32[]{:S(2)}) collective-permute-start(bf16[16,9,24,768]{3,2,1,0:T(8,128)(2,1)} %bitcast.60.half), channel_id=1, source_target_pairs={{0,1},{1,0},{2,3},{3,2},{4,5},{5,4},{6,7},{7,6},{8,9},{9,8},{10,11... | collective-permute-start | bytes 15925256 | tf_op jit(solution)/shard_map/ppermute | solution.py:34
  144.4 16.8 %all-to-all-start = ((bf16[8,64,384]{2,1,0:T(8,128)(2,1)}), bf16[8,64,384]{2,1,0:T(8,128)(2,1)}, u32[]{:S(2)}, u32[]{:S(2)}) async-start(bf16[8,64,384]{2,1,0:T(8,128)(2,1)} %bitcast.42), calls=%async_computation | async-start | bytes 786432 | tf_op jit(solution)/shard_map/all_to_all | solution.py:190
  511.6 18.6 %all-to-all-start.1 = ((bf16[8,64,384]{2,1,0:T(8,128)(2,1)}), bf16[8,64,384]{2,1,0:T(8,128)(2,1)S(1)}, u32[]{:S(2)}, u32[]{:S(2)}) async-start(bf16[8,64,384]{2,1,0:T(8,128)(2,1)} %reshape.381), calls=%async_computation.1 | async-start | bytes 786432 | tf_op jit(solution)/shard_map/all_to_all | solution.py:190
  529.8 64.7 %collective-permute-start.28 = (bf16[16,216,768]{2,1,0:T(8,128)(2,1)}, bf16[16,216,768]{2,1,0:T(8,128)(2,1)}, u32[]{:S(2)}, u32[]{:S(2)}) collective-permute-start(bf16[16,216,768]{2,1,0:T(8,128)(2,1)} %get-tuple-element.60), channel_id=1, source_target_pairs={{0,1},{1,0},{2,3},{3,2},{4,5},{5,4},{6,7},{7,6},{8,9},{9,8},{10,11... | collective-permute-start | bytes 15925256 | tf_op jit(solution)/shard_map/ppermute | solution.py:34
  560.7 17.8 %collective-permute-start.18 = (bf16[2,2,128,768]{3,2,1,0:T(8,128)(2,1)S(1)}, bf16[2,2,128,768]{3,2,1,0:T(8,128)(2,1)S(1)}, u32[]{:S(2)}, u32[]{:S(2)}) collective-permute-start(bf16[2,2,128,768]{3,2,1,0:T(8,128)(2,1)S(1)} %dynamic-slice_bitcast_fusion.2), channel_id=1, source_target_pairs={{0,1},{1,0},{2,3},{3,2},{4,5},{5,4},{6,7},{7,6},{8,9},{9,8},{10,11... | collective-permute-start | bytes 2359304 | tf_op jit(solution)/shard_map/ppermute | solution.py:34
  578.8 12.5 %collective-permute-start.19 = (bf16[2,128,768]{2,1,0:T(8,128)(2,1)S(1)}, bf16[2,128,768]{2,1,0:T(8,128)(2,1)S(1)}, u32[]{:S(2)}, u32[]{:S(2)}) collective-permute-start(bf16[2,128,768]{2,1,0:T(8,128)(2,1)S(1)} %dynamic-slice_bitcast_fusion.7), channel_id=1, source_target_pairs={{0,2},{1,3},{2,0},{3,1},{4,6},{5,7},{6,4},{7,5},{8,10},{9,11},{10,... | collective-permute-start | bytes 1179656 | tf_op jit(solution)/shard_map/ppermute | solution.py:64
  592.8 19.0 %collective-permute-start.20 = (bf16[128,768]{1,0:T(8,128)(2,1)}, bf16[128,768]{1,0:T(8,128)(2,1)}, u32[]{:S(2)}, u32[]{:S(2)}) collective-permute-start(bf16[128,768]{1,0:T(8,128)(2,1)} %dynamic-slice_bitcast_fusion.11), channel_id=1, source_target_pairs={{0,4},{1,5},{2,6},{3,7},{4,0},{5,1},{6,2},{7,3},{8,12},{9,13},{10,... | collective-permute-start | bytes 589832 | tf_op jit(solution)/shard_map/ppermute | solution.py:64
  601.7 28.3 %collective-permute-start.29 = (bf16[2,2,216,768]{3,2,1,0:T(8,128)(2,1)}, bf16[2,2,216,768]{3,2,1,0:T(8,128)(2,1)}, u32[]{:S(2)}, u32[]{:S(2)}) collective-permute-start(bf16[2,2,216,768]{3,2,1,0:T(8,128)(2,1)} %dynamic-slice_bitcast_fusion.1), channel_id=1, source_target_pairs={{0,16},{8,24},{16,0},{24,8},{1,17},{9,25},{17,1},{25,9},{2,18},{10... | collective-permute-start | bytes 3981320 | tf_op jit(solution)/shard_map/ppermute | solution.py:39
  603.6 29.0 %collective-permute-start.31 = (bf16[2,2,216,768]{3,2,1,0:T(8,128)(2,1)}, bf16[2,2,216,768]{3,2,1,0:T(8,128)(2,1)}, u32[]{:S(2)}, u32[]{:S(2)}) collective-permute-start(bf16[2,2,216,768]{3,2,1,0:T(8,128)(2,1)} %dynamic-slice_bitcast_fusion), channel_id=1, source_target_pairs={{0,8},{8,0},{16,24},{24,16},{1,9},{9,1},{17,25},{25,17},{2,10},{10... | collective-permute-start | bytes 3981320 | tf_op jit(solution)/shard_map/ppermute | solution.py:39
  632.1 13.6 %collective-permute-start.30 = (bf16[2,216,768]{2,1,0:T(8,128)(2,1)S(1)}, bf16[2,216,768]{2,1,0:T(8,128)(2,1)S(1)}, u32[]{:S(2)}, u32[]{:S(2)}) collective-permute-start(bf16[2,216,768]{2,1,0:T(8,128)(2,1)S(1)} %dynamic-slice_bitcast_fusion.4), channel_id=1, source_target_pairs={{0,8},{8,0},{16,24},{24,16},{1,9},{9,1},{17,25},{25,17},{2,10},{10... | collective-permute-start | bytes 1990664 | tf_op jit(solution)/shard_map/ppermute | solution.py:39
  634.3 12.6 %collective-permute-start.32 = (bf16[2,216,768]{2,1,0:T(8,128)(2,1)S(1)}, bf16[2,216,768]{2,1,0:T(8,128)(2,1)S(1)}, u32[]{:S(2)}, u32[]{:S(2)}) collective-permute-start(bf16[2,216,768]{2,1,0:T(8,128)(2,1)S(1)} %dynamic-slice_bitcast_fusion.3), channel_id=1, source_target_pairs={{0,16},{8,24},{16,0},{24,8},{1,17},{9,25},{17,1},{25,9},{2,18},{10... | collective-permute-start | bytes 1990664 | tf_op jit(solution)/shard_map/ppermute | solution.py:39
  649.2 26.1 %collective-permute-start.34 = (bf16[216,768]{1,0:T(8,128)(2,1)S(1)}, bf16[216,768]{1,0:T(8,128)(2,1)S(1)}, u32[]{:S(2)}, u32[]{:S(2)}) collective-permute-start(bf16[216,768]{1,0:T(8,128)(2,1)S(1)} %get-tuple-element.77), channel_id=1, source_target_pairs={{0,4},{1,5},{2,6},{3,7},{4,0},{5,1},{6,2},{7,3},{8,12},{9,13},{10,... | collective-permute-start | bytes 995336 | tf_op jit(solution)/shard_map/ppermute | solution.py:29
  651.1 24.2 %collective-permute-start.33 = (bf16[216,768]{1,0:T(8,128)(2,1)S(1)}, bf16[216,768]{1,0:T(8,128)(2,1)S(1)}, u32[]{:S(2)}, u32[]{:S(2)}) collective-permute-start(bf16[216,768]{1,0:T(8,128)(2,1)S(1)} %get-tuple-element.76), channel_id=1, source_target_pairs={{0,2},{1,3},{2,4},{3,5},{4,6},{5,7},{6,0},{7,1},{8,10},{9,11},{10,... | collective-permute-start | bytes 995336 | tf_op jit(solution)/shard_map/ppermute | solution.py:29
  (45 other events, 257.5 us)

commit v2 on v1

--- a/solution.py
+++ b/solution.py
@@ -1,4 +1,5 @@
 import functools
+import math
 
 import jax
 import jax.numpy as jnp
@@ -52,11 +53,9 @@
     return lax.dynamic_slice_in_dim(twice, lax.rem(count - place, count), count, 0)
 
 
-def gather_z(shard):
+def z_pieces(shard):
     heights = lax.axis_size("seq") // CORES
-    level = lax.axis_index("seq") // CORES
-    pieces = [shard] + [shift_z(shard, -step) for step in range(1, heights)]
-    return roll_blocks(pieces, level)
+    return [shard] + [shift_z(shard, -step) for step in range(1, heights)]
 
 
 def swap_z(value, bit):
@@ -64,63 +63,56 @@
     return lax.ppermute(value, "seq", [(i, i ^ (CORES * bit)) for i in range(size)])
 
 
-def gather_plane(tower):
-    heights = tower.shape[0]
-    shard = tower.shape[1:]
+def gather_plane(low, high, axis):
     if lax.axis_size("dp") == 4:
         plane = lax.axis_index("dp")
         y, x = plane // 2, plane % 2
-        low, high = tower[: heights // 2], tower[heights // 2 :]
-        low_x = ordered(x, low, swap_dp(low, 1), 0)
-        high_y = ordered(y, high, swap_dp(high, 2), 0)
-        low_all = ordered(y, low_x, swap_dp(low_x, 2), 0)
-        high_all = ordered(x, high_y, swap_dp(high_y, 1), 1)
-        half = jnp.concatenate([low_all, high_all], 2)
+        low_x = ordered(x, low, swap_dp(low, 1), axis)
+        high_y = ordered(y, high, swap_dp(high, 2), axis)
+        low_all = ordered(y, low_x, swap_dp(low_x, 2), axis)
+        high_all = ordered(x, high_y, swap_dp(high_y, 1), axis + 1)
+        half = jnp.concatenate([low_all, high_all], axis + 2)
+        count = 4 * half.shape[axis + 2]
     else:
-        half = lax.all_gather(tower, "dp", axis=0, tiled=False)
-    return half.reshape(-1, *shard)
+        tower = jnp.concatenate([low, high], axis)
+        half = lax.all_gather(tower, "dp", axis=axis, tiled=True)
+        return half
+    return half.reshape(*low.shape[:axis], count, *low.shape[axis + 1 :])
 
 
 def pick(value, index, axis):
     return lax.dynamic_index_in_dim(value, index, axis, keepdims=False)
 
 
-def split_cores(parts):
-    core = lax.axis_index("seq") % CORES
-    parts = [part.reshape(-1, CORES, *part.shape[1:]) for part in parts]
-    send = jnp.concatenate([pick(part, 1 - core, 1) for part in parts], 1)
-    keep = jnp.concatenate([pick(part, core, 1) for part in parts], 1)
-    return send, keep
-
-
 def add(mine, other):
     return (mine.astype(F32) + other.astype(F32)).astype(mine.dtype)
 
 
-def scatter_plane(split):
-    rows, columns = split.shape[1:]
+def scatter_plane(split, axis):
     planes = lax.axis_size("dp")
     heights = lax.axis_size("seq") // CORES
     if planes == 4:
         plane = lax.axis_index("dp")
         y, x = plane // 2, plane % 2
-        split = split.reshape(2, 2, heights, rows, columns)
-        low, high = split[:, :, : heights // 2], split[:, :, heights // 2 :]
-        low = add(pick(low, y, 0), swap_dp(pick(low, 1 - y, 0), 2))
-        high = add(pick(high, x, 1), swap_dp(pick(high, 1 - x, 1), 1))
-        low = add(pick(low, x, 0), swap_dp(pick(low, 1 - x, 0), 1))
-        high = add(pick(high, y, 0), swap_dp(pick(high, 1 - y, 0), 2))
-        return jnp.concatenate([low, high], 0)
-    split = split.reshape(planes, heights, rows, columns)
-    return lax.psum_scatter(split, "dp", scatter_dimension=0, tiled=False)
-
-
-def scatter_z(tower):
-    heights = tower.shape[0]
+        split = split.reshape(
+            *split.shape[:axis], 2, 2, heights, *split.shape[axis + 1 :]
+        )
+        low = lax.slice_in_dim(split, 0, heights // 2, axis=axis + 2)
+        high = lax.slice_in_dim(split, heights // 2, heights, axis=axis + 2)
+        low = add(pick(low, y, axis), swap_dp(pick(low, 1 - y, axis), 2))
+        high = add(pick(high, x, axis + 1), swap_dp(pick(high, 1 - x, axis + 1), 1))
+        low = add(pick(low, x, axis), swap_dp(pick(low, 1 - x, axis), 1))
+        high = add(pick(high, y, axis), swap_dp(pick(high, 1 - y, axis), 2))
+        return jnp.concatenate([low, high], axis)
+    return lax.psum_scatter(split, "dp", scatter_dimension=axis, tiled=True)
+
+
+def scatter_z(tower, axis):
+    heights = lax.axis_size("seq") // CORES
     level = lax.axis_index("seq") // CORES
-    mine = pick(tower, level, 0).astype(F32)
+    mine = pick(tower, level, axis).astype(F32)
     for step in range(1, heights):
-        mine += shift_z(pick(tower, lax.rem(level + step, heights), 0), step).astype(F32)
+        mine += shift_z(pick(tower, lax.rem(level + step, heights), axis), step).astype(F32)
     return mine
 
 
@@ -135,11 +127,12 @@
     level, top, half = z_bits()
     core = lax.axis_index("seq") % CORES
     held = ordered(half, pick(blocks, half, 0), swap_z(pick(blocks, 1 - half, 0), top), 0)
+    early = held
     axis, bit = 1, top // 2
     while bit:
         held = ordered(level // bit % 2, held, swap_z(held, bit), axis)
         axis, bit = axis + 1, bit // 2
-    return ordered(core, held, swap_core(held), axis).reshape(-1, *blocks.shape[1:])
+    return early, ordered(core, held, swap_core(held), axis).reshape(-1, *blocks.shape[1:])
 
 
 def scatter_sequence(partial):
@@ -259,62 +252,367 @@
     )(*grads)
 
 
-def stack_kernel(out_ref, fc_ref, proj_ref, after_ref, stacked):
+ANYWHERE = pl.BlockSpec(memory_space=pl.ANY)
+
+
+def first_kernel(group, weight, rows, marks, *refs):
+    vectors, (columns, blocks, lines, extra) = refs[:-4], refs[-4:]
+    classes, _, width_pair = columns.shape
+    shard_rows, width = weight.shape[0], weight.shape[1] // 3
+    lines[...] = jnp.zeros_like(lines)
+    for i, vector in enumerate(vectors):
+        for start in range(0, width_pair, 3 * group):
+            at = shard_rows + i
+            lines[at : at + 1, start : start + vector.shape[1]] = vector[...].astype(F32)
+    for kind in range(classes):
+        for core in range(CORES):
+            lo = (kind * CORES + core) * group
+            for part in range(3):
+                start = (core * 3 + part) * group
+                if lo < width:
+                    piece = weight[:, part * width + lo : part * width + lo + group].astype(F32)
+                else:
+                    piece = jnp.zeros((shard_rows, group), F32)
+                lines[:shard_rows, start : start + group] = piece
+        columns[kind] = lines[...].astype(BF16)
+    block = rows.shape[1]
+    extra[...] = jnp.zeros_like(extra)
+    for i in range(rows.shape[0]):
+        blocks[i, :block, :] = rows[i]
+        extra[:1, :block] = marks[i : i + 1, :].astype(F32)
+        blocks[i, block:, :] = extra[...].astype(BF16)
+
+
+def first_blocks(weight, rows, marks, vectors, classes, group):
+    shard_rows = weight.shape[0]
+    count, block, width = rows.shape
+    return pl.pallas_call(
+        functools.partial(first_kernel, group),
+        out_shape=[
+            jax.ShapeDtypeStruct((classes, shard_rows + ROWS, CORES * 3 * group), BF16),
+            jax.ShapeDtypeStruct((count, block + 16, width), BF16),
+        ],
+        in_specs=vmem_specs(3 + len(vectors)),
+        out_specs=vmem_specs(2),
+        scratch_shapes=[
+            pltpu.VMEM((shard_rows + ROWS, CORES * 3 * group), F32),
+            pltpu.VMEM((16, width), F32),
+        ],
+    )(weight, rows, marks, *vectors)
+
+
+def stack_kernel(out_ref, fc_ref, after, stacked):
     width = out_ref.shape[1]
     stacked[0] = out_ref[...]
-    parts = fc_ref.shape[1] // width
-    for i in range(parts):
+    for i in range(fc_ref.shape[1] // width):
         stacked[1 + i] = fc_ref[:, i * width : (i + 1) * width]
-    for i in range(parts):
-        stacked[1 + parts + i] = proj_ref[i]
-
-
-def stack_weights(w_out, w_fc, w_proj, after):
+
+
+def stack_weights(w_out, w_fc, after):
     rows, width = w_out.shape
-    parts = w_fc.shape[1] // width
     return pl.pallas_call(
         stack_kernel,
-        out_shape=jax.ShapeDtypeStruct((1 + 2 * parts, rows, width), BF16),
-        in_specs=vmem_specs(3) + [pl.BlockSpec(memory_space=pl.ANY)],
+        out_shape=jax.ShapeDtypeStruct((1 + w_fc.shape[1] // width, rows, width), BF16),
+        in_specs=vmem_specs(2) + [ANYWHERE],
         out_specs=vmem_specs(1)[0],
-    )(w_out, w_fc, w_proj, after)
-
-
-def spread_kernel(parts, half, other, out_ref, fc_ref, proj_ref, sems):
+    )(w_out, w_fc, after)
+
+
+def tower_kernel(axis, count, *refs):
+    pieces, low, high = refs[:count], refs[-2], refs[-1]
+    level = lax.axis_index("seq") // CORES
+    for step, piece in enumerate(pieces):
+        place = lax.rem(level + step, count)
+        for half, start in ((low, 0), (high, count // 2)):
+
+            @pl.when((place >= start) & (place < start + count // 2))
+            def _():
+                if axis == 1:
+                    half[:, place - start] = piece[...]
+                else:
+                    half[place - start] = piece[...]
+
+
+def build_tower(pieces, axis, after):
+    count = len(pieces)
+    shape = pieces[0].shape
+    shape = (*shape[:axis], count // 2, *shape[axis:])
+    return pl.pallas_call(
+        functools.partial(tower_kernel, axis, count),
+        out_shape=[jax.ShapeDtypeStruct(shape, BF16)] * 2,
+        in_specs=vmem_specs(count) + [ANYWHERE] * len(after),
+        out_specs=vmem_specs(2),
+        compiler_params=pltpu.CompilerParams(vmem_limit_bytes=32 * 2**20),
+    )(*pieces, *after)
+
+
+def one_hot_order(order_ref):
+    width = order_ref.shape[1]
+    features = lax.broadcasted_iota(jnp.int32, (width, width), 0)
+    return jnp.where(features == order_ref[...], 1.0, 0.0).astype(BF16)
+
+
+def contract_last(left, right):
+    return lax.dot_general(left, right, (((1,), (1,)), ((), ())), preferred_element_type=F32)
+
+
+def middle_kernel(
+    groups,
+    half1,
+    other1,
+    half2,
+    other2,
+    attended,
+    inputs,
+    cotangent,
+    order_ref,
+    bout,
+    gain,
+    bias,
+    bfc,
+    bproj,
+    outputs,
+    grad_middle,
+    grad_blocks,
+    placed_a,
+    placed_n,
+    hidden,
+    grad_pre,
+    grad_out,
+    sum_out,
+    sum_gain,
+    sum_bias,
+    sum_fc,
+    sum_proj,
+    weights1,
+    weights2,
+    attended_rows,
+    slopes,
+    permuted,
+    sems,
+):
+    parts = weights1.shape[0] - 1
+    width = weights1.shape[2]
+    side = width // CORES
+    seq_count, block, _ = inputs.shape
+    tokens = seq_count * block
     core = lax.rem(lax.axis_index("seq"), CORES)
+    chips, rows2 = half2.shape[:2]
     copies = []
-    for source, place in ((half, core), (other, 1 - core)):
-        pairs = [(source.at[:, 0], out_ref.at[:, place])]
-        pairs += [(source.at[:, 1 + i], fc_ref.at[i, :, place]) for i in range(parts)]
-        pairs += [(source.at[:, pl.ds(1 + parts, parts)], proj_ref.at[:, place])]
-        for pair in pairs:
-            copies.append(pltpu.make_async_copy(*pair, sems.at[len(copies)]))
+    for kind in range(parts + 1):
+        for index, source in enumerate((half1, other1)):
+            copies.append(
+                pltpu.make_async_copy(
+                    source.at[kind],
+                    weights1.at[kind, pl.ds(index * side, side)],
+                    sems.at[len(copies)],
+                )
+            )
+    ready1 = len(copies)
+    if chips == 1:
+        copies.append(pltpu.make_async_copy(half2.at[0], weights2, sems.at[len(copies)]))
+    for index, source in enumerate((half2, other2) if chips > 1 else ()):
+        place = core if index == 0 else 1 - core
+        for chip in range(chips):
+            start = pl.multiple_of((chip * CORES + place) * rows2, rows2)
+            copies.append(
+                pltpu.make_async_copy(
+                    source.at[chip], weights2.at[pl.ds(start, rows2)], sems.at[len(copies)]
+                )
+            )
     for copy in copies:
         copy.start()
-    for copy in copies:
+    order = one_hot_order(order_ref)
+
+    half_block = block // 2
+    group = attended.shape[2] // 2
+    for i in range(seq_count):
+        for g in range(groups):
+            for part in range(2):
+                start = i * block + part * half_block
+                attended_rows[start : start + half_block, g * group : (g + 1) * group] = attended[
+                    i * groups + g, :, part * group : (part + 1) * group
+                ]
+    placed = jnp.dot(attended_rows[:, :width], order, preferred_element_type=F32).astype(BF16)
+    placed_a[...] = placed
+    for copy in copies[:2]:
         copy.wait()
-
-
-def spread_weights(half, other):
-    chips, kinds, rows, width = half.shape
-    parts = (kinds - 1) // 2
-    anywhere = pl.BlockSpec(memory_space=pl.ANY)
-    wout, wfc, wproj = pl.pallas_call(
-        functools.partial(spread_kernel, parts),
+    rows = inputs[...].astype(F32).reshape(tokens, width)
+    middle = rows + (jnp.dot(placed, weights1[0], preferred_element_type=F32) + bout[...])
+    center = jnp.mean(middle, -1, keepdims=True)
+    centered = middle - center
+    scale = lax.rsqrt(jnp.mean(centered * centered, -1, keepdims=True) + EPSILON)
+    unit = centered * scale
+    normed = (unit * gain[...] + bias[...]).astype(BF16)
+    placed = jnp.dot(normed, order, preferred_element_type=F32).astype(BF16)
+    placed_n[...] = placed
+    for copy in copies[2:ready1]:
+        copy.wait()
+    curve = math.sqrt(2.0 / math.pi)
+    for q in range(parts):
+        lo = q * width
+        pre = jnp.dot(placed, weights1[1 + q], preferred_element_type=F32)
+        pre = pre + bfc[:, lo : lo + width]
+        square = pre * pre
+        tanh = jnp.tanh(curve * (pre + 0.044715 * (pre * square)))
+        hidden[:, lo : lo + width] = (0.5 * pre * (1.0 + tanh)).astype(BF16)
+        slopes[:, lo : lo + width] = 0.5 * (1.0 + tanh) + 0.5 * pre * (1.0 - tanh * tanh) * (
+            curve * (1.0 + 3 * 0.044715 * square)
+        )
+    for copy in copies[ready1:]:
+        copy.wait()
+    result = middle + bproj[...]
+    for q in range(parts):
+        lo = q * width
+        result += jnp.dot(
+            hidden[:, lo : lo + width], weights2[lo : lo + width], preferred_element_type=F32
+        )
+    outputs[...] = result.astype(BF16).reshape(seq_count, block, width)
+
+    branch = cotangent[...].reshape(tokens, width)
+    grad_rows = branch.astype(F32)
+    sum_proj[...] = jnp.sum(grad_rows, 0, keepdims=True)
+    grad_placed = jnp.zeros((tokens, width), F32)
+    for q in range(parts):
+        lo = q * width
+        grad = contract_last(branch, weights2[lo : lo + width]) * slopes[:, lo : lo + width]
+        grad = grad.astype(BF16)
+        grad_pre[:, lo : lo + width] = grad
+        sum_fc[:, lo : lo + width] = jnp.sum(grad.astype(F32), 0, keepdims=True)
+        grad_placed += contract_last(grad, weights1[1 + q])
+    high = grad_placed.astype(BF16)
+    rest = grad_placed - high.astype(F32)
+    mid = rest.astype(BF16)
+    low = (rest - mid.astype(F32)).astype(BF16)
+    grad_normed = contract_last(high, order) + (contract_last(mid, order) + contract_last(low, order))
+    sum_bias[...] = jnp.sum(grad_normed, 0, keepdims=True)
+    sum_gain[...] = jnp.sum(grad_normed * unit, 0, keepdims=True)
+    grad_unit = grad_normed * gain[...]
+    part = jnp.mean(grad_unit, -1, keepdims=True)
+    cross = jnp.mean(grad_unit * unit, -1, keepdims=True)
+    grad_mid = grad_rows + scale * (grad_unit - part - unit * cross)
+    grad_middle[...] = grad_mid
+    grad_attn = grad_mid.astype(BF16)
+    grad_out[...] = grad_attn
+    sum_out[...] = jnp.sum(grad_attn.astype(F32), 0, keepdims=True)
+    back = contract_last(grad_attn, weights1[0]).astype(BF16)
+    if permuted.shape[1] > width:
+        permuted[...] = jnp.zeros_like(permuted)
+    permuted[:, :width] = contract_last(back, order).astype(BF16)
+    for i in range(seq_count):
+        for g in range(groups):
+            for part in range(2):
+                start = i * block + part * half_block
+                grad_blocks[i * groups + g, :, part * group : (part + 1) * group] = permuted[
+                    start : start + half_block, g * group : (g + 1) * group
+                ]
+
+
+def middle_block(half1, other1, half2, other2, attended, inputs, cotangent, order, vectors, groups):
+    kinds, side, width = half1.shape
+    parts = kinds - 1
+    chips = half2.shape[0]
+    seq_count, block, _ = inputs.shape
+    tokens = seq_count * block
+    wide = groups * attended.shape[2] // 2
+
+    def shape(*dims, kind=BF16):
+        return jax.ShapeDtypeStruct(dims, kind)
+
+    return pl.pallas_call(
+        functools.partial(middle_kernel, groups),
         out_shape=[
-            jax.ShapeDtypeStruct((chips, CORES, rows, width), BF16),
-            jax.ShapeDtypeStruct((parts, chips, CORES, rows, width), BF16),
-            jax.ShapeDtypeStruct((chips, CORES, parts, rows, width), BF16),
+            shape(seq_count, block, width),
+            shape(tokens, width, kind=F32),
+            shape(*attended.shape),
+            shape(tokens, width),
+            shape(tokens, width),
+            shape(tokens, parts * width),
+            shape(tokens, parts * width),
+            shape(tokens, width),
+            shape(1, width, kind=F32),
+            shape(1, width, kind=F32),
+            shape(1, width, kind=F32),
+            shape(1, parts * width, kind=F32),
+            shape(1, width, kind=F32),
         ],
-        in_specs=[anywhere] * 2,
-        out_specs=[anywhere] * 3,
-        scratch_shapes=[pltpu.SemaphoreType.DMA((2 * (parts + 2),))],
-    )(half, other)
-    return (
-        wout.reshape(width, width),
-        wfc.reshape(parts, width, width),
-        wproj.reshape(parts, width, width),
-    )
+        in_specs=[ANYWHERE] * 4 + vmem_specs(9),
+        out_specs=vmem_specs(13),
+        scratch_shapes=[
+            pltpu.VMEM((kinds, width, width), BF16),
+            pltpu.VMEM((parts * width, width), BF16),
+            pltpu.VMEM((tokens, wide), BF16),
+            pltpu.VMEM((tokens, parts * width), F32),
+            pltpu.VMEM((tokens, wide), BF16),
+            pltpu.SemaphoreType.DMA((2 * kinds + 2 * chips,)),
+        ],
+        compiler_params=pltpu.CompilerParams(vmem_limit_bytes=50 * 2**20),
+        cost_estimate=pl.CostEstimate(
+            flops=tokens * width * width * 44, bytes_accessed=2**24, transcendentals=2**20
+        ),
+    )(half1, other1, half2, other2, attended, inputs, cotangent, order, *vectors)
+
+
+def gradient_kernel(
+    placed_a, placed_n, hidden, grad_pre, grad_out, cotangent, send1, keep1, send2, keep2, turned, some
+):
+    width = placed_a.shape[1]
+    side = width // CORES
+    parts = send1.shape[0] - 1
+    chips, rows2 = send2.shape[:2]
+    core = lax.rem(lax.axis_index("seq"), CORES)
+    for start in range(0, turned.shape[0], width):
+        turned[start : start + width, :] = (
+            hidden[:, start : start + width].astype(F32).T.astype(BF16)
+        )
+    branch = cotangent[...].reshape(-1, width)
+    for target, place in ((send2, 1 - core), (keep2, core)):
+        if rows2 % 16:
+            target[...] = jnp.zeros_like(target)
+            continue
+        for chip in range(chips):
+            start = pl.multiple_of((chip * CORES + place) * rows2, rows2)
+            some[chip * rows2 : (chip + 1) * rows2, :] = turned[pl.ds(start, rows2), :]
+        step = max(1, 4 * 96 // rows2)
+        for chip in range(0, chips, step):
+            product = jnp.dot(
+                some[chip * rows2 : (chip + step) * rows2, :], branch, preferred_element_type=F32
+            )
+            target[chip : chip + step] = product.astype(BF16).reshape(step, rows2, width)
+    turned_a = placed_a[...].astype(F32).T.astype(BF16)
+    turned_n = placed_n[...].astype(F32).T.astype(BF16)
+    for target, start in ((send1, side), (keep1, 0)):
+        target[0] = jnp.dot(
+            turned_a[start : start + side], grad_out[...], preferred_element_type=F32
+        ).astype(BF16)
+        for q in range(parts):
+            target[1 + q] = jnp.dot(
+                turned_n[start : start + side],
+                grad_pre[:, q * width : (q + 1) * width],
+                preferred_element_type=F32,
+            ).astype(BF16)
+
+
+def weight_gradients(placed_a, placed_n, hidden, grad_pre, grad_out, cotangent, chips):
+    tokens, width = placed_a.shape
+    parts = hidden.shape[1] // width
+    shape1 = jax.ShapeDtypeStruct((1 + parts, width // CORES, width), BF16)
+    rows2 = parts * width // (chips * CORES)
+    shape2 = jax.ShapeDtypeStruct((chips, rows2, width), BF16)
+    return pl.pallas_call(
+        gradient_kernel,
+        out_shape=[shape1, shape1, shape2, shape2],
+        in_specs=vmem_specs(6),
+        out_specs=vmem_specs(4),
+        scratch_shapes=[
+            pltpu.VMEM((parts * width, tokens), BF16),
+            pltpu.VMEM((parts * width // CORES, tokens), BF16),
+        ],
+        compiler_params=pltpu.CompilerParams(vmem_limit_bytes=50 * 2**20),
+        cost_estimate=pl.CostEstimate(
+            flops=tokens * width * width * 18, bytes_accessed=2**24, transcendentals=0
+        ),
+    )(placed_a, placed_n, hidden, grad_pre, grad_out, cotangent)
 
 
 def masked_scores(keys, queries, id_column, id_row, first):
@@ -331,6 +629,7 @@
 
 
 def forward_kernel(
+    seq_count,
     heads,
     head_size,
     step_rows,
@@ -339,16 +638,26 @@
     weight,
     gain,
     bias,
-    qkv_bias,
+    bqv,
+    after,
     out,
     stats,
     whole,
     normed,
     ids,
     result,
+    qkv_bias,
 ):
     length = whole.shape[0]
     group = heads * head_size
+    width = weight.shape[0]
+    index = lax.rem(lax.axis_index("seq"), lax.axis_size("seq") // seq_count)
+    qkv_bias[...] = jnp.zeros_like(qkv_bias)
+    for lo in range(0, width, group):
+        here = index == lo // group
+        for base, start in ((0, 0), (width, 2 * group)):
+            piece = jnp.where(here, bqv[:, base + lo : base + lo + group], 0.0)
+            qkv_bias[:, start : start + group] += piece
     for i in range(length // block):
         rows = norm_affine(rows_ref[i, :block, :].astype(F32), gain[...], bias[...])
         normed[i * block : (i + 1) * block, :] = rows.astype(BF16)
@@ -395,6 +704,7 @@
     grads,
     stats,
     ids,
+    after,
     out,
     grad_out,
     grad_query,
@@ -450,13 +760,13 @@
         out[:, 2 * group + lo : 2 * group + lo + head_size] = grad_value[head].astype(BF16)
 
 
-def attend_forward(rows, weight, gain, bias, qkv_bias, heads, head_size, block):
+def attend_forward(rows, weight, gain, bias, bqv, after, seq_count, heads, head_size, block):
     length = rows.shape[0] * block
     width = rows.shape[2]
     group = heads * head_size
     pairs = length * length // 2 * heads
     return pl.pallas_call(
-        functools.partial(forward_kernel, heads, head_size, min(256, length), block),
+        functools.partial(forward_kernel, seq_count, heads, head_size, min(256, length), block),
         out_shape=[
             jax.ShapeDtypeStruct((length // 2, 2 * group), BF16),
             jax.ShapeDtypeStruct((heads, length), F32),
@@ -464,26 +774,26 @@
             jax.ShapeDtypeStruct((length, width), BF16),
             jax.ShapeDtypeStruct((1, length), F32),
         ],
-        in_specs=vmem_specs(5),
+        in_specs=vmem_specs(5) + [ANYWHERE],
         out_specs=vmem_specs(5),
-        scratch_shapes=[pltpu.VMEM((length, group), BF16)],
+        scratch_shapes=[pltpu.VMEM((length, group), BF16), pltpu.VMEM((1, 3 * group), F32)],
         compiler_params=pltpu.CompilerParams(vmem_limit_bytes=48 * 2**20),
         cost_estimate=pl.CostEstimate(
             flops=pairs * head_size * 4 + length * width * group * 6,
             bytes_accessed=length * width * 8,
             transcendentals=pairs,
         ),
-    )(rows, weight, gain, bias, qkv_bias)
-
-
-def attend_backward(whole, grads, stats, ids, heads, head_size, block):
+    )(rows, weight, gain, bias, bqv, after)
+
+
+def attend_backward(whole, grads, stats, ids, after, heads, head_size, block):
     length, width = whole.shape
     group = heads * head_size
     pairs = length * length // 2 * heads
     return pl.pallas_call(
         functools.partial(backward_kernel, heads, head_size, min(256, length), block),
         out_shape=jax.ShapeDtypeStruct((length, 3 * group), BF16),
-        in_specs=vmem_specs(4),
+        in_specs=vmem_specs(4) + [ANYWHERE],
         out_specs=vmem_specs(1)[0],
         scratch_shapes=[
             pltpu.VMEM((length, group), BF16),
@@ -495,7 +805,7 @@
         cost_estimate=pl.CostEstimate(
             flops=pairs * head_size * 10, bytes_accessed=length * width * 6, transcendentals=pairs
         ),
-    )(whole, grads, stats, ids)
+    )(whole, grads, stats, ids, after)
 
 
 def on_device(
@@ -529,37 +839,24 @@
     sizes = tuple(vector.shape[0] for vector in vectors)
     shard_rows = w_out.shape[0] // width
     parts = w_fc.shape[0] // w_out.shape[0]
-    small = jnp.concatenate(
-        [jnp.pad(vector[None], ((0, 0), (0, 3 * group - vector.shape[0]))) for vector in vectors]
-    )
     classes = groups // CORES
+    chips = devices // CORES
     place = lax.axis_index("seq")
     core = place % CORES
     group_index = place % groups
 
-    def by_head(value, axis):
-        if not spare:
-            return value
-        pads = [(0, 0)] * value.ndim
-        pads[axis] = (0, spare)
-        return jnp.pad(value, pads)
-
-    marks = jnp.pad(segments.astype(BF16)[:, None], ((0, 0), (0, 15), (0, width - block)))
-    sequence = gather_sequence(jnp.concatenate([inputs, marks], 1))
-
-    columns = by_head(w_qkv.reshape(shard_rows, 3, HEADS, head_size), 2)
-    columns = columns.reshape(shard_rows, 3, classes, CORES, group).transpose(2, 0, 3, 1, 4)
-    columns = columns.reshape(classes, shard_rows, CORES * 3 * group)
-    extra = jnp.broadcast_to(jnp.concatenate([small] * CORES, 1), (classes, ROWS, 6 * group))
-    tower_a = gather_columns(jnp.concatenate([columns, extra], 1))
-    stacked = stack_weights(
-        w_out.reshape(-1, width),
-        w_fc.reshape(-1, parts * width),
-        w_proj.reshape(parts, -1, width),
-        tower_a,
-    )
-    tower_b = gather_z(stacked)
-    half_a = gather_plane(tower_a)
+    columns, blocks = first_blocks(
+        w_qkv.reshape(shard_rows, 3 * width),
+        inputs,
+        segments,
+        [vector.reshape(1, -1) for vector in vectors],
+        classes,
+        group,
+    )
+    early, sequence = gather_sequence(blocks)
+    tower_a = gather_columns(columns)
+    heights = tower_a.shape[0]
+    half_a = gather_plane(tower_a[: heights // 2], tower_a[heights // 2 :], 0)
     left, right = half_a[..., : 3 * group], half_a[..., 3 * group :]
     mine_a = jnp.where(core == 0, left, right)
     whole_a = ordered(core, mine_a, swap_core(jnp.where(core == 0, right, left)), 1)
@@ -568,65 +865,79 @@
     gain1, bias1, bqv, bout, gain2, bias2, bfc, bproj = unpack_small(
         whole_a[:, shard_rows:, :LANES], sizes
     )
-    half_b = gather_plane(tower_b)
-    wout, wfc, wproj = spread_weights(half_b, swap_core(half_b))
-
-    both = by_head(bqv.reshape(2, HEADS, head_size), 1).reshape(2, groups, group)
-    both = pick(both, group_index, 1)
-    qkv_bias = jnp.concatenate([both[0], jnp.zeros((group,), F32), both[1]]).reshape(1, -1)
+
+    stacked = stack_weights(w_out.reshape(-1, width), w_fc.reshape(-1, parts * width), tower_a)
+    low1, high1 = build_tower(z_pieces(stacked), 1, [half_a, early])
+    low2, high2 = build_tower(z_pieces(w_proj.reshape(-1, width)), 0, [low1])
+    half1 = gather_plane(low1, high1, 1).reshape(1 + parts, -1, width)
+    half2 = gather_plane(low2, high2, 0)
+    other1 = swap_core(half1)
+    other2 = swap_core(half2)
+    aligned = half2.shape[1] % 16 == 0
+    if not aligned:
+        half2 = ordered(core, half2, other2, 1).reshape(1, parts * width, width)
+
     attended, stats, qkv, normed1, ids = attend_forward(
-        sequence, wqkv, gain1, bias1, qkv_bias, heads, head_size, block
+        sequence, wqkv, gain1, bias1, bqv, low1, seq_count, heads, head_size, block
     )
     attended = exchange(attended.reshape(count, block // 2, 2 * group))
-    attended = attended.reshape(seq_count, groups, block // 2, 2, heads, head_size)
-    attended = attended.transpose(0, 3, 2, 1, 4, 5).reshape(tokens, groups * heads, head_size)
-    attended_rows = attended[:, :HEADS].reshape(tokens, width)
+
+    spot = jnp.arange(width, dtype=jnp.int32)
+    side = width // CORES
+    own_core = (core + spot // side) % CORES
+    order = (spot % side // shard_rows * CORES + own_core) * shard_rows + spot % shard_rows
+    (
+        outputs,
+        grad_middle,
+        grad_blocks,
+        placed_a,
+        placed_n,
+        hidden,
+        grad_pre,
+        grad_out,
+        grad_bout,
+        grad_gain2,
+        grad_bias2,
+        grad_bfc,
+        grad_bproj,
+    ) = middle_block(
+        half1,
+        other1,
+        half2,
+        other2,
+        attended,
+        inputs,
+        cotangent,
+        order.reshape(1, width),
+        (bout, gain2, bias2, bfc, bproj),
+        groups,
+    )
+    grad_blocks = exchange(grad_blocks).reshape(-1, 2 * group)
+    send1, keep1, send2, keep2 = weight_gradients(
+        placed_a, placed_n, hidden, grad_pre, grad_out, cotangent, chips
+    )
+    if not aligned:
+        grad_wproj = lax.dot_general(
+            hidden,
+            cotangent.reshape(tokens, width),
+            (((0,), (0,)), ((), ())),
+            preferred_element_type=F32,
+        )
+        grad_wproj = grad_wproj.astype(BF16).reshape(chips, CORES, -1, width)
+        send2, keep2 = pick(grad_wproj, 1 - core, 1), pick(grad_wproj, core, 1)
+    half1 = add(keep1, swap_core(send1))
+    half2 = add(keep2, swap_core(send2))
+    half1 = half1.reshape(1 + parts, chips, shard_rows, width)
+    own1 = scatter_z(scatter_plane(half1, 1), 1)
+    own2 = scatter_z(scatter_plane(half2, 0), 0)
+
+    def blocks_of(value, rows):
+        return value.astype(BF16).reshape(chips, CORES, rows, -1)
 
     rows = inputs.astype(F32).reshape(tokens, width)
-    middle = rows + (jnp.dot(attended_rows, wout, preferred_element_type=F32) + bout)
-    normed2 = norm_affine(middle, gain2, bias2).astype(BF16)
-    bfc_parts = bfc.reshape(parts, 1, width)
-    hidden_pre = jnp.einsum("td,qde->qte", normed2, wfc, preferred_element_type=F32) + bfc_parts
-    hidden = jax.nn.gelu(hidden_pre, approximate=True).astype(BF16)
-    projected = jnp.einsum("qte,qed->td", hidden, wproj, preferred_element_type=F32)
-    outputs = (middle + (projected + bproj)).astype(BF16).reshape(inputs.shape)
-
-    grad_rows = cotangent.astype(F32).reshape(tokens, width)
-    grad_branch = cotangent.reshape(tokens, width)
-    grad_bproj = jnp.sum(grad_branch, 0, dtype=F32)
-    grad_wproj = jnp.einsum("qte,td->qed", hidden, grad_branch, preferred_element_type=F32)
-    grad_hidden = jnp.einsum("td,qed->qte", grad_branch, wproj, preferred_element_type=F32)
-    _, gelu_back = jax.vjp(lambda value: jax.nn.gelu(value, approximate=True), hidden_pre)
-    grad_pre = gelu_back(grad_hidden)[0].astype(BF16)
-    grad_bfc = jnp.sum(grad_pre, 1, dtype=F32)
-    grad_wfc = jnp.einsum("td,qte->qde", normed2, grad_pre, preferred_element_type=F32)
-    grad_normed2 = jnp.einsum("qte,qde->td", grad_pre, wfc, preferred_element_type=F32)
-    _, norm2_back = jax.vjp(norm_affine, middle, gain2, bias2)
-    grad_mid_part, grad_gain2, grad_bias2 = norm2_back(grad_normed2)
-    grad_middle = grad_rows + grad_mid_part
-    grad_attn_out = grad_middle.astype(BF16)
-    grad_bout = jnp.sum(grad_attn_out, 0, dtype=F32)
-    grad_wout = jnp.einsum("td,te->de", attended_rows, grad_attn_out, preferred_element_type=F32)
-    grad_attended = jnp.einsum("te,de->td", grad_attn_out, wout, preferred_element_type=F32)
-    grad_attended = by_head(
-        grad_attended.astype(BF16).reshape(seq_count, 2, block // 2, HEADS, head_size), 3
-    )
-    grad_blocks = grad_attended.reshape(seq_count, 2, block // 2, groups, group)
-    grad_blocks = grad_blocks.transpose(0, 3, 2, 1, 4).reshape(count, block // 2, 2 * group)
-    grad_blocks = exchange(grad_blocks).reshape(-1, 2 * group)
-
-    def blocks_of(value, rows):
-        return value.astype(BF16).reshape(devices, rows, -1)
-
-    send_b, keep_b = split_cores(
-        [blocks_of(grad_wout, shard_rows)]
-        + [blocks_of(grad_wfc[i], shard_rows) for i in range(parts)]
-        + [blocks_of(grad_wproj, parts * shard_rows)]
-    )
-    tower_b = scatter_plane(add(keep_b, swap_core(send_b)))
-    own_b = scatter_z(tower_b)
-
-    grad_qkv = attend_backward(qkv, grad_blocks, stats, ids, heads, head_size, block)
+    grad_qkv = attend_backward(
+        qkv, grad_blocks, stats, ids, half1, heads, head_size, block
+    )
     grad_normed1 = lax.dot_general(
         grad_qkv, wqkv, (((1,), (1,)), ((), ())), preferred_element_type=F32
     )
@@ -657,12 +968,15 @@
     )
     small_grads = pack_small([grad.reshape(1, -1) for grad in grads], sizes, devices)
     small_grads = jnp.pad(small_grads, ((0, 0), (0, 0), (0, 3 * group - LANES)))
-    send_a, keep_a = split_cores([blocks_of(grad_wqkv, shard_rows), small_grads])
+    block_a = jnp.concatenate(
+        [blocks_of(grad_wqkv, shard_rows), small_grads.reshape(chips, CORES, ROWS, -1)], 2
+    )
+    send_a, keep_a = pick(block_a, 1 - core, 1), pick(block_a, core, 1)
     got_a = swap_core(send_a)
     pair_a = jnp.concatenate(
         [jnp.where(core == 0, keep_a, got_a), jnp.where(core == 0, got_a, keep_a)], -1
     )
-    own_a = scatter_columns(scatter_plane(pair_a))
+    own_a = scatter_columns(scatter_plane(pair_a, 0))
     own_small = jnp.sum(
         own_a[:, shard_rows:].reshape(classes, ROWS, CORES, 3 * group)[..., :LANES], (0, 2)
     )
@@ -670,7 +984,6 @@
     own_qkv = own_a[:, :shard_rows].reshape(classes, shard_rows, CORES, 3, group)
     own_qkv = own_qkv.transpose(1, 3, 0, 2, 4).reshape(shard_rows, 3, groups * heads, head_size)
     own_qkv = own_qkv[:, :, :HEADS].reshape(-1)
-    own_fc = own_b[shard_rows : (1 + parts) * shard_rows].reshape(parts, shard_rows, width)
     return (
         outputs,
         grad_inputs,
@@ -678,13 +991,13 @@
         own[1],
         own_qkv,
         own[2],
-        own_b[:shard_rows].reshape(-1),
+        own1[0].reshape(-1),
         own[3],
         own[4],
         own[5],
-        own_fc.transpose(1, 0, 2).reshape(-1),
+        own1[1:].transpose(1, 0, 2).reshape(-1),
         own[6],
-        own_b[(1 + parts) * shard_rows :].reshape(-1),
+        own2.reshape(-1),
         own[7],
     )
 

time: 683 us -> 334 us (0.49)
  Pallas kernels: 345 us -> 48 us
  local copies, waits for them, and re-layouts: 61.7 us -> 32.8 us
  matrix products: 30.6 us -> 4.21 us
  starting transfers between devices: 50.6 us -> 67.6 us
  waiting for transfers between devices: 159 us -> 143 us
    pallas_call x3 -> x7, Pallas kernels: 334 us -> 36.4 us  [the longest x1 13.8 us: middle_block(): pl.pallas_call(functools.partial(middle_kernel, groups), out_shape=[shape...]
    ppermute x6 -> x12, waiting for transfers between devices: 46.9 us -> 16.6 us  [shift_z(): lax.ppermute(value, 'seq', [(i, (i + CORES * step) % size) for i in range...]
    ppermute x8, waiting for transfers between devices: 13.7 us -> 39.3 us  [swap_z(): lax.ppermute(value, 'seq', [(i, i ^ CORES * bit) for i in range(size)])]
    dot_general x9 -> x0, matrix products: 23.6 us -> none  [the longest x1 5.16 us: on_device(): jnp.einsum('qte,qed->td', hidden, wproj, preferred_element_type=F32)]
    ppermute x16 -> x24, waiting for transfers between devices: 88.8 us -> 69.7 us  [swap_dp(): return lax.ppermute(value, 'dp', [(i, i ^ bit) for i in range(size)])]
    ppermute x16 -> x24, starting transfers between devices: 16.6 us -> 31.2 us  [swap_dp(): return lax.ppermute(value, 'dp', [(i, i ^ bit) for i in range(size)])]
    unnamed x76 -> x68, local copies, waits for them, and re-layouts: 15.5 us -> 6.96 us
    ppermute x6 -> x12, starting transfers between devices: 9.36 us -> 17.9 us  [shift_z(): lax.ppermute(value, 'seq', [(i, (i + CORES * step) % size) for i in range...]
  transfers between devices with their start and end apart: 38 -> 54, of which waited for: 21 -> 24; matrix products, arithmetic and copies ran while one was open for 12% -> 17% of each run, Pallas kernels for 3% -> 8%
where the time goes in v2:
time: 334 us; the launch traced here: 329 us
  waiting for transfers between devices  143 us (43%)
  starting transfers between devices  67.6 us (20%)
  Pallas kernels  48 us (14%)
  local copies, waits for them, and re-layouts  32.8 us (10%)
  other arithmetic  30.7 us (9%)
  matrix products  4.21 us (1%)
    ppermute x24, waiting for transfers between devices, swap_dp(): return lax.ppermute(value, 'dp', [(i, i ^ bit) for i in range(size)])  69.7 us
    ppermute x8, waiting for transfers between devices, swap_z(): lax.ppermute(value, 'seq', [(i, i ^ CORES * bit) for i in range(size)])  39.3 us
    ppermute x24, starting transfers between devices, swap_dp(): return lax.ppermute(value, 'dp', [(i, i ^ bit) for i in range(size)])  31.2 us
    ppermute x12, starting transfers between devices, shift_z(): lax.ppermute(value, 'seq', [(i, (i + CORES * step) % size) for i in range...  17.9 us
    ppermute x12, waiting for transfers between devices, shift_z(): lax.ppermute(value, 'seq', [(i, (i + CORES * step) % size) for i in range...  16.6 us
    convert_element_type x17, other arithmetic, add(): return (mine.astype(F32) + other.astype(F32)).astype(mine.dtype)  14.2 us
    pallas_call x1, Pallas kernels, middle_block(): pl.pallas_call(functools.partial(middle_kernel, groups), out_shape=[shape...  13.8 us
    all_to_all x2, waiting for transfers between devices, exchange(): lax.all_to_all(blocks, 'seq', split_axis=0, concat_axis=0, tiled=True)  12.1 us
  transfers between devices with their start and end apart: 54, of which 24 were waited for; matrix products, arithmetic and copies ran while one was open for 17% of the time, Pallas kernels for 8%

profile of v2, /device:TPU:0, one launch (start us, length us, event | category | flops | bytes accessed | tf_op | source)
XLA Modules:
  0.0 328.6 jit_solution(64194221608695817)
XLA Ops:
  22.4 10.6 %collective-permute-done.1 = bf16[2,32,1152]{2,1,0:T(8,128)(2,1)S(1)} collective-permute-done((bf16[2,32,1152]{2,1,0:T(8,128)(2,1)S(1)}, bf16[2,32,1152]{2,1,0:T(8,128)(2,1)S(1)}, u32[]{:S(2)}, u32[]{:S(2)}) %collective-permute-start.1) | collective-permute-done | bytes 147488 | tf_op jit(solution)/shard_map/ppermute | solution.py:63
  34.5 8.2 %collective-permute-done.9 = bf16[144,768]{1,0:T(8,128)(2,1)S(1)} collective-permute-done((bf16[144,768]{1,0:T(8,128)(2,1)S(1)}, bf16[144,768]{1,0:T(8,128)(2,1)S(1)}, u32[]{:S(2)}, u32[]{:S(2)}) %collective-permute-start.9) | collective-permute-done | bytes 221216 | tf_op jit(solution)/shard_map/ppermute | solution.py:63
  46.9 3.6 %collective-permute-start.2 = (bf16[5,24,768]{2,1,0:T(8,128)(2,1)}, bf16[5,24,768]{2,1,0:T(8,128)(2,1)S(1)}, u32[]{:S(2)}, u32[]{:S(2)}) collective-permute-start(bf16[5,24,768]{2,1,0:T(8,128)(2,1)} %shard_map.255.refs_0_), channel_id=1, source_target_pairs={{0,6},{1,7},{2,0},{3,1},{4,2},{5,3},{6,4},{7,5},{8,14},{9,15},{10,... | collective-permute-start | bytes 552968 | tf_op jit(solution)/shard_map/ppermute | solution.py:30
  51.3 7.8 %collective-permute-done.6 = bf16[2,2,32,1152]{3,2,1,0:T(8,128)(2,1)S(1)} collective-permute-done((bf16[2,2,32,1152]{3,2,1,0:T(8,128)(2,1)S(1)}, bf16[2,2,32,1152]{3,2,1,0:T(8,128)(2,1)S(1)}, u32[]{:S(2)}, u32[]{:S(2)}) %collective-permute-start.6) | collective-permute-done | bytes 294944 | tf_op jit(solution)/shard_map/ppermute | solution.py:40
  60.6 5.9 %collective-permute-done.8 = bf16[2,2,32,1152]{3,2,1,0:T(8,128)(2,1)S(1)} collective-permute-done((bf16[2,2,32,1152]{3,2,1,0:T(8,128)(2,1)S(1)}, bf16[2,2,32,1152]{3,2,1,0:T(8,128)(2,1)S(1)}, u32[]{:S(2)}, u32[]{:S(2)}) %collective-permute-start.8) | collective-permute-done | bytes 294944 | tf_op jit(solution)/shard_map/ppermute | solution.py:40
  68.3 9.2 %collective-permute-done.3.refs_2_ = bf16[5,24,768]{2,1,0:T(8,128)(2,1)S(1)} collective-permute-done((bf16[5,24,768]{2,1,0:T(8,128)(2,1)S(1)}, bf16[5,24,768]{2,1,0:T(8,128)(2,1)S(1)}, u32[]{:S(2)}, u32[]{:S(2)}) %collective-permute-start.3) | collective-permute-done | bytes 184352 | tf_op jit(solution)/shard_map/ppermute | solution.py:30
  81.7 6.1 %collective-permute-done.18 = bf16[2,96,768]{2,1,0:T(8,128)(2,1)S(1)} collective-permute-done((bf16[2,96,768]{2,1,0:T(8,128)(2,1)S(1)}, bf16[2,96,768]{2,1,0:T(8,128)(2,1)S(1)}, u32[]{:S(2)}, u32[]{:S(2)}) %collective-permute-start.18) | collective-permute-done | bytes 294944 | tf_op jit(solution)/shard_map/ppermute | solution.py:40
  89.2 4.3 %collective-permute-done.10 = bf16[5,2,24,768]{3,2,1,0:T(8,128)(2,1)S(1)} collective-permute-done((bf16[5,2,24,768]{3,2,1,0:T(8,128)(2,1)S(1)}, bf16[5,2,24,768]{3,2,1,0:T(8,128)(2,1)S(1)}, u32[]{:S(2)}, u32[]{:S(2)}) %collective-permute-start.10) | collective-permute-done | bytes 368672 | tf_op jit(solution)/shard_map/ppermute | solution.py:40
  101.9 9.7 %collective-permute-done.19 = bf16[2,2,96,768]{3,2,1,0:T(8,128)(2,1)S(1)} collective-permute-done((bf16[2,2,96,768]{3,2,1,0:T(8,128)(2,1)S(1)}, bf16[2,2,96,768]{3,2,1,0:T(8,128)(2,1)S(1)}, u32[]{:S(2)}, u32[]{:S(2)}) %collective-permute-start.19) | collective-permute-done | bytes 589856 | tf_op jit(solution)/shard_map/ppermute | solution.py:40
  113.1 12.8 %collective-permute-done.11 = bf16[5,2,2,24,768]{4,3,2,0,1:T(8,128)(2,1)S(1)} collective-permute-done((bf16[5,2,2,24,768]{4,3,2,0,1:T(8,128)(2,1)S(1)}, bf16[5,2,2,24,768]{4,3,2,0,1:T(8,128)(2,1)S(1)}, u32[]{:S(2)}, u32[]{:S(2)}) %collective-permute-start.11) | collective-permute-done | bytes 737312 | tf_op jit(solution)/shard_map/ppermute | solution.py:40
  133.0 3.6 %collective-permute-done.24 = bf16[2,2,144,768]{3,2,0,1:T(8,128)(2,1)S(1)} collective-permute-done((bf16[2,2,144,768]{3,2,0,1:T(8,128)(2,1)S(1)}, bf16[2,2,144,768]{3,2,0,1:T(8,128)(2,1)S(1)}, u32[]{:S(2)}, u32[]{:S(2)}) %collective-permute-start.24) | collective-permute-done | bytes 884768 | tf_op jit(solution)/shard_map/ppermute | solution.py:35
  138.3 11.5 %shard_map.259 = (bf16[512,384]{1,0:T(8,128)(2,1)}, f32[3,1024]{1,0:T(4,128)S(1)}, bf16[1024,576]{1,0:T(8,128)(2,1)S(1)}, bf16[1024,768]{1,0:T(8,128)(2,1)S(1)}, f32[1,1024]{1,0:T(1,128)S(1)}) custom-call(bf16[8,144,768]{2,1,0:T(8,128)(2,1)} %bitcast.330, bf16[768,576]{1,0:T(8,128)(2,1)S(1)} %bitcast.328, f32[1,768]{1,0:T(1,128)S(1)} %get-tuple-element.56.gain, ...), custom_call_target="tpu_custom_call" | custom-call | flops 1308622848 | bytes 6291456 | tf_op jit(solution)/shard_map/pallas_call | solution.py:768
  152.1 4.8 %all-to-all-start = ((bf16[8,64,384]{2,1,0:T(8,128)(2,1)}), bf16[8,64,384]{2,1,0:T(8,128)(2,1)S(1)}, u32[]{:S(2)}, u32[]{:S(2)}) async-start(bf16[8,64,384]{2,1,0:T(8,128)(2,1)} %bitcast.58), calls=%async_computation | async-start | bytes 786432 | tf_op jit(solution)/shard_map/all_to_all | solution.py:183
  157.0 12.1 %all-to-all-done.attended = bf16[8,64,384]{2,1,0:T(8,128)(2,1)S(1)} async-done(((bf16[8,64,384]{2,1,0:T(8,128)(2,1)}), bf16[8,64,384]{2,1,0:T(8,128)(2,1)S(1)}, u32[]{:S(2)}, u32[]{:S(2)}) %all-to-all-start) | async-done | bytes 393248 | tf_op jit(solution)/shard_map/all_to_all | solution.py:183
  169.1 13.8 %shard_map.260 = (bf16[2,128,768]{2,1,0:T(8,128)(2,1)}, f32[256,768]{1,0:T(8,128)S(1)}, bf16[8,64,384]{2,1,0:T(8,128)(2,1)}, bf16[256,768]{1,0:T(8,128)(2,1)S(1)...) custom-call(bf16[5,384,768]{2,1,0:T(8,128)(2,1)} %bitcast.38.half1, ...), custom_call_target="tpu_custom_call" | custom-call | flops 6643777536 | bytes 16777216 | tf_op jit(solution)/shard_map/pallas_call | solution.py:522
  185.3 7.2 %shard_map.261 = (bf16[5,384,768]{2,1,0:T(8,128)(2,1)}, bf16[5,384,768]{2,1,0:T(8,128)(2,1)}, bf16[16,96,768]{2,1,0:T(8,128)(2,1)}, bf16[16,96,768]{2,1,0:T(8,128)(2,1)}) custom-call(bf16[256,768]{1,0:T(8,128)(2,1)S(1)} %get-tuple-element.71.placed_a, bf16[256,768]{1,0:T(8,128)(2,1)S(1)} %get-tuple-element.72.placed_n, bf16[256,3072]{1,0:T(8,128)(2,1)S(1)} %copy-done.11, ...), custom_call_target="tpu_custom_call" | custom-call | flops 2717908992 | bytes 16777216 | tf_op jit(solution)/shard_map/pallas_call | solution.py:602
  205.0 4.1 %all-to-all-start.1 = ((bf16[8,64,384]{2,1,0:T(8,128)(2,1)}), bf16[8,64,384]{2,1,0:T(8,128)(2,1)}, u32[]{:S(2)}, u32[]{:S(2)}) async-start(bf16[8,64,384]{2,1,0:T(8,128)(2,1)} %get-tuple-element.68), calls=%async_computation.1 | async-start | bytes 786432 | tf_op jit(solution)/shard_map/all_to_all | solution.py:183
  209.1 7.5 %collective-permute-done.47 = bf16[2,2,96,768]{3,2,1,0:T(8,128)(2,1)} collective-permute-done((bf16[2,2,96,768]{3,2,1,0:T(8,128)(2,1)}, bf16[2,2,96,768]{3,2,1,0:T(8,128)(2,1)}, u32[]{:S(2)}, u32[]{:S(2)}) %collective-permute-start.47) | collective-permute-done | bytes 589856 | tf_op jit(solution)/shard_map/ppermute | solution.py:40
  230.3 9.9 %shard_map.262 = bf16[1024,576]{1,0:T(8,128)(2,1)S(1)} custom-call(bf16[1024,576]{1,0:T(8,128)(2,1)S(1)} %copy-done.2, bf16[512,384]{1,0:T(8,128)(2,1)} %bitcast.59.grads, f32[3,1024]{1,0:T(4,128)S(1)} %get-tuple-element.69.stats, f32[1,1024]{1,0:T(1,128)S(1)} %get-tuple-element.70.ids, bf16[5,16,24,768]{3,2,1,0:T(8,128)(2,1)S(1)} %bitcast.324), custom_call_target="tpu_custom_call" | custom-call | flops 1006632960 | bytes 3538944 | tf_op jit(solution)/shard_map/pallas_call | solution.py:793
  260.7 4.5 %collective-permute-done.50 = bf16[96,768]{1,0:T(8,128)(2,1)S(1)} collective-permute-done((bf16[96,768]{1,0:T(8,128)(2,1)S(1)}, bf16[96,768]{1,0:T(8,128)(2,1)S(1)}, u32[]{:S(2)}, u32[]{:S(2)}) %collective-permute-start.50) | collective-permute-done | bytes 147488 | tf_op jit(solution)/shard_map/ppermute | solution.py:30
  274.7 4.8 %collective-permute-done.37 = bf16[5,2,2,24,768]{4,3,2,1,0:T(8,128)(2,1)} collective-permute-done((bf16[5,2,2,24,768]{4,3,2,1,0:T(8,128)(2,1)}, bf16[5,2,2,24,768]{4,3,2,1,0:T(8,128)(2,1)}, u32[]{:S(2)}, u32[]{:S(2)}) %collective-permute-start.37) | collective-permute-done | bytes 737312 | tf_op jit(solution)/shard_map/ppermute | solution.py:40
  301.9 8.3 %collective-permute-done.35 = bf16[2,32,1152]{2,1,0:T(8,128)(2,1)S(1)} collective-permute-done((bf16[2,32,1152]{2,1,0:T(8,128)(2,1)S(1)}, bf16[2,32,1152]{2,1,0:T(8,128)(2,1)S(1)}, u32[]{:S(2)}, u32[]{:S(2)}) %collective-permute-start.35) | collective-permute-done | bytes 147488 | tf_op jit(solution)/shard_map/ppermute | solution.py:63
  310.6 5.1 %collective-permute-done.36 = bf16[32,1152]{1,0:T(8,128)(2,1)S(1)} collective-permute-done((bf16[32,1152]{1,0:T(8,128)(2,1)S(1)}, bf16[32,1152]{1,0:T(8,128)(2,1)S(1)}, u32[]{:S(2)}, u32[]{:S(2)}) %collective-permute-start.36) | collective-permute-done | bytes 73760 | tf_op jit(solution)/shard_map/ppermute | solution.py:63
  321.6 4.8 %collective-permute-done.29 = bf16[128,768]{1,0:T(8,128)(2,1)S(1)} collective-permute-done((bf16[128,768]{1,0:T(8,128)(2,1)S(1)}, bf16[128,768]{1,0:T(8,128)(2,1)S(1)}, u32[]{:S(2)}, u32[]{:S(2)}) %collective-permute-start.29) | collective-permute-done | bytes 196640 | tf_op jit(solution)/shard_map/ppermute | solution.py:63
  (299 shorter events, 146.2 us)
Async XLA Ops:
  11.7 21.2 %collective-permute-start.1 = (bf16[2,32,1152]{2,1,0:T(8,128)(2,1)S(1)}, bf16[2,32,1152]{2,1,0:T(8,128)(2,1)S(1)}, u32[]{:S(2)}, u32[]{:S(2)}) collective-permute-start(bf16[2,32,1152]{2,1,0:T(8,128)(2,1)S(1)} %pad_maximum_fusion.14), channel_id=1, source_target_pairs={{0,4},{1,5},{2,6},{3,7},{4,0},{5,1},{6,2},{7,3},{8,12},{9,13},{10,... | collective-permute-start | bytes 442376 | tf_op jit(solution)/shard_map/ppermute | solution.py:63
  14.9 62.7 %collective-permute-start.15 = (bf16[96,768]{1,0:T(8,128)(2,1)S(1)}, bf16[96,768]{1,0:T(8,128)(2,1)S(1)}, u32[]{:S(2)}, u32[]{:S(2)}) collective-permute-start(bf16[96,768]{1,0:T(8,128)(2,1)S(1)} %reshape.468.refs_0_), channel_id=1, source_target_pairs={{0,6},{1,7},{2,0},{3,1},{4,2},{5,3},{6,4},{7,5},{8,14},{9,15},{10,... | collective-permute-start | bytes 442376 | tf_op jit(solution)/shard_map/ppermute | solution.py:30
  16.3 61.3 %collective-permute-start.16 = (bf16[96,768]{1,0:T(8,128)(2,1)S(1)}, bf16[96,768]{1,0:T(8,128)(2,1)S(1)}, u32[]{:S(2)}, u32[]{:S(2)}) collective-permute-start(bf16[96,768]{1,0:T(8,128)(2,1)S(1)} %reshape.468.refs_0_), channel_id=1, source_target_pairs={{0,4},{1,5},{2,6},{3,7},{4,0},{5,1},{6,2},{7,3},{8,12},{9,13},{10,... | collective-permute-start | bytes 442376 | tf_op jit(solution)/shard_map/ppermute | solution.py:30
  18.0 59.6 %collective-permute-start.17 = (bf16[96,768]{1,0:T(8,128)(2,1)S(1)}, bf16[96,768]{1,0:T(8,128)(2,1)S(1)}, u32[]{:S(2)}, u32[]{:S(2)}) collective-permute-start(bf16[96,768]{1,0:T(8,128)(2,1)S(1)} %reshape.468.refs_0_), channel_id=1, source_target_pairs={{0,2},{1,3},{2,4},{3,5},{4,6},{5,7},{6,0},{7,1},{8,10},{9,11},{10,... | collective-permute-start | bytes 442376 | tf_op jit(solution)/shard_map/ppermute | solution.py:30
  19.0 23.8 %collective-permute-start.9 = (bf16[144,768]{1,0:T(8,128)(2,1)S(1)}, bf16[144,768]{1,0:T(8,128)(2,1)S(1)}, u32[]{:S(2)}, u32[]{:S(2)}) collective-permute-start(bf16[144,768]{1,0:T(8,128)(2,1)S(1)} %dynamic-slice_bitcast_fusion.12), channel_id=1, source_target_pairs={{0,4},{1,5},{2,6},{3,7},{4,0},{5,1},{6,2},{7,3},{8,12},{9,13},{10,... | collective-permute-start | bytes 663560 | tf_op jit(solution)/shard_map/ppermute | solution.py:63
  46.9 19.7 %collective-permute-start.2 = (bf16[5,24,768]{2,1,0:T(8,128)(2,1)}, bf16[5,24,768]{2,1,0:T(8,128)(2,1)S(1)}, u32[]{:S(2)}, u32[]{:S(2)}) collective-permute-start(bf16[5,24,768]{2,1,0:T(8,128)(2,1)} %shard_map.255.refs_0_), channel_id=1, source_target_pairs={{0,6},{1,7},{2,0},{3,1},{4,2},{5,3},{6,4},{7,5},{8,14},{9,15},{10,... | collective-permute-start | bytes 552968 | tf_op jit(solution)/shard_map/ppermute | solution.py:30
  79.3 51.9 %collective-permute-start.23 = (bf16[2,144,768]{2,1,0:T(8,128)(2,1)S(1)}, bf16[2,144,768]{2,1,0:T(8,128)(2,1)S(1)}, u32[]{:S(2)}, u32[]{:S(2)}) collective-permute-start(bf16[2,144,768]{2,1,0:T(8,128)(2,1)S(1)} %pad_maximum_fusion.8.refs_5_), channel_id=1, source_target_pairs={{0,2},{1,3},{2,0},{3,1},{4,6},{5,7},{6,4},{7,5},{8,10},{9,11},{10,... | collective-permute-start | bytes 1327112 | tf_op jit(solution)/shard_map/ppermute | solution.py:63
  80.1 51.4 %collective-permute-start.25 = (bf16[16,32,576]{2,1,0:T(8,128)(2,1)S(1)}, bf16[16,32,576]{2,1,0:T(8,128)(2,1)S(1)}, u32[]{:S(2)}, u32[]{:S(2)}) collective-permute-start(bf16[16,32,576]{2,1,0:T(8,128)(2,1)S(1)} %broadcast_select_fusion.2), channel_id=1, source_target_pairs={{0,1},{1,0},{2,3},{3,2},{4,5},{5,4},{6,7},{7,6},{8,9},{9,8},{10,11... | collective-permute-start | bytes 1769480 | tf_op jit(solution)/shard_map/ppermute | solution.py:35
  80.2 20.0 %collective-permute-start.20 = (bf16[2,96,768]{2,1,0:T(8,128)(2,1)S(1)}, bf16[2,96,768]{2,1,0:T(8,128)(2,1)S(1)}, u32[]{:S(2)}, u32[]{:S(2)}) collective-permute-start(bf16[2,96,768]{2,1,0:T(8,128)(2,1)S(1)} %get-tuple-element.55), channel_id=1, source_target_pairs={{0,16},{8,24},{16,0},{24,8},{1,17},{9,25},{17,1},{25,9},{2,18},{10... | collective-permute-start | bytes 884744 | tf_op jit(solution)/shard_map/ppermute | solution.py:40
  98.9 27.0 %collective-permute-start.11 = (bf16[5,2,2,24,768]{4,3,2,0,1:T(8,128)(2,1)S(1)}, bf16[5,2,2,24,768]{4,3,2,0,1:T(8,128)(2,1)S(1)}, u32[]{:S(2)}, u32[]{:S(2)}) collective-permute-start(bf16[5,2,2,24,768]{4,3,2,0,1:T(8,128)(2,1)S(1)} %pad_maximum_fusion.4), channel_id=1, source_target_pairs={{0,16},{8,24},{16,0},{24,8},{1,17},{9,25},{17,1},{25,9},{2,18},{10... | collective-permute-start | bytes 2211848 | tf_op jit(solution)/shard_map/ppermute | solution.py:40
  100.2 25.9 %collective-permute-start.13 = (bf16[5,2,2,24,768]{4,3,2,0,1:T(8,128)(2,1)S(1)}, bf16[5,2,2,24,768]{4,3,2,0,1:T(8,128)(2,1)S(1)}, u32[]{:S(2)}, u32[]{:S(2)}) collective-permute-start(bf16[5,2,2,24,768]{4,3,2,0,1:T(8,128)(2,1)S(1)} %pad_maximum_fusion.5), channel_id=1, source_target_pairs={{0,8},{8,0},{16,24},{24,16},{1,9},{9,1},{17,25},{25,17},{2,10},{10... | collective-permute-start | bytes 2211848 | tf_op jit(solution)/shard_map/ppermute | solution.py:40
  128.8 40.3 %collective-permute-start.14 = (bf16[5,384,768]{2,1,0:T(8,128)(2,1)}, bf16[5,384,768]{2,1,0:T(8,128)(2,1)}, u32[]{:S(2)}, u32[]{:S(2)}) collective-permute-start(bf16[5,384,768]{2,1,0:T(8,128)(2,1)} %bitcast.38.half1), channel_id=1, source_target_pairs={{0,1},{1,0},{2,3},{3,2},{4,5},{5,4},{6,7},{7,6},{8,9},{9,8},{10,11... | collective-permute-start | bytes 8847368 | tf_op jit(solution)/shard_map/ppermute | solution.py:35
  130.7 38.4 %collective-permute-start.22 = (bf16[16,96,768]{2,1,0:T(8,128)(2,1)}, bf16[16,96,768]{2,1,0:T(8,128)(2,1)}, u32[]{:S(2)}, u32[]{:S(2)}) collective-permute-start(bf16[16,96,768]{2,1,0:T(8,128)(2,1)} %bitcast.48.half2), channel_id=1, source_target_pairs={{0,1},{1,0},{2,3},{3,2},{4,5},{5,4},{6,7},{7,6},{8,9},{9,8},{10,11... | collective-permute-start | bytes 7077896 | tf_op jit(solution)/shard_map/ppermute | solution.py:35
  192.7 30.5 %collective-permute-start.26 = (bf16[5,384,768]{2,1,0:T(8,128)(2,1)}, bf16[5,384,768]{2,1,0:T(8,128)(2,1)}, u32[]{:S(2)}, u32[]{:S(2)}) collective-permute-start(bf16[5,384,768]{2,1,0:T(8,128)(2,1)} %get-tuple-element.77), channel_id=1, source_target_pairs={{0,1},{1,0},{2,3},{3,2},{4,5},{5,4},{6,7},{7,6},{8,9},{9,8},{10,11... | collective-permute-start | bytes 8847368 | tf_op jit(solution)/shard_map/ppermute | solution.py:35
  205.0 24.0 %all-to-all-start.1 = ((bf16[8,64,384]{2,1,0:T(8,128)(2,1)}), bf16[8,64,384]{2,1,0:T(8,128)(2,1)}, u32[]{:S(2)}, u32[]{:S(2)}) async-start(bf16[8,64,384]{2,1,0:T(8,128)(2,1)} %get-tuple-element.68), calls=%async_computation.1 | async-start | bytes 786432 | tf_op jit(solution)/shard_map/all_to_all | solution.py:183
  218.5 30.0 %collective-permute-start.48 = (bf16[2,96,768]{2,1,0:T(8,128)(2,1)}, bf16[2,96,768]{2,1,0:T(8,128)(2,1)}, u32[]{:S(2)}, u32[]{:S(2)}) collective-permute-start(bf16[2,96,768]{2,1,0:T(8,128)(2,1)} %dynamic-slice_bitcast_fusion.8), channel_id=1, source_target_pairs={{0,16},{8,24},{16,0},{24,8},{1,17},{9,25},{17,1},{25,9},{2,18},{10... | collective-permute-start | bytes 884744 | tf_op jit(solution)/shard_map/ppermute | solution.py:40
  221.7 28.0 %collective-permute-start.46 = (bf16[2,96,768]{2,1,0:T(8,128)(2,1)}, bf16[2,96,768]{2,1,0:T(8,128)(2,1)}, u32[]{:S(2)}, u32[]{:S(2)}) collective-permute-start(bf16[2,96,768]{2,1,0:T(8,128)(2,1)} %dynamic-slice_bitcast_fusion.9), channel_id=1, source_target_pairs={{0,8},{8,0},{16,24},{24,16},{1,9},{9,1},{17,25},{25,17},{2,10},{10... | collective-permute-start | bytes 884744 | tf_op jit(solution)/shard_map/ppermute | solution.py:40
  228.4 43.7 %collective-permute-start.39 = (bf16[5,2,2,24,768]{4,3,2,1,0:T(8,128)(2,1)}, bf16[5,2,2,24,768]{4,3,2,1,0:T(8,128)(2,1)}, u32[]{:S(2)}, u32[]{:S(2)}) collective-permute-start(bf16[5,2,2,24,768]{4,3,2,1,0:T(8,128)(2,1)} %get-tuple-element.101), channel_id=1, source_target_pairs={{0,8},{8,0},{16,24},{24,16},{1,9},{9,1},{17,25},{25,17},{2,10},{10... | collective-permute-start | bytes 2211848 | tf_op jit(solution)/shard_map/ppermute | solution.py:40
  259.8 19.7 %collective-permute-start.37 = (bf16[5,2,2,24,768]{4,3,2,1,0:T(8,128)(2,1)}, bf16[5,2,2,24,768]{4,3,2,1,0:T(8,128)(2,1)}, u32[]{:S(2)}, u32[]{:S(2)}) collective-permute-start(bf16[5,2,2,24,768]{4,3,2,1,0:T(8,128)(2,1)} %dynamic-slice_bitcast_fusion.2), channel_id=1, source_target_pairs={{0,16},{8,24},{16,0},{24,8},{1,17},{9,25},{17,1},{25,9},{2,18},{10... | collective-permute-start | bytes 2211848 | tf_op jit(solution)/shard_map/ppermute | solution.py:40
  273.5 21.3 %collective-permute-start.40 = (bf16[5,2,24,768]{3,2,1,0:T(8,128)(2,1)S(1)}, bf16[5,2,24,768]{3,2,1,0:T(8,128)(2,1)S(1)}, u32[]{:S(2)}, u32[]{:S(2)}) collective-permute-start(bf16[5,2,24,768]{3,2,1,0:T(8,128)(2,1)S(1)} %dynamic-slice_bitcast_fusion.6), channel_id=1, source_target_pairs={{0,16},{8,24},{16,0},{24,8},{1,17},{9,25},{17,1},{25,9},{2,18},{10... | collective-permute-start | bytes 1105928 | tf_op jit(solution)/shard_map/ppermute | solution.py:40
  283.8 26.6 %collective-permute-start.28 = (bf16[2,128,768]{2,1,0:T(8,128)(2,1)S(1)}, bf16[2,128,768]{2,1,0:T(8,128)(2,1)S(1)}, u32[]{:S(2)}, u32[]{:S(2)}) collective-permute-start(bf16[2,128,768]{2,1,0:T(8,128)(2,1)S(1)} %dynamic-slice_bitcast_fusion.5), channel_id=1, source_target_pairs={{0,2},{1,3},{2,0},{3,1},{4,6},{5,7},{6,4},{7,5},{8,10},{9,11},{10,... | collective-permute-start | bytes 1179656 | tf_op jit(solution)/shard_map/ppermute | solution.py:63
  296.1 22.7 %collective-permute-start.41 = (bf16[5,24,768]{2,1,0:T(8,128)(2,1)}, bf16[5,24,768]{2,1,0:T(8,128)(2,1)S(1)}, u32[]{:S(2)}, u32[]{:S(2)}) collective-permute-start(bf16[5,24,768]{2,1,0:T(8,128)(2,1)} %get-tuple-element.115), channel_id=1, source_target_pairs={{0,2},{1,3},{2,4},{3,5},{4,6},{5,7},{6,0},{7,1},{8,10},{9,11},{10,... | collective-permute-start | bytes 552968 | tf_op jit(solution)/shard_map/ppermute | solution.py:30
  296.1 22.6 %collective-permute-start.42 = (bf16[5,24,768]{2,1,0:T(8,128)(2,1)}, bf16[5,24,768]{2,1,0:T(8,128)(2,1)}, u32[]{:S(2)}, u32[]{:S(2)}) collective-permute-start(bf16[5,24,768]{2,1,0:T(8,128)(2,1)} %get-tuple-element.116), channel_id=1, source_target_pairs={{0,4},{1,5},{2,6},{3,7},{4,0},{5,1},{6,2},{7,3},{8,12},{9,13},{10,... | collective-permute-start | bytes 552968 | tf_op jit(solution)/shard_map/ppermute | solution.py:30
  299.0 19.8 %collective-permute-start.43 = (bf16[5,24,768]{2,1,0:T(8,128)(2,1)}, bf16[5,24,768]{2,1,0:T(8,128)(2,1)}, u32[]{:S(2)}, u32[]{:S(2)}) collective-permute-start(bf16[5,24,768]{2,1,0:T(8,128)(2,1)} %get-tuple-element.117), channel_id=1, source_target_pairs={{0,6},{1,7},{2,0},{3,1},{4,2},{5,3},{6,4},{7,5},{8,14},{9,15},{10,... | collective-permute-start | bytes 552968 | tf_op jit(solution)/shard_map/ppermute | solution.py:30
  (64 other events, 654.3 us)

commit v3 on v2

--- a/solution.py
+++ b/solution.py
@@ -23,6 +23,9 @@
     centered = values - center
     variance = jnp.mean(centered * centered, -1, keepdims=True)
     return centered * lax.rsqrt(variance + EPSILON) * gain + bias
+
+
+ANYWHERE = pl.BlockSpec(memory_space=pl.ANY)
 
 
 def shift_z(value, step):
@@ -88,23 +91,28 @@
     return (mine.astype(F32) + other.astype(F32)).astype(mine.dtype)
 
 
-def scatter_plane(split, axis):
+def scatter_plane(split, axis, between=None):
     planes = lax.axis_size("dp")
     heights = lax.axis_size("seq") // CORES
-    if planes == 4:
-        plane = lax.axis_index("dp")
-        y, x = plane // 2, plane % 2
-        split = split.reshape(
-            *split.shape[:axis], 2, 2, heights, *split.shape[axis + 1 :]
-        )
-        low = lax.slice_in_dim(split, 0, heights // 2, axis=axis + 2)
-        high = lax.slice_in_dim(split, heights // 2, heights, axis=axis + 2)
-        low = add(pick(low, y, axis), swap_dp(pick(low, 1 - y, axis), 2))
-        high = add(pick(high, x, axis + 1), swap_dp(pick(high, 1 - x, axis + 1), 1))
-        low = add(pick(low, x, axis), swap_dp(pick(low, 1 - x, axis), 1))
-        high = add(pick(high, y, axis), swap_dp(pick(high, 1 - y, axis), 2))
-        return jnp.concatenate([low, high], axis)
-    return lax.psum_scatter(split, "dp", scatter_dimension=axis, tiled=True)
+    if planes != 4:
+        if between is not None:
+            between(split, split)
+        return lax.psum_scatter(split, "dp", scatter_dimension=axis, tiled=True)
+    plane = lax.axis_index("dp")
+    y, x = plane // 2, plane % 2
+    split = split.reshape(*split.shape[:axis], 2, 2, heights, *split.shape[axis + 1 :])
+    low = lax.slice_in_dim(split, 0, heights // 2, axis=axis + 2)
+    high = lax.slice_in_dim(split, heights // 2, heights, axis=axis + 2)
+    low_send, high_send = pick(low, 1 - y, axis), pick(high, 1 - x, axis + 1)
+    low_got, high_got = swap_dp(low_send, 2), swap_dp(high_send, 1)
+    if between is not None:
+        after = between(low_send, high_send)
+        low_got, high_got = gate(low_got, after), gate(high_got, after)
+    low = add(pick(low, y, axis), low_got)
+    high = add(pick(high, x, axis + 1), high_got)
+    low = add(pick(low, x, axis), swap_dp(pick(low, 1 - x, axis), 1))
+    high = add(pick(high, y, axis), swap_dp(pick(high, 1 - y, axis), 2))
+    return jnp.concatenate([low, high], axis)
 
 
 def scatter_z(tower, axis):
@@ -127,12 +135,11 @@
     level, top, half = z_bits()
     core = lax.axis_index("seq") % CORES
     held = ordered(half, pick(blocks, half, 0), swap_z(pick(blocks, 1 - half, 0), top), 0)
-    early = held
     axis, bit = 1, top // 2
     while bit:
         held = ordered(level // bit % 2, held, swap_z(held, bit), axis)
         axis, bit = axis + 1, bit // 2
-    return early, ordered(core, held, swap_core(held), axis).reshape(-1, *blocks.shape[1:])
+    return held, ordered(core, held, swap_core(held), axis).reshape(-1, *blocks.shape[1:])
 
 
 def scatter_sequence(partial):
@@ -252,7 +259,17 @@
     )(*grads)
 
 
-ANYWHERE = pl.BlockSpec(memory_space=pl.ANY)
+def gate(value, *after):
+    def kernel(*refs):
+        pass
+
+    return pl.pallas_call(
+        kernel,
+        out_shape=jax.ShapeDtypeStruct(value.shape, value.dtype),
+        in_specs=[ANYWHERE] * (1 + len(after)),
+        out_specs=ANYWHERE,
+        input_output_aliases={0: 0},
+    )(value, *after)
 
 
 def first_kernel(group, weight, rows, marks, *refs):
@@ -554,34 +571,33 @@
 
 
 def gradient_kernel(
-    placed_a, placed_n, hidden, grad_pre, grad_out, cotangent, send1, keep1, send2, keep2, turned, some
+    shard_rows, placed_a, placed_n, hidden, grad_pre, grad_out, cotangent, send, keep, turned, some
 ):
     width = placed_a.shape[1]
     side = width // CORES
-    parts = send1.shape[0] - 1
-    chips, rows2 = send2.shape[:2]
+    parts = hidden.shape[1] // width
+    chips = side // shard_rows
     core = lax.rem(lax.axis_index("seq"), CORES)
-    for start in range(0, turned.shape[0], width):
-        turned[start : start + width, :] = (
-            hidden[:, start : start + width].astype(F32).T.astype(BF16)
-        )
     branch = cotangent[...].reshape(-1, width)
-    for target, place in ((send2, 1 - core), (keep2, core)):
-        if rows2 % 16:
-            target[...] = jnp.zeros_like(target)
-            continue
-        for chip in range(chips):
-            start = pl.multiple_of((chip * CORES + place) * rows2, rows2)
-            some[chip * rows2 : (chip + 1) * rows2, :] = turned[pl.ds(start, rows2), :]
-        step = max(1, 4 * 96 // rows2)
-        for chip in range(0, chips, step):
-            product = jnp.dot(
-                some[chip * rows2 : (chip + step) * rows2, :], branch, preferred_element_type=F32
-            )
-            target[chip : chip + step] = product.astype(BF16).reshape(step, rows2, width)
+    if send.shape[0] > 1 + parts:
+        for start in range(0, turned.shape[0], width):
+            turned[start : start + width, :] = hidden[:, start : start + width].astype(F32).T
+        for target, place in ((send, 1 - core), (keep, core)):
+            for chip in range(chips):
+                for i in range(parts):
+                    start = ((chip * CORES + place) * parts + i) * shard_rows
+                    start = pl.multiple_of(start, shard_rows)
+                    to = i * side + chip * shard_rows
+                    some[to : to + shard_rows, :] = turned[pl.ds(start, shard_rows), :]
+            for i in range(parts):
+                target[1 + parts + i] = jnp.dot(
+                    some[i * side : (i + 1) * side, :].astype(BF16),
+                    branch,
+                    preferred_element_type=F32,
+                ).astype(BF16)
     turned_a = placed_a[...].astype(F32).T.astype(BF16)
     turned_n = placed_n[...].astype(F32).T.astype(BF16)
-    for target, start in ((send1, side), (keep1, 0)):
+    for target, start in ((send, side), (keep, 0)):
         target[0] = jnp.dot(
             turned_a[start : start + side], grad_out[...], preferred_element_type=F32
         ).astype(BF16)
@@ -593,20 +609,19 @@
             ).astype(BF16)
 
 
-def weight_gradients(placed_a, placed_n, hidden, grad_pre, grad_out, cotangent, chips):
+def weight_gradients(placed_a, placed_n, hidden, grad_pre, grad_out, cotangent, shard_rows):
     tokens, width = placed_a.shape
     parts = hidden.shape[1] // width
-    shape1 = jax.ShapeDtypeStruct((1 + parts, width // CORES, width), BF16)
-    rows2 = parts * width // (chips * CORES)
-    shape2 = jax.ShapeDtypeStruct((chips, rows2, width), BF16)
+    kinds = 1 + parts * (1 if shard_rows % 8 else 2)
+    shape = jax.ShapeDtypeStruct((kinds, width // CORES, width), BF16)
     return pl.pallas_call(
-        gradient_kernel,
-        out_shape=[shape1, shape1, shape2, shape2],
+        functools.partial(gradient_kernel, shard_rows),
+        out_shape=[shape, shape],
         in_specs=vmem_specs(6),
-        out_specs=vmem_specs(4),
+        out_specs=vmem_specs(2),
         scratch_shapes=[
-            pltpu.VMEM((parts * width, tokens), BF16),
-            pltpu.VMEM((parts * width // CORES, tokens), BF16),
+            pltpu.VMEM((parts * width, tokens), F32),
+            pltpu.VMEM((parts * width // CORES, tokens), F32),
         ],
         compiler_params=pltpu.CompilerParams(vmem_limit_bytes=50 * 2**20),
         cost_estimate=pl.CostEstimate(
@@ -704,7 +719,8 @@
     grads,
     stats,
     ids,
-    after,
+    after1,
+    after2,
     out,
     grad_out,
     grad_query,
@@ -793,7 +809,7 @@
     return pl.pallas_call(
         functools.partial(backward_kernel, heads, head_size, min(256, length), block),
         out_shape=jax.ShapeDtypeStruct((length, 3 * group), BF16),
-        in_specs=vmem_specs(4) + [ANYWHERE],
+        in_specs=vmem_specs(4) + [ANYWHERE] * 2,
         out_specs=vmem_specs(1)[0],
         scratch_shapes=[
             pltpu.VMEM((length, group), BF16),
@@ -805,7 +821,7 @@
         cost_estimate=pl.CostEstimate(
             flops=pairs * head_size * 10, bytes_accessed=length * width * 6, transcendentals=pairs
         ),
-    )(whole, grads, stats, ids, after)
+    )(whole, grads, stats, ids, *after)
 
 
 def on_device(
@@ -853,7 +869,7 @@
         classes,
         group,
     )
-    early, sequence = gather_sequence(blocks)
+    lines, sequence = gather_sequence(blocks)
     tower_a = gather_columns(columns)
     heights = tower_a.shape[0]
     half_a = gather_plane(tower_a[: heights // 2], tower_a[heights // 2 :], 0)
@@ -867,8 +883,13 @@
     )
 
     stacked = stack_weights(w_out.reshape(-1, width), w_fc.reshape(-1, parts * width), tower_a)
-    low1, high1 = build_tower(z_pieces(stacked), 1, [half_a, early])
-    low2, high2 = build_tower(z_pieces(w_proj.reshape(-1, width)), 0, [low1])
+    low1, high1 = build_tower(z_pieces(stacked), 1, [whole_a, lines])
+    attended, stats, qkv, normed1, ids = attend_forward(
+        sequence, wqkv, gain1, bias1, bqv, low1, seq_count, heads, head_size, block
+    )
+    pieces2 = z_pieces(gate(w_proj.reshape(-1, width), lines))
+    low2, high2 = build_tower(pieces2, 0, [attended])
+    attended = exchange(attended.reshape(count, block // 2, 2 * group))
     half1 = gather_plane(low1, high1, 1).reshape(1 + parts, -1, width)
     half2 = gather_plane(low2, high2, 0)
     other1 = swap_core(half1)
@@ -876,11 +897,6 @@
     aligned = half2.shape[1] % 16 == 0
     if not aligned:
         half2 = ordered(core, half2, other2, 1).reshape(1, parts * width, width)
-
-    attended, stats, qkv, normed1, ids = attend_forward(
-        sequence, wqkv, gain1, bias1, bqv, low1, seq_count, heads, head_size, block
-    )
-    attended = exchange(attended.reshape(count, block // 2, 2 * group))
 
     spot = jnp.arange(width, dtype=jnp.int32)
     side = width // CORES
@@ -913,31 +929,36 @@
         groups,
     )
     grad_blocks = exchange(grad_blocks).reshape(-1, 2 * group)
-    send1, keep1, send2, keep2 = weight_gradients(
-        placed_a, placed_n, hidden, grad_pre, grad_out, cotangent, chips
-    )
-    if not aligned:
+    send_b, keep_b = weight_gradients(
+        placed_a, placed_n, hidden, grad_pre, grad_out, cotangent, shard_rows
+    )
+    if send_b.shape[0] == 1 + parts:
         grad_wproj = lax.dot_general(
             hidden,
             cotangent.reshape(tokens, width),
             (((0,), (0,)), ((), ())),
             preferred_element_type=F32,
         )
-        grad_wproj = grad_wproj.astype(BF16).reshape(chips, CORES, -1, width)
-        send2, keep2 = pick(grad_wproj, 1 - core, 1), pick(grad_wproj, core, 1)
-    half1 = add(keep1, swap_core(send1))
-    half2 = add(keep2, swap_core(send2))
-    half1 = half1.reshape(1 + parts, chips, shard_rows, width)
-    own1 = scatter_z(scatter_plane(half1, 1), 1)
-    own2 = scatter_z(scatter_plane(half2, 0), 0)
+        grad_wproj = grad_wproj.astype(BF16).reshape(chips, CORES, parts, shard_rows, width)
+        grad_wproj = grad_wproj.transpose(1, 2, 0, 3, 4).reshape(CORES, parts, -1, width)
+        send_b = jnp.concatenate([send_b, pick(grad_wproj, 1 - core, 0)], 0)
+        keep_b = jnp.concatenate([keep_b, pick(grad_wproj, core, 0)], 0)
+    sum_b = add(keep_b, swap_core(send_b)).reshape(-1, chips, shard_rows, width)
+    attention_grads = []
+
+    def between(*after):
+        attention_grads.append(
+            attend_backward(qkv, grad_blocks, stats, ids, after, heads, head_size, block)
+        )
+        return attention_grads[0]
+
+    own_b = scatter_z(scatter_plane(sum_b, 1, between), 1)
+    grad_qkv = attention_grads[0]
 
     def blocks_of(value, rows):
         return value.astype(BF16).reshape(chips, CORES, rows, -1)
 
     rows = inputs.astype(F32).reshape(tokens, width)
-    grad_qkv = attend_backward(
-        qkv, grad_blocks, stats, ids, half1, heads, head_size, block
-    )
     grad_normed1 = lax.dot_general(
         grad_qkv, wqkv, (((1,), (1,)), ((), ())), preferred_element_type=F32
     )
@@ -991,13 +1012,13 @@
         own[1],
         own_qkv,
         own[2],
-        own1[0].reshape(-1),
+        own_b[0].reshape(-1),
         own[3],
         own[4],
         own[5],
-        own1[1:].transpose(1, 0, 2).reshape(-1),
+        own_b[1 : 1 + parts].transpose(1, 0, 2).reshape(-1),
         own[6],
-        own2.reshape(-1),
+        own_b[1 + parts :].reshape(-1),
         own[7],
     )
 

time: 334 us -> 349 us (1.045)
  the two profiles are of different devices: /device:TPU:0 before, /device:TPU:9 now
where the time goes in v3:
time: 349 us; the launch traced here: 344 us
  waiting for transfers between devices  152 us (44%)
  starting transfers between devices  63 us (18%)
  Pallas kernels  47.8 us (14%)
  local copies, waits for them, and re-layouts  37.1 us (11%)
  other arithmetic  34.5 us (10%)
  matrix products  7.36 us (2%)
    ppermute x20, waiting for transfers between devices, swap_dp(): return lax.ppermute(value, 'dp', [(i, i ^ bit) for i in range(size)])  75.6 us
    ppermute x9, waiting for transfers between devices, shift_z(): lax.ppermute(value, 'seq', [(i, (i + CORES * step) % size) for i in range...  41.4 us
    ppermute x8, waiting for transfers between devices, swap_z(): lax.ppermute(value, 'seq', [(i, i ^ CORES * bit) for i in range(size)])  25.9 us
    ppermute x20, starting transfers between devices, swap_dp(): return lax.ppermute(value, 'dp', [(i, i ^ bit) for i in range(size)])  16 us
    ppermute x7, starting transfers between devices, swap_core(): return lax.ppermute(value, 'seq', [(i, i ^ 1) for i in range(size)])  14.2 us
    pallas_call x1, Pallas kernels, middle_block(): pl.pallas_call(functools.partial(middle_kernel, groups), out_shape=[shape...  13.8 us
    ppermute x9, starting transfers between devices, shift_z(): lax.ppermute(value, 'seq', [(i, (i + CORES * step) % size) for i in range...  12.7 us
    pallas_call x1, Pallas kernels, attend_forward(): pl.pallas_call(functools.partial(forward_kernel, seq_count, heads, head_s...  11.3 us
  transfers between devices with their start and end apart: 46, of which 24 were waited for; matrix products, arithmetic and copies ran while one was open for 15% of the time, Pallas kernels for 4%

profile of v3, /device:TPU:9, one launch (start us, length us, event | category | flops | bytes accessed | tf_op | source)
XLA Modules:
  0.0 344.1 jit_solution(2150600395578606581)
XLA Ops:
  12.9 10.3 %collective-permute-done.1 = bf16[2,32,1152]{2,1,0:T(8,128)(2,1)S(1)} collective-permute-done((bf16[2,32,1152]{2,1,0:T(8,128)(2,1)S(1)}, bf16[2,32,1152]{2,1,0:T(8,128)(2,1)S(1)}, u32[]{:S(2)}, u32[]{:S(2)}) %collective-permute-start.1) | collective-permute-done | bytes 147488 | tf_op jit(solution)/shard_map/ppermute | solution.py:66
  33.8 4.3 %collective-permute-done.6 = bf16[2,2,32,1152]{3,2,1,0:T(8,128)(2,1)S(1)} collective-permute-done((bf16[2,2,32,1152]{3,2,1,0:T(8,128)(2,1)S(1)}, bf16[2,2,32,1152]{3,2,1,0:T(8,128)(2,1)S(1)}, u32[]{:S(2)}, u32[]{:S(2)}) %collective-permute-start.6) | collective-permute-done | bytes 294944 | tf_op jit(solution)/shard_map/ppermute | solution.py:43
  39.8 5.1 %collective-permute-start.9 = (bf16[16,32,576]{2,1,0:T(8,128)(2,1)}, bf16[16,32,576]{2,1,0:T(8,128)(2,1)}, u32[]{:S(2)}, u32[]{:S(2)}) collective-permute-start(bf16[16,32,576]{2,1,0:T(8,128)(2,1)} %broadcast_select_fusion.2), channel_id=1, source_target_pairs={{0,1},{1,0},{2,3},{3,2},{4,5},{5,4},{6,7},{7,6},{8,9},{9,8},{10,11... | collective-permute-start | bytes 1769480 | tf_op jit(solution)/shard_map/ppermute | solution.py:38
  60.9 5.9 %collective-permute-done.3.refs_2_ = bf16[5,24,768]{2,1,0:T(8,128)(2,1)S(1)} collective-permute-done((bf16[5,24,768]{2,1,0:T(8,128)(2,1)}, bf16[5,24,768]{2,1,0:T(8,128)(2,1)S(1)}, u32[]{:S(2)}, u32[]{:S(2)}) %collective-permute-start.3) | collective-permute-done | bytes 184352 | tf_op jit(solution)/shard_map/ppermute | solution.py:33
  69.2 7.6 %collective-permute-done.4.refs_3_ = bf16[5,24,768]{2,1,0:T(8,128)(2,1)S(1)} collective-permute-done((bf16[5,24,768]{2,1,0:T(8,128)(2,1)}, bf16[5,24,768]{2,1,0:T(8,128)(2,1)S(1)}, u32[]{:S(2)}, u32[]{:S(2)}) %collective-permute-start.4) | collective-permute-done | bytes 184352 | tf_op jit(solution)/shard_map/ppermute | solution.py:33
  82.4 11.3 %shard_map.259 = (bf16[512,384]{1,0:T(8,128)(2,1)}, f32[3,1024]{1,0:T(4,128)S(1)}, bf16[1024,576]{1,0:T(8,128)(2,1)S(1)}, bf16[1024,768]{1,0:T(8,128)(2,1)S(1)}, f32[1,1024]{1,0:T(1,128)S(1)}) custom-call(bf16[8,144,768]{2,1,0:T(8,128)(2,1)} %bitcast.298, bf16[768,576]{1,0:T(8,128)(2,1)S(1)} %bitcast.296, f32[1,768]{1,0:T(1,128)S(1)} %get-tuple-element.52.gain, ...), custom_call_target="tpu_custom_call" | custom-call | flops 1308622848 | bytes 6291456 | tf_op jit(solution)/shard_map/pallas_call | solution.py:784
  97.3 4.0 %collective-permute-done.21 = bf16[2,96,768]{2,1,0:T(8,128)(2,1)S(1)} collective-permute-done((bf16[2,96,768]{2,1,0:T(8,128)(2,1)S(1)}, bf16[2,96,768]{2,1,0:T(8,128)(2,1)S(1)}, u32[]{:S(2)}, u32[]{:S(2)}) %collective-permute-start.21) | collective-permute-done | bytes 294944 | tf_op jit(solution)/shard_map/ppermute | solution.py:43
  102.6 14.4 %collective-permute-done.13 = bf16[5,2,2,24,768]{4,3,2,0,1:T(8,128)(2,1)S(1)} collective-permute-done((bf16[5,2,2,24,768]{4,3,2,0,1:T(8,128)(2,1)S(1)}, bf16[5,2,2,24,768]{4,3,2,0,1:T(8,128)(2,1)S(1)}, u32[]{:S(2)}, u32[]{:S(2)}) %collective-permute-start.13) | collective-permute-done | bytes 737312 | tf_op jit(solution)/shard_map/ppermute | solution.py:43
  119.5 4.3 %collective-permute-start.16 = (bf16[5,384,768]{2,1,0:T(8,128)(2,1)}, bf16[5,384,768]{2,1,0:T(8,128)(2,1)}, u32[]{:S(2)}, u32[]{:S(2)}) collective-permute-start(bf16[5,384,768]{2,1,0:T(8,128)(2,1)} %bitcast.44.half1), channel_id=1, source_target_pairs={{0,1},{1,0},{2,3},{3,2},{4,5},{5,4},{6,7},{7,6},{8,9},{9,8},{10,11... | collective-permute-start | bytes 8847368 | tf_op jit(solution)/shard_map/ppermute | solution.py:38
  123.8 5.9 %collective-permute-done.22 = bf16[2,2,96,768]{3,2,1,0:T(8,128)(2,1)S(1)} collective-permute-done((bf16[2,2,96,768]{3,2,1,0:T(8,128)(2,1)S(1)}, bf16[2,2,96,768]{3,2,1,0:T(8,128)(2,1)S(1)}, u32[]{:S(2)}, u32[]{:S(2)}) %collective-permute-start.22) | collective-permute-done | bytes 589856 | tf_op jit(solution)/shard_map/ppermute | solution.py:43
  134.1 5.2 %all-to-all-start = ((bf16[8,64,384]{2,1,0:T(8,128)(2,1)}), bf16[8,64,384]{2,1,0:T(8,128)(2,1)S(1)}, u32[]{:S(2)}, u32[]{:S(2)}) async-start(bf16[8,64,384]{2,1,0:T(8,128)(2,1)} %bitcast.59), calls=%async_computation | async-start | bytes 786432 | tf_op jit(solution)/shard_map/all_to_all | solution.py:190
  139.4 9.0 %all-to-all-done.attended = bf16[8,64,384]{2,1,0:T(8,128)(2,1)S(1)} async-done(((bf16[8,64,384]{2,1,0:T(8,128)(2,1)}), bf16[8,64,384]{2,1,0:T(8,128)(2,1)S(1)}, u32[]{:S(2)}, u32[]{:S(2)}) %all-to-all-start) | async-done | bytes 393248 | tf_op jit(solution)/shard_map/all_to_all | solution.py:190
  148.4 13.8 %shard_map.261 = (bf16[2,128,768]{2,1,0:T(8,128)(2,1)}, f32[256,768]{1,0:T(8,128)S(1)}, bf16[8,64,384]{2,1,0:T(8,128)(2,1)}, bf16[256,768]{1,0:T(8,128)(2,1)S(1)...) custom-call(bf16[5,384,768]{2,1,0:T(8,128)(2,1)} %bitcast.44.half1, ...), custom_call_target="tpu_custom_call" | custom-call | flops 6643777536 | bytes 16777216 | tf_op jit(solution)/shard_map/pallas_call | solution.py:539
  164.6 8.2 %shard_map.262 = (bf16[9,384,768]{2,1,0:T(8,128)(2,1)}, bf16[9,384,768]{2,1,0:T(8,128)(2,1)}) custom-call(bf16[256,768]{1,0:T(8,128)(2,1)S(1)} %get-tuple-element.69.placed_a, bf16[256,768]{1,0:T(8,128)(2,1)S(1)} %get-tuple-element.70.placed_n, bf16[256,3072]{1,0:T(8,128)(2,1)S(1)} %copy-done.16, bf16[256,3072]{1,0:T(8,128)(2,1)} %get-tuple-element.72.grad_pre, ...), custom_call_target="tpu_custom_call" | custom-call | flops 2717908992 | bytes 16777216 | tf_op jit(solution)/shard_map/pallas_call | solution.py:617
  179.5 5.6 %all-to-all-start.1 = ((bf16[8,64,384]{2,1,0:T(8,128)(2,1)}), bf16[8,64,384]{2,1,0:T(8,128)(2,1)S(1)}, u32[]{:S(2)}, u32[]{:S(2)}) async-start(bf16[8,64,384]{2,1,0:T(8,128)(2,1)} %get-tuple-element.66), calls=%async_computation.1 | async-start | bytes 786432 | tf_op jit(solution)/shard_map/all_to_all | solution.py:190
  185.0 5.5 %add_convert_fusion = bf16[9,384,768]{2,1,0:T(8,128)(2,1)S(1)} fusion(bf16[9,384,768]{2,1,0:T(8,128)(2,1)} %collective-permute-done.26, bf16[9,384,768]{2,1,0:T(8,128)(2,1)} %get-tuple-element.74), kind=kLoop, calls=%fused_computation | loop fusion | flops 10616832 | bytes 15925248 | tf_op jit(solution)/shard_map/convert_element_type | solution.py:91
  197.2 8.8 %shard_map.263.refs_1_ = bf16[1024,576]{1,0:T(8,128)(2,1)S(1)} custom-call(bf16[1024,576]{1,0:T(8,128)(2,1)S(1)} %copy-done.8, bf16[512,384]{1,0:T(8,128)(2,1)S(1)} %bitcast.295, f32[3,1024]{1,0:T(4,128)S(1)} %get-tuple-element.67.stats, f32[1,1024]{1,0:T(1,128)S(1)} %get-tuple-element.68.ids, bf16[9,2,2,24,768]{4,3,2,1,0:T(8,128)(2,1)S(1)} %get-tuple-element.90.after1, ...), custom_call_target="tpu_custom_call" | custom-call | flops 1006632960 | bytes 3538944 | tf_op jit(solution)/shard_map/pallas_call | solution.py:809
  206.4 5.2 %fusion.52 = (f32[768]{0:T(1024)S(1)}, f32[768]{0:T(1024)S(1)}, bf16[1024,768]{1,0:T(8,128)(2,1)}) fusion(f32[1024]{0:T(1024)S(1)} %rsqrt_bitcast_fusion, f32[1024]{0:T(1024)S(1)} %get-tuple-element.148, f32[8,128,768]{2,1,0:T(8,128)} %slice_convert_fusion, bf16[1024,576]{1,0:T(8,128)(2,1)S(1)} %shard_map.263.refs_1_, bf16[768,576]{1,0:T(8,128)(2,1)} %bitcast.297), kind=kOutput, calls=%fused_computation.201 | convolution fusion | flops 910686720 | bytes 6797312 | tf_op jit(solution)/shard_map/dot_general | solution.py:962
  227.3 30.9 %collective-permute-done.31 = bf16[2,2,32,1152]{3,2,1,0:T(8,128)(2,1)S(1)} collective-permute-done((bf16[2,2,32,1152]{3,2,1,0:T(8,128)(2,1)S(1)}, bf16[2,2,32,1152]{3,2,1,0:T(8,128)(2,1)S(1)}, u32[]{:S(2)}, u32[]{:S(2)}) %collective-permute-start.31) | collective-permute-done | bytes 294944 | tf_op jit(solution)/shard_map/ppermute | solution.py:43
  265.8 4.1 %collective-permute-done.35 = bf16[2,32,1152]{2,1,0:T(8,128)(2,1)S(1)} collective-permute-done((bf16[2,32,1152]{2,1,0:T(8,128)(2,1)S(1)}, bf16[2,32,1152]{2,1,0:T(8,128)(2,1)S(1)}, u32[]{:S(2)}, u32[]{:S(2)}) %collective-permute-start.35) | collective-permute-done | bytes 147488 | tf_op jit(solution)/shard_map/ppermute | solution.py:66
  271.6 4.9 %collective-permute-done.28 = bf16[2,128,768]{2,1,0:T(8,128)(2,1)S(1)} collective-permute-done((bf16[2,128,768]{2,1,0:T(8,128)(2,1)S(1)}, bf16[2,128,768]{2,1,0:T(8,128)(2,1)S(1)}, u32[]{:S(2)}, u32[]{:S(2)}) %collective-permute-start.28) | collective-permute-done | bytes 393248 | tf_op jit(solution)/shard_map/ppermute | solution.py:66
  298.1 7.6 %collective-permute-done.40 = bf16[9,2,24,768]{3,2,1,0:T(8,128)(2,1)} collective-permute-done((bf16[9,2,24,768]{3,2,1,0:T(8,128)(2,1)}, bf16[9,2,24,768]{3,2,1,0:T(8,128)(2,1)}, u32[]{:S(2)}, u32[]{:S(2)}) %collective-permute-start.40) | collective-permute-done | bytes 663584 | tf_op jit(solution)/shard_map/ppermute | solution.py:43
  315.2 19.4 %collective-permute-done.42 = bf16[9,24,768]{2,1,0:T(8,128)(2,1)S(1)} collective-permute-done((bf16[9,24,768]{2,1,0:T(8,128)(2,1)S(1)}, bf16[9,24,768]{2,1,0:T(8,128)(2,1)S(1)}, u32[]{:S(2)}, u32[]{:S(2)}) %collective-permute-start.42) | collective-permute-done | bytes 331808 | tf_op jit(solution)/shard_map/ppermute | solution.py:33
  334.7 6.5 %collective-permute-done.43 = bf16[9,24,768]{2,1,0:T(8,128)(2,1)S(1)} collective-permute-done((bf16[9,24,768]{2,1,0:T(8,128)(2,1)S(1)}, bf16[9,24,768]{2,1,0:T(8,128)(2,1)S(1)}, u32[]{:S(2)}, u32[]{:S(2)}) %collective-permute-start.43) | collective-permute-done | bytes 331808 | tf_op jit(solution)/shard_map/ppermute | solution.py:33
  (267 shorter events, 134.5 us)
Async XLA Ops:
  28.0 16.9 %collective-permute-start.11 = (bf16[2,144,768]{2,1,0:T(8,128)(2,1)S(1)}, bf16[2,144,768]{2,1,0:T(8,128)(2,1)S(1)}, u32[]{:S(2)}, u32[]{:S(2)}) collective-permute-start(bf16[2,144,768]{2,1,0:T(8,128)(2,1)S(1)} %pad_maximum_fusion.8), channel_id=1, source_target_pairs={{0,2},{1,3},{2,0},{3,1},{4,6},{5,7},{6,4},{7,5},{8,10},{9,11},{10,... | collective-permute-start | bytes 1327112 | tf_op jit(solution)/shard_map/ppermute | solution.py:66
  39.8 15.6 %collective-permute-start.9 = (bf16[16,32,576]{2,1,0:T(8,128)(2,1)}, bf16[16,32,576]{2,1,0:T(8,128)(2,1)}, u32[]{:S(2)}, u32[]{:S(2)}) collective-permute-start(bf16[16,32,576]{2,1,0:T(8,128)(2,1)} %broadcast_select_fusion.2), channel_id=1, source_target_pairs={{0,1},{1,0},{2,3},{3,2},{4,5},{5,4},{6,7},{7,6},{8,9},{9,8},{10,11... | collective-permute-start | bytes 1769480 | tf_op jit(solution)/shard_map/ppermute | solution.py:38
  45.0 33.3 %collective-permute-start.20 = (bf16[2,2,144,768]{3,2,1,0:T(8,128)(2,1)S(1)}, bf16[2,2,144,768]{3,2,1,0:T(8,128)(2,1)}, u32[]{:S(2)}, u32[]{:S(2)}) collective-permute-start(bf16[2,2,144,768]{3,2,1,0:T(8,128)(2,1)S(1)} %pad_maximum_fusion.3.refs_5_.refs_1_), channel_id=1, source_target_pairs={{0,1},{1,0},{2,3},{3,2},{4,5},{5,4},{6,7},{7,6},{8,9},{9,8},{10,11... | collective-permute-start | bytes 2654216 | tf_op jit(solution)/shard_map/ppermute | solution.py:38
  51.2 15.6 %collective-permute-start.3 = (bf16[5,24,768]{2,1,0:T(8,128)(2,1)}, bf16[5,24,768]{2,1,0:T(8,128)(2,1)S(1)}, u32[]{:S(2)}, u32[]{:S(2)}) collective-permute-start(bf16[5,24,768]{2,1,0:T(8,128)(2,1)} %shard_map.255.refs_0_), channel_id=1, source_target_pairs={{0,4},{1,5},{2,6},{3,7},{4,0},{5,1},{6,2},{7,3},{8,12},{9,13},{10,... | collective-permute-start | bytes 552968 | tf_op jit(solution)/shard_map/ppermute | solution.py:33
  54.3 22.5 %collective-permute-start.4 = (bf16[5,24,768]{2,1,0:T(8,128)(2,1)}, bf16[5,24,768]{2,1,0:T(8,128)(2,1)S(1)}, u32[]{:S(2)}, u32[]{:S(2)}) collective-permute-start(bf16[5,24,768]{2,1,0:T(8,128)(2,1)} %shard_map.255.refs_0_), channel_id=1, source_target_pairs={{0,2},{1,3},{2,4},{3,5},{4,6},{5,7},{6,0},{7,1},{8,10},{9,11},{10,... | collective-permute-start | bytes 552968 | tf_op jit(solution)/shard_map/ppermute | solution.py:33
  55.4 38.3 %collective-permute-start.17 = (bf16[96,768]{1,0:T(8,128)(2,1)}, bf16[96,768]{1,0:T(8,128)(2,1)S(1)}, u32[]{:S(2)}, u32[]{:S(2)}) collective-permute-start(bf16[96,768]{1,0:T(8,128)(2,1)} %shard_map.257.refs_0_), channel_id=1, source_target_pairs={{0,6},{1,7},{2,0},{3,1},{4,2},{5,3},{6,4},{7,5},{8,14},{9,15},{10,... | collective-permute-start | bytes 442376 | tf_op jit(solution)/shard_map/ppermute | solution.py:33
  58.5 35.2 %collective-permute-start.18 = (bf16[96,768]{1,0:T(8,128)(2,1)S(1)}, bf16[96,768]{1,0:T(8,128)(2,1)S(1)}, u32[]{:S(2)}, u32[]{:S(2)}) collective-permute-start(bf16[96,768]{1,0:T(8,128)(2,1)S(1)} %copy-done.6), channel_id=1, source_target_pairs={{0,4},{1,5},{2,6},{3,7},{4,0},{5,1},{6,2},{7,3},{8,12},{9,13},{10,... | collective-permute-start | bytes 442376 | tf_op jit(solution)/shard_map/ppermute | solution.py:33
  66.8 26.9 %collective-permute-start.19 = (bf16[96,768]{1,0:T(8,128)(2,1)S(1)}, bf16[96,768]{1,0:T(8,128)(2,1)S(1)}, u32[]{:S(2)}, u32[]{:S(2)}) collective-permute-start(bf16[96,768]{1,0:T(8,128)(2,1)S(1)} %copy-done.6), channel_id=1, source_target_pairs={{0,2},{1,3},{2,4},{3,5},{4,6},{5,7},{6,0},{7,1},{8,10},{9,11},{10,... | collective-permute-start | bytes 442376 | tf_op jit(solution)/shard_map/ppermute | solution.py:33
  77.1 17.3 %collective-permute-start.12 = (bf16[5,2,24,768]{3,2,1,0:T(8,128)(2,1)S(1)}, bf16[5,2,24,768]{3,2,1,0:T(8,128)(2,1)S(1)}, u32[]{:S(2)}, u32[]{:S(2)}) collective-permute-start(bf16[5,2,24,768]{3,2,1,0:T(8,128)(2,1)S(1)} %get-tuple-element.50.after), channel_id=1, source_target_pairs={{0,8},{8,0},{16,24},{24,16},{1,9},{9,1},{17,25},{25,17},{2,10},{10... | collective-permute-start | bytes 1105928 | tf_op jit(solution)/shard_map/ppermute | solution.py:43
  78.4 17.5 %collective-permute-start.14 = (bf16[5,2,24,768]{3,2,1,0:T(8,128)(2,1)S(1)}, bf16[5,2,24,768]{3,2,1,0:T(8,128)(2,1)S(1)}, u32[]{:S(2)}, u32[]{:S(2)}) collective-permute-start(bf16[5,2,24,768]{3,2,1,0:T(8,128)(2,1)S(1)} %get-tuple-element.51), channel_id=1, source_target_pairs={{0,16},{8,24},{16,0},{24,8},{1,17},{9,25},{17,1},{25,9},{2,18},{10... | collective-permute-start | bytes 1105928 | tf_op jit(solution)/shard_map/ppermute | solution.py:43
  95.3 21.7 %collective-permute-start.13 = (bf16[5,2,2,24,768]{4,3,2,0,1:T(8,128)(2,1)S(1)}, bf16[5,2,2,24,768]{4,3,2,0,1:T(8,128)(2,1)S(1)}, u32[]{:S(2)}, u32[]{:S(2)}) collective-permute-start(bf16[5,2,2,24,768]{4,3,2,0,1:T(8,128)(2,1)S(1)} %pad_maximum_fusion.4), channel_id=1, source_target_pairs={{0,16},{8,24},{16,0},{24,8},{1,17},{9,25},{17,1},{25,9},{2,18},{10... | collective-permute-start | bytes 2211848 | tf_op jit(solution)/shard_map/ppermute | solution.py:43
  96.0 21.2 %collective-permute-start.15 = (bf16[5,2,2,24,768]{4,3,2,0,1:T(8,128)(2,1)S(1)}, bf16[5,2,2,24,768]{4,3,2,0,1:T(8,128)(2,1)S(1)}, u32[]{:S(2)}, u32[]{:S(2)}) collective-permute-start(bf16[5,2,2,24,768]{4,3,2,0,1:T(8,128)(2,1)S(1)} %pad_maximum_fusion.5), channel_id=1, source_target_pairs={{0,8},{8,0},{16,24},{24,16},{1,9},{9,1},{17,25},{25,17},{2,10},{10... | collective-permute-start | bytes 2211848 | tf_op jit(solution)/shard_map/ppermute | solution.py:43
  101.4 28.3 %collective-permute-start.22 = (bf16[2,2,96,768]{3,2,1,0:T(8,128)(2,1)S(1)}, bf16[2,2,96,768]{3,2,1,0:T(8,128)(2,1)S(1)}, u32[]{:S(2)}, u32[]{:S(2)}) collective-permute-start(bf16[2,2,96,768]{3,2,1,0:T(8,128)(2,1)S(1)} %pad_maximum_fusion.6), channel_id=1, source_target_pairs={{0,16},{8,24},{16,0},{24,8},{1,17},{9,25},{17,1},{25,9},{2,18},{10... | collective-permute-start | bytes 1769480 | tf_op jit(solution)/shard_map/ppermute | solution.py:43
  101.8 27.9 %collective-permute-start.24 = (bf16[2,2,96,768]{3,2,1,0:T(8,128)(2,1)S(1)}, bf16[2,2,96,768]{3,2,1,0:T(8,128)(2,1)S(1)}, u32[]{:S(2)}, u32[]{:S(2)}) collective-permute-start(bf16[2,2,96,768]{3,2,1,0:T(8,128)(2,1)S(1)} %pad_maximum_fusion.7), channel_id=1, source_target_pairs={{0,8},{8,0},{16,24},{24,16},{1,9},{9,1},{17,25},{25,17},{2,10},{10... | collective-permute-start | bytes 1769480 | tf_op jit(solution)/shard_map/ppermute | solution.py:43
  119.5 28.9 %collective-permute-start.16 = (bf16[5,384,768]{2,1,0:T(8,128)(2,1)}, bf16[5,384,768]{2,1,0:T(8,128)(2,1)}, u32[]{:S(2)}, u32[]{:S(2)}) collective-permute-start(bf16[5,384,768]{2,1,0:T(8,128)(2,1)} %bitcast.44.half1), channel_id=1, source_target_pairs={{0,1},{1,0},{2,3},{3,2},{4,5},{5,4},{6,7},{7,6},{8,9},{9,8},{10,11... | collective-permute-start | bytes 8847368 | tf_op jit(solution)/shard_map/ppermute | solution.py:38
  131.7 16.7 %collective-permute-start.25 = (bf16[16,96,768]{2,1,0:T(8,128)(2,1)}, bf16[16,96,768]{2,1,0:T(8,128)(2,1)}, u32[]{:S(2)}, u32[]{:S(2)}) collective-permute-start(bf16[16,96,768]{2,1,0:T(8,128)(2,1)} %bitcast.58.half2), channel_id=1, source_target_pairs={{0,1},{1,0},{2,3},{3,2},{4,5},{5,4},{6,7},{7,6},{8,9},{9,8},{10,11... | collective-permute-start | bytes 7077896 | tf_op jit(solution)/shard_map/ppermute | solution.py:38
  220.1 67.8 %collective-permute-start.39 = (bf16[9,2,2,24,768]{4,3,2,1,0:T(8,128)(2,1)S(1)}, bf16[9,2,2,24,768]{4,3,2,1,0:T(8,128)(2,1)}, u32[]{:S(2)}, u32[]{:S(2)}) collective-permute-start(bf16[9,2,2,24,768]{4,3,2,1,0:T(8,128)(2,1)S(1)} %copy-done.5), channel_id=1, source_target_pairs={{0,8},{8,0},{16,24},{24,16},{1,9},{9,1},{17,25},{25,17},{2,10},{10... | collective-permute-start | bytes 3981320 | tf_op jit(solution)/shard_map/ppermute | solution.py:43
  221.4 70.9 %collective-permute-start.37 = (bf16[9,2,2,24,768]{4,3,2,1,0:T(8,128)(2,1)S(1)}, bf16[9,2,2,24,768]{4,3,2,1,0:T(8,128)(2,1)}, u32[]{:S(2)}, u32[]{:S(2)}) collective-permute-start(bf16[9,2,2,24,768]{4,3,2,1,0:T(8,128)(2,1)S(1)} %get-tuple-element.90.after1), channel_id=1, source_target_pairs={{0,16},{8,24},{16,0},{24,8},{1,17},{9,25},{17,1},{25,9},{2,18},{10... | collective-permute-start | bytes 3981320 | tf_op jit(solution)/shard_map/ppermute | solution.py:43
  224.3 33.9 %collective-permute-start.31 = (bf16[2,2,32,1152]{3,2,1,0:T(8,128)(2,1)S(1)}, bf16[2,2,32,1152]{3,2,1,0:T(8,128)(2,1)S(1)}, u32[]{:S(2)}, u32[]{:S(2)}) collective-permute-start(bf16[2,2,32,1152]{3,2,1,0:T(8,128)(2,1)S(1)} %dynamic-slice_bitcast_fusion.7), channel_id=1, source_target_pairs={{0,16},{8,24},{16,0},{24,8},{1,17},{9,25},{17,1},{25,9},{2,18},{10... | collective-permute-start | bytes 884744 | tf_op jit(solution)/shard_map/ppermute | solution.py:43
  225.6 39.6 %collective-permute-start.27 = (bf16[2,2,128,768]{3,2,1,0:T(8,128)(2,1)S(1)}, bf16[2,2,128,768]{3,2,1,0:T(8,128)(2,1)S(1)}, u32[]{:S(2)}, u32[]{:S(2)}) collective-permute-start(bf16[2,2,128,768]{3,2,1,0:T(8,128)(2,1)S(1)} %dynamic-slice_bitcast_fusion.2), channel_id=1, source_target_pairs={{0,1},{1,0},{2,3},{3,2},{4,5},{5,4},{6,7},{7,6},{8,9},{9,8},{10,11... | collective-permute-start | bytes 2359304 | tf_op jit(solution)/shard_map/ppermute | solution.py:38
  226.2 32.4 %collective-permute-start.33 = (bf16[2,2,32,1152]{3,2,1,0:T(8,128)(2,1)S(1)}, bf16[2,2,32,1152]{3,2,1,0:T(8,128)(2,1)S(1)}, u32[]{:S(2)}, u32[]{:S(2)}) collective-permute-start(bf16[2,2,32,1152]{3,2,1,0:T(8,128)(2,1)S(1)} %dynamic-slice_bitcast_fusion.6), channel_id=1, source_target_pairs={{0,8},{8,0},{16,24},{24,16},{1,9},{9,1},{17,25},{25,17},{2,10},{10... | collective-permute-start | bytes 884744 | tf_op jit(solution)/shard_map/ppermute | solution.py:43
  277.3 19.0 %collective-permute-start.29 = (bf16[128,768]{1,0:T(8,128)(2,1)}, bf16[128,768]{1,0:T(8,128)(2,1)}, u32[]{:S(2)}, u32[]{:S(2)}) collective-permute-start(bf16[128,768]{1,0:T(8,128)(2,1)} %dynamic-slice_bitcast_fusion.9), channel_id=1, source_target_pairs={{0,4},{1,5},{2,6},{3,7},{4,0},{5,1},{6,2},{7,3},{8,12},{9,13},{10,... | collective-permute-start | bytes 589832 | tf_op jit(solution)/shard_map/ppermute | solution.py:66
  309.9 24.7 %collective-permute-start.42 = (bf16[9,24,768]{2,1,0:T(8,128)(2,1)S(1)}, bf16[9,24,768]{2,1,0:T(8,128)(2,1)S(1)}, u32[]{:S(2)}, u32[]{:S(2)}) collective-permute-start(bf16[9,24,768]{2,1,0:T(8,128)(2,1)S(1)} %get-tuple-element.102), channel_id=1, source_target_pairs={{0,4},{1,5},{2,6},{3,7},{4,0},{5,1},{6,2},{7,3},{8,12},{9,13},{10,... | collective-permute-start | bytes 995336 | tf_op jit(solution)/shard_map/ppermute | solution.py:33
  311.5 29.7 %collective-permute-start.43 = (bf16[9,24,768]{2,1,0:T(8,128)(2,1)S(1)}, bf16[9,24,768]{2,1,0:T(8,128)(2,1)S(1)}, u32[]{:S(2)}, u32[]{:S(2)}) collective-permute-start(bf16[9,24,768]{2,1,0:T(8,128)(2,1)S(1)} %get-tuple-element.103), channel_id=1, source_target_pairs={{0,6},{1,7},{2,0},{3,1},{4,2},{5,3},{6,4},{7,5},{8,14},{9,15},{10,... | collective-permute-start | bytes 995336 | tf_op jit(solution)/shard_map/ppermute | solution.py:33
  (53 other events, 419.9 us)

commit v4 on v3

--- a/solution.py
+++ b/solution.py
@@ -26,6 +26,7 @@
 
 
 ANYWHERE = pl.BlockSpec(memory_space=pl.ANY)
+LIGHT = pl.CostEstimate(flops=1, bytes_accessed=1, transcendentals=0)
 
 
 def shift_z(value, step):
@@ -66,14 +67,18 @@
     return lax.ppermute(value, "seq", [(i, i ^ (CORES * bit)) for i in range(size)])
 
 
-def gather_plane(low, high, axis):
+def gather_plane(low, high, axis, first=None, second=None):
+    def move(value, bit, after):
+        moved = swap_dp(value, bit)
+        return moved if after is None else gate(moved, after)
+
     if lax.axis_size("dp") == 4:
         plane = lax.axis_index("dp")
         y, x = plane // 2, plane % 2
-        low_x = ordered(x, low, swap_dp(low, 1), axis)
-        high_y = ordered(y, high, swap_dp(high, 2), axis)
-        low_all = ordered(y, low_x, swap_dp(low_x, 2), axis)
-        high_all = ordered(x, high_y, swap_dp(high_y, 1), axis + 1)
+        low_x = ordered(x, low, move(low, 1, first), axis)
+        high_y = ordered(y, high, move(high, 2, first), axis)
+        low_all = ordered(y, low_x, move(low_x, 2, second), axis)
+        high_all = ordered(x, high_y, move(high_y, 1, second), axis + 1)
         half = jnp.concatenate([low_all, high_all], axis + 2)
         count = 4 * half.shape[axis + 2]
     else:
@@ -96,6 +101,7 @@
     heights = lax.axis_size("seq") // CORES
     if planes != 4:
         if between is not None:
+            between(split, split)
             between(split, split)
         return lax.psum_scatter(split, "dp", scatter_dimension=axis, tiled=True)
     plane = lax.axis_index("dp")
@@ -110,6 +116,8 @@
         low_got, high_got = gate(low_got, after), gate(high_got, after)
     low = add(pick(low, y, axis), low_got)
     high = add(pick(high, x, axis + 1), high_got)
+    if between is not None:
+        between(low, high)
     low = add(pick(low, x, axis), swap_dp(pick(low, 1 - x, axis), 1))
     high = add(pick(high, y, axis), swap_dp(pick(high, 1 - y, axis), 2))
     return jnp.concatenate([low, high], axis)
@@ -168,15 +176,16 @@
         got = swap_z(pick(held, 1 - flag, 0), bit)
         held = ordered(flag, pick(held, flag, 0), got, count - 1)
         bit //= 2
-    return ordered(half, held, swap_z(held, top), 0).reshape(-1, *shape)
-
-
-def scatter_columns(tower):
+    return held, ordered(half, held, swap_z(held, top), 0).reshape(-1, *shape)
+
+
+def scatter_columns(tower, after):
     level, top, half = z_bits()
     shape = tower.shape[1:]
     count = top.bit_length() - 1
     held = tower.reshape(*[2] * (count + 1), *shape)
-    held = add(pick(held, half, 0), swap_z(pick(held, 1 - half, 0), top))
+    got = gate(swap_z(pick(held, 1 - half, 0), top), after)
+    held = add(pick(held, half, 0), got)
     bit = 1
     while bit < top:
         flag = level // bit % 2
@@ -231,6 +240,7 @@
         in_specs=vmem_specs(1),
         out_specs=vmem_specs(len(sizes)),
         compiler_params=pltpu.CompilerParams(vmem_limit_bytes=32 * 2**20),
+        cost_estimate=LIGHT,
     )(small)
 
 
@@ -256,6 +266,7 @@
         out_specs=vmem_specs(1)[0],
         scratch_shapes=[pltpu.VMEM((devices, ROWS, LANES), F32)],
         compiler_params=pltpu.CompilerParams(vmem_limit_bytes=32 * 2**20),
+        cost_estimate=LIGHT,
     )(*grads)
 
 
@@ -269,6 +280,7 @@
         in_specs=[ANYWHERE] * (1 + len(after)),
         out_specs=ANYWHERE,
         input_output_aliases={0: 0},
+        cost_estimate=LIGHT,
     )(value, *after)
 
 
@@ -332,6 +344,7 @@
         out_shape=jax.ShapeDtypeStruct((1 + w_fc.shape[1] // width, rows, width), BF16),
         in_specs=vmem_specs(2) + [ANYWHERE],
         out_specs=vmem_specs(1)[0],
+        cost_estimate=LIGHT,
     )(w_out, w_fc, after)
 
 
@@ -360,6 +373,7 @@
         in_specs=vmem_specs(count) + [ANYWHERE] * len(after),
         out_specs=vmem_specs(2),
         compiler_params=pltpu.CompilerParams(vmem_limit_bytes=32 * 2**20),
+        cost_estimate=LIGHT,
     )(*pieces, *after)
 
 
@@ -564,9 +578,7 @@
             pltpu.SemaphoreType.DMA((2 * kinds + 2 * chips,)),
         ],
         compiler_params=pltpu.CompilerParams(vmem_limit_bytes=50 * 2**20),
-        cost_estimate=pl.CostEstimate(
-            flops=tokens * width * width * 44, bytes_accessed=2**24, transcendentals=2**20
-        ),
+        cost_estimate=LIGHT,
     )(half1, other1, half2, other2, attended, inputs, cotangent, order, *vectors)
 
 
@@ -624,9 +636,7 @@
             pltpu.VMEM((parts * width // CORES, tokens), F32),
         ],
         compiler_params=pltpu.CompilerParams(vmem_limit_bytes=50 * 2**20),
-        cost_estimate=pl.CostEstimate(
-            flops=tokens * width * width * 18, bytes_accessed=2**24, transcendentals=0
-        ),
+        cost_estimate=LIGHT,
     )(placed_a, placed_n, hidden, grad_pre, grad_out, cotangent)
 
 
@@ -780,7 +790,6 @@
     length = rows.shape[0] * block
     width = rows.shape[2]
     group = heads * head_size
-    pairs = length * length // 2 * heads
     return pl.pallas_call(
         functools.partial(forward_kernel, seq_count, heads, head_size, min(256, length), block),
         out_shape=[
@@ -794,18 +803,13 @@
         out_specs=vmem_specs(5),
         scratch_shapes=[pltpu.VMEM((length, group), BF16), pltpu.VMEM((1, 3 * group), F32)],
         compiler_params=pltpu.CompilerParams(vmem_limit_bytes=48 * 2**20),
-        cost_estimate=pl.CostEstimate(
-            flops=pairs * head_size * 4 + length * width * group * 6,
-            bytes_accessed=length * width * 8,
-            transcendentals=pairs,
-        ),
+        cost_estimate=LIGHT,
     )(rows, weight, gain, bias, bqv, after)
 
 
 def attend_backward(whole, grads, stats, ids, after, heads, head_size, block):
     length, width = whole.shape
     group = heads * head_size
-    pairs = length * length // 2 * heads
     return pl.pallas_call(
         functools.partial(backward_kernel, heads, head_size, min(256, length), block),
         out_shape=jax.ShapeDtypeStruct((length, 3 * group), BF16),
@@ -818,9 +822,7 @@
             pltpu.VMEM((heads, length, head_size), F32),
         ],
         compiler_params=pltpu.CompilerParams(vmem_limit_bytes=48 * 2**20),
-        cost_estimate=pl.CostEstimate(
-            flops=pairs * head_size * 10, bytes_accessed=length * width * 6, transcendentals=pairs
-        ),
+        cost_estimate=LIGHT,
     )(whole, grads, stats, ids, *after)
 
 
@@ -870,9 +872,12 @@
         group,
     )
     lines, sequence = gather_sequence(blocks)
-    tower_a = gather_columns(columns)
+    early_a, tower_a = gather_columns(columns)
+    stacked = stack_weights(w_out.reshape(-1, width), w_fc.reshape(-1, parts * width), early_a)
+    low1, high1 = build_tower(z_pieces(stacked), 1, [])
+    tower_a = gate(tower_a, stacked)
     heights = tower_a.shape[0]
-    half_a = gather_plane(tower_a[: heights // 2], tower_a[heights // 2 :], 0)
+    half_a = gather_plane(tower_a[: heights // 2], tower_a[heights // 2 :], 0, None, low1)
     left, right = half_a[..., : 3 * group], half_a[..., 3 * group :]
     mine_a = jnp.where(core == 0, left, right)
     whole_a = ordered(core, mine_a, swap_core(jnp.where(core == 0, right, left)), 1)
@@ -882,16 +887,14 @@
         whole_a[:, shard_rows:, :LANES], sizes
     )
 
-    stacked = stack_weights(w_out.reshape(-1, width), w_fc.reshape(-1, parts * width), tower_a)
-    low1, high1 = build_tower(z_pieces(stacked), 1, [whole_a, lines])
-    attended, stats, qkv, normed1, ids = attend_forward(
+    raw, stats, qkv, normed1, ids = attend_forward(
         sequence, wqkv, gain1, bias1, bqv, low1, seq_count, heads, head_size, block
     )
     pieces2 = z_pieces(gate(w_proj.reshape(-1, width), lines))
-    low2, high2 = build_tower(pieces2, 0, [attended])
-    attended = exchange(attended.reshape(count, block // 2, 2 * group))
-    half1 = gather_plane(low1, high1, 1).reshape(1 + parts, -1, width)
-    half2 = gather_plane(low2, high2, 0)
+    low2, high2 = build_tower(pieces2, 0, [raw])
+    attended = exchange(raw.reshape(count, block // 2, 2 * group))
+    half1 = gather_plane(low1, high1, 1, raw, attended).reshape(1 + parts, -1, width)
+    half2 = gather_plane(low2, high2, 0, attended)
     other1 = swap_core(half1)
     other2 = swap_core(half2)
     aligned = half2.shape[1] % 16 == 0
@@ -944,16 +947,20 @@
         send_b = jnp.concatenate([send_b, pick(grad_wproj, 1 - core, 0)], 0)
         keep_b = jnp.concatenate([keep_b, pick(grad_wproj, core, 0)], 0)
     sum_b = add(keep_b, swap_core(send_b)).reshape(-1, chips, shard_rows, width)
-    attention_grads = []
+    steps = []
 
     def between(*after):
-        attention_grads.append(
-            attend_backward(qkv, grad_blocks, stats, ids, after, heads, head_size, block)
-        )
-        return attention_grads[0]
-
-    own_b = scatter_z(scatter_plane(sum_b, 1, between), 1)
-    grad_qkv = attention_grads[0]
+        if steps:
+            steps.append(after[0])
+        else:
+            steps.append(
+                attend_backward(qkv, grad_blocks, stats, ids, after, heads, head_size, block)
+            )
+        return steps[0]
+
+    tower_b = scatter_plane(sum_b, 1, between)
+    own_b = scatter_z(tower_b, 1)
+    grad_qkv, first_sums = steps
 
     def blocks_of(value, rows):
         return value.astype(BF16).reshape(chips, CORES, rows, -1)
@@ -997,7 +1004,9 @@
     pair_a = jnp.concatenate(
         [jnp.where(core == 0, keep_a, got_a), jnp.where(core == 0, got_a, keep_a)], -1
     )
-    own_a = scatter_columns(scatter_plane(pair_a, 0))
+    pair_a = gate(pair_a, first_sums)
+    tower_a = scatter_plane(pair_a, 0, lambda *_: tower_b)
+    own_a = scatter_columns(tower_a, own_b)
     own_small = jnp.sum(
         own_a[:, shard_rows:].reshape(classes, ROWS, CORES, 3 * group)[..., :LANES], (0, 2)
     )

time: 349 us -> 318 us (0.911)
  the two profiles are of different devices: /device:TPU:9 before, /device:TPU:0 now
where the time goes in v4:
time: 318 us; the launch traced here: 312 us
  waiting for transfers between devices  97.2 us (31%)
  other arithmetic  57.4 us (18%)
  starting transfers between devices  57.2 us (18%)
  Pallas kernels  48 us (15%)
  local copies, waits for them, and re-layouts  45.1 us (14%)
  matrix products  5.36 us (2%)
    ppermute x20, waiting for transfers between devices, swap_dp(): return lax.ppermute(value, 'dp', [(i, i ^ bit) for i in range(size)])  47.4 us
    ppermute x8, waiting for transfers between devices, swap_z(): lax.ppermute(value, 'seq', [(i, i ^ CORES * bit) for i in range(size)])  30.6 us
    another operation x31, other arithmetic, ordered(): return jnp.stack([first, second], axis)  24.5 us
    ppermute x20, starting transfers between devices, swap_dp(): return lax.ppermute(value, 'dp', [(i, i ^ bit) for i in range(size)])  23.7 us
    convert_element_type x12, other arithmetic, add(): return (mine.astype(F32) + other.astype(F32)).astype(mine.dtype)  17.7 us
    unnamed x90, local copies, waits for them, and re-layouts  14.8 us
    ppermute x9, starting transfers between devices, shift_z(): lax.ppermute(value, 'seq', [(i, (i + CORES * step) % size) for i in range...  14.7 us
    pallas_call x1, Pallas kernels, middle_block(): pl.pallas_call(functools.partial(middle_kernel, groups), out_shape=[shape...  13.8 us
  transfers between devices with their start and end apart: 46, of which 22 were waited for; matrix products, arithmetic and copies ran while one was open for 27% of the time, Pallas kernels for 8%

profile of v4, /device:TPU:0, one launch (start us, length us, event | category | flops | bytes accessed | tf_op | source)
XLA Modules:
  0.0 312.0 jit_solution(11364121269214383238)
XLA Ops:
  5.3 3.0 collective-permute-start
  11.6 3.1 collective-permute-start.8
  18.8 3.9 %collective-permute-start.1 = (bf16[5,24,768]{2,1,0:T(8,128)(2,1)}, bf16[5,24,768]{2,1,0:T(8,128)(2,1)S(1)}, u32[]{:S(2)}, u32[]{:S(2)}) collective-permute-start(bf16[5,24,768]{2,1,0:T(8,128)(2,1)} %shard_map.255.refs_0_.refs_1_), channel_id=1, source_target_pairs={{0,6},{1,7},{2,0},{3,1},{4,2},{5,3},{6,4},{7,5},{8,14},{9,15},{10,... | collective-permute-start | bytes 552968 | tf_op jit(solution)/shard_map/ppermute | solution.py:34
  23.7 3.4 %collective-permute-done.8 = bf16[2,32,1152]{2,1,0:T(8,128)(2,1)S(1)} collective-permute-done((bf16[2,32,1152]{2,1,0:T(8,128)(2,1)S(1)}, bf16[2,32,1152]{2,1,0:T(8,128)(2,1)S(1)}, u32[]{:S(2)}, u32[]{:S(2)}) %collective-permute-start.8) | collective-permute-done | bytes 147488 | tf_op jit(solution)/shard_map/ppermute | solution.py:67
  30.5 8.7 %collective-permute-done.5 = bf16[144,768]{1,0:T(8,128)(2,1)S(1)} collective-permute-done((bf16[144,768]{1,0:T(8,128)(2,1)S(1)}, bf16[144,768]{1,0:T(8,128)(2,1)S(1)}, u32[]{:S(2)}, u32[]{:S(2)}) %collective-permute-start.5) | collective-permute-done | bytes 221216 | tf_op jit(solution)/shard_map/ppermute | solution.py:67
  40.7 3.6 %collective-permute-done.9 = bf16[2,32,1152]{2,1,0:T(8,128)(2,1)S(1)} collective-permute-done((bf16[2,32,1152]{2,1,0:T(8,128)(2,1)S(1)}, bf16[2,32,1152]{2,1,0:T(8,128)(2,1)S(1)}, u32[]{:S(2)}, u32[]{:S(2)}) %collective-permute-start.9) | collective-permute-done | bytes 147488 | tf_op jit(solution)/shard_map/ppermute | solution.py:44
  77.4 11.3 %shard_map.261 = (bf16[512,384]{1,0:T(8,128)(2,1)}, f32[3,1024]{1,0:T(4,128)S(1)}, bf16[1024,576]{1,0:T(8,128)(2,1)S(1)}, bf16[1024,768]{1,0:T(8,128)(2,1)S(1)}, f32[1,1024]{1,0:T(1,128)S(1)}) custom-call(bf16[8,144,768]{2,1,0:T(8,128)(2,1)} %bitcast.299, bf16[768,576]{1,0:T(8,128)(2,1)S(1)} %bitcast.296, f32[1,768]{1,0:T(1,128)S(1)} %get-tuple-element.51.gain, ...), custom_call_target="tpu_custom_call" | custom-call | flops 1 | bytes 1 | tf_op jit(solution)/shard_map/pallas_call | solution.py:793
  91.7 3.5 %all-to-all-start = ((bf16[8,64,384]{2,1,0:T(8,128)(2,1)}), bf16[8,64,384]{2,1,0:T(8,128)(2,1)S(1)}, u32[]{:S(2)}, u32[]{:S(2)}) async-start(bf16[8,64,384]{2,1,0:T(8,128)(2,1)} %bitcast.41), calls=%async_computation | async-start | bytes 786432 | tf_op jit(solution)/shard_map/all_to_all | solution.py:199
  103.5 4.2 %all-to-all-done.refs_1_.attended = bf16[8,64,384]{2,1,0:T(8,128)(2,1)S(1)} async-done(((bf16[8,64,384]{2,1,0:T(8,128)(2,1)}), bf16[8,64,384]{2,1,0:T(8,128)(2,1)S(1)}, u32[]{:S(2)}, u32[]{:S(2)}) %all-to-all-start) | async-done | bytes 393248 | tf_op jit(solution)/shard_map/all_to_all | solution.py:199
  112.8 8.2 %collective-permute-done.14 = bf16[5,2,2,24,768]{4,3,2,0,1:T(8,128)(2,1)} collective-permute-done((bf16[5,2,2,24,768]{4,3,2,0,1:T(8,128)(2,1)}, bf16[5,2,2,24,768]{4,3,2,0,1:T(8,128)(2,1)}, u32[]{:S(2)}, u32[]{:S(2)}) %collective-permute-start.14) | collective-permute-done | bytes 737312 | tf_op jit(solution)/shard_map/ppermute | solution.py:44
  129.2 3.9 %collective-permute-done.22 = bf16[2,2,96,768]{3,2,1,0:T(8,128)(2,1)} collective-permute-done((bf16[2,2,96,768]{3,2,1,0:T(8,128)(2,1)}, bf16[2,2,96,768]{3,2,1,0:T(8,128)(2,1)}, u32[]{:S(2)}, u32[]{:S(2)}) %collective-permute-start.22) | collective-permute-done | bytes 589856 | tf_op jit(solution)/shard_map/ppermute | solution.py:44
  134.2 3.3 %collective-permute-done.24 = bf16[2,2,96,768]{3,2,1,0:T(8,128)(2,1)} collective-permute-done((bf16[2,2,96,768]{3,2,1,0:T(8,128)(2,1)}, bf16[2,2,96,768]{3,2,1,0:T(8,128)(2,1)}, u32[]{:S(2)}, u32[]{:S(2)}) %collective-permute-start.24) | collective-permute-done | bytes 589856 | tf_op jit(solution)/shard_map/ppermute | solution.py:44
  139.3 4.5 %collective-permute-done.25.other2 = bf16[16,96,768]{2,1,0:T(8,128)(2,1)S(1)} collective-permute-done((bf16[16,96,768]{2,1,0:T(8,128)(2,1)S(1)}, bf16[16,96,768]{2,1,0:T(8,128)(2,1)S(1)}, u32[]{:S(2)}, u32[]{:S(2)}) %collective-permute-start.25) | collective-permute-done | bytes 2359328 | tf_op jit(solution)/shard_map/ppermute | solution.py:39
  146.1 13.8 %shard_map.270 = (bf16[2,128,768]{2,1,0:T(8,128)(2,1)}, f32[256,768]{1,0:T(8,128)S(1)}, bf16[8,64,384]{2,1,0:T(8,128)(2,1)}, bf16[256,768]{1,0:T(8,128)(2,1)S(1)...) custom-call(bf16[5,384,768]{2,1,0:T(8,128)(2,1)} %bitcast.307, ...), custom_call_target="tpu_custom_call" | custom-call | flops 1 | bytes 1 | tf_op jit(solution)/shard_map/pallas_call | solution.py:553
  162.3 8.5 %shard_map.271 = (bf16[9,384,768]{2,1,0:T(8,128)(2,1)}, bf16[9,384,768]{2,1,0:T(8,128)(2,1)}) custom-call(bf16[256,768]{1,0:T(8,128)(2,1)S(1)} %get-tuple-element.69.placed_a, bf16[256,768]{1,0:T(8,128)(2,1)S(1)} %get-tuple-element.70.placed_n, bf16[256,3072]{1,0:T(8,128)(2,1)S(1)} %copy-done.10, bf16[256,3072]{1,0:T(8,128)(2,1)} %get-tuple-element.72.grad_pre, ...), custom_call_target="tpu_custom_call" | custom-call | flops 1 | bytes 1 | tf_op jit(solution)/shard_map/pallas_call | solution.py:629
  174.4 4.6 %all-to-all-start.1 = ((bf16[8,64,384]{2,1,0:T(8,128)(2,1)}), bf16[8,64,384]{2,1,0:T(8,128)(2,1)S(1)}, u32[]{:S(2)}, u32[]{:S(2)}) async-start(bf16[8,64,384]{2,1,0:T(8,128)(2,1)} %get-tuple-element.66), calls=%async_computation.1 | async-start | bytes 786432 | tf_op jit(solution)/shard_map/all_to_all | solution.py:199
  179.9 5.5 %add_convert_fusion = bf16[9,384,768]{2,1,0:T(8,128)(2,1)S(1)} fusion(bf16[9,384,768]{2,1,0:T(8,128)(2,1)} %collective-permute-done.26, bf16[9,384,768]{2,1,0:T(8,128)(2,1)} %get-tuple-element.74), kind=kLoop, calls=%fused_computation | loop fusion | flops 10616832 | bytes 15925248 | tf_op jit(solution)/shard_map/convert_element_type | solution.py:96
  192.9 8.8 %shard_map.272.refs_1_ = bf16[1024,576]{1,0:T(8,128)(2,1)S(1)} custom-call(bf16[1024,576]{1,0:T(8,128)(2,1)S(1)} %copy-done.13, bf16[512,384]{1,0:T(8,128)(2,1)S(1)} %bitcast.298, f32[3,1024]{1,0:T(4,128)S(1)} %get-tuple-element.67.stats, f32[1,1024]{1,0:T(1,128)S(1)} %get-tuple-element.68.ids, bf16[9,2,2,24,768]{4,3,2,1,0:T(8,128)(2,1)} %get-tuple-element.92.after1, ...), custom_call_target="tpu_custom_call" | custom-call | flops 1 | bytes 1 | tf_op jit(solution)/shard_map/pallas_call | solution.py:813
  206.3 3.6 %convolution_convert_fusion = bf16[768,576]{0,1:T(8,128)(2,1)} fusion(bf16[1024,768]{1,0:T(8,128)(2,1)} %copy-done.16, bf16[1024,576]{1,0:T(8,128)(2,1)S(1)} %shard_map.272.refs_1_), kind=kOutput, calls=%fused_computation.28 | convolution fusion | flops 906412032 | bytes 3637248 | tf_op jit(solution)/shard_map/dot_general | solution.py:980
  218.6 8.3 %collective-permute-done.28 = bf16[2,128,768]{2,1,0:T(8,128)(2,1)S(1)} collective-permute-done((bf16[2,128,768]{2,1,0:T(8,128)(2,1)S(1)}, bf16[2,128,768]{2,1,0:T(8,128)(2,1)S(1)}, u32[]{:S(2)}, u32[]{:S(2)}) %collective-permute-start.28) | collective-permute-done | bytes 393248 | tf_op jit(solution)/shard_map/ppermute | solution.py:67
  232.5 12.2 %collective-permute-done.34.refs_0_ = bf16[9,2,2,24,768]{4,3,2,1,0:T(8,128)(2,1)} collective-permute-done((bf16[9,2,2,24,768]{4,3,2,1,0:T(8,128)(2,1)S(1)}, bf16[9,2,2,24,768]{4,3,2,1,0:T(8,128)(2,1)}, u32[]{:S(2)}, u32[]{:S(2)}) %collective-permute-start.34) | collective-permute-done | bytes 1327136 | tf_op jit(solution)/shard_map/ppermute | solution.py:44
  260.2 5.7 %collective-permute-done.35 = bf16[9,2,24,768]{3,2,0,1:T(8,128)(2,1)} collective-permute-done((bf16[9,2,24,768]{3,2,0,1:T(8,128)(2,1)}, bf16[9,2,24,768]{3,2,0,1:T(8,128)(2,1)}, u32[]{:S(2)}, u32[]{:S(2)}) %collective-permute-start.35) | collective-permute-done | bytes 663584 | tf_op jit(solution)/shard_map/ppermute | solution.py:44
  286.2 7.4 %collective-permute-done.41 = bf16[9,24,768]{2,1,0:T(8,128)(2,1)S(1)} collective-permute-done((bf16[9,24,768]{2,1,0:T(8,128)(2,1)S(1)}, bf16[9,24,768]{2,1,0:T(8,128)(2,1)S(1)}, u32[]{:S(2)}, u32[]{:S(2)}) %collective-permute-start.41) | collective-permute-done | bytes 331808 | tf_op jit(solution)/shard_map/ppermute | solution.py:34
  295.7 6.9 %collective-permute-done.39.refs_0_ = bf16[2,32,1152]{2,1,0:T(8,128)(2,1)S(1)} collective-permute-done((bf16[2,32,1152]{2,1,0:T(8,128)(2,1)S(1)}, bf16[2,32,1152]{2,1,0:T(8,128)(2,1)S(1)}, u32[]{:S(2)}, u32[]{:S(2)}) %collective-permute-start.39) | collective-permute-done | bytes 147488 | tf_op jit(solution)/shard_map/ppermute | solution.py:67
  (314 shorter events, 160.6 us)
Async XLA Ops:
  15.6 23.5 %collective-permute-start.5 = (bf16[144,768]{1,0:T(8,128)(2,1)S(1)}, bf16[144,768]{1,0:T(8,128)(2,1)S(1)}, u32[]{:S(2)}, u32[]{:S(2)}) collective-permute-start(bf16[144,768]{1,0:T(8,128)(2,1)S(1)} %dynamic-slice_bitcast_fusion.8), channel_id=1, source_target_pairs={{0,4},{1,5},{2,6},{3,7},{4,0},{5,1},{6,2},{7,3},{8,12},{9,13},{10,... | collective-permute-start | bytes 663560 | tf_op jit(solution)/shard_map/ppermute | solution.py:67
  18.8 27.5 %collective-permute-start.1 = (bf16[5,24,768]{2,1,0:T(8,128)(2,1)}, bf16[5,24,768]{2,1,0:T(8,128)(2,1)S(1)}, u32[]{:S(2)}, u32[]{:S(2)}) collective-permute-start(bf16[5,24,768]{2,1,0:T(8,128)(2,1)} %shard_map.255.refs_0_.refs_1_), channel_id=1, source_target_pairs={{0,6},{1,7},{2,0},{3,1},{4,2},{5,3},{6,4},{7,5},{8,14},{9,15},{10,... | collective-permute-start | bytes 552968 | tf_op jit(solution)/shard_map/ppermute | solution.py:34
  22.7 23.7 %collective-permute-start.2 = (bf16[5,24,768]{2,1,0:T(8,128)(2,1)}, bf16[5,24,768]{2,1,0:T(8,128)(2,1)S(1)}, u32[]{:S(2)}, u32[]{:S(2)}) collective-permute-start(bf16[5,24,768]{2,1,0:T(8,128)(2,1)} %shard_map.255.refs_0_.refs_1_), channel_id=1, source_target_pairs={{0,4},{1,5},{2,6},{3,7},{4,0},{5,1},{6,2},{7,3},{8,12},{9,13},{10,... | collective-permute-start | bytes 552968 | tf_op jit(solution)/shard_map/ppermute | solution.py:34
  22.7 23.7 %collective-permute-start.3 = (bf16[5,24,768]{2,1,0:T(8,128)(2,1)}, bf16[5,24,768]{2,1,0:T(8,128)(2,1)S(1)}, u32[]{:S(2)}, u32[]{:S(2)}) collective-permute-start(bf16[5,24,768]{2,1,0:T(8,128)(2,1)} %shard_map.255.refs_0_.refs_1_), channel_id=1, source_target_pairs={{0,2},{1,3},{2,4},{3,5},{4,6},{5,7},{6,0},{7,1},{8,10},{9,11},{10,... | collective-permute-start | bytes 552968 | tf_op jit(solution)/shard_map/ppermute | solution.py:34
  62.2 33.6 %collective-permute-start.4 = (bf16[5,2,24,768]{3,2,1,0:T(8,128)(2,1)S(1)}, bf16[5,2,24,768]{3,2,1,0:T(8,128)(2,1)}, u32[]{:S(2)}, u32[]{:S(2)}) collective-permute-start(bf16[5,2,24,768]{3,2,1,0:T(8,128)(2,1)S(1)} %copy-done.5), channel_id=1, source_target_pairs={{0,8},{8,0},{16,24},{24,16},{1,9},{9,1},{17,25},{25,17},{2,10},{10... | collective-permute-start | bytes 1105928 | tf_op jit(solution)/shard_map/ppermute | solution.py:44
  63.7 35.6 %collective-permute-start.15 = (bf16[5,2,24,768]{3,2,1,0:T(8,128)(2,1)S(1)}, bf16[5,2,24,768]{3,2,1,0:T(8,128)(2,1)S(1)}, u32[]{:S(2)}, u32[]{:S(2)}) collective-permute-start(bf16[5,2,24,768]{3,2,1,0:T(8,128)(2,1)S(1)} %get-tuple-element.55), channel_id=1, source_target_pairs={{0,16},{8,24},{16,0},{24,8},{1,17},{9,25},{17,1},{25,9},{2,18},{10... | collective-permute-start | bytes 1105928 | tf_op jit(solution)/shard_map/ppermute | solution.py:44
  65.1 25.9 %collective-permute-start.18 = (bf16[96,768]{1,0:T(8,128)(2,1)}, bf16[96,768]{1,0:T(8,128)(2,1)S(1)}, u32[]{:S(2)}, u32[]{:S(2)}) collective-permute-start(bf16[96,768]{1,0:T(8,128)(2,1)} %shard_map.266.refs_0_), channel_id=1, source_target_pairs={{0,6},{1,7},{2,0},{3,1},{4,2},{5,3},{6,4},{7,5},{8,14},{9,15},{10,... | collective-permute-start | bytes 442376 | tf_op jit(solution)/shard_map/ppermute | solution.py:34
  69.8 21.2 %collective-permute-start.19 = (bf16[96,768]{1,0:T(8,128)(2,1)S(1)}, bf16[96,768]{1,0:T(8,128)(2,1)S(1)}, u32[]{:S(2)}, u32[]{:S(2)}) collective-permute-start(bf16[96,768]{1,0:T(8,128)(2,1)S(1)} %copy-done.11), channel_id=1, source_target_pairs={{0,4},{1,5},{2,6},{3,7},{4,0},{5,1},{6,2},{7,3},{8,12},{9,13},{10,... | collective-permute-start | bytes 442376 | tf_op jit(solution)/shard_map/ppermute | solution.py:34
  72.3 18.7 %collective-permute-start.20 = (bf16[96,768]{1,0:T(8,128)(2,1)S(1)}, bf16[96,768]{1,0:T(8,128)(2,1)S(1)}, u32[]{:S(2)}, u32[]{:S(2)}) collective-permute-start(bf16[96,768]{1,0:T(8,128)(2,1)S(1)} %copy-done.11), channel_id=1, source_target_pairs={{0,2},{1,3},{2,4},{3,5},{4,6},{5,7},{6,0},{7,1},{8,10},{9,11},{10,... | collective-permute-start | bytes 442376 | tf_op jit(solution)/shard_map/ppermute | solution.py:34
  97.7 23.2 %collective-permute-start.14 = (bf16[5,2,2,24,768]{4,3,2,0,1:T(8,128)(2,1)}, bf16[5,2,2,24,768]{4,3,2,0,1:T(8,128)(2,1)}, u32[]{:S(2)}, u32[]{:S(2)}) collective-permute-start(bf16[5,2,2,24,768]{4,3,2,0,1:T(8,128)(2,1)} %pad_maximum_fusion.5), channel_id=1, source_target_pairs={{0,16},{8,24},{16,0},{24,8},{1,17},{9,25},{17,1},{25,9},{2,18},{10... | collective-permute-start | bytes 2211848 | tf_op jit(solution)/shard_map/ppermute | solution.py:44
  102.0 24.7 %collective-permute-start.16 = (bf16[5,2,2,24,768]{4,3,2,1,0:T(8,128)(2,1)}, bf16[5,2,2,24,768]{4,3,2,1,0:T(8,128)(2,1)}, u32[]{:S(2)}, u32[]{:S(2)}) collective-permute-start(bf16[5,2,2,24,768]{4,3,2,1,0:T(8,128)(2,1)} %pad_maximum_fusion.6), channel_id=1, source_target_pairs={{0,8},{8,0},{16,24},{24,16},{1,9},{9,1},{17,25},{25,17},{2,10},{10... | collective-permute-start | bytes 2211848 | tf_op jit(solution)/shard_map/ppermute | solution.py:44
  110.3 22.7 %collective-permute-start.22 = (bf16[2,2,96,768]{3,2,1,0:T(8,128)(2,1)}, bf16[2,2,96,768]{3,2,1,0:T(8,128)(2,1)}, u32[]{:S(2)}, u32[]{:S(2)}) collective-permute-start(bf16[2,2,96,768]{3,2,1,0:T(8,128)(2,1)} %pad_maximum_fusion.7), channel_id=1, source_target_pairs={{0,16},{8,24},{16,0},{24,8},{1,17},{9,25},{17,1},{25,9},{2,18},{10... | collective-permute-start | bytes 1769480 | tf_op jit(solution)/shard_map/ppermute | solution.py:44
  174.4 17.1 %all-to-all-start.1 = ((bf16[8,64,384]{2,1,0:T(8,128)(2,1)}), bf16[8,64,384]{2,1,0:T(8,128)(2,1)S(1)}, u32[]{:S(2)}, u32[]{:S(2)}) async-start(bf16[8,64,384]{2,1,0:T(8,128)(2,1)} %get-tuple-element.66), calls=%async_computation.1 | async-start | bytes 786432 | tf_op jit(solution)/shard_map/all_to_all | solution.py:199
  187.5 40.3 %collective-permute-start.31 = (bf16[9,2,2,24,768]{4,3,2,1,0:T(8,128)(2,1)}, bf16[9,2,2,24,768]{4,3,2,1,0:T(8,128)(2,1)}, u32[]{:S(2)}, u32[]{:S(2)}) collective-permute-start(bf16[9,2,2,24,768]{4,3,2,1,0:T(8,128)(2,1)} %get-tuple-element.92.after1), channel_id=1, source_target_pairs={{0,16},{8,24},{16,0},{24,8},{1,17},{9,25},{17,1},{25,9},{2,18},{10... | collective-permute-start | bytes 3981320 | tf_op jit(solution)/shard_map/ppermute | solution.py:44
  212.6 32.1 %collective-permute-start.34 = (bf16[9,2,2,24,768]{4,3,2,1,0:T(8,128)(2,1)S(1)}, bf16[9,2,2,24,768]{4,3,2,1,0:T(8,128)(2,1)}, u32[]{:S(2)}, u32[]{:S(2)}) collective-permute-start(bf16[9,2,2,24,768]{4,3,2,1,0:T(8,128)(2,1)S(1)} %get-tuple-element.90.after2), channel_id=1, source_target_pairs={{0,8},{8,0},{16,24},{24,16},{1,9},{9,1},{17,25},{25,17},{2,10},{10... | collective-permute-start | bytes 3981320 | tf_op jit(solution)/shard_map/ppermute | solution.py:44
  227.7 25.8 %collective-permute-start.29 = (bf16[128,768]{1,0:T(8,128)(2,1)}, bf16[128,768]{1,0:T(8,128)(2,1)}, u32[]{:S(2)}, u32[]{:S(2)}) collective-permute-start(bf16[128,768]{1,0:T(8,128)(2,1)} %dynamic-slice_bitcast_fusion.9), channel_id=1, source_target_pairs={{0,4},{1,5},{2,6},{3,7},{4,0},{5,1},{6,2},{7,3},{8,12},{9,13},{10,... | collective-permute-start | bytes 589832 | tf_op jit(solution)/shard_map/ppermute | solution.py:67
  232.0 26.9 %collective-permute-start.33 = (bf16[9,2,24,768]{3,2,0,1:T(8,128)(2,1)}, bf16[9,2,24,768]{3,2,0,1:T(8,128)(2,1)}, u32[]{:S(2)}, u32[]{:S(2)}) collective-permute-start(bf16[9,2,24,768]{3,2,0,1:T(8,128)(2,1)} %dynamic-slice_bitcast_fusion.4), channel_id=1, source_target_pairs={{0,8},{8,0},{16,24},{24,16},{1,9},{9,1},{17,25},{25,17},{2,10},{10... | collective-permute-start | bytes 1990664 | tf_op jit(solution)/shard_map/ppermute | solution.py:44
  247.7 18.2 %collective-permute-start.35 = (bf16[9,2,24,768]{3,2,0,1:T(8,128)(2,1)}, bf16[9,2,24,768]{3,2,0,1:T(8,128)(2,1)}, u32[]{:S(2)}, u32[]{:S(2)}) collective-permute-start(bf16[9,2,24,768]{3,2,0,1:T(8,128)(2,1)} %dynamic-slice_bitcast_fusion.3), channel_id=1, source_target_pairs={{0,16},{8,24},{16,0},{24,8},{1,17},{9,25},{17,1},{25,9},{2,18},{10... | collective-permute-start | bytes 1990664 | tf_op jit(solution)/shard_map/ppermute | solution.py:44
  249.6 23.8 %collective-permute-start.32 = (bf16[2,2,32,1152]{3,2,1,0:T(8,128)(2,1)S(1)}, bf16[2,2,32,1152]{3,2,1,0:T(8,128)(2,1)}, u32[]{:S(2)}, u32[]{:S(2)}) collective-permute-start(bf16[2,2,32,1152]{3,2,1,0:T(8,128)(2,1)S(1)} %dynamic-slice_bitcast_fusion.7), channel_id=1, source_target_pairs={{0,16},{8,24},{16,0},{24,8},{1,17},{9,25},{17,1},{25,9},{2,18},{10... | collective-permute-start | bytes 884744 | tf_op jit(solution)/shard_map/ppermute | solution.py:44
  252.0 25.7 %collective-permute-start.37 = (bf16[2,2,32,1152]{3,2,1,0:T(8,128)(2,1)}, bf16[2,2,32,1152]{3,2,1,0:T(8,128)(2,1)}, u32[]{:S(2)}, u32[]{:S(2)}) collective-permute-start(bf16[2,2,32,1152]{3,2,1,0:T(8,128)(2,1)} %dynamic-slice_bitcast_fusion.6), channel_id=1, source_target_pairs={{0,8},{8,0},{16,24},{24,16},{1,9},{9,1},{17,25},{25,17},{2,10},{10... | collective-permute-start | bytes 884744 | tf_op jit(solution)/shard_map/ppermute | solution.py:44
  268.3 17.9 %collective-permute-start.40 = (bf16[9,24,768]{2,1,0:T(8,128)(2,1)}, bf16[9,24,768]{2,1,0:T(8,128)(2,1)S(1)}, u32[]{:S(2)}, u32[]{:S(2)}) collective-permute-start(bf16[9,24,768]{2,1,0:T(8,128)(2,1)} %get-tuple-element.103), channel_id=1, source_target_pairs={{0,2},{1,3},{2,4},{3,5},{4,6},{5,7},{6,0},{7,1},{8,10},{9,11},{10,... | collective-permute-start | bytes 995336 | tf_op jit(solution)/shard_map/ppermute | solution.py:34
  268.3 25.3 %collective-permute-start.41 = (bf16[9,24,768]{2,1,0:T(8,128)(2,1)S(1)}, bf16[9,24,768]{2,1,0:T(8,128)(2,1)S(1)}, u32[]{:S(2)}, u32[]{:S(2)}) collective-permute-start(bf16[9,24,768]{2,1,0:T(8,128)(2,1)S(1)} %get-tuple-element.104), channel_id=1, source_target_pairs={{0,4},{1,5},{2,6},{3,7},{4,0},{5,1},{6,2},{7,3},{8,12},{9,13},{10,... | collective-permute-start | bytes 995336 | tf_op jit(solution)/shard_map/ppermute | solution.py:34
  270.1 23.5 %collective-permute-start.42 = (bf16[9,24,768]{2,1,0:T(8,128)(2,1)S(1)}, bf16[9,24,768]{2,1,0:T(8,128)(2,1)}, u32[]{:S(2)}, u32[]{:S(2)}) collective-permute-start(bf16[9,24,768]{2,1,0:T(8,128)(2,1)S(1)} %get-tuple-element.105), channel_id=1, source_target_pairs={{0,6},{1,7},{2,0},{3,1},{4,2},{5,3},{6,4},{7,5},{8,14},{9,15},{10,... | collective-permute-start | bytes 995336 | tf_op jit(solution)/shard_map/ppermute | solution.py:34
  284.1 18.5 %collective-permute-start.39 = (bf16[2,32,1152]{2,1,0:T(8,128)(2,1)S(1)}, bf16[2,32,1152]{2,1,0:T(8,128)(2,1)S(1)}, u32[]{:S(2)}, u32[]{:S(2)}) collective-permute-start(bf16[2,32,1152]{2,1,0:T(8,128)(2,1)S(1)} %dynamic-slice_bitcast_fusion.10), channel_id=1, source_target_pairs={{0,4},{1,5},{2,6},{3,7},{4,0},{5,1},{6,2},{7,3},{8,12},{9,13},{10,... | collective-permute-start | bytes 442376 | tf_op jit(solution)/shard_map/ppermute | solution.py:67
  (68 other events, 439.5 us)

commit v5 on v4

--- a/solution.py
+++ b/solution.py
@@ -113,7 +113,7 @@
     low_got, high_got = swap_dp(low_send, 2), swap_dp(high_send, 1)
     if between is not None:
         after = between(low_send, high_send)
-        low_got, high_got = gate(low_got, after), gate(high_got, after)
+        low_got, high_got = gate_both(low_got, high_got, after)
     low = add(pick(low, y, axis), low_got)
     high = add(pick(high, x, axis + 1), high_got)
     if between is not None:
@@ -139,10 +139,11 @@
     return level, top, level // top
 
 
-def gather_sequence(blocks):
+def gather_sequence(blocks, after):
     level, top, half = z_bits()
     core = lax.axis_index("seq") % CORES
-    held = ordered(half, pick(blocks, half, 0), swap_z(pick(blocks, 1 - half, 0), top), 0)
+    got = gate(swap_z(pick(blocks, 1 - half, 0), top), after)
+    held = ordered(half, pick(blocks, half, 0), got, 0)
     axis, bit = 1, top // 2
     while bit:
         held = ordered(level // bit % 2, held, swap_z(held, bit), axis)
@@ -150,49 +151,57 @@
     return held, ordered(core, held, swap_core(held), axis).reshape(-1, *blocks.shape[1:])
 
 
-def scatter_sequence(partial):
+def scatter_sequence(partial, first, second):
     level, top, half = z_bits()
     core = lax.axis_index("seq") % CORES
     shape = partial.shape[1:]
     count = top.bit_length()
     held = partial.reshape(*[2] * (count + 1), *shape)
-    held = add(pick(held, core, count), swap_core(pick(held, 1 - core, count)))
+    got = gate(swap_core(pick(held, 1 - core, count)), first)
+    held = add(pick(held, core, count), got)
     axis, bit = count - 1, 1
     while bit < top:
         flag = level // bit % 2
-        held = add(pick(held, flag, axis), swap_z(pick(held, 1 - flag, axis), bit))
+        got = gate(swap_z(pick(held, 1 - flag, axis), bit), second)
+        held = add(pick(held, flag, axis), got)
         axis, bit = axis - 1, bit * 2
     return ordered(half, pick(held, half, 0), swap_z(pick(held, 1 - half, 0), top), 0)
 
 
+def class_of(level):
+    return level % (lax.axis_size("seq") // CORES // 2)
+
+
 def gather_columns(blocks):
-    level, top, half = z_bits()
-    shape = blocks.shape[1:]
-    count = top.bit_length() - 1
-    held = blocks.reshape(*[2] * count, *shape)
-    bit = top // 2
-    while bit:
-        flag = level // bit % 2
-        got = swap_z(pick(held, 1 - flag, 0), bit)
-        held = ordered(flag, pick(held, flag, 0), got, count - 1)
-        bit //= 2
-    return held, ordered(half, held, swap_z(held, top), 0).reshape(-1, *shape)
+    heights = lax.axis_size("seq") // CORES
+    level = lax.axis_index("seq") // CORES
+    moved = [
+        swap_z(pick(blocks, class_of(level ^ mask), 0), mask) for mask in range(1, heights)
+    ]
+    return [pick(blocks, class_of(level), 0)] + moved
 
 
 def scatter_columns(tower, after):
-    level, top, half = z_bits()
-    shape = tower.shape[1:]
-    count = top.bit_length() - 1
-    held = tower.reshape(*[2] * (count + 1), *shape)
-    got = gate(swap_z(pick(held, 1 - half, 0), top), after)
-    held = add(pick(held, half, 0), got)
-    bit = 1
-    while bit < top:
-        flag = level // bit % 2
-        got = swap_z(pick(held, 1 - flag, count - 1), bit)
-        held = ordered(flag, pick(held, flag, count - 1), got, 0)
-        bit *= 2
-    return held.reshape(-1, *shape).astype(F32)
+    heights = tower.shape[0]
+    level = lax.axis_index("seq") // CORES
+    kinds = jnp.arange(heights // 2)[:, None, None]
+    total = jnp.where(kinds == class_of(level), pick(tower, level, 0).astype(F32)[None], 0.0)
+    for mask in range(1, heights):
+        got = gate(swap_z(pick(tower, level ^ mask, 0), mask), after)
+        total += jnp.where(kinds == class_of(level ^ mask), got.astype(F32)[None], 0.0)
+    return total
+
+
+def scatter_plane_direct(split, after):
+    planes = lax.axis_size("dp")
+    if planes != 4:
+        return lax.psum_scatter(split, "dp", scatter_dimension=0, tiled=True)
+    plane = lax.axis_index("dp")
+    split = split.reshape(planes, -1, *split.shape[1:])
+    total = pick(split, plane, 0).astype(F32)
+    for mask in range(1, planes):
+        total += gate(swap_dp(pick(split, plane ^ mask, 0), mask), after).astype(F32)
+    return total.astype(split.dtype)
 
 
 def exchange(blocks):
@@ -220,9 +229,72 @@
     return (offset >= 0) & (offset < size)
 
 
-def unpack_kernel(sizes, small_ref, *outs):
-    devices = small_ref.shape[0]
-    small = small_ref[...].astype(F32)
+def line_kernel(*refs):
+    pieces, tower = refs[:-1], refs[-1]
+    level = lax.axis_index("seq") // CORES
+    for mask, piece in enumerate(pieces):
+        tower[level ^ mask] = piece[...]
+
+
+def build_line(pieces):
+    return pl.pallas_call(
+        line_kernel,
+        out_shape=jax.ShapeDtypeStruct((len(pieces), *pieces[0].shape), BF16),
+        in_specs=vmem_specs(len(pieces)),
+        out_specs=vmem_specs(1)[0],
+        cost_estimate=LIGHT,
+    )(*pieces)
+
+
+def halves_kernel(count, *refs):
+    towers, (keep, send) = refs[:count], refs[-2:]
+    heights, _, columns = towers[0].shape
+    half = columns // CORES
+    core = lax.rem(lax.axis_index("seq"), CORES)
+    plane = lax.axis_index("dp")
+    for own in range(CORES):
+
+        @pl.when(core == own)
+        def _():
+            for mask, tower in enumerate(towers):
+                base = (plane ^ mask) * heights if count > 1 else 0
+                for i in range(heights):
+                    line = tower[i]
+                    keep[base + i] = line[:, own * half : (own + 1) * half]
+                    send[base + i] = line[:, (1 - own) * half : (2 - own) * half]
+
+
+def split_halves(towers, after):
+    heights, rows, columns = towers[0].shape
+    shape = jax.ShapeDtypeStruct((len(towers) * heights, rows, columns // CORES), BF16)
+    return pl.pallas_call(
+        functools.partial(halves_kernel, len(towers)),
+        out_shape=[shape, shape],
+        in_specs=vmem_specs(len(towers)) + [ANYWHERE] * len(after),
+        out_specs=vmem_specs(2),
+        compiler_params=pltpu.CompilerParams(vmem_limit_bytes=40 * 2**20),
+        cost_estimate=LIGHT,
+    )(*towers, *after)
+
+
+def unpack_kernel(sizes, keep, got, weight, *refs):
+    outs, (lines, small) = refs[:-2], refs[-2:]
+    chips, rows = keep.shape[:2]
+    shard = rows - ROWS
+    core = lax.rem(lax.axis_index("seq"), CORES)
+    for own in range(CORES):
+
+        @pl.when(core == own)
+        def _():
+            for source, place in ((keep, own), (got, 1 - own)):
+                for chip in range(chips):
+                    device = chip * CORES + place
+                    line = source[chip].astype(F32)
+                    lines[device * shard : (device + 1) * shard, :] = line[:shard]
+                    small[device] = line[shard:, :LANES]
+
+    weight[...] = lines[...].astype(BF16)
+    devices = chips * CORES
     for i, (size, out) in enumerate(zip(sizes, outs)):
         spread = jnp.dot(
             small[:, i, :].astype(BF16),
@@ -232,16 +304,23 @@
         out[...] = jnp.sum(jnp.where(owned_lanes(devices, size), spread, 0.0), 0, keepdims=True)
 
 
-def unpack_small(small, sizes):
-    devices = small.shape[0]
+def unpack_first(keep, got, sizes):
+    chips, rows, columns = keep.shape
+    devices = chips * CORES
+    width = devices * (rows - ROWS)
     return pl.pallas_call(
         functools.partial(unpack_kernel, sizes),
-        out_shape=[jax.ShapeDtypeStruct((1, devices * size), F32) for size in sizes],
-        in_specs=vmem_specs(1),
-        out_specs=vmem_specs(len(sizes)),
-        compiler_params=pltpu.CompilerParams(vmem_limit_bytes=32 * 2**20),
+        out_shape=[jax.ShapeDtypeStruct((width, columns), BF16)]
+        + [jax.ShapeDtypeStruct((1, devices * size), F32) for size in sizes],
+        in_specs=vmem_specs(2),
+        out_specs=vmem_specs(1 + len(sizes)),
+        scratch_shapes=[
+            pltpu.VMEM((width, columns), F32),
+            pltpu.VMEM((devices, ROWS, LANES), F32),
+        ],
+        compiler_params=pltpu.CompilerParams(vmem_limit_bytes=40 * 2**20),
         cost_estimate=LIGHT,
-    )(small)
+    )(keep, got)
 
 
 def pack_kernel(sizes, *refs):
@@ -282,6 +361,20 @@
         input_output_aliases={0: 0},
         cost_estimate=LIGHT,
     )(value, *after)
+
+
+def gate_both(one, two, *after):
+    def kernel(*refs):
+        pass
+
+    return pl.pallas_call(
+        kernel,
+        out_shape=[jax.ShapeDtypeStruct(value.shape, value.dtype) for value in (one, two)],
+        in_specs=[ANYWHERE] * (2 + len(after)),
+        out_specs=[ANYWHERE] * 2,
+        input_output_aliases={0: 0, 1: 1},
+        cost_estimate=LIGHT,
+    )(one, two, *after)
 
 
 def first_kernel(group, weight, rows, marks, *refs):
@@ -871,20 +964,17 @@
         classes,
         group,
     )
-    lines, sequence = gather_sequence(blocks)
-    early_a, tower_a = gather_columns(columns)
-    stacked = stack_weights(w_out.reshape(-1, width), w_fc.reshape(-1, parts * width), early_a)
-    low1, high1 = build_tower(z_pieces(stacked), 1, [])
-    tower_a = gate(tower_a, stacked)
-    heights = tower_a.shape[0]
-    half_a = gather_plane(tower_a[: heights // 2], tower_a[heights // 2 :], 0, None, low1)
-    left, right = half_a[..., : 3 * group], half_a[..., 3 * group :]
-    mine_a = jnp.where(core == 0, left, right)
-    whole_a = ordered(core, mine_a, swap_core(jnp.where(core == 0, right, left)), 1)
-    whole_a = whole_a.reshape(devices, shard_rows + ROWS, 3 * group)
-    wqkv = whole_a[:, :shard_rows].reshape(width, 3 * group)
-    gain1, bias1, bqv, bout, gain2, bias2, bfc, bproj = unpack_small(
-        whole_a[:, shard_rows:, :LANES], sizes
+    tower_a = build_line(gather_columns(columns))
+    lines, sequence = gather_sequence(blocks, tower_a)
+    stacked = stack_weights(w_out.reshape(-1, width), w_fc.reshape(-1, parts * width), columns)
+    low1, high1 = build_tower(z_pieces(stacked), 1, [tower_a])
+    if lax.axis_size("dp") == 4:
+        towers = [tower_a] + [swap_dp(tower_a, mask) for mask in range(1, 4)]
+    else:
+        towers = [lax.all_gather(tower_a, "dp", axis=0, tiled=True)]
+    keep_a, send_a = split_halves(towers, [low1, lines])
+    wqkv, gain1, bias1, bqv, bout, gain2, bias2, bfc, bproj = unpack_first(
+        keep_a, swap_core(send_a), sizes
     )
 
     raw, stats, qkv, normed1, ids = attend_forward(
@@ -969,11 +1059,14 @@
     grad_normed1 = lax.dot_general(
         grad_qkv, wqkv, (((1,), (1,)), ((), ())), preferred_element_type=F32
     )
-    own_normed1 = scatter_sequence(grad_normed1.astype(BF16).reshape(count, block, width))
+    own_normed1 = scatter_sequence(
+        grad_normed1.astype(BF16).reshape(count, block, width), first_sums, tower_b
+    )
     _, norm1_back = jax.vjp(lambda value: norm_affine(value, gain1, bias1), rows)
     (grad_in_part,) = norm1_back(own_normed1.astype(F32).reshape(tokens, width))
     grad_inputs = (grad_middle + grad_in_part).astype(BF16).reshape(inputs.shape)
 
+    grad_qkv = gate(grad_qkv, first_sums)
     long_rows = sequence[:, :block].astype(F32).reshape(count * block, width)
     _, norm1_long_back = jax.vjp(lambda g, b: norm_affine(long_rows, g, b), gain1, bias1)
     grad_gain1, grad_bias1 = norm1_long_back(grad_normed1)
@@ -1004,8 +1097,7 @@
     pair_a = jnp.concatenate(
         [jnp.where(core == 0, keep_a, got_a), jnp.where(core == 0, got_a, keep_a)], -1
     )
-    pair_a = gate(pair_a, first_sums)
-    tower_a = scatter_plane(pair_a, 0, lambda *_: tower_b)
+    tower_a = scatter_plane_direct(pair_a, tower_b)
     own_a = scatter_columns(tower_a, own_b)
     own_small = jnp.sum(
         own_a[:, shard_rows:].reshape(classes, ROWS, CORES, 3 * group)[..., :LANES], (0, 2)

time: 318 us -> 315 us (level)
  other arithmetic: 57.4 us -> 50.2 us
  Pallas kernels: 48 us -> 51.2 us
    ppermute x20 -> x18, waiting for transfers between devices: 47.4 us -> 36.7 us  [swap_dp(): return lax.ppermute(value, 'dp', [(i, i ^ bit) for i in range(size)])]
    ppermute x8 -> x10, starting transfers between devices: 9.74 us -> 18.6 us  [swap_z(): lax.ppermute(value, 'seq', [(i, i ^ CORES * bit) for i in range(size)])]
    another operation x31 -> x19, other arithmetic: 24.5 us -> 16.1 us  [ordered(): return jnp.stack([first, second], axis)]
    ppermute x9, waiting for transfers between devices: 7.43 us -> 12 us  [shift_z(): lax.ppermute(value, 'seq', [(i, (i + CORES * step) % size) for i in range...]
    convert_element_type x1 -> x4, other arithmetic: 0.02 us -> 3.95 us  [the longest x3 2.75 us: scatter_columns(): got.astype(F32)[None]]
    ppermute x8 -> x10, waiting for transfers between devices: 30.6 us -> 34.4 us  [swap_z(): lax.ppermute(value, 'seq', [(i, i ^ CORES * bit) for i in range(size)])]
    pallas_call x1 -> x4, Pallas kernels: 0.75 us -> 4 us  [the longest x1 1.75 us: build_line(): pl.pallas_call(line_kernel, out_shape=jax.ShapeDtypeStruct((len(pieces),...]
    convert_element_type x12 -> x7, other arithmetic: 17.7 us -> 14.5 us  [add(): return (mine.astype(F32) + other.astype(F32)).astype(mine.dtype)]
  transfers between devices with their start and end apart: 46 -> 46, of which waited for: 22 -> 16; matrix products, arithmetic and copies ran while one was open for 27% -> 23% of each run, Pallas kernels for 8% -> 9%
where the time goes in v5:
time: 315 us; the launch traced here: 310 us
  waiting for transfers between devices  95.4 us (30%)
  starting transfers between devices  60.2 us (19%)
  Pallas kernels  51.2 us (16%)
  other arithmetic  50.2 us (16%)
  local copies, waits for them, and re-layouts  45.6 us (14%)
  matrix products  5.2 us (2%)
    ppermute x18, waiting for transfers between devices, swap_dp(): return lax.ppermute(value, 'dp', [(i, i ^ bit) for i in range(size)])  36.7 us
    ppermute x10, waiting for transfers between devices, swap_z(): lax.ppermute(value, 'seq', [(i, i ^ CORES * bit) for i in range(size)])  34.4 us
    ppermute x18, starting transfers between devices, swap_dp(): return lax.ppermute(value, 'dp', [(i, i ^ bit) for i in range(size)])  20.7 us
    ppermute x10, starting transfers between devices, swap_z(): lax.ppermute(value, 'seq', [(i, i ^ CORES * bit) for i in range(size)])  18.6 us
    unnamed x120, local copies, waits for them, and re-layouts  16.9 us
    another operation x19, other arithmetic, ordered(): return jnp.stack([first, second], axis)  16.1 us
    convert_element_type x7, other arithmetic, add(): return (mine.astype(F32) + other.astype(F32)).astype(mine.dtype)  14.5 us
    pallas_call x1, Pallas kernels, middle_block(): pl.pallas_call(functools.partial(middle_kernel, groups), out_shape=[shape...  13.8 us
  transfers between devices with their start and end apart: 46, of which 16 were waited for; matrix products, arithmetic and copies ran while one was open for 23% of the time, Pallas kernels for 9%

profile of v5, /device:TPU:0, one launch (start us, length us, event | category | flops | bytes accessed | tf_op | source)
XLA Modules:
  0.0 309.6 jit_solution(581274217720231259)
XLA Ops:
  5.4 4.1 %collective-permute-start.7 = (bf16[144,768]{1,0:T(8,128)(2,1)S(1)}, bf16[144,768]{1,0:T(8,128)(2,1)S(1)}, u32[]{:S(2)}, u32[]{:S(2)}) collective-permute-start(bf16[144,768]{1,0:T(8,128)(2,1)S(1)} %dynamic-slice_bitcast_fusion.9), channel_id=1, source_target_pairs={{0,4},{1,5},{2,6},{3,7},{4,0},{5,1},{6,2},{7,3},{8,12},{9,13},{10,... | collective-permute-start | bytes 663560 | tf_op jit(solution)/shard_map/ppermute | solution.py:67
  16.9 8.2 %collective-permute-done.4.refs_2_ = bf16[32,1152]{1,0:T(8,128)(2,1)S(1)} collective-permute-done((bf16[32,1152]{1,0:T(8,128)(2,1)S(1)}, bf16[32,1152]{1,0:T(8,128)(2,1)S(1)}, u32[]{:S(2)}, u32[]{:S(2)}) %collective-permute-start.4) | collective-permute-done | bytes 73760 | tf_op jit(solution)/shard_map/ppermute | solution.py:67
  33.9 3.4 %collective-permute-start = (bf16[5,24,768]{2,1,0:T(8,128)(2,1)}, bf16[5,24,768]{2,1,0:T(8,128)(2,1)S(1)}, u32[]{:S(2)}, u32[]{:S(2)}) collective-permute-start(bf16[5,24,768]{2,1,0:T(8,128)(2,1)} %shard_map.255.refs_0_), channel_id=1, source_target_pairs={{0,6},{1,7},{2,0},{3,1},{4,2},{5,3},{6,4},{7,5},{8,14},{9,15},{10,... | collective-permute-start | bytes 552968 | tf_op jit(solution)/shard_map/ppermute | solution.py:34
  40.3 6.0 %collective-permute-done.8 = bf16[2,144,768]{2,1,0:T(8,128)(2,1)S(1)} collective-permute-done((bf16[2,144,768]{2,1,0:T(8,128)(2,1)S(1)}, bf16[2,144,768]{2,1,0:T(8,128)(2,1)S(1)}, u32[]{:S(2)}, u32[]{:S(2)}) %collective-permute-start.8) | collective-permute-done | bytes 442400 | tf_op jit(solution)/shard_map/ppermute | solution.py:67
  52.8 7.8 %collective-permute-done.2.refs_3_ = bf16[5,24,768]{2,1,0:T(8,128)(2,1)S(1)} collective-permute-done((bf16[5,24,768]{2,1,0:T(8,128)(2,1)S(1)}, bf16[5,24,768]{2,1,0:T(8,128)(2,1)S(1)}, u32[]{:S(2)}, u32[]{:S(2)}) %collective-permute-start.2) | collective-permute-done | bytes 184352 | tf_op jit(solution)/shard_map/ppermute | solution.py:34
  72.5 11.3 %shard_map.261 = (bf16[512,384]{1,0:T(8,128)(2,1)}, f32[3,1024]{1,0:T(4,128)S(1)}, bf16[1024,576]{1,0:T(8,128)(2,1)S(1)}, bf16[1024,768]{1,0:T(8,128)(2,1)S(1)}, f32[1,1024]{1,0:T(1,128)S(1)}) custom-call(bf16[8,144,768]{2,1,0:T(8,128)(2,1)} %bitcast.243, bf16[768,576]{1,0:T(8,128)(2,1)S(1)} %get-tuple-element.58.weight, ...), custom_call_target="tpu_custom_call" | custom-call | flops 1 | bytes 1 | tf_op jit(solution)/shard_map/pallas_call | solution.py:886
  85.8 4.5 %all-to-all-start = ((bf16[8,64,384]{2,1,0:T(8,128)(2,1)}), bf16[8,64,384]{2,1,0:T(8,128)(2,1)S(1)}, u32[]{:S(2)}, u32[]{:S(2)}) async-start(bf16[8,64,384]{2,1,0:T(8,128)(2,1)} %bitcast.24), calls=%async_computation | async-start | bytes 786432 | tf_op jit(solution)/shard_map/all_to_all | solution.py:208
  98.5 4.3 %all-to-all-done.refs_1_.attended = bf16[8,64,384]{2,1,0:T(8,128)(2,1)S(1)} async-done(((bf16[8,64,384]{2,1,0:T(8,128)(2,1)}), bf16[8,64,384]{2,1,0:T(8,128)(2,1)S(1)}, u32[]{:S(2)}, u32[]{:S(2)}) %all-to-all-start) | async-done | bytes 393248 | tf_op jit(solution)/shard_map/all_to_all | solution.py:208
  110.0 6.0 %collective-permute-done.14 = bf16[5,2,2,24,768]{4,3,2,0,1:T(8,128)(2,1)} collective-permute-done((bf16[5,2,2,24,768]{4,3,2,0,1:T(8,128)(2,1)}, bf16[5,2,2,24,768]{4,3,2,0,1:T(8,128)(2,1)}, u32[]{:S(2)}, u32[]{:S(2)}) %collective-permute-start.14) | collective-permute-done | bytes 737312 | tf_op jit(solution)/shard_map/ppermute | solution.py:44
  129.4 3.5 %collective-permute-done.24 = bf16[2,2,96,768]{3,2,1,0:T(8,128)(2,1)} collective-permute-done((bf16[2,2,96,768]{3,2,1,0:T(8,128)(2,1)}, bf16[2,2,96,768]{3,2,1,0:T(8,128)(2,1)}, u32[]{:S(2)}, u32[]{:S(2)}) %collective-permute-start.24) | collective-permute-done | bytes 589856 | tf_op jit(solution)/shard_map/ppermute | solution.py:44
  134.6 4.5 %collective-permute-done.25.other2 = bf16[16,96,768]{2,1,0:T(8,128)(2,1)S(1)} collective-permute-done((bf16[16,96,768]{2,1,0:T(8,128)(2,1)S(1)}, bf16[16,96,768]{2,1,0:T(8,128)(2,1)S(1)}, u32[]{:S(2)}, u32[]{:S(2)}) %collective-permute-start.25) | collective-permute-done | bytes 2359328 | tf_op jit(solution)/shard_map/ppermute | solution.py:39
  141.4 13.8 %shard_map.270 = (bf16[2,128,768]{2,1,0:T(8,128)(2,1)}, f32[256,768]{1,0:T(8,128)S(1)}, bf16[8,64,384]{2,1,0:T(8,128)(2,1)}, bf16[256,768]{1,0:T(8,128)(2,1)S(1)...) custom-call(bf16[5,384,768]{2,1,0:T(8,128)(2,1)} %bitcast.249, ...), custom_call_target="tpu_custom_call" | custom-call | flops 1 | bytes 1 | tf_op jit(solution)/shard_map/pallas_call | solution.py:646
  157.5 8.5 %shard_map.271 = (bf16[9,384,768]{2,1,0:T(8,128)(2,1)}, bf16[9,384,768]{2,1,0:T(8,128)(2,1)}) custom-call(bf16[256,768]{1,0:T(8,128)(2,1)S(1)} %get-tuple-element.77.placed_a, bf16[256,768]{1,0:T(8,128)(2,1)S(1)} %get-tuple-element.78.placed_n, bf16[256,3072]{1,0:T(8,128)(2,1)S(1)} %copy-done.7, bf16[256,3072]{1,0:T(8,128)(2,1)} %get-tuple-element.80.grad_pre, ...), custom_call_target="tpu_custom_call" | custom-call | flops 1 | bytes 1 | tf_op jit(solution)/shard_map/pallas_call | solution.py:722
  167.2 4.4 %all-to-all-start.1 = ((bf16[8,64,384]{2,1,0:T(8,128)(2,1)}), bf16[8,64,384]{2,1,0:T(8,128)(2,1)S(1)}, u32[]{:S(2)}, u32[]{:S(2)}) async-start(bf16[8,64,384]{2,1,0:T(8,128)(2,1)} %get-tuple-element.74), calls=%async_computation.1 | async-start | bytes 786432 | tf_op jit(solution)/shard_map/all_to_all | solution.py:208
  171.6 3.6 %collective-permute-done.26 = bf16[9,384,768]{2,1,0:T(8,128)(2,1)} collective-permute-done((bf16[9,384,768]{2,1,0:T(8,128)(2,1)}, bf16[9,384,768]{2,1,0:T(8,128)(2,1)}, u32[]{:S(2)}, u32[]{:S(2)}) %collective-permute-start.26) | collective-permute-done | bytes 5308448 | tf_op jit(solution)/shard_map/ppermute | solution.py:39
  175.2 5.5 %add_convert_fusion = bf16[9,384,768]{2,1,0:T(8,128)(2,1)S(1)} fusion(bf16[9,384,768]{2,1,0:T(8,128)(2,1)} %collective-permute-done.26, bf16[9,384,768]{2,1,0:T(8,128)(2,1)} %get-tuple-element.82), kind=kLoop, calls=%fused_computation | loop fusion | flops 10616832 | bytes 15925248 | tf_op jit(solution)/shard_map/convert_element_type | solution.py:96
  189.1 8.8 %shard_map.272.refs_2_.refs_0_ = bf16[1024,576]{1,0:T(8,128)(2,1)S(1)} custom-call(bf16[1024,576]{1,0:T(8,128)(2,1)S(1)} %get-tuple-element.73.whole, bf16[512,384]{1,0:T(8,128)(2,1)S(1)} %bitcast.242, f32[3,1024]{1,0:T(4,128)S(1)} %get-tuple-element.75.stats, f32[1,1024]{1,0:T(1,128)S(1)} %get-tuple-element.76.ids, ...), custom_call_target="tpu_custom_call" | custom-call | flops 1 | bytes 1 | tf_op jit(solution)/shard_map/pallas_call | solution.py:906
  201.0 13.0 %collective-permute-done.29.refs_1_ = bf16[9,2,2,24,768]{4,3,2,1,0:T(8,128)(2,1)} collective-permute-done((bf16[9,2,2,24,768]{4,3,2,1,0:T(8,128)(2,1)S(1)}, bf16[9,2,2,24,768]{4,3,2,1,0:T(8,128)(2,1)}, u32[]{:S(2)}, u32[]{:S(2)}) %collective-permute-start.29) | collective-permute-done | bytes 1327136 | tf_op jit(solution)/shard_map/ppermute | solution.py:44
  214.0 3.2 %collective-permute-done.28.refs_0_ = bf16[9,2,2,24,768]{4,3,2,1,0:T(8,128)(2,1)} collective-permute-done((bf16[9,2,2,24,768]{4,3,2,1,0:T(8,128)(2,1)}, bf16[9,2,2,24,768]{4,3,2,1,0:T(8,128)(2,1)}, u32[]{:S(2)}, u32[]{:S(2)}) %collective-permute-start.28) | collective-permute-done | bytes 1327136 | tf_op jit(solution)/shard_map/ppermute | solution.py:44
  224.7 3.4 %convolution_convert_fusion = bf16[768,576]{0,1:T(8,128)(2,1)} fusion(bf16[1024,768]{1,0:T(8,128)(2,1)S(1)} %copy-done.15, bf16[1024,576]{1,0:T(8,128)(2,1)} %shard_map.276), kind=kOutput, calls=%fused_computation.28 | convolution fusion | flops 906412032 | bytes 3637248 | tf_op jit(solution)/shard_map/dot_general | solution.py:1073
  242.8 7.9 %collective-permute-done.32 = bf16[9,2,24,768]{3,2,0,1:T(8,128)(2,1)} collective-permute-done((bf16[9,2,24,768]{3,2,0,1:T(8,128)(2,1)}, bf16[9,2,24,768]{3,2,0,1:T(8,128)(2,1)}, u32[]{:S(2)}, u32[]{:S(2)}) %collective-permute-start.32) | collective-permute-done | bytes 663584 | tf_op jit(solution)/shard_map/ppermute | solution.py:44
  264.0 15.4 %collective-permute-done.33 = bf16[128,768]{1,0:T(8,128)(2,1)S(1)} collective-permute-done((bf16[128,768]{1,0:T(8,128)(2,1)S(1)}, bf16[128,768]{1,0:T(8,128)(2,1)S(1)}, u32[]{:S(2)}, u32[]{:S(2)}) %collective-permute-start.33) | collective-permute-done | bytes 196640 | tf_op jit(solution)/shard_map/ppermute | solution.py:67
  289.3 4.2 %collective-permute-done.40 = bf16[9,24,768]{2,1,0:T(8,128)(2,1)} collective-permute-done((bf16[9,24,768]{2,1,0:T(8,128)(2,1)}, bf16[9,24,768]{2,1,0:T(8,128)(2,1)}, u32[]{:S(2)}, u32[]{:S(2)}) %collective-permute-start.40) | collective-permute-done | bytes 331808 | tf_op jit(solution)/shard_map/ppermute | solution.py:34
  296.4 3.3 %collective-permute-done.42.refs_0_ = bf16[32,1152]{1,0:T(8,128)(2,1)S(1)} collective-permute-done((bf16[32,1152]{1,0:T(8,128)(2,1)S(1)}, bf16[32,1152]{1,0:T(8,128)(2,1)S(1)}, u32[]{:S(2)}, u32[]{:S(2)}) %collective-permute-start.42) | collective-permute-done | bytes 73760 | tf_op jit(solution)/shard_map/ppermute | solution.py:67
  (325 shorter events, 149.3 us)
Async XLA Ops:
  5.4 22.2 %collective-permute-start.7 = (bf16[144,768]{1,0:T(8,128)(2,1)S(1)}, bf16[144,768]{1,0:T(8,128)(2,1)S(1)}, u32[]{:S(2)}, u32[]{:S(2)}) collective-permute-start(bf16[144,768]{1,0:T(8,128)(2,1)S(1)} %dynamic-slice_bitcast_fusion.9), channel_id=1, source_target_pairs={{0,4},{1,5},{2,6},{3,7},{4,0},{5,1},{6,2},{7,3},{8,12},{9,13},{10,... | collective-permute-start | bytes 663560 | tf_op jit(solution)/shard_map/ppermute | solution.py:67
  29.3 17.1 %collective-permute-start.8 = (bf16[2,144,768]{2,1,0:T(8,128)(2,1)S(1)}, bf16[2,144,768]{2,1,0:T(8,128)(2,1)S(1)}, u32[]{:S(2)}, u32[]{:S(2)}) collective-permute-start(bf16[2,144,768]{2,1,0:T(8,128)(2,1)S(1)} %pad_maximum_fusion.8), channel_id=1, source_target_pairs={{0,2},{1,3},{2,0},{3,1},{4,6},{5,7},{6,4},{7,5},{8,10},{9,11},{10,... | collective-permute-start | bytes 1327112 | tf_op jit(solution)/shard_map/ppermute | solution.py:67
  37.2 23.4 %collective-permute-start.10 = (bf16[4,32,1152]{2,1,0:T(8,128)(2,1)S(1)}, bf16[4,32,1152]{2,1,0:T(8,128)(2,1)S(1)}, u32[]{:S(2)}, u32[]{:S(2)}) collective-permute-start(bf16[4,32,1152]{2,1,0:T(8,128)(2,1)S(1)} %copy-done.5), channel_id=1, source_target_pairs={{0,8},{8,0},{16,24},{24,16},{1,9},{9,1},{17,25},{25,17},{2,10},{10... | collective-permute-start | bytes 884744 | tf_op jit(solution)/shard_map/ppermute | solution.py:44
  38.8 21.9 %collective-permute-start.11 = (bf16[4,32,1152]{2,1,0:T(8,128)(2,1)S(1)}, bf16[4,32,1152]{2,1,0:T(8,128)(2,1)S(1)}, u32[]{:S(2)}, u32[]{:S(2)}) collective-permute-start(bf16[4,32,1152]{2,1,0:T(8,128)(2,1)S(1)} %copy-done.5), channel_id=1, source_target_pairs={{0,16},{8,24},{16,0},{24,8},{1,17},{9,25},{17,1},{25,9},{2,18},{10... | collective-permute-start | bytes 884744 | tf_op jit(solution)/shard_map/ppermute | solution.py:44
  49.1 19.7 %collective-permute-start.9 = (bf16[2,2,144,768]{3,2,1,0:T(8,128)(2,1)S(1)}, bf16[2,2,144,768]{3,2,1,0:T(8,128)(2,1)}, u32[]{:S(2)}, u32[]{:S(2)}) collective-permute-start(bf16[2,2,144,768]{3,2,1,0:T(8,128)(2,1)S(1)} %pad_maximum_fusion.3.refs_5_.refs_1_), channel_id=1, source_target_pairs={{0,1},{1,0},{2,3},{3,2},{4,5},{5,4},{6,7},{7,6},{8,9},{9,8},{10,11... | collective-permute-start | bytes 2654216 | tf_op jit(solution)/shard_map/ppermute | solution.py:39
  63.6 27.8 %collective-permute-start.6 = (bf16[5,2,24,768]{3,2,1,0:T(8,128)(2,1)S(1)}, bf16[5,2,24,768]{3,2,1,0:T(8,128)(2,1)}, u32[]{:S(2)}, u32[]{:S(2)}) collective-permute-start(bf16[5,2,24,768]{3,2,1,0:T(8,128)(2,1)S(1)} %get-tuple-element.54.refs_4_.after), channel_id=1, source_target_pairs={{0,8},{8,0},{16,24},{24,16},{1,9},{9,1},{17,25},{25,17},{2,10},{10... | collective-permute-start | bytes 1105928 | tf_op jit(solution)/shard_map/ppermute | solution.py:44
  64.2 30.8 %collective-permute-start.15 = (bf16[5,2,24,768]{3,2,1,0:T(8,128)(2,1)S(1)}, bf16[5,2,24,768]{3,2,1,0:T(8,128)(2,1)}, u32[]{:S(2)}, u32[]{:S(2)}) collective-permute-start(bf16[5,2,24,768]{3,2,1,0:T(8,128)(2,1)S(1)} %get-tuple-element.63), channel_id=1, source_target_pairs={{0,16},{8,24},{16,0},{24,8},{1,17},{9,25},{17,1},{25,9},{2,18},{10... | collective-permute-start | bytes 1105928 | tf_op jit(solution)/shard_map/ppermute | solution.py:44
  64.7 20.4 %collective-permute-start.18 = (bf16[96,768]{1,0:T(8,128)(2,1)}, bf16[96,768]{1,0:T(8,128)(2,1)S(1)}, u32[]{:S(2)}, u32[]{:S(2)}) collective-permute-start(bf16[96,768]{1,0:T(8,128)(2,1)} %shard_map.266.refs_0_), channel_id=1, source_target_pairs={{0,6},{1,7},{2,0},{3,1},{4,2},{5,3},{6,4},{7,5},{8,14},{9,15},{10,... | collective-permute-start | bytes 442376 | tf_op jit(solution)/shard_map/ppermute | solution.py:34
  67.7 17.3 %collective-permute-start.19 = (bf16[96,768]{1,0:T(8,128)(2,1)}, bf16[96,768]{1,0:T(8,128)(2,1)S(1)}, u32[]{:S(2)}, u32[]{:S(2)}) collective-permute-start(bf16[96,768]{1,0:T(8,128)(2,1)} %shard_map.266.refs_0_), channel_id=1, source_target_pairs={{0,4},{1,5},{2,6},{3,7},{4,0},{5,1},{6,2},{7,3},{8,12},{9,13},{10,... | collective-permute-start | bytes 442376 | tf_op jit(solution)/shard_map/ppermute | solution.py:34
  90.2 17.1 %collective-permute-start.23 = (bf16[2,96,768]{2,1,0:T(8,128)(2,1)S(1)}, bf16[2,96,768]{2,1,0:T(8,128)(2,1)}, u32[]{:S(2)}, u32[]{:S(2)}) collective-permute-start(bf16[2,96,768]{2,1,0:T(8,128)(2,1)S(1)} %get-tuple-element.65), channel_id=1, source_target_pairs={{0,16},{8,24},{16,0},{24,8},{1,17},{9,25},{17,1},{25,9},{2,18},{10... | collective-permute-start | bytes 884744 | tf_op jit(solution)/shard_map/ppermute | solution.py:44
  94.2 21.8 %collective-permute-start.14 = (bf16[5,2,2,24,768]{4,3,2,0,1:T(8,128)(2,1)}, bf16[5,2,2,24,768]{4,3,2,0,1:T(8,128)(2,1)}, u32[]{:S(2)}, u32[]{:S(2)}) collective-permute-start(bf16[5,2,2,24,768]{4,3,2,0,1:T(8,128)(2,1)} %pad_maximum_fusion.4), channel_id=1, source_target_pairs={{0,16},{8,24},{16,0},{24,8},{1,17},{9,25},{17,1},{25,9},{2,18},{10... | collective-permute-start | bytes 2211848 | tf_op jit(solution)/shard_map/ppermute | solution.py:44
  97.0 24.6 %collective-permute-start.16 = (bf16[5,2,2,24,768]{4,3,2,1,0:T(8,128)(2,1)}, bf16[5,2,2,24,768]{4,3,2,1,0:T(8,128)(2,1)}, u32[]{:S(2)}, u32[]{:S(2)}) collective-permute-start(bf16[5,2,2,24,768]{4,3,2,1,0:T(8,128)(2,1)} %pad_maximum_fusion.5), channel_id=1, source_target_pairs={{0,8},{8,0},{16,24},{24,16},{1,9},{9,1},{17,25},{25,17},{2,10},{10... | collective-permute-start | bytes 2211848 | tf_op jit(solution)/shard_map/ppermute | solution.py:44
  106.2 22.0 %collective-permute-start.22 = (bf16[2,2,96,768]{3,2,1,0:T(8,128)(2,1)}, bf16[2,2,96,768]{3,2,1,0:T(8,128)(2,1)}, u32[]{:S(2)}, u32[]{:S(2)}) collective-permute-start(bf16[2,2,96,768]{3,2,1,0:T(8,128)(2,1)} %pad_maximum_fusion.6), channel_id=1, source_target_pairs={{0,16},{8,24},{16,0},{24,8},{1,17},{9,25},{17,1},{25,9},{2,18},{10... | collective-permute-start | bytes 1769480 | tf_op jit(solution)/shard_map/ppermute | solution.py:44
  167.2 21.9 %all-to-all-start.1 = ((bf16[8,64,384]{2,1,0:T(8,128)(2,1)}), bf16[8,64,384]{2,1,0:T(8,128)(2,1)S(1)}, u32[]{:S(2)}, u32[]{:S(2)}) async-start(bf16[8,64,384]{2,1,0:T(8,128)(2,1)} %get-tuple-element.74), calls=%async_computation.1 | async-start | bytes 786432 | tf_op jit(solution)/shard_map/all_to_all | solution.py:208
  182.7 31.3 %collective-permute-start.29 = (bf16[9,2,2,24,768]{4,3,2,1,0:T(8,128)(2,1)S(1)}, bf16[9,2,2,24,768]{4,3,2,1,0:T(8,128)(2,1)}, u32[]{:S(2)}, u32[]{:S(2)}) collective-permute-start(bf16[9,2,2,24,768]{4,3,2,1,0:T(8,128)(2,1)S(1)} %get-tuple-element.100.after2), channel_id=1, source_target_pairs={{0,8},{8,0},{16,24},{24,16},{1,9},{9,1},{17,25},{25,17},{2,10},{10... | collective-permute-start | bytes 3981320 | tf_op jit(solution)/shard_map/ppermute | solution.py:44
  185.9 31.2 %collective-permute-start.28 = (bf16[9,2,2,24,768]{4,3,2,1,0:T(8,128)(2,1)}, bf16[9,2,2,24,768]{4,3,2,1,0:T(8,128)(2,1)}, u32[]{:S(2)}, u32[]{:S(2)}) collective-permute-start(bf16[9,2,2,24,768]{4,3,2,1,0:T(8,128)(2,1)} %get-tuple-element.102.after1), channel_id=1, source_target_pairs={{0,16},{8,24},{16,0},{24,8},{1,17},{9,25},{17,1},{25,9},{2,18},{10... | collective-permute-start | bytes 3981320 | tf_op jit(solution)/shard_map/ppermute | solution.py:44
  201.0 33.9 %collective-permute-start.27 = (bf16[2,2,128,768]{3,2,1,0:T(8,128)(2,1)}, bf16[2,2,128,768]{3,2,1,0:T(8,128)(2,1)}, u32[]{:S(2)}, u32[]{:S(2)}) collective-permute-start(bf16[2,2,128,768]{3,2,1,0:T(8,128)(2,1)} %get-tuple-element.107), channel_id=1, source_target_pairs={{0,1},{1,0},{2,3},{3,2},{4,5},{5,4},{6,7},{7,6},{8,9},{9,8},{10,11... | collective-permute-start | bytes 2359304 | tf_op jit(solution)/shard_map/ppermute | solution.py:39
  221.4 20.2 %collective-permute-start.31 = (bf16[9,2,24,768]{3,2,0,1:T(8,128)(2,1)}, bf16[9,2,24,768]{3,2,0,1:T(8,128)(2,1)}, u32[]{:S(2)}, u32[]{:S(2)}) collective-permute-start(bf16[9,2,24,768]{3,2,0,1:T(8,128)(2,1)} %dynamic-slice_bitcast_fusion.4), channel_id=1, source_target_pairs={{0,8},{8,0},{16,24},{24,16},{1,9},{9,1},{17,25},{25,17},{2,10},{10... | collective-permute-start | bytes 1990664 | tf_op jit(solution)/shard_map/ppermute | solution.py:44
  233.7 17.0 %collective-permute-start.32 = (bf16[9,2,24,768]{3,2,0,1:T(8,128)(2,1)}, bf16[9,2,24,768]{3,2,0,1:T(8,128)(2,1)}, u32[]{:S(2)}, u32[]{:S(2)}) collective-permute-start(bf16[9,2,24,768]{3,2,0,1:T(8,128)(2,1)} %dynamic-slice_bitcast_fusion.3), channel_id=1, source_target_pairs={{0,16},{8,24},{16,0},{24,8},{1,17},{9,25},{17,1},{25,9},{2,18},{10... | collective-permute-start | bytes 1990664 | tf_op jit(solution)/shard_map/ppermute | solution.py:44
  254.7 24.7 %collective-permute-start.33 = (bf16[128,768]{1,0:T(8,128)(2,1)S(1)}, bf16[128,768]{1,0:T(8,128)(2,1)S(1)}, u32[]{:S(2)}, u32[]{:S(2)}) collective-permute-start(bf16[128,768]{1,0:T(8,128)(2,1)S(1)} %dynamic-slice_bitcast_fusion.10), channel_id=1, source_target_pairs={{0,4},{1,5},{2,6},{3,7},{4,0},{5,1},{6,2},{7,3},{8,12},{9,13},{10,... | collective-permute-start | bytes 589832 | tf_op jit(solution)/shard_map/ppermute | solution.py:67
  257.8 23.5 %collective-permute-start.35 = (bf16[4,32,1152]{2,1,0:T(8,128)(2,1)S(1)}, bf16[4,32,1152]{2,1,0:T(8,128)(2,1)}, u32[]{:S(2)}, u32[]{:S(2)}) collective-permute-start(bf16[4,32,1152]{2,1,0:T(8,128)(2,1)S(1)} %get-tuple-element.116), channel_id=1, source_target_pairs={{0,8},{8,0},{16,24},{24,16},{1,9},{9,1},{17,25},{25,17},{2,10},{10... | collective-permute-start | bytes 884744 | tf_op jit(solution)/shard_map/ppermute | solution.py:44
  259.3 22.0 %collective-permute-start.36 = (bf16[4,32,1152]{2,1,0:T(8,128)(2,1)}, bf16[4,32,1152]{2,1,0:T(8,128)(2,1)S(1)}, u32[]{:S(2)}, u32[]{:S(2)}) collective-permute-start(bf16[4,32,1152]{2,1,0:T(8,128)(2,1)} %get-tuple-element.118), channel_id=1, source_target_pairs={{0,16},{8,24},{16,0},{24,8},{1,17},{9,25},{17,1},{25,9},{2,18},{10... | collective-permute-start | bytes 884744 | tf_op jit(solution)/shard_map/ppermute | solution.py:44
  259.8 22.2 %collective-permute-start.37 = (bf16[4,32,1152]{2,1,0:T(8,128)(2,1)}, bf16[4,32,1152]{2,1,0:T(8,128)(2,1)S(1)}, u32[]{:S(2)}, u32[]{:S(2)}) collective-permute-start(bf16[4,32,1152]{2,1,0:T(8,128)(2,1)} %get-tuple-element.117), channel_id=1, source_target_pairs={{0,24},{8,16},{16,8},{24,0},{1,25},{9,17},{17,9},{25,1},{2,26},{10... | collective-permute-start | bytes 884744 | tf_op jit(solution)/shard_map/ppermute | solution.py:44
  262.5 26.8 %collective-permute-start.39 = (bf16[9,24,768]{2,1,0:T(8,128)(2,1)}, bf16[9,24,768]{2,1,0:T(8,128)(2,1)}, u32[]{:S(2)}, u32[]{:S(2)}) collective-permute-start(bf16[9,24,768]{2,1,0:T(8,128)(2,1)} %get-tuple-element.113), channel_id=1, source_target_pairs={{0,2},{1,3},{2,4},{3,5},{4,6},{5,7},{6,0},{7,1},{8,10},{9,11},{10,... | collective-permute-start | bytes 995336 | tf_op jit(solution)/shard_map/ppermute | solution.py:34
  (83 other events, 577.9 us)

commit v6 on v5

--- a/solution.py
+++ b/solution.py
@@ -67,24 +67,23 @@
     return lax.ppermute(value, "seq", [(i, i ^ (CORES * bit)) for i in range(size)])
 
 
-def gather_plane(low, high, axis, first=None, second=None):
-    def move(value, bit, after):
-        moved = swap_dp(value, bit)
-        return moved if after is None else gate(moved, after)
-
-    if lax.axis_size("dp") == 4:
-        plane = lax.axis_index("dp")
-        y, x = plane // 2, plane % 2
-        low_x = ordered(x, low, move(low, 1, first), axis)
-        high_y = ordered(y, high, move(high, 2, first), axis)
-        low_all = ordered(y, low_x, move(low_x, 2, second), axis)
-        high_all = ordered(x, high_y, move(high_y, 1, second), axis + 1)
-        half = jnp.concatenate([low_all, high_all], axis + 2)
-        count = 4 * half.shape[axis + 2]
-    else:
-        tower = jnp.concatenate([low, high], axis)
-        half = lax.all_gather(tower, "dp", axis=axis, tiled=True)
-        return half
+def gather_plane(low, high, axis, between, after):
+    if lax.axis_size("dp") != 4:
+        between(low)
+        return lax.all_gather(jnp.concatenate([low, high], axis), "dp", axis=axis, tiled=True)
+    plane = lax.axis_index("dp")
+    y, x = plane // 2, plane % 2
+    low_got, high_got = swap_dp(low, 1), swap_dp(high, 2)
+    if after is not None:
+        low_got, high_got = gate_both(low_got, high_got, after)
+    low_x = ordered(x, low, low_got, axis)
+    high_y = ordered(y, high, high_got, axis)
+    second = between(low_x, high_y)
+    low_got, high_got = gate_both(swap_dp(low_x, 2), swap_dp(high_y, 1), second)
+    low_all = ordered(y, low_x, low_got, axis)
+    high_all = ordered(x, high_y, high_got, axis + 1)
+    half = jnp.concatenate([low_all, high_all], axis + 2)
+    count = 4 * half.shape[axis + 2]
     return half.reshape(*low.shape[:axis], count, *low.shape[axis + 1 :])
 
 
@@ -151,7 +150,7 @@
     return held, ordered(core, held, swap_core(held), axis).reshape(-1, *blocks.shape[1:])
 
 
-def scatter_sequence(partial, first, second):
+def scatter_sequence(partial, first, second, third):
     level, top, half = z_bits()
     core = lax.axis_index("seq") % CORES
     shape = partial.shape[1:]
@@ -165,7 +164,8 @@
         got = gate(swap_z(pick(held, 1 - flag, axis), bit), second)
         held = add(pick(held, flag, axis), got)
         axis, bit = axis - 1, bit * 2
-    return ordered(half, pick(held, half, 0), swap_z(pick(held, 1 - half, 0), top), 0)
+    got = gate(swap_z(pick(held, 1 - half, 0), top), third)
+    return ordered(half, pick(held, half, 0), got, 0)
 
 
 def class_of(level):
@@ -181,15 +181,11 @@
     return [pick(blocks, class_of(level), 0)] + moved
 
 
-def scatter_columns(tower, after):
+def scatter_columns(tower):
     heights = tower.shape[0]
     level = lax.axis_index("seq") // CORES
-    kinds = jnp.arange(heights // 2)[:, None, None]
-    total = jnp.where(kinds == class_of(level), pick(tower, level, 0).astype(F32)[None], 0.0)
-    for mask in range(1, heights):
-        got = gate(swap_z(pick(tower, level ^ mask, 0), mask), after)
-        total += jnp.where(kinds == class_of(level ^ mask), got.astype(F32)[None], 0.0)
-    return total
+    moved = [swap_z(pick(tower, level ^ mask, 0), mask) for mask in range(1, heights)]
+    return [pick(tower, level, 0)] + moved
 
 
 def scatter_plane_direct(split, after):
@@ -275,6 +271,43 @@
         compiler_params=pltpu.CompilerParams(vmem_limit_bytes=40 * 2**20),
         cost_estimate=LIGHT,
     )(*towers, *after)
+
+
+def finish_kernel(count, group, *refs):
+    pieces, (weight, small) = refs[:count], refs[-2:]
+    shard, width = weight.shape[0], weight.shape[1] // 3
+    heights = count
+    level = lax.axis_index("seq") // CORES
+    terms = [piece[...].astype(F32) for piece in pieces]
+    small_sum = jnp.zeros((ROWS, LANES), F32)
+    for kind in range(heights // 2):
+        total = jnp.zeros_like(terms[0])
+        for mask, term in enumerate(terms):
+            total += jnp.where(lax.rem(level ^ mask, heights // 2) == kind, term, 0.0)
+        for core in range(CORES):
+            start = core * 3 * group
+            small_sum += total[shard:, start : start + LANES]
+            lo = (kind * CORES + core) * group
+            for part in range(3 if lo < width else 0):
+                at = start + part * group
+                weight[:, part * width + lo : part * width + lo + group] = total[
+                    :shard, at : at + group
+                ]
+    small[...] = small_sum
+
+
+def finish_columns(pieces, width, group, after):
+    rows = pieces[0].shape[0]
+    return pl.pallas_call(
+        functools.partial(finish_kernel, len(pieces), group),
+        out_shape=[
+            jax.ShapeDtypeStruct((rows - ROWS, 3 * width), F32),
+            jax.ShapeDtypeStruct((ROWS, LANES), F32),
+        ],
+        in_specs=vmem_specs(len(pieces)) + [ANYWHERE],
+        out_specs=vmem_specs(2),
+        cost_estimate=LIGHT,
+    )(*pieces, after)
 
 
 def unpack_kernel(sizes, keep, got, weight, *refs):
@@ -965,9 +998,9 @@
         group,
     )
     tower_a = build_line(gather_columns(columns))
-    lines, sequence = gather_sequence(blocks, tower_a)
     stacked = stack_weights(w_out.reshape(-1, width), w_fc.reshape(-1, parts * width), columns)
     low1, high1 = build_tower(z_pieces(stacked), 1, [tower_a])
+    lines, sequence = gather_sequence(gate(blocks, tower_a), low1)
     if lax.axis_size("dp") == 4:
         towers = [tower_a] + [swap_dp(tower_a, mask) for mask in range(1, 4)]
     else:
@@ -977,14 +1010,20 @@
         keep_a, swap_core(send_a), sizes
     )
 
-    raw, stats, qkv, normed1, ids = attend_forward(
-        sequence, wqkv, gain1, bias1, bqv, low1, seq_count, heads, head_size, block
-    )
+    steps = []
+
+    def attend(*after):
+        raw, *rest = attend_forward(
+            sequence, wqkv, gain1, bias1, bqv, after[0], seq_count, heads, head_size, block
+        )
+        steps.extend([raw, exchange(raw.reshape(count, block // 2, 2 * group)), rest])
+        return steps[1]
+
+    half1 = gather_plane(low1, high1, 1, attend, None).reshape(1 + parts, -1, width)
+    raw, attended, (stats, qkv, normed1, ids) = steps
     pieces2 = z_pieces(gate(w_proj.reshape(-1, width), lines))
     low2, high2 = build_tower(pieces2, 0, [raw])
-    attended = exchange(raw.reshape(count, block // 2, 2 * group))
-    half1 = gather_plane(low1, high1, 1, raw, attended).reshape(1 + parts, -1, width)
-    half2 = gather_plane(low2, high2, 0, attended)
+    half2 = gather_plane(low2, high2, 0, lambda *_: attended, attended)
     other1 = swap_core(half1)
     other2 = swap_core(half2)
     aligned = half2.shape[1] % 16 == 0
@@ -1041,7 +1080,7 @@
 
     def between(*after):
         if steps:
-            steps.append(after[0])
+            steps.append(after)
         else:
             steps.append(
                 attend_backward(qkv, grad_blocks, stats, ids, after, heads, head_size, block)
@@ -1060,13 +1099,13 @@
         grad_qkv, wqkv, (((1,), (1,)), ((), ())), preferred_element_type=F32
     )
     own_normed1 = scatter_sequence(
-        grad_normed1.astype(BF16).reshape(count, block, width), first_sums, tower_b
+        grad_normed1.astype(BF16).reshape(count, block, width), first_sums[0], tower_b, own_b
     )
     _, norm1_back = jax.vjp(lambda value: norm_affine(value, gain1, bias1), rows)
     (grad_in_part,) = norm1_back(own_normed1.astype(F32).reshape(tokens, width))
     grad_inputs = (grad_middle + grad_in_part).astype(BF16).reshape(inputs.shape)
 
-    grad_qkv = gate(grad_qkv, first_sums)
+    grad_qkv = gate(grad_qkv, *first_sums)
     long_rows = sequence[:, :block].astype(F32).reshape(count * block, width)
     _, norm1_long_back = jax.vjp(lambda g, b: norm_affine(long_rows, g, b), gain1, bias1)
     grad_gain1, grad_bias1 = norm1_long_back(grad_normed1)
@@ -1098,14 +1137,9 @@
         [jnp.where(core == 0, keep_a, got_a), jnp.where(core == 0, got_a, keep_a)], -1
     )
     tower_a = scatter_plane_direct(pair_a, tower_b)
-    own_a = scatter_columns(tower_a, own_b)
-    own_small = jnp.sum(
-        own_a[:, shard_rows:].reshape(classes, ROWS, CORES, 3 * group)[..., :LANES], (0, 2)
-    )
+    own_qkv, own_small = finish_columns(scatter_columns(tower_a), width, group, own_b)
     own = [own_small[i, :size] for i, size in enumerate(sizes)]
-    own_qkv = own_a[:, :shard_rows].reshape(classes, shard_rows, CORES, 3, group)
-    own_qkv = own_qkv.transpose(1, 3, 0, 2, 4).reshape(shard_rows, 3, groups * heads, head_size)
-    own_qkv = own_qkv[:, :, :HEADS].reshape(-1)
+    own_qkv = own_qkv.reshape(-1)
     return (
         outputs,
         grad_inputs,

time: 315 us -> 353 us (1.12)
  waiting for transfers between devices: 95.4 us -> 117 us
  starting transfers between devices: 60.2 us -> 74.4 us
  local copies, waits for them, and re-layouts: 45.6 us -> 50.7 us
  other arithmetic: 50.2 us -> 46.5 us
    ppermute x9, waiting for transfers between devices: 12 us -> 40.6 us  [shift_z(): lax.ppermute(value, 'seq', [(i, (i + CORES * step) % size) for i in range...]
    ppermute x10, waiting for transfers between devices: 34.4 us -> 15.7 us  [swap_z(): lax.ppermute(value, 'seq', [(i, i ^ CORES * bit) for i in range(size)])]
    ppermute x10, starting transfers between devices: 18.6 us -> 36.3 us  [swap_z(): lax.ppermute(value, 'seq', [(i, i ^ CORES * bit) for i in range(size)])]
    ppermute x18, waiting for transfers between devices: 36.7 us -> 50.9 us  [swap_dp(): return lax.ppermute(value, 'dp', [(i, i ^ bit) for i in range(size)])]
    all_to_all x2, waiting for transfers between devices: 4.26 us -> 0.01 us  [exchange(): lax.all_to_all(blocks, 'seq', split_axis=0, concat_axis=0, tiled=True)]
    unnamed x120 -> x136, local copies, waits for them, and re-layouts: 16.9 us -> 15.2 us
    squeeze x8 -> x9, local copies, waits for them, and re-layouts: 6.79 us -> 8.13 us  [pick(): return lax.dynamic_index_in_dim(value, index, axis, keepdims=False)]
  transfers between devices with their start and end apart: 46 -> 46, of which waited for: 16 -> 20; matrix products, arithmetic and copies ran while one was open for 23% -> 20% of each run, Pallas kernels for 9% -> 8%
where the time goes in v6:
time: 353 us; the launch traced here: 348 us
  waiting for transfers between devices  117 us (33%)
  starting transfers between devices  74.4 us (21%)
  Pallas kernels  53.3 us (15%)
  local copies, waits for them, and re-layouts  50.7 us (14%)
  other arithmetic  46.5 us (13%)
  matrix products  4.25 us (1%)
    ppermute x18, waiting for transfers between devices, swap_dp(): return lax.ppermute(value, 'dp', [(i, i ^ bit) for i in range(size)])  50.9 us
    ppermute x9, waiting for transfers between devices, shift_z(): lax.ppermute(value, 'seq', [(i, (i + CORES * step) % size) for i in range...  40.6 us
    ppermute x10, starting transfers between devices, swap_z(): lax.ppermute(value, 'seq', [(i, i ^ CORES * bit) for i in range(size)])  36.3 us
    ppermute x18, starting transfers between devices, swap_dp(): return lax.ppermute(value, 'dp', [(i, i ^ bit) for i in range(size)])  19.3 us
    ppermute x10, waiting for transfers between devices, swap_z(): lax.ppermute(value, 'seq', [(i, i ^ CORES * bit) for i in range(size)])  15.7 us
    another operation x19, other arithmetic, ordered(): return jnp.stack([first, second], axis)  15.7 us
    unnamed x136, local copies, waits for them, and re-layouts  15.2 us
    convert_element_type x7, other arithmetic, add(): return (mine.astype(F32) + other.astype(F32)).astype(mine.dtype)  14.3 us
  transfers between devices with their start and end apart: 46, of which 20 were waited for; matrix products, arithmetic and copies ran while one was open for 20% of the time, Pallas kernels for 8%

profile of v6, /device:TPU:0, one launch (start us, length us, event | category | flops | bytes accessed | tf_op | source)
XLA Modules:
  0.0 347.8 jit_solution(12842110742373580961)
XLA Ops:
  11.7 5.2 %collective-permute-done.4.refs_2_ = bf16[32,1152]{1,0:T(8,128)(2,1)S(1)} collective-permute-done((bf16[32,1152]{1,0:T(8,128)(2,1)S(1)}, bf16[32,1152]{1,0:T(8,128)(2,1)S(1)}, u32[]{:S(2)}, u32[]{:S(2)}) %collective-permute-start.4) | collective-permute-done | bytes 73760 | tf_op jit(solution)/shard_map/ppermute | solution.py:67
  29.4 5.8 %collective-permute-done.refs_1_ = bf16[5,24,768]{2,1,0:T(8,128)(2,1)S(1)} collective-permute-done((bf16[5,24,768]{2,1,0:T(8,128)(2,1)}, bf16[5,24,768]{2,1,0:T(8,128)(2,1)S(1)}, u32[]{:S(2)}, u32[]{:S(2)}) %collective-permute-start) | collective-permute-done | bytes 184352 | tf_op jit(solution)/shard_map/ppermute | solution.py:34
  35.2 13.1 %collective-permute-done.1.refs_2_ = bf16[5,24,768]{2,1,0:T(8,128)(2,1)S(1)} collective-permute-done((bf16[5,24,768]{2,1,0:T(8,128)(2,1)}, bf16[5,24,768]{2,1,0:T(8,128)(2,1)S(1)}, u32[]{:S(2)}, u32[]{:S(2)}) %collective-permute-start.1) | collective-permute-done | bytes 184352 | tf_op jit(solution)/shard_map/ppermute | solution.py:34
  55.5 7.9 %collective-permute-done.11 = bf16[2,144,768]{2,1,0:T(8,128)(2,1)S(1)} collective-permute-done((bf16[2,144,768]{2,1,0:T(8,128)(2,1)S(1)}, bf16[2,144,768]{2,1,0:T(8,128)(2,1)S(1)}, u32[]{:S(2)}, u32[]{:S(2)}) %collective-permute-start.11) | collective-permute-done | bytes 442400 | tf_op jit(solution)/shard_map/ppermute | solution.py:67
  70.5 4.2 %collective-permute-done.6 = bf16[5,2,24,768]{3,2,1,0:T(8,128)(2,1)} collective-permute-done((bf16[5,2,24,768]{3,2,1,0:T(8,128)(2,1)S(1)}, bf16[5,2,24,768]{3,2,1,0:T(8,128)(2,1)}, u32[]{:S(2)}, u32[]{:S(2)}) %collective-permute-start.6) | collective-permute-done | bytes 368672 | tf_op jit(solution)/shard_map/ppermute | solution.py:44
  84.2 11.3 %shard_map.262 = (bf16[512,384]{1,0:T(8,128)(2,1)}, f32[3,1024]{1,0:T(4,128)S(1)}, bf16[1024,576]{1,0:T(8,128)(2,1)S(1)}, bf16[1024,768]{1,0:T(8,128)(2,1)S(1)}, f32[1,1024]{1,0:T(1,128)S(1)}) custom-call(bf16[8,144,768]{2,1,0:T(8,128)(2,1)} %bitcast.241, bf16[768,576]{1,0:T(8,128)(2,1)S(1)} %get-tuple-element.67.weight, ...), custom_call_target="tpu_custom_call" | custom-call | flops 1 | bytes 1 | tf_op jit(solution)/shard_map/pallas_call | solution.py:919
  96.7 3.5 all-to-all-start
  101.0 3.7 %collective-permute-start.18 = (bf16[96,768]{1,0:T(8,128)(2,1)}, bf16[96,768]{1,0:T(8,128)(2,1)S(1)}, u32[]{:S(2)}, u32[]{:S(2)}) collective-permute-start(bf16[96,768]{1,0:T(8,128)(2,1)} %shard_map.264.refs_0_), channel_id=1, source_target_pairs={{0,6},{1,7},{2,0},{3,1},{4,2},{5,3},{6,4},{7,5},{8,14},{9,15},{10,... | collective-permute-start | bytes 442376 | tf_op jit(solution)/shard_map/ppermute | solution.py:34
  105.8 6.3 %collective-permute-done.18.refs_1_ = bf16[96,768]{1,0:T(8,128)(2,1)S(1)} collective-permute-done((bf16[96,768]{1,0:T(8,128)(2,1)}, bf16[96,768]{1,0:T(8,128)(2,1)S(1)}, u32[]{:S(2)}, u32[]{:S(2)}) %collective-permute-start.18) | collective-permute-done | bytes 147488 | tf_op jit(solution)/shard_map/ppermute | solution.py:34
  112.1 13.2 %collective-permute-done.19.refs_2_ = bf16[96,768]{1,0:T(8,128)(2,1)S(1)} collective-permute-done((bf16[96,768]{1,0:T(8,128)(2,1)}, bf16[96,768]{1,0:T(8,128)(2,1)S(1)}, u32[]{:S(2)}, u32[]{:S(2)}) %collective-permute-start.19) | collective-permute-done | bytes 147488 | tf_op jit(solution)/shard_map/ppermute | solution.py:34
  133.0 3.3 collective-permute-done.21.refs_0_
  142.8 9.4 %collective-permute-done.9.refs_1_ = bf16[5,2,2,24,768]{4,3,2,1,0:T(8,128)(2,1)} collective-permute-done((bf16[5,2,2,24,768]{4,3,2,1,0:T(8,128)(2,1)}, bf16[5,2,2,24,768]{4,3,2,1,0:T(8,128)(2,1)}, u32[]{:S(2)}, u32[]{:S(2)}) %collective-permute-start.9) | collective-permute-done | bytes 737312 | tf_op jit(solution)/shard_map/ppermute | solution.py:44
  157.3 6.1 %collective-permute-done.24.refs_1_ = bf16[2,2,96,768]{3,2,1,0:T(8,128)(2,1)} collective-permute-done((bf16[2,2,96,768]{3,2,1,0:T(8,128)(2,1)}, bf16[2,2,96,768]{3,2,1,0:T(8,128)(2,1)}, u32[]{:S(2)}, u32[]{:S(2)}) %collective-permute-start.24) | collective-permute-done | bytes 589856 | tf_op jit(solution)/shard_map/ppermute | solution.py:44
  166.4 4.5 %collective-permute-done.25.other2 = bf16[16,96,768]{2,1,0:T(8,128)(2,1)S(1)} collective-permute-done((bf16[16,96,768]{2,1,0:T(8,128)(2,1)S(1)}, bf16[16,96,768]{2,1,0:T(8,128)(2,1)S(1)}, u32[]{:S(2)}, u32[]{:S(2)}) %collective-permute-start.25) | collective-permute-done | bytes 2359328 | tf_op jit(solution)/shard_map/ppermute | solution.py:39
  172.3 13.8 %shard_map.268 = (bf16[2,128,768]{2,1,0:T(8,128)(2,1)}, f32[256,768]{1,0:T(8,128)S(1)}, bf16[8,64,384]{2,1,0:T(8,128)(2,1)}, bf16[256,768]{1,0:T(8,128)(2,1)S(1)...) custom-call(bf16[5,384,768]{2,1,0:T(8,128)(2,1)} %bitcast.33.half1, ...), custom_call_target="tpu_custom_call" | custom-call | flops 1 | bytes 1 | tf_op jit(solution)/shard_map/pallas_call | solution.py:679
  188.4 8.5 %shard_map.269 = (bf16[9,384,768]{2,1,0:T(8,128)(2,1)}, bf16[9,384,768]{2,1,0:T(8,128)(2,1)}) custom-call(bf16[256,768]{1,0:T(8,128)(2,1)S(1)} %get-tuple-element.91.placed_a, bf16[256,768]{1,0:T(8,128)(2,1)S(1)} %get-tuple-element.92.placed_n, bf16[256,3072]{1,0:T(8,128)(2,1)S(1)} %copy-done.9, bf16[256,3072]{1,0:T(8,128)(2,1)} %get-tuple-element.94.grad_pre, ...), custom_call_target="tpu_custom_call" | custom-call | flops 1 | bytes 1 | tf_op jit(solution)/shard_map/pallas_call | solution.py:755
  197.5 3.5 all-to-all-start.1
  201.0 5.0 %collective-permute-done.26 = bf16[9,384,768]{2,1,0:T(8,128)(2,1)} collective-permute-done((bf16[9,384,768]{2,1,0:T(8,128)(2,1)}, bf16[9,384,768]{2,1,0:T(8,128)(2,1)}, u32[]{:S(2)}, u32[]{:S(2)}) %collective-permute-start.26) | collective-permute-done | bytes 5308448 | tf_op jit(solution)/shard_map/ppermute | solution.py:39
  206.0 5.5 %add_convert_fusion = bf16[9,384,768]{2,1,0:T(8,128)(2,1)S(1)} fusion(bf16[9,384,768]{2,1,0:T(8,128)(2,1)} %collective-permute-done.26, bf16[9,384,768]{2,1,0:T(8,128)(2,1)} %get-tuple-element.96), kind=kLoop, calls=%fused_computation | loop fusion | flops 10616832 | bytes 15925248 | tf_op jit(solution)/shard_map/convert_element_type | solution.py:95
  219.9 8.8 %shard_map.270.refs_2_.refs_0_ = bf16[1024,576]{1,0:T(8,128)(2,1)S(1)} custom-call(bf16[1024,576]{1,0:T(8,128)(2,1)S(1)} %get-tuple-element.87.whole, bf16[512,384]{1,0:T(8,128)(2,1)S(1)} %bitcast.240, f32[3,1024]{1,0:T(4,128)S(1)} %get-tuple-element.89.stats, f32[1,1024]{1,0:T(1,128)S(1)} %get-tuple-element.90.ids, ...), custom_call_target="tpu_custom_call" | custom-call | flops 1 | bytes 1 | tf_op jit(solution)/shard_map/pallas_call | solution.py:939
  231.8 13.0 %collective-permute-done.29.refs_1_ = bf16[9,2,2,24,768]{4,3,2,1,0:T(8,128)(2,1)} collective-permute-done((bf16[9,2,2,24,768]{4,3,2,1,0:T(8,128)(2,1)S(1)}, bf16[9,2,2,24,768]{4,3,2,1,0:T(8,128)(2,1)}, u32[]{:S(2)}, u32[]{:S(2)}) %collective-permute-start.29) | collective-permute-done | bytes 1327136 | tf_op jit(solution)/shard_map/ppermute | solution.py:44
  275.7 7.7 %collective-permute-done.31 = bf16[9,2,24,768]{3,2,0,1:T(8,128)(2,1)} collective-permute-done((bf16[9,2,24,768]{3,2,0,1:T(8,128)(2,1)}, bf16[9,2,24,768]{3,2,0,1:T(8,128)(2,1)}, u32[]{:S(2)}, u32[]{:S(2)}) %collective-permute-start.31) | collective-permute-done | bytes 663584 | tf_op jit(solution)/shard_map/ppermute | solution.py:44
  302.1 18.0 %collective-permute-start.42 = (bf16[32,1152]{1,0:T(8,128)(2,1)S(1)}, bf16[32,1152]{1,0:T(8,128)(2,1)S(1)}, u32[]{:S(2)}, u32[]{:S(2)}) collective-permute-start(bf16[32,1152]{1,0:T(8,128)(2,1)S(1)} %get-tuple-element.156), channel_id=1, source_target_pairs={{0,4},{1,5},{2,6},{3,7},{4,0},{5,1},{6,2},{7,3},{8,12},{9,13},{10,... | collective-permute-start | bytes 221192 | tf_op jit(solution)/shard_map/ppermute | solution.py:67
  320.1 9.6 %collective-permute-start.43 = (bf16[32,1152]{1,0:T(8,128)(2,1)S(1)}, bf16[32,1152]{1,0:T(8,128)(2,1)S(1)}, u32[]{:S(2)}, u32[]{:S(2)}) collective-permute-start(bf16[32,1152]{1,0:T(8,128)(2,1)S(1)} %get-tuple-element.155), channel_id=1, source_target_pairs={{0,6},{1,7},{2,4},{3,5},{4,2},{5,3},{6,0},{7,1},{8,14},{9,15},{10,... | collective-permute-start | bytes 221192 | tf_op jit(solution)/shard_map/ppermute | solution.py:67
  (328 shorter events, 155.1 us)
Async XLA Ops:
  21.4 28.7 %collective-permute-start.10 = (bf16[144,768]{1,0:T(8,128)(2,1)S(1)}, bf16[144,768]{1,0:T(8,128)(2,1)S(1)}, u32[]{:S(2)}, u32[]{:S(2)}) collective-permute-start(bf16[144,768]{1,0:T(8,128)(2,1)S(1)} %dynamic-slice_bitcast_fusion.9), channel_id=1, source_target_pairs={{0,4},{1,5},{2,6},{3,7},{4,0},{5,1},{6,2},{7,3},{8,12},{9,13},{10,... | collective-permute-start | bytes 663560 | tf_op jit(solution)/shard_map/ppermute | solution.py:67
  27.9 20.4 %collective-permute-start.1 = (bf16[5,24,768]{2,1,0:T(8,128)(2,1)}, bf16[5,24,768]{2,1,0:T(8,128)(2,1)S(1)}, u32[]{:S(2)}, u32[]{:S(2)}) collective-permute-start(bf16[5,24,768]{2,1,0:T(8,128)(2,1)} %shard_map.255.refs_0_), channel_id=1, source_target_pairs={{0,4},{1,5},{2,6},{3,7},{4,0},{5,1},{6,2},{7,3},{8,12},{9,13},{10,... | collective-permute-start | bytes 552968 | tf_op jit(solution)/shard_map/ppermute | solution.py:34
  28.7 19.6 %collective-permute-start.2 = (bf16[5,24,768]{2,1,0:T(8,128)(2,1)}, bf16[5,24,768]{2,1,0:T(8,128)(2,1)S(1)}, u32[]{:S(2)}, u32[]{:S(2)}) collective-permute-start(bf16[5,24,768]{2,1,0:T(8,128)(2,1)} %shard_map.255.refs_0_), channel_id=1, source_target_pairs={{0,2},{1,3},{2,4},{3,5},{4,6},{5,7},{6,0},{7,1},{8,10},{9,11},{10,... | collective-permute-start | bytes 552968 | tf_op jit(solution)/shard_map/ppermute | solution.py:34
  69.0 59.4 %collective-permute-start.8 = (bf16[5,2,24,768]{3,2,1,0:T(8,128)(2,1)S(1)}, bf16[5,2,24,768]{3,2,1,0:T(8,128)(2,1)}, u32[]{:S(2)}, u32[]{:S(2)}) collective-permute-start(bf16[5,2,24,768]{3,2,1,0:T(8,128)(2,1)S(1)} %get-tuple-element.63), channel_id=1, source_target_pairs={{0,16},{8,24},{16,0},{24,8},{1,17},{9,25},{17,1},{25,9},{2,18},{10... | collective-permute-start | bytes 1105928 | tf_op jit(solution)/shard_map/ppermute | solution.py:44
  78.1 52.8 %collective-permute-start.7 = (bf16[5,2,2,24,768]{4,3,2,0,1:T(8,128)(2,1)}, bf16[5,2,2,24,768]{4,3,2,0,1:T(8,128)(2,1)}, u32[]{:S(2)}, u32[]{:S(2)}) collective-permute-start(bf16[5,2,2,24,768]{4,3,2,0,1:T(8,128)(2,1)} %pad_maximum_fusion.4), channel_id=1, source_target_pairs={{0,16},{8,24},{16,0},{24,8},{1,17},{9,25},{17,1},{25,9},{2,18},{10... | collective-permute-start | bytes 2211848 | tf_op jit(solution)/shard_map/ppermute | solution.py:44
  96.7 40.3 %all-to-all-start = ((bf16[8,64,384]{2,1,0:T(8,128)(2,1)}), bf16[8,64,384]{2,1,0:T(8,128)(2,1)S(1)}, u32[]{:S(2)}, u32[]{:S(2)}) async-start(bf16[8,64,384]{2,1,0:T(8,128)(2,1)} %bitcast.27), calls=%async_computation | async-start | bytes 786432 | tf_op jit(solution)/shard_map/all_to_all | solution.py:204
  104.7 20.6 %collective-permute-start.19 = (bf16[96,768]{1,0:T(8,128)(2,1)}, bf16[96,768]{1,0:T(8,128)(2,1)S(1)}, u32[]{:S(2)}, u32[]{:S(2)}) collective-permute-start(bf16[96,768]{1,0:T(8,128)(2,1)} %shard_map.264.refs_0_), channel_id=1, source_target_pairs={{0,4},{1,5},{2,6},{3,7},{4,0},{5,1},{6,2},{7,3},{8,12},{9,13},{10,... | collective-permute-start | bytes 442376 | tf_op jit(solution)/shard_map/ppermute | solution.py:34
  104.7 20.6 %collective-permute-start.20 = (bf16[96,768]{1,0:T(8,128)(2,1)}, bf16[96,768]{1,0:T(8,128)(2,1)S(1)}, u32[]{:S(2)}, u32[]{:S(2)}) collective-permute-start(bf16[96,768]{1,0:T(8,128)(2,1)} %shard_map.264.refs_0_), channel_id=1, source_target_pairs={{0,2},{1,3},{2,4},{3,5},{4,6},{5,7},{6,0},{7,1},{8,10},{9,11},{10,... | collective-permute-start | bytes 442376 | tf_op jit(solution)/shard_map/ppermute | solution.py:34
  130.4 21.8 %collective-permute-start.9 = (bf16[5,2,2,24,768]{4,3,2,1,0:T(8,128)(2,1)}, bf16[5,2,2,24,768]{4,3,2,1,0:T(8,128)(2,1)}, u32[]{:S(2)}, u32[]{:S(2)}) collective-permute-start(bf16[5,2,2,24,768]{4,3,2,1,0:T(8,128)(2,1)} %pad_maximum_fusion.5), channel_id=1, source_target_pairs={{0,8},{8,0},{16,24},{24,16},{1,9},{9,1},{17,25},{25,17},{2,10},{10... | collective-permute-start | bytes 2211848 | tf_op jit(solution)/shard_map/ppermute | solution.py:44
  139.8 23.6 %collective-permute-start.24 = (bf16[2,2,96,768]{3,2,1,0:T(8,128)(2,1)}, bf16[2,2,96,768]{3,2,1,0:T(8,128)(2,1)}, u32[]{:S(2)}, u32[]{:S(2)}) collective-permute-start(bf16[2,2,96,768]{3,2,1,0:T(8,128)(2,1)} %pad_maximum_fusion.7), channel_id=1, source_target_pairs={{0,8},{8,0},{16,24},{24,16},{1,9},{9,1},{17,25},{25,17},{2,10},{10... | collective-permute-start | bytes 1769480 | tf_op jit(solution)/shard_map/ppermute | solution.py:44
  142.3 21.2 %collective-permute-start.23 = (bf16[2,2,96,768]{3,2,1,0:T(8,128)(2,1)}, bf16[2,2,96,768]{3,2,1,0:T(8,128)(2,1)}, u32[]{:S(2)}, u32[]{:S(2)}) collective-permute-start(bf16[2,2,96,768]{3,2,1,0:T(8,128)(2,1)} %pad_maximum_fusion.6), channel_id=1, source_target_pairs={{0,16},{8,24},{16,0},{24,8},{1,17},{9,25},{17,1},{25,9},{2,18},{10... | collective-permute-start | bytes 1769480 | tf_op jit(solution)/shard_map/ppermute | solution.py:44
  197.5 22.3 %all-to-all-start.1 = ((bf16[8,64,384]{2,1,0:T(8,128)(2,1)}), bf16[8,64,384]{2,1,0:T(8,128)(2,1)S(1)}, u32[]{:S(2)}, u32[]{:S(2)}) async-start(bf16[8,64,384]{2,1,0:T(8,128)(2,1)} %get-tuple-element.88), calls=%async_computation.1 | async-start | bytes 786432 | tf_op jit(solution)/shard_map/all_to_all | solution.py:204
  213.5 31.3 %collective-permute-start.29 = (bf16[9,2,2,24,768]{4,3,2,1,0:T(8,128)(2,1)S(1)}, bf16[9,2,2,24,768]{4,3,2,1,0:T(8,128)(2,1)}, u32[]{:S(2)}, u32[]{:S(2)}) collective-permute-start(bf16[9,2,2,24,768]{4,3,2,1,0:T(8,128)(2,1)S(1)} %get-tuple-element.116.after2), channel_id=1, source_target_pairs={{0,8},{8,0},{16,24},{24,16},{1,9},{9,1},{17,25},{25,17},{2,10},{10... | collective-permute-start | bytes 3981320 | tf_op jit(solution)/shard_map/ppermute | solution.py:44
  216.8 31.2 %collective-permute-start.28 = (bf16[9,2,2,24,768]{4,3,2,1,0:T(8,128)(2,1)}, bf16[9,2,2,24,768]{4,3,2,1,0:T(8,128)(2,1)}, u32[]{:S(2)}, u32[]{:S(2)}) collective-permute-start(bf16[9,2,2,24,768]{4,3,2,1,0:T(8,128)(2,1)} %get-tuple-element.118.after1), channel_id=1, source_target_pairs={{0,16},{8,24},{16,0},{24,8},{1,17},{9,25},{17,1},{25,9},{2,18},{10... | collective-permute-start | bytes 3981320 | tf_op jit(solution)/shard_map/ppermute | solution.py:44
  265.3 18.1 %collective-permute-start.31 = (bf16[9,2,24,768]{3,2,0,1:T(8,128)(2,1)}, bf16[9,2,24,768]{3,2,0,1:T(8,128)(2,1)}, u32[]{:S(2)}, u32[]{:S(2)}) collective-permute-start(bf16[9,2,24,768]{3,2,0,1:T(8,128)(2,1)} %dynamic-slice_bitcast_fusion.4), channel_id=1, source_target_pairs={{0,8},{8,0},{16,24},{24,16},{1,9},{9,1},{17,25},{25,17},{2,10},{10... | collective-permute-start | bytes 1990664 | tf_op jit(solution)/shard_map/ppermute | solution.py:44
  266.7 18.4 %collective-permute-start.32 = (bf16[9,2,24,768]{3,2,0,1:T(8,128)(2,1)}, bf16[9,2,24,768]{3,2,0,1:T(8,128)(2,1)}, u32[]{:S(2)}, u32[]{:S(2)}) collective-permute-start(bf16[9,2,24,768]{3,2,0,1:T(8,128)(2,1)} %dynamic-slice_bitcast_fusion.3), channel_id=1, source_target_pairs={{0,16},{8,24},{16,0},{24,8},{1,17},{9,25},{17,1},{25,9},{2,18},{10... | collective-permute-start | bytes 1990664 | tf_op jit(solution)/shard_map/ppermute | solution.py:44
  269.7 19.4 %collective-permute-start.30 = (bf16[2,128,768]{2,1,0:T(8,128)(2,1)S(1)}, bf16[2,128,768]{2,1,0:T(8,128)(2,1)}, u32[]{:S(2)}, u32[]{:S(2)}) collective-permute-start(bf16[2,128,768]{2,1,0:T(8,128)(2,1)S(1)} %dynamic-slice_bitcast_fusion.5), channel_id=1, source_target_pairs={{0,2},{1,3},{2,0},{3,1},{4,6},{5,7},{6,4},{7,5},{8,10},{9,11},{10,... | collective-permute-start | bytes 1179656 | tf_op jit(solution)/shard_map/ppermute | solution.py:67
  272.7 19.4 %collective-permute-start.38 = (bf16[4,32,1152]{2,1,0:T(8,128)(2,1)}, bf16[4,32,1152]{2,1,0:T(8,128)(2,1)}, u32[]{:S(2)}, u32[]{:S(2)}) collective-permute-start(bf16[4,32,1152]{2,1,0:T(8,128)(2,1)} %get-tuple-element.132), channel_id=1, source_target_pairs={{0,8},{8,0},{16,24},{24,16},{1,9},{9,1},{17,25},{25,17},{2,10},{10... | collective-permute-start | bytes 884744 | tf_op jit(solution)/shard_map/ppermute | solution.py:44
  274.2 22.0 %collective-permute-start.39 = (bf16[4,32,1152]{2,1,0:T(8,128)(2,1)}, bf16[4,32,1152]{2,1,0:T(8,128)(2,1)S(1)}, u32[]{:S(2)}, u32[]{:S(2)}) collective-permute-start(bf16[4,32,1152]{2,1,0:T(8,128)(2,1)} %get-tuple-element.134), channel_id=1, source_target_pairs={{0,16},{8,24},{16,0},{24,8},{1,17},{9,25},{17,1},{25,9},{2,18},{10... | collective-permute-start | bytes 884744 | tf_op jit(solution)/shard_map/ppermute | solution.py:44
  289.2 31.0 %collective-permute-start.35 = (bf16[9,24,768]{2,1,0:T(8,128)(2,1)}, bf16[9,24,768]{2,1,0:T(8,128)(2,1)}, u32[]{:S(2)}, u32[]{:S(2)}) collective-permute-start(bf16[9,24,768]{2,1,0:T(8,128)(2,1)} %get-tuple-element.130), channel_id=1, source_target_pairs={{0,4},{1,5},{2,6},{3,7},{4,0},{5,1},{6,2},{7,3},{8,12},{9,13},{10,... | collective-permute-start | bytes 995336 | tf_op jit(solution)/shard_map/ppermute | solution.py:34
  292.1 37.6 %collective-permute-start.36 = (bf16[9,24,768]{2,1,0:T(8,128)(2,1)}, bf16[9,24,768]{2,1,0:T(8,128)(2,1)}, u32[]{:S(2)}, u32[]{:S(2)}) collective-permute-start(bf16[9,24,768]{2,1,0:T(8,128)(2,1)} %get-tuple-element.131), channel_id=1, source_target_pairs={{0,6},{1,7},{2,0},{3,1},{4,2},{5,3},{6,4},{7,5},{8,14},{9,15},{10,... | collective-permute-start | bytes 995336 | tf_op jit(solution)/shard_map/ppermute | solution.py:34
  296.2 44.9 %collective-permute-start.33 = (bf16[128,768]{1,0:T(8,128)(2,1)}, bf16[128,768]{1,0:T(8,128)(2,1)S(1)}, u32[]{:S(2)}, u32[]{:S(2)}) collective-permute-start(bf16[128,768]{1,0:T(8,128)(2,1)} %dynamic-slice_bitcast_fusion.10), channel_id=1, source_target_pairs={{0,4},{1,5},{2,6},{3,7},{4,0},{5,1},{6,2},{7,3},{8,12},{9,13},{10,... | collective-permute-start | bytes 589832 | tf_op jit(solution)/shard_map/ppermute | solution.py:67
  299.9 32.1 %collective-permute-start.41 = (bf16[32,1152]{1,0:T(8,128)(2,1)S(1)}, bf16[32,1152]{1,0:T(8,128)(2,1)S(1)}, u32[]{:S(2)}, u32[]{:S(2)}) collective-permute-start(bf16[32,1152]{1,0:T(8,128)(2,1)S(1)} %get-tuple-element.157), channel_id=1, source_target_pairs={{0,2},{1,3},{2,0},{3,1},{4,6},{5,7},{6,4},{7,5},{8,10},{9,11},{10,... | collective-permute-start | bytes 221192 | tf_op jit(solution)/shard_map/ppermute | solution.py:67
  302.1 31.5 %collective-permute-start.42 = (bf16[32,1152]{1,0:T(8,128)(2,1)S(1)}, bf16[32,1152]{1,0:T(8,128)(2,1)S(1)}, u32[]{:S(2)}, u32[]{:S(2)}) collective-permute-start(bf16[32,1152]{1,0:T(8,128)(2,1)S(1)} %get-tuple-element.156), channel_id=1, source_target_pairs={{0,4},{1,5},{2,6},{3,7},{4,0},{5,1},{6,2},{7,3},{8,12},{9,13},{10,... | collective-permute-start | bytes 221192 | tf_op jit(solution)/shard_map/ppermute | solution.py:67
  (91 other events, 620.3 us)

commit v7 on v5

--- a/solution.py
+++ b/solution.py
@@ -151,18 +151,18 @@
     return held, ordered(core, held, swap_core(held), axis).reshape(-1, *blocks.shape[1:])
 
 
-def scatter_sequence(partial, first, second):
+def scatter_sequence(partial, after):
     level, top, half = z_bits()
     core = lax.axis_index("seq") % CORES
     shape = partial.shape[1:]
     count = top.bit_length()
     held = partial.reshape(*[2] * (count + 1), *shape)
-    got = gate(swap_core(pick(held, 1 - core, count)), first)
+    got = gate(swap_core(pick(held, 1 - core, count)), after)
     held = add(pick(held, core, count), got)
     axis, bit = count - 1, 1
     while bit < top:
         flag = level // bit % 2
-        got = gate(swap_z(pick(held, 1 - flag, axis), bit), second)
+        got = swap_z(pick(held, 1 - flag, axis), bit)
         held = add(pick(held, flag, axis), got)
         axis, bit = axis - 1, bit * 2
     return ordered(half, pick(held, half, 0), swap_z(pick(held, 1 - half, 0), top), 0)
@@ -181,15 +181,11 @@
     return [pick(blocks, class_of(level), 0)] + moved
 
 
-def scatter_columns(tower, after):
+def scatter_columns(tower):
     heights = tower.shape[0]
     level = lax.axis_index("seq") // CORES
-    kinds = jnp.arange(heights // 2)[:, None, None]
-    total = jnp.where(kinds == class_of(level), pick(tower, level, 0).astype(F32)[None], 0.0)
-    for mask in range(1, heights):
-        got = gate(swap_z(pick(tower, level ^ mask, 0), mask), after)
-        total += jnp.where(kinds == class_of(level ^ mask), got.astype(F32)[None], 0.0)
-    return total
+    moved = [swap_z(pick(tower, level ^ mask, 0), mask) for mask in range(1, heights)]
+    return [pick(tower, level, 0)] + moved
 
 
 def scatter_plane_direct(split, after):
@@ -229,21 +225,21 @@
     return (offset >= 0) & (offset < size)
 
 
-def line_kernel(*refs):
-    pieces, tower = refs[:-1], refs[-1]
+def line_kernel(count, *refs):
+    pieces, tower = refs[:count], refs[-1]
     level = lax.axis_index("seq") // CORES
     for mask, piece in enumerate(pieces):
         tower[level ^ mask] = piece[...]
 
 
-def build_line(pieces):
-    return pl.pallas_call(
-        line_kernel,
+def build_line(pieces, after):
+    return pl.pallas_call(
+        functools.partial(line_kernel, len(pieces)),
         out_shape=jax.ShapeDtypeStruct((len(pieces), *pieces[0].shape), BF16),
-        in_specs=vmem_specs(len(pieces)),
+        in_specs=vmem_specs(len(pieces)) + [ANYWHERE],
         out_specs=vmem_specs(1)[0],
         cost_estimate=LIGHT,
-    )(*pieces)
+    )(*pieces, after)
 
 
 def halves_kernel(count, *refs):
@@ -275,6 +271,43 @@
         compiler_params=pltpu.CompilerParams(vmem_limit_bytes=40 * 2**20),
         cost_estimate=LIGHT,
     )(*towers, *after)
+
+
+def finish_kernel(count, group, *refs):
+    pieces, (weight, small) = refs[:count], refs[-2:]
+    shard, width = weight.shape[0], weight.shape[1] // 3
+    heights = count
+    level = lax.axis_index("seq") // CORES
+    terms = [piece[...].astype(F32) for piece in pieces]
+    small_sum = jnp.zeros((ROWS, LANES), F32)
+    for kind in range(heights // 2):
+        total = jnp.zeros_like(terms[0])
+        for mask, term in enumerate(terms):
+            total += jnp.where(lax.rem(level ^ mask, heights // 2) == kind, term, 0.0)
+        for core in range(CORES):
+            start = core * 3 * group
+            small_sum += total[shard:, start : start + LANES]
+            lo = (kind * CORES + core) * group
+            for part in range(3 if lo < width else 0):
+                at = start + part * group
+                weight[:, part * width + lo : part * width + lo + group] = total[
+                    :shard, at : at + group
+                ]
+    small[...] = small_sum
+
+
+def finish_columns(pieces, width, group, after):
+    rows = pieces[0].shape[0]
+    return pl.pallas_call(
+        functools.partial(finish_kernel, len(pieces), group),
+        out_shape=[
+            jax.ShapeDtypeStruct((rows - ROWS, 3 * width), F32),
+            jax.ShapeDtypeStruct((ROWS, LANES), F32),
+        ],
+        in_specs=vmem_specs(len(pieces)) + [ANYWHERE],
+        out_specs=vmem_specs(2),
+        cost_estimate=LIGHT,
+    )(*pieces, after)
 
 
 def unpack_kernel(sizes, keep, got, weight, *refs):
@@ -964,9 +997,9 @@
         classes,
         group,
     )
-    tower_a = build_line(gather_columns(columns))
+    stacked = stack_weights(w_out.reshape(-1, width), w_fc.reshape(-1, parts * width), columns)
+    tower_a = build_line(gather_columns(columns), stacked)
     lines, sequence = gather_sequence(blocks, tower_a)
-    stacked = stack_weights(w_out.reshape(-1, width), w_fc.reshape(-1, parts * width), columns)
     low1, high1 = build_tower(z_pieces(stacked), 1, [tower_a])
     if lax.axis_size("dp") == 4:
         towers = [tower_a] + [swap_dp(tower_a, mask) for mask in range(1, 4)]
@@ -1060,13 +1093,13 @@
         grad_qkv, wqkv, (((1,), (1,)), ((), ())), preferred_element_type=F32
     )
     own_normed1 = scatter_sequence(
-        grad_normed1.astype(BF16).reshape(count, block, width), first_sums, tower_b
+        grad_normed1.astype(BF16).reshape(count, block, width), first_sums
     )
     _, norm1_back = jax.vjp(lambda value: norm_affine(value, gain1, bias1), rows)
     (grad_in_part,) = norm1_back(own_normed1.astype(F32).reshape(tokens, width))
     grad_inputs = (grad_middle + grad_in_part).astype(BF16).reshape(inputs.shape)
 
-    grad_qkv = gate(grad_qkv, first_sums)
+    grad_qkv = gate(grad_qkv, tower_b)
     long_rows = sequence[:, :block].astype(F32).reshape(count * block, width)
     _, norm1_long_back = jax.vjp(lambda g, b: norm_affine(long_rows, g, b), gain1, bias1)
     grad_gain1, grad_bias1 = norm1_long_back(grad_normed1)
@@ -1098,14 +1131,9 @@
         [jnp.where(core == 0, keep_a, got_a), jnp.where(core == 0, got_a, keep_a)], -1
     )
     tower_a = scatter_plane_direct(pair_a, tower_b)
-    own_a = scatter_columns(tower_a, own_b)
-    own_small = jnp.sum(
-        own_a[:, shard_rows:].reshape(classes, ROWS, CORES, 3 * group)[..., :LANES], (0, 2)
-    )
+    own_qkv, own_small = finish_columns(scatter_columns(tower_a), width, group, own_b)
     own = [own_small[i, :size] for i, size in enumerate(sizes)]
-    own_qkv = own_a[:, :shard_rows].reshape(classes, shard_rows, CORES, 3, group)
-    own_qkv = own_qkv.transpose(1, 3, 0, 2, 4).reshape(shard_rows, 3, groups * heads, head_size)
-    own_qkv = own_qkv[:, :, :HEADS].reshape(-1)
+    own_qkv = own_qkv.reshape(-1)
     return (
         outputs,
         grad_inputs,

time: 315 us -> 324 us (1.029)
  starting transfers between devices: 60.2 us -> 69 us
  other arithmetic: 50.2 us -> 41.7 us
  waiting for transfers between devices: 95.4 us -> 103 us
    ppermute x9, waiting for transfers between devices: 12 us -> 23.1 us  [shift_z(): lax.ppermute(value, 'seq', [(i, (i + CORES * step) % size) for i in range...]
    ppermute x10, starting transfers between devices: 18.6 us -> 23.9 us  [swap_z(): lax.ppermute(value, 'seq', [(i, i ^ CORES * bit) for i in range(size)])]
    ppermute x7, waiting for transfers between devices: 8.09 us -> 4.48 us  [swap_core(): return lax.ppermute(value, 'seq', [(i, i ^ 1) for i in range(size)])]
    squeeze x8 -> x9, local copies, waits for them, and re-layouts: 6.79 us -> 6.16 us  [pick(): return lax.dynamic_index_in_dim(value, index, axis, keepdims=False)]
  transfers between devices with their start and end apart: 46 -> 46, of which waited for: 16 -> 17; matrix products, arithmetic and copies ran while one was open for 23% -> 17% of each run, Pallas kernels for 9% -> 8%
where the time goes in v7:
time: 324 us; the launch traced here: 318 us
  waiting for transfers between devices  103 us (32%)
  starting transfers between devices  69 us (21%)
  Pallas kernels  52.8 us (16%)
  local copies, waits for them, and re-layouts  45.1 us (14%)
  other arithmetic  41.7 us (13%)
  matrix products  5.16 us (2%)
    ppermute x18, waiting for transfers between devices, swap_dp(): return lax.ppermute(value, 'dp', [(i, i ^ bit) for i in range(size)])  36.7 us
    ppermute x10, waiting for transfers between devices, swap_z(): lax.ppermute(value, 'seq', [(i, i ^ CORES * bit) for i in range(size)])  32.5 us
    ppermute x10, starting transfers between devices, swap_z(): lax.ppermute(value, 'seq', [(i, i ^ CORES * bit) for i in range(size)])  23.9 us
    ppermute x9, waiting for transfers between devices, shift_z(): lax.ppermute(value, 'seq', [(i, (i + CORES * step) % size) for i in range...  23.1 us
    ppermute x18, starting transfers between devices, swap_dp(): return lax.ppermute(value, 'dp', [(i, i ^ bit) for i in range(size)])  21.4 us
    another operation x19, other arithmetic, ordered(): return jnp.stack([first, second], axis)  16.6 us
    unnamed x120, local copies, waits for them, and re-layouts  14.6 us
    ppermute x9, starting transfers between devices, shift_z(): lax.ppermute(value, 'seq', [(i, (i + CORES * step) % size) for i in range...  14.4 us
  transfers between devices with their start and end apart: 46, of which 17 were waited for; matrix products, arithmetic and copies ran while one was open for 17% of the time, Pallas kernels for 8%

profile of v7, /device:TPU:0, one launch (start us, length us, event | category | flops | bytes accessed | tf_op | source)
XLA Modules:
  0.0 318.2 jit_solution(10046164652877711935)
XLA Ops:
  5.4 4.1 %collective-permute-start.7 = (bf16[144,768]{1,0:T(8,128)(2,1)S(1)}, bf16[144,768]{1,0:T(8,128)(2,1)S(1)}, u32[]{:S(2)}, u32[]{:S(2)}) collective-permute-start(bf16[144,768]{1,0:T(8,128)(2,1)S(1)} %dynamic-slice_bitcast_fusion.9), channel_id=1, source_target_pairs={{0,4},{1,5},{2,6},{3,7},{4,0},{5,1},{6,2},{7,3},{8,12},{9,13},{10,... | collective-permute-start | bytes 663560 | tf_op jit(solution)/shard_map/ppermute | solution.py:67
  18.5 6.6 %collective-permute-done.4.refs_2_ = bf16[32,1152]{1,0:T(8,128)(2,1)S(1)} collective-permute-done((bf16[32,1152]{1,0:T(8,128)(2,1)S(1)}, bf16[32,1152]{1,0:T(8,128)(2,1)S(1)}, u32[]{:S(2)}, u32[]{:S(2)}) %collective-permute-start.4) | collective-permute-done | bytes 73760 | tf_op jit(solution)/shard_map/ppermute | solution.py:67
  30.9 3.4 %collective-permute-start = (bf16[5,24,768]{2,1,0:T(8,128)(2,1)S(1)}, bf16[5,24,768]{2,1,0:T(8,128)(2,1)S(1)}, u32[]{:S(2)}, u32[]{:S(2)}) collective-permute-start(bf16[5,24,768]{2,1,0:T(8,128)(2,1)S(1)} %copy-done.6), channel_id=1, source_target_pairs={{0,6},{1,7},{2,0},{3,1},{4,2},{5,3},{6,4},{7,5},{8,14},{9,15},{10,... | collective-permute-start | bytes 552968 | tf_op jit(solution)/shard_map/ppermute | solution.py:34
  37.3 9.1 %collective-permute-done.8 = bf16[2,144,768]{2,1,0:T(8,128)(2,1)S(1)} collective-permute-done((bf16[2,144,768]{2,1,0:T(8,128)(2,1)S(1)}, bf16[2,144,768]{2,1,0:T(8,128)(2,1)S(1)}, u32[]{:S(2)}, u32[]{:S(2)}) %collective-permute-start.8) | collective-permute-done | bytes 442400 | tf_op jit(solution)/shard_map/ppermute | solution.py:67
  49.2 3.6 %collective-permute-start.2 = (bf16[5,24,768]{2,1,0:T(8,128)(2,1)S(1)}, bf16[5,24,768]{2,1,0:T(8,128)(2,1)S(1)}, u32[]{:S(2)}, u32[]{:S(2)}) collective-permute-start(bf16[5,24,768]{2,1,0:T(8,128)(2,1)S(1)} %copy-done.6), channel_id=1, source_target_pairs={{0,2},{1,3},{2,4},{3,5},{4,6},{5,7},{6,0},{7,1},{8,10},{9,11},{10,... | collective-permute-start | bytes 552968 | tf_op jit(solution)/shard_map/ppermute | solution.py:34
  52.8 7.7 %collective-permute-done.2.refs_3_ = bf16[5,24,768]{2,1,0:T(8,128)(2,1)S(1)} collective-permute-done((bf16[5,24,768]{2,1,0:T(8,128)(2,1)S(1)}, bf16[5,24,768]{2,1,0:T(8,128)(2,1)S(1)}, u32[]{:S(2)}, u32[]{:S(2)}) %collective-permute-start.2) | collective-permute-done | bytes 184352 | tf_op jit(solution)/shard_map/ppermute | solution.py:34
  71.8 11.3 %shard_map.261 = (bf16[512,384]{1,0:T(8,128)(2,1)}, f32[3,1024]{1,0:T(4,128)S(1)}, bf16[1024,576]{1,0:T(8,128)(2,1)S(1)}, bf16[1024,768]{1,0:T(8,128)(2,1)S(1)}, f32[1,1024]{1,0:T(1,128)S(1)}) custom-call(bf16[8,144,768]{2,1,0:T(8,128)(2,1)} %bitcast.241, bf16[768,576]{1,0:T(8,128)(2,1)S(1)} %get-tuple-element.60.weight, ...), custom_call_target="tpu_custom_call" | custom-call | flops 1 | bytes 1 | tf_op jit(solution)/shard_map/pallas_call | solution.py:919
  85.3 4.5 %all-to-all-start = ((bf16[8,64,384]{2,1,0:T(8,128)(2,1)}), bf16[8,64,384]{2,1,0:T(8,128)(2,1)S(1)}, u32[]{:S(2)}, u32[]{:S(2)}) async-start(bf16[8,64,384]{2,1,0:T(8,128)(2,1)} %bitcast.24), calls=%async_computation | async-start | bytes 786432 | tf_op jit(solution)/shard_map/all_to_all | solution.py:204
  97.2 5.2 %all-to-all-done.refs_1_.attended = bf16[8,64,384]{2,1,0:T(8,128)(2,1)S(1)} async-done(((bf16[8,64,384]{2,1,0:T(8,128)(2,1)}), bf16[8,64,384]{2,1,0:T(8,128)(2,1)S(1)}, u32[]{:S(2)}, u32[]{:S(2)}) %all-to-all-start) | async-done | bytes 393248 | tf_op jit(solution)/shard_map/all_to_all | solution.py:204
  109.9 5.6 %collective-permute-done.14 = bf16[5,2,2,24,768]{4,3,2,0,1:T(8,128)(2,1)} collective-permute-done((bf16[5,2,2,24,768]{4,3,2,0,1:T(8,128)(2,1)}, bf16[5,2,2,24,768]{4,3,2,0,1:T(8,128)(2,1)}, u32[]{:S(2)}, u32[]{:S(2)}) %collective-permute-start.14) | collective-permute-done | bytes 737312 | tf_op jit(solution)/shard_map/ppermute | solution.py:44
  129.0 3.5 %collective-permute-done.24 = bf16[2,2,96,768]{3,2,1,0:T(8,128)(2,1)} collective-permute-done((bf16[2,2,96,768]{3,2,1,0:T(8,128)(2,1)}, bf16[2,2,96,768]{3,2,1,0:T(8,128)(2,1)}, u32[]{:S(2)}, u32[]{:S(2)}) %collective-permute-start.24) | collective-permute-done | bytes 589856 | tf_op jit(solution)/shard_map/ppermute | solution.py:44
  134.3 4.5 %collective-permute-done.25.other2 = bf16[16,96,768]{2,1,0:T(8,128)(2,1)S(1)} collective-permute-done((bf16[16,96,768]{2,1,0:T(8,128)(2,1)S(1)}, bf16[16,96,768]{2,1,0:T(8,128)(2,1)S(1)}, u32[]{:S(2)}, u32[]{:S(2)}) %collective-permute-start.25) | collective-permute-done | bytes 2359328 | tf_op jit(solution)/shard_map/ppermute | solution.py:39
  141.1 13.8 %shard_map.270 = (bf16[2,128,768]{2,1,0:T(8,128)(2,1)}, f32[256,768]{1,0:T(8,128)S(1)}, bf16[8,64,384]{2,1,0:T(8,128)(2,1)}, bf16[256,768]{1,0:T(8,128)(2,1)S(1)...) custom-call(bf16[5,384,768]{2,1,0:T(8,128)(2,1)} %bitcast.247, ...), custom_call_target="tpu_custom_call" | custom-call | flops 1 | bytes 1 | tf_op jit(solution)/shard_map/pallas_call | solution.py:679
  157.2 8.4 %shard_map.271 = (bf16[9,384,768]{2,1,0:T(8,128)(2,1)}, bf16[9,384,768]{2,1,0:T(8,128)(2,1)}) custom-call(bf16[256,768]{1,0:T(8,128)(2,1)S(1)} %get-tuple-element.79.placed_a, bf16[256,768]{1,0:T(8,128)(2,1)S(1)} %get-tuple-element.80.placed_n, bf16[256,3072]{1,0:T(8,128)(2,1)S(1)} %copy-done.8, bf16[256,3072]{1,0:T(8,128)(2,1)} %get-tuple-element.82.grad_pre, ...), custom_call_target="tpu_custom_call" | custom-call | flops 1 | bytes 1 | tf_op jit(solution)/shard_map/pallas_call | solution.py:755
  170.8 4.3 %all-to-all-start.1 = ((bf16[8,64,384]{2,1,0:T(8,128)(2,1)}), bf16[8,64,384]{2,1,0:T(8,128)(2,1)S(1)}, u32[]{:S(2)}, u32[]{:S(2)}) async-start(bf16[8,64,384]{2,1,0:T(8,128)(2,1)} %get-tuple-element.76), calls=%async_computation.1 | async-start | bytes 786432 | tf_op jit(solution)/shard_map/all_to_all | solution.py:204
  175.1 5.5 %add_convert_fusion = bf16[9,384,768]{2,1,0:T(8,128)(2,1)S(1)} fusion(bf16[9,384,768]{2,1,0:T(8,128)(2,1)} %collective-permute-done.26, bf16[9,384,768]{2,1,0:T(8,128)(2,1)} %get-tuple-element.84), kind=kLoop, calls=%fused_computation | loop fusion | flops 10616832 | bytes 15925248 | tf_op jit(solution)/shard_map/convert_element_type | solution.py:96
  187.7 8.8 %shard_map.272.refs_2_.refs_0_ = bf16[1024,576]{1,0:T(8,128)(2,1)S(1)} custom-call(bf16[1024,576]{1,0:T(8,128)(2,1)S(1)} %get-tuple-element.75.whole, bf16[512,384]{1,0:T(8,128)(2,1)S(1)} %bitcast.240, f32[3,1024]{1,0:T(4,128)S(1)} %get-tuple-element.77.stats, f32[1,1024]{1,0:T(1,128)S(1)} %get-tuple-element.78.ids, ...), custom_call_target="tpu_custom_call" | custom-call | flops 1 | bytes 1 | tf_op jit(solution)/shard_map/pallas_call | solution.py:939
  199.9 14.4 %collective-permute-done.29.refs_1_ = bf16[9,2,2,24,768]{4,3,2,1,0:T(8,128)(2,1)} collective-permute-done((bf16[9,2,2,24,768]{4,3,2,1,0:T(8,128)(2,1)S(1)}, bf16[9,2,2,24,768]{4,3,2,1,0:T(8,128)(2,1)}, u32[]{:S(2)}, u32[]{:S(2)}) %collective-permute-start.29) | collective-permute-done | bytes 1327136 | tf_op jit(solution)/shard_map/ppermute | solution.py:44
  225.9 8.1 %collective-permute-done.30 = bf16[2,128,768]{2,1,0:T(8,128)(2,1)} collective-permute-done((bf16[2,128,768]{2,1,0:T(8,128)(2,1)}, bf16[2,128,768]{2,1,0:T(8,128)(2,1)}, u32[]{:S(2)}, u32[]{:S(2)}) %collective-permute-start.30) | collective-permute-done | bytes 393248 | tf_op jit(solution)/shard_map/ppermute | solution.py:67
  240.1 5.6 %collective-permute-done.31 = bf16[128,768]{1,0:T(8,128)(2,1)S(1)} collective-permute-done((bf16[128,768]{1,0:T(8,128)(2,1)S(1)}, bf16[128,768]{1,0:T(8,128)(2,1)S(1)}, u32[]{:S(2)}, u32[]{:S(2)}) %collective-permute-start.31) | collective-permute-done | bytes 196640 | tf_op jit(solution)/shard_map/ppermute | solution.py:67
  246.6 7.3 %collective-permute-done.33 = bf16[9,2,24,768]{3,2,0,1:T(8,128)(2,1)S(1)} collective-permute-done((bf16[9,2,24,768]{3,2,0,1:T(8,128)(2,1)S(1)}, bf16[9,2,24,768]{3,2,0,1:T(8,128)(2,1)S(1)}, u32[]{:S(2)}, u32[]{:S(2)}) %collective-permute-start.33) | collective-permute-done | bytes 663584 | tf_op jit(solution)/shard_map/ppermute | solution.py:44
  272.4 4.4 %collective-permute-done.41 = bf16[9,24,768]{2,1,0:T(8,128)(2,1)S(1)} collective-permute-done((bf16[9,24,768]{2,1,0:T(8,128)(2,1)S(1)}, bf16[9,24,768]{2,1,0:T(8,128)(2,1)S(1)}, u32[]{:S(2)}, u32[]{:S(2)}) %collective-permute-start.41) | collective-permute-done | bytes 331808 | tf_op jit(solution)/shard_map/ppermute | solution.py:34
  279.7 10.9 %collective-permute-done.42 = bf16[9,24,768]{2,1,0:T(8,128)(2,1)S(1)} collective-permute-done((bf16[9,24,768]{2,1,0:T(8,128)(2,1)S(1)}, bf16[9,24,768]{2,1,0:T(8,128)(2,1)S(1)}, u32[]{:S(2)}, u32[]{:S(2)}) %collective-permute-start.42) | collective-permute-done | bytes 331808 | tf_op jit(solution)/shard_map/ppermute | solution.py:34
  294.6 7.6 %collective-permute-start.38 = (bf16[32,1152]{1,0:T(8,128)(2,1)S(1)}, bf16[32,1152]{1,0:T(8,128)(2,1)S(1)}, u32[]{:S(2)}, u32[]{:S(2)}) collective-permute-start(bf16[32,1152]{1,0:T(8,128)(2,1)S(1)} %get-tuple-element.143), channel_id=1, source_target_pairs={{0,2},{1,3},{2,0},{3,1},{4,6},{5,7},{6,4},{7,5},{8,10},{9,11},{10,... | collective-permute-start | bytes 221192 | tf_op jit(solution)/shard_map/ppermute | solution.py:67
  (310 shorter events, 148.1 us)
Async XLA Ops:
  5.4 22.2 %collective-permute-start.7 = (bf16[144,768]{1,0:T(8,128)(2,1)S(1)}, bf16[144,768]{1,0:T(8,128)(2,1)S(1)}, u32[]{:S(2)}, u32[]{:S(2)}) collective-permute-start(bf16[144,768]{1,0:T(8,128)(2,1)S(1)} %dynamic-slice_bitcast_fusion.9), channel_id=1, source_target_pairs={{0,4},{1,5},{2,6},{3,7},{4,0},{5,1},{6,2},{7,3},{8,12},{9,13},{10,... | collective-permute-start | bytes 663560 | tf_op jit(solution)/shard_map/ppermute | solution.py:67
  29.3 17.1 %collective-permute-start.8 = (bf16[2,144,768]{2,1,0:T(8,128)(2,1)S(1)}, bf16[2,144,768]{2,1,0:T(8,128)(2,1)S(1)}, u32[]{:S(2)}, u32[]{:S(2)}) collective-permute-start(bf16[2,144,768]{2,1,0:T(8,128)(2,1)S(1)} %pad_maximum_fusion.8), channel_id=1, source_target_pairs={{0,2},{1,3},{2,0},{3,1},{4,6},{5,7},{6,4},{7,5},{8,10},{9,11},{10,... | collective-permute-start | bytes 1327112 | tf_op jit(solution)/shard_map/ppermute | solution.py:67
  30.9 18.2 %collective-permute-start = (bf16[5,24,768]{2,1,0:T(8,128)(2,1)S(1)}, bf16[5,24,768]{2,1,0:T(8,128)(2,1)S(1)}, u32[]{:S(2)}, u32[]{:S(2)}) collective-permute-start(bf16[5,24,768]{2,1,0:T(8,128)(2,1)S(1)} %copy-done.6), channel_id=1, source_target_pairs={{0,6},{1,7},{2,0},{3,1},{4,2},{5,3},{6,4},{7,5},{8,14},{9,15},{10,... | collective-permute-start | bytes 552968 | tf_op jit(solution)/shard_map/ppermute | solution.py:34
  34.2 27.1 %collective-permute-start.10 = (bf16[4,32,1152]{2,1,0:T(8,128)(2,1)S(1)}, bf16[4,32,1152]{2,1,0:T(8,128)(2,1)S(1)}, u32[]{:S(2)}, u32[]{:S(2)}) collective-permute-start(bf16[4,32,1152]{2,1,0:T(8,128)(2,1)S(1)} %copy-done.5), channel_id=1, source_target_pairs={{0,8},{8,0},{16,24},{24,16},{1,9},{9,1},{17,25},{25,17},{2,10},{10... | collective-permute-start | bytes 884744 | tf_op jit(solution)/shard_map/ppermute | solution.py:44
  35.7 25.6 %collective-permute-start.11 = (bf16[4,32,1152]{2,1,0:T(8,128)(2,1)S(1)}, bf16[4,32,1152]{2,1,0:T(8,128)(2,1)S(1)}, u32[]{:S(2)}, u32[]{:S(2)}) collective-permute-start(bf16[4,32,1152]{2,1,0:T(8,128)(2,1)S(1)} %copy-done.5), channel_id=1, source_target_pairs={{0,16},{8,24},{16,0},{24,8},{1,17},{9,25},{17,1},{25,9},{2,18},{10... | collective-permute-start | bytes 884744 | tf_op jit(solution)/shard_map/ppermute | solution.py:44
  49.1 19.0 %collective-permute-start.9 = (bf16[2,2,144,768]{3,2,1,0:T(8,128)(2,1)S(1)}, bf16[2,2,144,768]{3,2,1,0:T(8,128)(2,1)}, u32[]{:S(2)}, u32[]{:S(2)}) collective-permute-start(bf16[2,2,144,768]{3,2,1,0:T(8,128)(2,1)S(1)} %pad_maximum_fusion.3.refs_5_.refs_1_), channel_id=1, source_target_pairs={{0,1},{1,0},{2,3},{3,2},{4,5},{5,4},{6,7},{7,6},{8,9},{9,8},{10,11... | collective-permute-start | bytes 2654216 | tf_op jit(solution)/shard_map/ppermute | solution.py:39
  63.5 27.8 %collective-permute-start.6 = (bf16[5,2,24,768]{3,2,1,0:T(8,128)(2,1)S(1)}, bf16[5,2,24,768]{3,2,1,0:T(8,128)(2,1)}, u32[]{:S(2)}, u32[]{:S(2)}) collective-permute-start(bf16[5,2,24,768]{3,2,1,0:T(8,128)(2,1)S(1)} %get-tuple-element.56.refs_4_.after), channel_id=1, source_target_pairs={{0,8},{8,0},{16,24},{24,16},{1,9},{9,1},{17,25},{25,17},{2,10},{10... | collective-permute-start | bytes 1105928 | tf_op jit(solution)/shard_map/ppermute | solution.py:44
  64.0 29.8 %collective-permute-start.15 = (bf16[5,2,24,768]{3,2,1,0:T(8,128)(2,1)}, bf16[5,2,24,768]{3,2,1,0:T(8,128)(2,1)}, u32[]{:S(2)}, u32[]{:S(2)}) collective-permute-start(bf16[5,2,24,768]{3,2,1,0:T(8,128)(2,1)} %get-tuple-element.65), channel_id=1, source_target_pairs={{0,16},{8,24},{16,0},{24,8},{1,17},{9,25},{17,1},{25,9},{2,18},{10... | collective-permute-start | bytes 1105928 | tf_op jit(solution)/shard_map/ppermute | solution.py:44
  64.6 19.8 %collective-permute-start.18 = (bf16[96,768]{1,0:T(8,128)(2,1)}, bf16[96,768]{1,0:T(8,128)(2,1)S(1)}, u32[]{:S(2)}, u32[]{:S(2)}) collective-permute-start(bf16[96,768]{1,0:T(8,128)(2,1)} %shard_map.266.refs_0_), channel_id=1, source_target_pairs={{0,6},{1,7},{2,0},{3,1},{4,2},{5,3},{6,4},{7,5},{8,14},{9,15},{10,... | collective-permute-start | bytes 442376 | tf_op jit(solution)/shard_map/ppermute | solution.py:34
  67.0 17.4 %collective-permute-start.19 = (bf16[96,768]{1,0:T(8,128)(2,1)}, bf16[96,768]{1,0:T(8,128)(2,1)S(1)}, u32[]{:S(2)}, u32[]{:S(2)}) collective-permute-start(bf16[96,768]{1,0:T(8,128)(2,1)} %shard_map.266.refs_0_), channel_id=1, source_target_pairs={{0,4},{1,5},{2,6},{3,7},{4,0},{5,1},{6,2},{7,3},{8,12},{9,13},{10,... | collective-permute-start | bytes 442376 | tf_op jit(solution)/shard_map/ppermute | solution.py:34
  85.3 17.0 %all-to-all-start = ((bf16[8,64,384]{2,1,0:T(8,128)(2,1)}), bf16[8,64,384]{2,1,0:T(8,128)(2,1)S(1)}, u32[]{:S(2)}, u32[]{:S(2)}) async-start(bf16[8,64,384]{2,1,0:T(8,128)(2,1)} %bitcast.24), calls=%async_computation | async-start | bytes 786432 | tf_op jit(solution)/shard_map/all_to_all | solution.py:204
  89.8 17.5 %collective-permute-start.23 = (bf16[2,96,768]{2,1,0:T(8,128)(2,1)S(1)}, bf16[2,96,768]{2,1,0:T(8,128)(2,1)}, u32[]{:S(2)}, u32[]{:S(2)}) collective-permute-start(bf16[2,96,768]{2,1,0:T(8,128)(2,1)S(1)} %get-tuple-element.67), channel_id=1, source_target_pairs={{0,16},{8,24},{16,0},{24,8},{1,17},{9,25},{17,1},{25,9},{2,18},{10... | collective-permute-start | bytes 884744 | tf_op jit(solution)/shard_map/ppermute | solution.py:44
  93.3 22.2 %collective-permute-start.14 = (bf16[5,2,2,24,768]{4,3,2,0,1:T(8,128)(2,1)}, bf16[5,2,2,24,768]{4,3,2,0,1:T(8,128)(2,1)}, u32[]{:S(2)}, u32[]{:S(2)}) collective-permute-start(bf16[5,2,2,24,768]{4,3,2,0,1:T(8,128)(2,1)} %pad_maximum_fusion.4), channel_id=1, source_target_pairs={{0,16},{8,24},{16,0},{24,8},{1,17},{9,25},{17,1},{25,9},{2,18},{10... | collective-permute-start | bytes 2211848 | tf_op jit(solution)/shard_map/ppermute | solution.py:44
  96.0 25.2 %collective-permute-start.16 = (bf16[5,2,2,24,768]{4,3,2,1,0:T(8,128)(2,1)}, bf16[5,2,2,24,768]{4,3,2,1,0:T(8,128)(2,1)}, u32[]{:S(2)}, u32[]{:S(2)}) collective-permute-start(bf16[5,2,2,24,768]{4,3,2,1,0:T(8,128)(2,1)} %pad_maximum_fusion.5), channel_id=1, source_target_pairs={{0,8},{8,0},{16,24},{24,16},{1,9},{9,1},{17,25},{25,17},{2,10},{10... | collective-permute-start | bytes 2211848 | tf_op jit(solution)/shard_map/ppermute | solution.py:44
  105.7 22.0 %collective-permute-start.22 = (bf16[2,2,96,768]{3,2,1,0:T(8,128)(2,1)}, bf16[2,2,96,768]{3,2,1,0:T(8,128)(2,1)}, u32[]{:S(2)}, u32[]{:S(2)}) collective-permute-start(bf16[2,2,96,768]{3,2,1,0:T(8,128)(2,1)} %pad_maximum_fusion.6), channel_id=1, source_target_pairs={{0,16},{8,24},{16,0},{24,8},{1,17},{9,25},{17,1},{25,9},{2,18},{10... | collective-permute-start | bytes 1769480 | tf_op jit(solution)/shard_map/ppermute | solution.py:44
  170.8 16.9 %all-to-all-start.1 = ((bf16[8,64,384]{2,1,0:T(8,128)(2,1)}), bf16[8,64,384]{2,1,0:T(8,128)(2,1)S(1)}, u32[]{:S(2)}, u32[]{:S(2)}) async-start(bf16[8,64,384]{2,1,0:T(8,128)(2,1)} %get-tuple-element.76), calls=%async_computation.1 | async-start | bytes 786432 | tf_op jit(solution)/shard_map/all_to_all | solution.py:204
  182.7 31.6 %collective-permute-start.29 = (bf16[9,2,2,24,768]{4,3,2,1,0:T(8,128)(2,1)S(1)}, bf16[9,2,2,24,768]{4,3,2,1,0:T(8,128)(2,1)}, u32[]{:S(2)}, u32[]{:S(2)}) collective-permute-start(bf16[9,2,2,24,768]{4,3,2,1,0:T(8,128)(2,1)S(1)} %get-tuple-element.104.after2), channel_id=1, source_target_pairs={{0,8},{8,0},{16,24},{24,16},{1,9},{9,1},{17,25},{25,17},{2,10},{10... | collective-permute-start | bytes 3981320 | tf_op jit(solution)/shard_map/ppermute | solution.py:44
  185.6 31.6 %collective-permute-start.28 = (bf16[9,2,2,24,768]{4,3,2,1,0:T(8,128)(2,1)}, bf16[9,2,2,24,768]{4,3,2,1,0:T(8,128)(2,1)}, u32[]{:S(2)}, u32[]{:S(2)}) collective-permute-start(bf16[9,2,2,24,768]{4,3,2,1,0:T(8,128)(2,1)} %get-tuple-element.106.after1), channel_id=1, source_target_pairs={{0,16},{8,24},{16,0},{24,8},{1,17},{9,25},{17,1},{25,9},{2,18},{10... | collective-permute-start | bytes 3981320 | tf_op jit(solution)/shard_map/ppermute | solution.py:44
  199.4 20.7 %collective-permute-start.27 = (bf16[2,2,128,768]{3,2,1,0:T(8,128)(2,1)}, bf16[2,2,128,768]{3,2,1,0:T(8,128)(2,1)}, u32[]{:S(2)}, u32[]{:S(2)}) collective-permute-start(bf16[2,2,128,768]{3,2,1,0:T(8,128)(2,1)} %dynamic-slice_bitcast_fusion.2), channel_id=1, source_target_pairs={{0,1},{1,0},{2,3},{3,2},{4,5},{5,4},{6,7},{7,6},{8,9},{9,8},{10,11... | collective-permute-start | bytes 2359304 | tf_op jit(solution)/shard_map/ppermute | solution.py:39
  225.0 21.4 %collective-permute-start.32 = (bf16[9,2,24,768]{3,2,0,1:T(8,128)(2,1)S(1)}, bf16[9,2,24,768]{3,2,0,1:T(8,128)(2,1)S(1)}, u32[]{:S(2)}, u32[]{:S(2)}) collective-permute-start(bf16[9,2,24,768]{3,2,0,1:T(8,128)(2,1)S(1)} %dynamic-slice_bitcast_fusion.4), channel_id=1, source_target_pairs={{0,8},{8,0},{16,24},{24,16},{1,9},{9,1},{17,25},{25,17},{2,10},{10... | collective-permute-start | bytes 1990664 | tf_op jit(solution)/shard_map/ppermute | solution.py:44
  265.7 24.9 %collective-permute-start.42 = (bf16[9,24,768]{2,1,0:T(8,128)(2,1)S(1)}, bf16[9,24,768]{2,1,0:T(8,128)(2,1)S(1)}, u32[]{:S(2)}, u32[]{:S(2)}) collective-permute-start(bf16[9,24,768]{2,1,0:T(8,128)(2,1)S(1)} %get-tuple-element.116), channel_id=1, source_target_pairs={{0,4},{1,5},{2,6},{3,7},{4,0},{5,1},{6,2},{7,3},{8,12},{9,13},{10,... | collective-permute-start | bytes 995336 | tf_op jit(solution)/shard_map/ppermute | solution.py:34
  266.3 24.3 %collective-permute-start.43 = (bf16[9,24,768]{2,1,0:T(8,128)(2,1)S(1)}, bf16[9,24,768]{2,1,0:T(8,128)(2,1)S(1)}, u32[]{:S(2)}, u32[]{:S(2)}) collective-permute-start(bf16[9,24,768]{2,1,0:T(8,128)(2,1)S(1)} %get-tuple-element.117), channel_id=1, source_target_pairs={{0,6},{1,7},{2,0},{3,1},{4,2},{5,3},{6,4},{7,5},{8,14},{9,15},{10,... | collective-permute-start | bytes 995336 | tf_op jit(solution)/shard_map/ppermute | solution.py:34
  270.1 20.8 %collective-permute-start.35 = (bf16[4,32,1152]{2,1,0:T(8,128)(2,1)S(1)}, bf16[4,32,1152]{2,1,0:T(8,128)(2,1)}, u32[]{:S(2)}, u32[]{:S(2)}) collective-permute-start(bf16[4,32,1152]{2,1,0:T(8,128)(2,1)S(1)} %get-tuple-element.118), channel_id=1, source_target_pairs={{0,8},{8,0},{16,24},{24,16},{1,9},{9,1},{17,25},{25,17},{2,10},{10... | collective-permute-start | bytes 884744 | tf_op jit(solution)/shard_map/ppermute | solution.py:44
  270.9 20.0 %collective-permute-start.36 = (bf16[4,32,1152]{2,1,0:T(8,128)(2,1)}, bf16[4,32,1152]{2,1,0:T(8,128)(2,1)S(1)}, u32[]{:S(2)}, u32[]{:S(2)}) collective-permute-start(bf16[4,32,1152]{2,1,0:T(8,128)(2,1)} %get-tuple-element.120), channel_id=1, source_target_pairs={{0,16},{8,24},{16,0},{24,8},{1,17},{9,25},{17,1},{25,9},{2,18},{10... | collective-permute-start | bytes 884744 | tf_op jit(solution)/shard_map/ppermute | solution.py:44
  (83 other events, 580.6 us)

commit v8 on v7

--- a/solution.py
+++ b/solution.py
@@ -1099,7 +1099,7 @@
     (grad_in_part,) = norm1_back(own_normed1.astype(F32).reshape(tokens, width))
     grad_inputs = (grad_middle + grad_in_part).astype(BF16).reshape(inputs.shape)
 
-    grad_qkv = gate(grad_qkv, tower_b)
+    grad_qkv = gate(grad_qkv, first_sums)
     long_rows = sequence[:, :block].astype(F32).reshape(count * block, width)
     _, norm1_long_back = jax.vjp(lambda g, b: norm_affine(long_rows, g, b), gain1, bias1)
     grad_gain1, grad_bias1 = norm1_long_back(grad_normed1)

time: 324 us -> 310 us (0.957)
  starting transfers between devices: 69 us -> 62.6 us
  waiting for transfers between devices: 103 us -> 96.7 us
    ppermute x18, waiting for transfers between devices: 36.7 us -> 29.7 us  [swap_dp(): return lax.ppermute(value, 'dp', [(i, i ^ bit) for i in range(size)])]
    ppermute x10, starting transfers between devices: 23.9 us -> 18 us  [swap_z(): lax.ppermute(value, 'seq', [(i, i ^ CORES * bit) for i in range(size)])]
    ppermute x9, waiting for transfers between devices: 23.1 us -> 18.7 us  [shift_z(): lax.ppermute(value, 'seq', [(i, (i + CORES * step) % size) for i in range...]
    ppermute x10, waiting for transfers between devices: 32.5 us -> 35.9 us  [swap_z(): lax.ppermute(value, 'seq', [(i, i ^ CORES * bit) for i in range(size)])]
    unnamed x120 -> x122, local copies, waits for them, and re-layouts: 14.6 us -> 13.1 us
  transfers between devices with their start and end apart: 46 -> 46, of which waited for: 17 -> 16; matrix products, arithmetic and copies ran while one was open for 17% -> 22% of each run, Pallas kernels for 8% -> 9%
where the time goes in v8:
time: 310 us; the launch traced here: 305 us
  waiting for transfers between devices  96.7 us (31%)
  starting transfers between devices  62.6 us (20%)
  Pallas kernels  52.8 us (17%)
  other arithmetic  43.7 us (14%)
  local copies, waits for them, and re-layouts  42.9 us (14%)
  matrix products  3.91 us (1%)
    ppermute x10, waiting for transfers between devices, swap_z(): lax.ppermute(value, 'seq', [(i, i ^ CORES * bit) for i in range(size)])  35.9 us
    ppermute x18, waiting for transfers between devices, swap_dp(): return lax.ppermute(value, 'dp', [(i, i ^ bit) for i in range(size)])  29.7 us
    ppermute x18, starting transfers between devices, swap_dp(): return lax.ppermute(value, 'dp', [(i, i ^ bit) for i in range(size)])  21.3 us
    ppermute x9, waiting for transfers between devices, shift_z(): lax.ppermute(value, 'seq', [(i, (i + CORES * step) % size) for i in range...  18.7 us
    ppermute x10, starting transfers between devices, swap_z(): lax.ppermute(value, 'seq', [(i, i ^ CORES * bit) for i in range(size)])  18 us
    another operation x19, other arithmetic, ordered(): return jnp.stack([first, second], axis)  16.6 us
    ppermute x9, starting transfers between devices, shift_z(): lax.ppermute(value, 'seq', [(i, (i + CORES * step) % size) for i in range...  14.1 us
    pallas_call x1, Pallas kernels, middle_block(): pl.pallas_call(functools.partial(middle_kernel, groups), out_shape=[shape...  13.8 us
  transfers between devices with their start and end apart: 46, of which 16 were waited for; matrix products, arithmetic and copies ran while one was open for 22% of the time, Pallas kernels for 9%

profile of v8, /device:TPU:0, one launch (start us, length us, event | category | flops | bytes accessed | tf_op | source)
XLA Modules:
  0.0 304.5 jit_solution(3021812803452539251)
XLA Ops:
  5.3 4.1 %collective-permute-start.7 = (bf16[144,768]{1,0:T(8,128)(2,1)S(1)}, bf16[144,768]{1,0:T(8,128)(2,1)S(1)}, u32[]{:S(2)}, u32[]{:S(2)}) collective-permute-start(bf16[144,768]{1,0:T(8,128)(2,1)S(1)} %dynamic-slice_bitcast_fusion.9), channel_id=1, source_target_pairs={{0,4},{1,5},{2,6},{3,7},{4,0},{5,1},{6,2},{7,3},{8,12},{9,13},{10,... | collective-permute-start | bytes 663560 | tf_op jit(solution)/shard_map/ppermute | solution.py:67
  18.5 6.6 %collective-permute-done.4.refs_2_ = bf16[32,1152]{1,0:T(8,128)(2,1)S(1)} collective-permute-done((bf16[32,1152]{1,0:T(8,128)(2,1)S(1)}, bf16[32,1152]{1,0:T(8,128)(2,1)S(1)}, u32[]{:S(2)}, u32[]{:S(2)}) %collective-permute-start.4) | collective-permute-done | bytes 73760 | tf_op jit(solution)/shard_map/ppermute | solution.py:67
  30.9 3.4 %collective-permute-start = (bf16[5,24,768]{2,1,0:T(8,128)(2,1)S(1)}, bf16[5,24,768]{2,1,0:T(8,128)(2,1)S(1)}, u32[]{:S(2)}, u32[]{:S(2)}) collective-permute-start(bf16[5,24,768]{2,1,0:T(8,128)(2,1)S(1)} %copy-done.7), channel_id=1, source_target_pairs={{0,6},{1,7},{2,0},{3,1},{4,2},{5,3},{6,4},{7,5},{8,14},{9,15},{10,... | collective-permute-start | bytes 552968 | tf_op jit(solution)/shard_map/ppermute | solution.py:34
  37.3 9.1 %collective-permute-done.8 = bf16[2,144,768]{2,1,0:T(8,128)(2,1)S(1)} collective-permute-done((bf16[2,144,768]{2,1,0:T(8,128)(2,1)S(1)}, bf16[2,144,768]{2,1,0:T(8,128)(2,1)S(1)}, u32[]{:S(2)}, u32[]{:S(2)}) %collective-permute-start.8) | collective-permute-done | bytes 442400 | tf_op jit(solution)/shard_map/ppermute | solution.py:67
  49.2 3.6 %collective-permute-start.2 = (bf16[5,24,768]{2,1,0:T(8,128)(2,1)S(1)}, bf16[5,24,768]{2,1,0:T(8,128)(2,1)S(1)}, u32[]{:S(2)}, u32[]{:S(2)}) collective-permute-start(bf16[5,24,768]{2,1,0:T(8,128)(2,1)S(1)} %copy-done.7), channel_id=1, source_target_pairs={{0,2},{1,3},{2,4},{3,5},{4,6},{5,7},{6,0},{7,1},{8,10},{9,11},{10,... | collective-permute-start | bytes 552968 | tf_op jit(solution)/shard_map/ppermute | solution.py:34
  52.8 7.7 %collective-permute-done.2.refs_3_ = bf16[5,24,768]{2,1,0:T(8,128)(2,1)S(1)} collective-permute-done((bf16[5,24,768]{2,1,0:T(8,128)(2,1)S(1)}, bf16[5,24,768]{2,1,0:T(8,128)(2,1)S(1)}, u32[]{:S(2)}, u32[]{:S(2)}) %collective-permute-start.2) | collective-permute-done | bytes 184352 | tf_op jit(solution)/shard_map/ppermute | solution.py:34
  71.8 11.3 %shard_map.261 = (bf16[512,384]{1,0:T(8,128)(2,1)}, f32[3,1024]{1,0:T(4,128)S(1)}, bf16[1024,576]{1,0:T(8,128)(2,1)S(1)}, bf16[1024,768]{1,0:T(8,128)(2,1)S(1)}, f32[1,1024]{1,0:T(1,128)S(1)}) custom-call(bf16[8,144,768]{2,1,0:T(8,128)(2,1)} %bitcast.241, bf16[768,576]{1,0:T(8,128)(2,1)S(1)} %get-tuple-element.60.weight, ...), custom_call_target="tpu_custom_call" | custom-call | flops 1 | bytes 1 | tf_op jit(solution)/shard_map/pallas_call | solution.py:919
  85.3 4.5 %all-to-all-start = ((bf16[8,64,384]{2,1,0:T(8,128)(2,1)}), bf16[8,64,384]{2,1,0:T(8,128)(2,1)S(1)}, u32[]{:S(2)}, u32[]{:S(2)}) async-start(bf16[8,64,384]{2,1,0:T(8,128)(2,1)} %bitcast.24), calls=%async_computation | async-start | bytes 786432 | tf_op jit(solution)/shard_map/all_to_all | solution.py:204
  97.1 5.2 %all-to-all-done.refs_1_.attended = bf16[8,64,384]{2,1,0:T(8,128)(2,1)S(1)} async-done(((bf16[8,64,384]{2,1,0:T(8,128)(2,1)}), bf16[8,64,384]{2,1,0:T(8,128)(2,1)S(1)}, u32[]{:S(2)}, u32[]{:S(2)}) %all-to-all-start) | async-done | bytes 393248 | tf_op jit(solution)/shard_map/all_to_all | solution.py:204
  109.9 5.7 %collective-permute-done.14 = bf16[5,2,2,24,768]{4,3,2,0,1:T(8,128)(2,1)} collective-permute-done((bf16[5,2,2,24,768]{4,3,2,0,1:T(8,128)(2,1)}, bf16[5,2,2,24,768]{4,3,2,0,1:T(8,128)(2,1)}, u32[]{:S(2)}, u32[]{:S(2)}) %collective-permute-start.14) | collective-permute-done | bytes 737312 | tf_op jit(solution)/shard_map/ppermute | solution.py:44
  129.0 3.5 %collective-permute-done.24 = bf16[2,2,96,768]{3,2,1,0:T(8,128)(2,1)} collective-permute-done((bf16[2,2,96,768]{3,2,1,0:T(8,128)(2,1)}, bf16[2,2,96,768]{3,2,1,0:T(8,128)(2,1)}, u32[]{:S(2)}, u32[]{:S(2)}) %collective-permute-start.24) | collective-permute-done | bytes 589856 | tf_op jit(solution)/shard_map/ppermute | solution.py:44
  134.3 4.5 %collective-permute-done.25.other2 = bf16[16,96,768]{2,1,0:T(8,128)(2,1)S(1)} collective-permute-done((bf16[16,96,768]{2,1,0:T(8,128)(2,1)S(1)}, bf16[16,96,768]{2,1,0:T(8,128)(2,1)S(1)}, u32[]{:S(2)}, u32[]{:S(2)}) %collective-permute-start.25) | collective-permute-done | bytes 2359328 | tf_op jit(solution)/shard_map/ppermute | solution.py:39
  141.1 13.8 %shard_map.270 = (bf16[2,128,768]{2,1,0:T(8,128)(2,1)}, f32[256,768]{1,0:T(8,128)S(1)}, bf16[8,64,384]{2,1,0:T(8,128)(2,1)}, bf16[256,768]{1,0:T(8,128)(2,1)S(1)...) custom-call(bf16[5,384,768]{2,1,0:T(8,128)(2,1)} %bitcast.247, ...), custom_call_target="tpu_custom_call" | custom-call | flops 1 | bytes 1 | tf_op jit(solution)/shard_map/pallas_call | solution.py:679
  157.2 8.4 %shard_map.271 = (bf16[9,384,768]{2,1,0:T(8,128)(2,1)}, bf16[9,384,768]{2,1,0:T(8,128)(2,1)}) custom-call(bf16[256,768]{1,0:T(8,128)(2,1)S(1)} %get-tuple-element.79.placed_a, bf16[256,768]{1,0:T(8,128)(2,1)S(1)} %get-tuple-element.80.placed_n, bf16[256,3072]{1,0:T(8,128)(2,1)S(1)} %copy-done.9, bf16[256,3072]{1,0:T(8,128)(2,1)} %get-tuple-element.82.grad_pre, ...), custom_call_target="tpu_custom_call" | custom-call | flops 1 | bytes 1 | tf_op jit(solution)/shard_map/pallas_call | solution.py:755
  167.6 4.4 %all-to-all-start.1 = ((bf16[8,64,384]{2,1,0:T(8,128)(2,1)}), bf16[8,64,384]{2,1,0:T(8,128)(2,1)S(1)}, u32[]{:S(2)}, u32[]{:S(2)}) async-start(bf16[8,64,384]{2,1,0:T(8,128)(2,1)} %get-tuple-element.76), calls=%async_computation.1 | async-start | bytes 786432 | tf_op jit(solution)/shard_map/all_to_all | solution.py:204
  174.7 5.5 %add_convert_fusion = bf16[9,384,768]{2,1,0:T(8,128)(2,1)S(1)} fusion(bf16[9,384,768]{2,1,0:T(8,128)(2,1)} %collective-permute-done.26, bf16[9,384,768]{2,1,0:T(8,128)(2,1)} %get-tuple-element.84), kind=kLoop, calls=%fused_computation | loop fusion | flops 10616832 | bytes 15925248 | tf_op jit(solution)/shard_map/convert_element_type | solution.py:96
  188.6 8.8 %shard_map.272.refs_2_.refs_0_ = bf16[1024,576]{1,0:T(8,128)(2,1)S(1)} custom-call(bf16[1024,576]{1,0:T(8,128)(2,1)S(1)} %get-tuple-element.75.whole, bf16[512,384]{1,0:T(8,128)(2,1)S(1)} %bitcast.240, f32[3,1024]{1,0:T(4,128)S(1)} %get-tuple-element.77.stats, f32[1,1024]{1,0:T(1,128)S(1)} %get-tuple-element.78.ids, ...), custom_call_target="tpu_custom_call" | custom-call | flops 1 | bytes 1 | tf_op jit(solution)/shard_map/pallas_call | solution.py:939
  200.4 13.1 %collective-permute-done.29.refs_1_ = bf16[9,2,2,24,768]{4,3,2,1,0:T(8,128)(2,1)} collective-permute-done((bf16[9,2,2,24,768]{4,3,2,1,0:T(8,128)(2,1)S(1)}, bf16[9,2,2,24,768]{4,3,2,1,0:T(8,128)(2,1)}, u32[]{:S(2)}, u32[]{:S(2)}) %collective-permute-start.29) | collective-permute-done | bytes 1327136 | tf_op jit(solution)/shard_map/ppermute | solution.py:44
  232.6 6.0 %collective-permute-done.30 = bf16[2,128,768]{2,1,0:T(8,128)(2,1)S(1)} collective-permute-done((bf16[2,128,768]{2,1,0:T(8,128)(2,1)S(1)}, bf16[2,128,768]{2,1,0:T(8,128)(2,1)S(1)}, u32[]{:S(2)}, u32[]{:S(2)}) %collective-permute-start.30) | collective-permute-done | bytes 393248 | tf_op jit(solution)/shard_map/ppermute | solution.py:67
  242.9 5.4 %collective-permute-done.31 = bf16[128,768]{1,0:T(8,128)(2,1)S(1)} collective-permute-done((bf16[128,768]{1,0:T(8,128)(2,1)S(1)}, bf16[128,768]{1,0:T(8,128)(2,1)S(1)}, u32[]{:S(2)}, u32[]{:S(2)}) %collective-permute-start.31) | collective-permute-done | bytes 196640 | tf_op jit(solution)/shard_map/ppermute | solution.py:67
  259.3 3.4 %collective-permute-start.42 = (bf16[9,24,768]{2,1,0:T(8,128)(2,1)}, bf16[9,24,768]{2,1,0:T(8,128)(2,1)}, u32[]{:S(2)}, u32[]{:S(2)}) collective-permute-start(bf16[9,24,768]{2,1,0:T(8,128)(2,1)} %get-tuple-element.116), channel_id=1, source_target_pairs={{0,4},{1,5},{2,6},{3,7},{4,0},{5,1},{6,2},{7,3},{8,12},{9,13},{10,... | collective-permute-start | bytes 995336 | tf_op jit(solution)/shard_map/ppermute | solution.py:34
  269.7 3.3 %collective-permute-start.39 = (bf16[32,1152]{1,0:T(8,128)(2,1)S(1)}, bf16[32,1152]{1,0:T(8,128)(2,1)S(1)}, u32[]{:S(2)}, u32[]{:S(2)}) collective-permute-start(bf16[32,1152]{1,0:T(8,128)(2,1)S(1)} %get-tuple-element.142), channel_id=1, source_target_pairs={{0,4},{1,5},{2,6},{3,7},{4,0},{5,1},{6,2},{7,3},{8,12},{9,13},{10,... | collective-permute-start | bytes 221192 | tf_op jit(solution)/shard_map/ppermute | solution.py:67
  273.8 10.9 %collective-permute-done.42 = bf16[9,24,768]{2,1,0:T(8,128)(2,1)} collective-permute-done((bf16[9,24,768]{2,1,0:T(8,128)(2,1)}, bf16[9,24,768]{2,1,0:T(8,128)(2,1)}, u32[]{:S(2)}, u32[]{:S(2)}) %collective-permute-start.42) | collective-permute-done | bytes 331808 | tf_op jit(solution)/shard_map/ppermute | solution.py:34
  286.3 8.7 %collective-permute-done.39.refs_2_ = bf16[32,1152]{1,0:T(8,128)(2,1)S(1)} collective-permute-done((bf16[32,1152]{1,0:T(8,128)(2,1)S(1)}, bf16[32,1152]{1,0:T(8,128)(2,1)S(1)}, u32[]{:S(2)}, u32[]{:S(2)}) %collective-permute-start.39) | collective-permute-done | bytes 73760 | tf_op jit(solution)/shard_map/ppermute | solution.py:67
  (312 shorter events, 141.7 us)
Async XLA Ops:
  5.3 22.2 %collective-permute-start.7 = (bf16[144,768]{1,0:T(8,128)(2,1)S(1)}, bf16[144,768]{1,0:T(8,128)(2,1)S(1)}, u32[]{:S(2)}, u32[]{:S(2)}) collective-permute-start(bf16[144,768]{1,0:T(8,128)(2,1)S(1)} %dynamic-slice_bitcast_fusion.9), channel_id=1, source_target_pairs={{0,4},{1,5},{2,6},{3,7},{4,0},{5,1},{6,2},{7,3},{8,12},{9,13},{10,... | collective-permute-start | bytes 663560 | tf_op jit(solution)/shard_map/ppermute | solution.py:67
  29.3 17.1 %collective-permute-start.8 = (bf16[2,144,768]{2,1,0:T(8,128)(2,1)S(1)}, bf16[2,144,768]{2,1,0:T(8,128)(2,1)S(1)}, u32[]{:S(2)}, u32[]{:S(2)}) collective-permute-start(bf16[2,144,768]{2,1,0:T(8,128)(2,1)S(1)} %pad_maximum_fusion.8), channel_id=1, source_target_pairs={{0,2},{1,3},{2,0},{3,1},{4,6},{5,7},{6,4},{7,5},{8,10},{9,11},{10,... | collective-permute-start | bytes 1327112 | tf_op jit(solution)/shard_map/ppermute | solution.py:67
  30.9 18.2 %collective-permute-start = (bf16[5,24,768]{2,1,0:T(8,128)(2,1)S(1)}, bf16[5,24,768]{2,1,0:T(8,128)(2,1)S(1)}, u32[]{:S(2)}, u32[]{:S(2)}) collective-permute-start(bf16[5,24,768]{2,1,0:T(8,128)(2,1)S(1)} %copy-done.7), channel_id=1, source_target_pairs={{0,6},{1,7},{2,0},{3,1},{4,2},{5,3},{6,4},{7,5},{8,14},{9,15},{10,... | collective-permute-start | bytes 552968 | tf_op jit(solution)/shard_map/ppermute | solution.py:34
  34.2 27.1 %collective-permute-start.10 = (bf16[4,32,1152]{2,1,0:T(8,128)(2,1)S(1)}, bf16[4,32,1152]{2,1,0:T(8,128)(2,1)S(1)}, u32[]{:S(2)}, u32[]{:S(2)}) collective-permute-start(bf16[4,32,1152]{2,1,0:T(8,128)(2,1)S(1)} %copy-done.6), channel_id=1, source_target_pairs={{0,8},{8,0},{16,24},{24,16},{1,9},{9,1},{17,25},{25,17},{2,10},{10... | collective-permute-start | bytes 884744 | tf_op jit(solution)/shard_map/ppermute | solution.py:44
  35.7 25.6 %collective-permute-start.11 = (bf16[4,32,1152]{2,1,0:T(8,128)(2,1)S(1)}, bf16[4,32,1152]{2,1,0:T(8,128)(2,1)S(1)}, u32[]{:S(2)}, u32[]{:S(2)}) collective-permute-start(bf16[4,32,1152]{2,1,0:T(8,128)(2,1)S(1)} %copy-done.6), channel_id=1, source_target_pairs={{0,16},{8,24},{16,0},{24,8},{1,17},{9,25},{17,1},{25,9},{2,18},{10... | collective-permute-start | bytes 884744 | tf_op jit(solution)/shard_map/ppermute | solution.py:44
  49.1 19.0 %collective-permute-start.9 = (bf16[2,2,144,768]{3,2,1,0:T(8,128)(2,1)S(1)}, bf16[2,2,144,768]{3,2,1,0:T(8,128)(2,1)}, u32[]{:S(2)}, u32[]{:S(2)}) collective-permute-start(bf16[2,2,144,768]{3,2,1,0:T(8,128)(2,1)S(1)} %pad_maximum_fusion.3.refs_5_.refs_1_), channel_id=1, source_target_pairs={{0,1},{1,0},{2,3},{3,2},{4,5},{5,4},{6,7},{7,6},{8,9},{9,8},{10,11... | collective-permute-start | bytes 2654216 | tf_op jit(solution)/shard_map/ppermute | solution.py:39
  63.5 27.8 %collective-permute-start.6 = (bf16[5,2,24,768]{3,2,1,0:T(8,128)(2,1)S(1)}, bf16[5,2,24,768]{3,2,1,0:T(8,128)(2,1)}, u32[]{:S(2)}, u32[]{:S(2)}) collective-permute-start(bf16[5,2,24,768]{3,2,1,0:T(8,128)(2,1)S(1)} %get-tuple-element.56.refs_4_.after), channel_id=1, source_target_pairs={{0,8},{8,0},{16,24},{24,16},{1,9},{9,1},{17,25},{25,17},{2,10},{10... | collective-permute-start | bytes 1105928 | tf_op jit(solution)/shard_map/ppermute | solution.py:44
  64.0 29.8 %collective-permute-start.15 = (bf16[5,2,24,768]{3,2,1,0:T(8,128)(2,1)}, bf16[5,2,24,768]{3,2,1,0:T(8,128)(2,1)}, u32[]{:S(2)}, u32[]{:S(2)}) collective-permute-start(bf16[5,2,24,768]{3,2,1,0:T(8,128)(2,1)} %get-tuple-element.65), channel_id=1, source_target_pairs={{0,16},{8,24},{16,0},{24,8},{1,17},{9,25},{17,1},{25,9},{2,18},{10... | collective-permute-start | bytes 1105928 | tf_op jit(solution)/shard_map/ppermute | solution.py:44
  64.6 19.8 %collective-permute-start.18 = (bf16[96,768]{1,0:T(8,128)(2,1)}, bf16[96,768]{1,0:T(8,128)(2,1)S(1)}, u32[]{:S(2)}, u32[]{:S(2)}) collective-permute-start(bf16[96,768]{1,0:T(8,128)(2,1)} %shard_map.266.refs_0_), channel_id=1, source_target_pairs={{0,6},{1,7},{2,0},{3,1},{4,2},{5,3},{6,4},{7,5},{8,14},{9,15},{10,... | collective-permute-start | bytes 442376 | tf_op jit(solution)/shard_map/ppermute | solution.py:34
  67.0 17.4 %collective-permute-start.19 = (bf16[96,768]{1,0:T(8,128)(2,1)}, bf16[96,768]{1,0:T(8,128)(2,1)S(1)}, u32[]{:S(2)}, u32[]{:S(2)}) collective-permute-start(bf16[96,768]{1,0:T(8,128)(2,1)} %shard_map.266.refs_0_), channel_id=1, source_target_pairs={{0,4},{1,5},{2,6},{3,7},{4,0},{5,1},{6,2},{7,3},{8,12},{9,13},{10,... | collective-permute-start | bytes 442376 | tf_op jit(solution)/shard_map/ppermute | solution.py:34
  89.8 17.4 %collective-permute-start.23 = (bf16[2,96,768]{2,1,0:T(8,128)(2,1)S(1)}, bf16[2,96,768]{2,1,0:T(8,128)(2,1)}, u32[]{:S(2)}, u32[]{:S(2)}) collective-permute-start(bf16[2,96,768]{2,1,0:T(8,128)(2,1)S(1)} %get-tuple-element.67), channel_id=1, source_target_pairs={{0,16},{8,24},{16,0},{24,8},{1,17},{9,25},{17,1},{25,9},{2,18},{10... | collective-permute-start | bytes 884744 | tf_op jit(solution)/shard_map/ppermute | solution.py:44
  93.3 22.2 %collective-permute-start.14 = (bf16[5,2,2,24,768]{4,3,2,0,1:T(8,128)(2,1)}, bf16[5,2,2,24,768]{4,3,2,0,1:T(8,128)(2,1)}, u32[]{:S(2)}, u32[]{:S(2)}) collective-permute-start(bf16[5,2,2,24,768]{4,3,2,0,1:T(8,128)(2,1)} %pad_maximum_fusion.4), channel_id=1, source_target_pairs={{0,16},{8,24},{16,0},{24,8},{1,17},{9,25},{17,1},{25,9},{2,18},{10... | collective-permute-start | bytes 2211848 | tf_op jit(solution)/shard_map/ppermute | solution.py:44
  96.0 25.2 %collective-permute-start.16 = (bf16[5,2,2,24,768]{4,3,2,1,0:T(8,128)(2,1)}, bf16[5,2,2,24,768]{4,3,2,1,0:T(8,128)(2,1)}, u32[]{:S(2)}, u32[]{:S(2)}) collective-permute-start(bf16[5,2,2,24,768]{4,3,2,1,0:T(8,128)(2,1)} %pad_maximum_fusion.5), channel_id=1, source_target_pairs={{0,8},{8,0},{16,24},{24,16},{1,9},{9,1},{17,25},{25,17},{2,10},{10... | collective-permute-start | bytes 2211848 | tf_op jit(solution)/shard_map/ppermute | solution.py:44
  105.7 22.0 %collective-permute-start.22 = (bf16[2,2,96,768]{3,2,1,0:T(8,128)(2,1)}, bf16[2,2,96,768]{3,2,1,0:T(8,128)(2,1)}, u32[]{:S(2)}, u32[]{:S(2)}) collective-permute-start(bf16[2,2,96,768]{3,2,1,0:T(8,128)(2,1)} %pad_maximum_fusion.6), channel_id=1, source_target_pairs={{0,16},{8,24},{16,0},{24,8},{1,17},{9,25},{17,1},{25,9},{2,18},{10... | collective-permute-start | bytes 1769480 | tf_op jit(solution)/shard_map/ppermute | solution.py:44
  167.6 21.0 %all-to-all-start.1 = ((bf16[8,64,384]{2,1,0:T(8,128)(2,1)}), bf16[8,64,384]{2,1,0:T(8,128)(2,1)S(1)}, u32[]{:S(2)}, u32[]{:S(2)}) async-start(bf16[8,64,384]{2,1,0:T(8,128)(2,1)} %get-tuple-element.76), calls=%async_computation.1 | async-start | bytes 786432 | tf_op jit(solution)/shard_map/all_to_all | solution.py:204
  182.2 31.3 %collective-permute-start.29 = (bf16[9,2,2,24,768]{4,3,2,1,0:T(8,128)(2,1)S(1)}, bf16[9,2,2,24,768]{4,3,2,1,0:T(8,128)(2,1)}, u32[]{:S(2)}, u32[]{:S(2)}) collective-permute-start(bf16[9,2,2,24,768]{4,3,2,1,0:T(8,128)(2,1)S(1)} %get-tuple-element.104.after2), channel_id=1, source_target_pairs={{0,8},{8,0},{16,24},{24,16},{1,9},{9,1},{17,25},{25,17},{2,10},{10... | collective-permute-start | bytes 3981320 | tf_op jit(solution)/shard_map/ppermute | solution.py:44
  185.2 31.2 %collective-permute-start.28 = (bf16[9,2,2,24,768]{4,3,2,1,0:T(8,128)(2,1)}, bf16[9,2,2,24,768]{4,3,2,1,0:T(8,128)(2,1)}, u32[]{:S(2)}, u32[]{:S(2)}) collective-permute-start(bf16[9,2,2,24,768]{4,3,2,1,0:T(8,128)(2,1)} %get-tuple-element.106.after1), channel_id=1, source_target_pairs={{0,16},{8,24},{16,0},{24,8},{1,17},{9,25},{17,1},{25,9},{2,18},{10... | collective-permute-start | bytes 3981320 | tf_op jit(solution)/shard_map/ppermute | solution.py:44
  200.4 26.9 %collective-permute-start.27 = (bf16[2,2,128,768]{3,2,1,0:T(8,128)(2,1)}, bf16[2,2,128,768]{3,2,1,0:T(8,128)(2,1)}, u32[]{:S(2)}, u32[]{:S(2)}) collective-permute-start(bf16[2,2,128,768]{3,2,1,0:T(8,128)(2,1)} %dynamic-slice_bitcast_fusion.2), channel_id=1, source_target_pairs={{0,1},{1,0},{2,3},{3,2},{4,5},{5,4},{6,7},{7,6},{8,9},{9,8},{10,11... | collective-permute-start | bytes 2359304 | tf_op jit(solution)/shard_map/ppermute | solution.py:39
  220.6 34.7 %collective-permute-start.34 = (bf16[9,2,24,768]{3,2,0,1:T(8,128)(2,1)}, bf16[9,2,24,768]{3,2,0,1:T(8,128)(2,1)}, u32[]{:S(2)}, u32[]{:S(2)}) collective-permute-start(bf16[9,2,24,768]{3,2,0,1:T(8,128)(2,1)} %dynamic-slice_bitcast_fusion.4), channel_id=1, source_target_pairs={{0,8},{8,0},{16,24},{24,16},{1,9},{9,1},{17,25},{25,17},{2,10},{10... | collective-permute-start | bytes 1990664 | tf_op jit(solution)/shard_map/ppermute | solution.py:44
  224.2 32.4 %collective-permute-start.35 = (bf16[9,2,24,768]{3,2,0,1:T(8,128)(2,1)}, bf16[9,2,24,768]{3,2,0,1:T(8,128)(2,1)}, u32[]{:S(2)}, u32[]{:S(2)}) collective-permute-start(bf16[9,2,24,768]{3,2,0,1:T(8,128)(2,1)} %dynamic-slice_bitcast_fusion.3), channel_id=1, source_target_pairs={{0,16},{8,24},{16,0},{24,8},{1,17},{9,25},{17,1},{25,9},{2,18},{10... | collective-permute-start | bytes 1990664 | tf_op jit(solution)/shard_map/ppermute | solution.py:44
  259.3 25.4 %collective-permute-start.42 = (bf16[9,24,768]{2,1,0:T(8,128)(2,1)}, bf16[9,24,768]{2,1,0:T(8,128)(2,1)}, u32[]{:S(2)}, u32[]{:S(2)}) collective-permute-start(bf16[9,24,768]{2,1,0:T(8,128)(2,1)} %get-tuple-element.116), channel_id=1, source_target_pairs={{0,4},{1,5},{2,6},{3,7},{4,0},{5,1},{6,2},{7,3},{8,12},{9,13},{10,... | collective-permute-start | bytes 995336 | tf_op jit(solution)/shard_map/ppermute | solution.py:34
  264.0 20.8 %collective-permute-start.43 = (bf16[9,24,768]{2,1,0:T(8,128)(2,1)}, bf16[9,24,768]{2,1,0:T(8,128)(2,1)}, u32[]{:S(2)}, u32[]{:S(2)}) collective-permute-start(bf16[9,24,768]{2,1,0:T(8,128)(2,1)} %get-tuple-element.117), channel_id=1, source_target_pairs={{0,6},{1,7},{2,0},{3,1},{4,2},{5,3},{6,4},{7,5},{8,14},{9,15},{10,... | collective-permute-start | bytes 995336 | tf_op jit(solution)/shard_map/ppermute | solution.py:34
  269.7 25.3 %collective-permute-start.39 = (bf16[32,1152]{1,0:T(8,128)(2,1)S(1)}, bf16[32,1152]{1,0:T(8,128)(2,1)S(1)}, u32[]{:S(2)}, u32[]{:S(2)}) collective-permute-start(bf16[32,1152]{1,0:T(8,128)(2,1)S(1)} %get-tuple-element.142), channel_id=1, source_target_pairs={{0,4},{1,5},{2,6},{3,7},{4,0},{5,1},{6,2},{7,3},{8,12},{9,13},{10,... | collective-permute-start | bytes 221192 | tf_op jit(solution)/shard_map/ppermute | solution.py:67
  273.1 21.9 %collective-permute-start.40 = (bf16[32,1152]{1,0:T(8,128)(2,1)S(1)}, bf16[32,1152]{1,0:T(8,128)(2,1)S(1)}, u32[]{:S(2)}, u32[]{:S(2)}) collective-permute-start(bf16[32,1152]{1,0:T(8,128)(2,1)S(1)} %get-tuple-element.141), channel_id=1, source_target_pairs={{0,6},{1,7},{2,4},{3,5},{4,2},{5,3},{6,0},{7,1},{8,14},{9,15},{10,... | collective-permute-start | bytes 221192 | tf_op jit(solution)/shard_map/ppermute | solution.py:67
  (84 other events, 594.8 us)
